TPU v7x, 512 devices: a whole 4x8x8 slice. The times are simulated.
512 devices in a mesh: dp: 32 (over z, x), proto: 16 (over y, core).
Axes of the slice: x: 4, y: 8, z: 8, core: 2. Of those that a mesh axis runs over, the one named last changes fastest.
Arguments:
- student_patches: bfloat16 [512, 256, 256], P(('dp', 'proto')), may hold values from -9 to 9
- teacher_patches: bfloat16 [512, 256, 256], P(('dp', 'proto')), may hold values from -9 to 9
- mask_order: int32 [512, 256], P(('dp', 'proto')), may hold values from 0 to 255, each once within a row
- counts: int32 [32, 16], P('dp', 'proto'), may hold values from 1 to 72, 384 in all within a row
- student_protos: bfloat16 [256, 65536], P(None, 'proto'), may hold values from -0.375 to 0.375
- teacher_protos: bfloat16 [256, 65536], P(None, 'proto'), may hold values from -0.375 to 0.375
Outputs:
- student_grad: bfloat16 [512, 256, 256], P(('dp', 'proto'))
- image_loss: float32 [32, 16], P('dp', 'proto')
Inputs may be any that keep to these rules, and one draw needn't show every extreme that they name: Each dp index's 16 counts sum to 384, and the largest of them is 72. `mask_order`: each image's row names every patch once; its first counts entries are that image's masked patches.
All inputs are finite; a program needn't handle non-finite values. No bound on the sum of `counts` on one device may be relied on, other than what follows from the above.
Results may differ from a plain program's by a relative error of at most 0.02.
Values may be sent and summed in bfloat16 or wider, within the bound.
No kernel may reach another device: no remote copies, remote signals or barrier semaphores. Data moves between devices by JAX's collectives and lax.ppermute only.
A program may use at most 64 MiB of HBM per device.

v0:
```python
import jax
import jax.numpy as jnp
from jax import lax
from jax.sharding import PartitionSpec as P

MASK_DEV = 24
ITERS = 3
MOST = 72


teach_temp = 0.07
stud_temp = 0.1


def column_lse(values):
    highest = lax.pmax(jnp.max(values, axis=0), "dp")
    totals = lax.psum(jnp.sum(jnp.exp(values - highest[None, :]), axis=0), "dp")
    return highest + jnp.log(totals)


def row_lse(values):
    highest = lax.pmax(jnp.max(values, axis=1), "proto")
    totals = lax.psum(jnp.sum(jnp.exp(values - highest[:, None]), axis=1), "proto")
    return highest + jnp.log(totals)


def body(student_patches, teacher_patches, mask_order, counts, student_protos, teacher_protos):
    width = lax.axis_size("proto")
    own_index = lax.axis_index("proto")
    row_total = MASK_DEV * width
    slots = MOST
    group_sizes = lax.all_gather(counts, "proto", axis=1, tiled=True)[0]
    group_ends = jnp.cumsum(group_sizes)
    group_starts = group_ends - group_sizes
    peers = jnp.arange(width, dtype=jnp.int32)
    own_start = jnp.sum(jnp.where(peers == own_index, group_starts, 0))
    own_count = counts[0, 0]
    masked_order = mask_order[0, :slots]
    picked_student = student_patches[0][masked_order]
    picked_teacher = teacher_patches[0][masked_order]
    row_index = jnp.arange(row_total, dtype=jnp.int32)
    holder = jnp.sum((row_index[:, None] >= group_ends[None, :]).astype(jnp.int32), axis=1)
    member = holder[:, None] == peers[None, :]
    within = row_index - jnp.sum(jnp.where(member, group_starts[None, :], 0), axis=1)
    gathered_student, gathered_teacher = (
        lax.all_gather(picked_student, "proto", axis=0, tiled=True),
        lax.all_gather(picked_teacher, "proto", axis=0, tiled=True),
    )
    source = holder * slots + within
    student_rows = gathered_student[source]
    teacher_rows = gathered_teacher[source]
    teacher_logits = (
        jnp.dot(teacher_rows, teacher_protos, preferred_element_type=jnp.float32) / teach_temp
    )
    row_potential = jnp.zeros((row_total,), jnp.float32)
    for sweep in range(ITERS):
        col_potential = -column_lse(teacher_logits + row_potential[:, None])
        row_potential = -row_lse(teacher_logits + col_potential[None, :])
    target = jnp.exp(teacher_logits + col_potential[None, :] + row_potential[:, None])
    student_logits = (
        jnp.dot(student_rows, student_protos, preferred_element_type=jnp.float32) / stud_temp
    )
    weighted = jnp.sum(target * student_logits, axis=1)
    local_high = jnp.max(student_logits, axis=1)
    highest = lax.pmax(local_high, "proto")
    totals, products = lax.psum(
        (jnp.sum(jnp.exp(student_logits - highest[:, None]), axis=1), weighted), "proto"
    )
    student_lse = highest + jnp.log(totals)
    cross = student_lse - products
    own_loss = jnp.sum(jnp.where(holder == own_index, cross, 0.0)) / own_count.astype(jnp.float32)
    difference = ((jnp.exp(student_logits - student_lse[:, None]) - target) / stud_temp).astype(
        jnp.bfloat16
    )
    partial_grad = lax.dot_general(
        difference, student_protos, (((1,), (1,)), ((), ())), preferred_element_type=jnp.float32
    )
    slot_index = jnp.arange(slots, dtype=jnp.int32)
    gathered = lax.psum(partial_grad.astype(jnp.bfloat16), "proto").astype(jnp.float32)
    rows_back = gathered[jnp.clip(own_start + slot_index, 0, row_total - 1)]
    own_rows = jnp.where((slot_index < own_count)[:, None], rows_back, 0.0)
    student_grad = (
        jnp.zeros((student_patches.shape[1], student_patches.shape[2]), jnp.bfloat16)
        .at[masked_order]
        .set(own_rows.astype(jnp.bfloat16))
    )
    return (student_grad[None], own_loss.reshape(1, 1))


def solution(mesh):
    placed = (
        P(("dp", "proto"), None, None),
        P(("dp", "proto"), None, None),
        P(("dp", "proto"), None),
        P("dp", "proto"),
        P(None, "proto"),
        P(None, "proto"),
    )
    return jax.shard_map(
        body,
        mesh=mesh,
        in_specs=placed,
        out_specs=(P(("dp", "proto"), None, None), P("dp", "proto")),
        check_vma=False,
    )
```

profile of v0, /device:TPU:1, one launch (start us, length us, event | category | flops | bytes accessed | tf_op | source)
XLA Modules:
  0.0 1245.2 jit_solution(4539637210532057174)
XLA Ops:
  8.0 1.3 dynamic-slice
  9.3 0.7 bitcast_dynamic-update-slice_fusion
  10.0 12.3 all-reduce
  22.3 0.1 copy.10
  22.4 0.1 reduce
  22.5 0.1 convert_reduce_fusion
  22.6 0.7 fusion.8
  23.3 1.6 gather_fusion
  24.9 23.8 %all-gather = bf16[1152,256]{1,0:T(8,128)(2,1)S(1)} all-gather(bf16[72,256]{1,0:T(8,128)(2,1)S(1)} %gather_fusion), channel_id=2, replica_groups=mesh['dp'=32,'proto'=16] {'proto'}, dimensions={0}, use_global_device_ids=true | all-gather | bytes 626688 | tf_op jit(solution)/shard_map/all_gather | solution.py:46
  48.7 0.1 select_reduce_fusion
  48.8 1.6 gather_fusion.2
  50.4 16.1 %all-gather.1 = bf16[1152,256]{1,0:T(8,128)(2,1)S(1)} all-gather(bf16[72,256]{1,0:T(8,128)(2,1)S(1)} %gather_fusion.2), channel_id=3, replica_groups=mesh['dp'=32,'proto'=16] {'proto'}, dimensions={0}, use_global_device_ids=true | all-gather | bytes 626688 | tf_op jit(solution)/shard_map/all_gather | solution.py:47
  66.5 2.0 gather_fusion.1
  68.6 2.1 gather_fusion.3
  70.6 5.3 fusion.13
  75.9 118.1 %pmax.50 = f32[4096]{0:T(1024)S(1)} all-reduce(f32[4096]{0:T(1024)S(1)} %get-tuple-element.10), channel_id=1, replica_groups=mesh['dp'=32,'proto'=16] {'dp'}, use_global_device_ids=true, to_apply=%region_8.9 | all-reduce | flops 4096 | bytes 32768 | tf_op jit(solution)/shard_map/pmax | solution.py:16
  194.0 3.7 exponential_reduce_fusion.5
  197.6 110.4 %psum.64 = f32[4096]{0:T(1024)S(1)} all-reduce(f32[4096]{0:T(1024)S(1)} %exponential_reduce_fusion.5), channel_id=1, replica_groups=mesh['dp'=32,'proto'=16] {'dp'}, use_global_device_ids=true, to_apply=%region_10.11 | all-reduce | flops 4096 | bytes 32768 | tf_op jit(solution)/shard_map/psum | solution.py:17
  308.1 3.3 add_reduce_fusion.3
  311.4 77.8 %pmax.51 = f32[384]{0:T(512)S(1)} all-reduce(f32[384]{0:T(512)S(1)} %add_reduce_fusion.3), channel_id=1, replica_groups=mesh['dp'=32,'proto'=16] {'proto'}, use_global_device_ids=true, to_apply=%region_12.13 | all-reduce | flops 384 | bytes 3072 | tf_op jit(solution)/shard_map/pmax | solution.py:22
  389.2 3.9 exponential_reduce_fusion.4
  393.1 23.5 %psum.65 = f32[384]{0:T(512)S(1)} all-reduce(f32[384]{0:T(512)S(1)} %exponential_reduce_fusion.4), channel_id=1, replica_groups=mesh['dp'=32,'proto'=16] {'proto'}, use_global_device_ids=true, to_apply=%region_14.15 | all-reduce | flops 384 | bytes 3072 | tf_op jit(solution)/shard_map/psum | solution.py:23
  416.7 3.6 add_reduce_fusion.2
  420.3 109.9 %pmax.52 = f32[4096]{0:T(1024)S(1)} all-reduce(f32[4096]{0:T(1024)S(1)} %add_reduce_fusion.2), channel_id=1, replica_groups=mesh['dp'=32,'proto'=16] {'dp'}, use_global_device_ids=true, to_apply=%region_16.17 | all-reduce | flops 4096 | bytes 32768 | tf_op jit(solution)/shard_map/pmax | solution.py:16
  530.2 4.0 exponential_reduce_fusion.3
  534.2 110.3 %psum.66 = f32[4096]{0:T(1024)S(1)} all-reduce(f32[4096]{0:T(1024)S(1)} %exponential_reduce_fusion.3), channel_id=1, replica_groups=mesh['dp'=32,'proto'=16] {'dp'}, use_global_device_ids=true, to_apply=%region_18.19 | all-reduce | flops 4096 | bytes 32768 | tf_op jit(solution)/shard_map/psum | solution.py:17
  644.5 3.3 add_reduce_fusion.1
  647.8 78.7 %pmax.53 = f32[384]{0:T(512)S(1)} all-reduce(f32[384]{0:T(512)S(1)} %add_reduce_fusion.1), channel_id=1, replica_groups=mesh['dp'=32,'proto'=16] {'proto'}, use_global_device_ids=true, to_apply=%region_20.21 | all-reduce | flops 384 | bytes 3072 | tf_op jit(solution)/shard_map/pmax | solution.py:22
  726.5 3.9 exponential_reduce_fusion.2
  730.4 23.7 %psum.67 = f32[384]{0:T(512)S(1)} all-reduce(f32[384]{0:T(512)S(1)} %exponential_reduce_fusion.2), channel_id=1, replica_groups=mesh['dp'=32,'proto'=16] {'proto'}, use_global_device_ids=true, to_apply=%region_22.23 | all-reduce | flops 384 | bytes 3072 | tf_op jit(solution)/shard_map/psum | solution.py:23
  754.2 3.6 add_reduce_fusion
  757.8 109.9 %pmax.54 = f32[4096]{0:T(1024)S(1)} all-reduce(f32[4096]{0:T(1024)S(1)} %add_reduce_fusion), channel_id=1, replica_groups=mesh['dp'=32,'proto'=16] {'dp'}, use_global_device_ids=true, to_apply=%region_24.25 | all-reduce | flops 4096 | bytes 32768 | tf_op jit(solution)/shard_map/pmax | solution.py:16
  867.7 4.0 exponential_reduce_fusion.1
  871.7 110.3 %psum.68 = f32[4096]{0:T(1024)S(1)} all-reduce(f32[4096]{0:T(1024)S(1)} %exponential_reduce_fusion.1), channel_id=1, replica_groups=mesh['dp'=32,'proto'=16] {'dp'}, use_global_device_ids=true, to_apply=%region_26.27 | all-reduce | flops 4096 | bytes 32768 | tf_op jit(solution)/shard_map/psum | solution.py:17
  982.0 3.3 add_reduce_fusion.4
  985.3 3.7 fusion.14
  988.9 78.7 %all-reduce.2 = (f32[384]{0:T(512)S(1)}, f32[384]{0:T(512)S(1)}) all-reduce(f32[384]{0:T(512)S(1)} %add_reduce_fusion.4, f32[384]{0:T(512)S(1)} %get-tuple-element.12), channel_id=1, replica_groups=mesh['dp'=32,'proto'=16] {'proto'}, use_global_device_ids=true, to_apply=%region_28.29 | all-reduce | flops 768 | bytes 6144 | tf_op jit(solution)/shard_map/pmax | solution.py:22
  1067.6 3.9 exponential_reduce_fusion
  1071.6 23.5 %psum.69 = f32[384]{0:T(512)S(1)} all-reduce(f32[384]{0:T(512)S(1)} %exponential_reduce_fusion), channel_id=1, replica_groups=mesh['dp'=32,'proto'=16] {'proto'}, use_global_device_ids=true, to_apply=%region_30.31 | all-reduce | flops 384 | bytes 3072 | tf_op jit(solution)/shard_map/psum | solution.py:23
  1095.1 5.9 multiply_reduce_fusion
  1101.1 23.5 %all-reduce.1 = (f32[384]{0:T(512)S(1)}, f32[384]{0:T(512)S(1)}) all-reduce(f32[384]{0:T(512)S(1)} %get-tuple-element.3, f32[384]{0:T(512)S(1)} %get-tuple-element.2), channel_id=1, replica_groups=mesh['dp'=32,'proto'=16] {'proto'}, use_global_device_ids=true, to_apply=%region_6.7 | all-reduce | flops 768 | bytes 6144 | tf_op jit(solution)/shard_map/psum | solution.py:66
  1124.6 0.6 select_reduce_fusion.1
  1125.2 7.5 fusion.1
  1132.7 0.7 fusion.7
  1133.4 0.6 fusion.9
  1134.7 99.9 %all-reduce.5.cloned.1.call-done = bf16[384,256]{1,0:T(8,128)(2,1)} async-done(((bf16[384,256]{1,0:T(8,128)(2,1)}), bf16[384,256]{1,0:T(8,128)(2,1)}) %all-reduce.5.cloned.1.call-update) | async-done | bytes 196624 | tf_op jit(solution)/shard_map/psum | solution.py:79
  1234.6 1.0 convert_element_type.21
  1235.6 1.6 scatter_custom_fusion
  (19 shorter events, 0.2 us)
Async XLA Ops:
  7.2 978.1 %copy-start = (bf16[256,4096]{1,0:T(8,128)(2,1)S(1)}, bf16[256,4096]{1,0:T(8,128)(2,1)}, u32[]{:S(2)}) copy-start(bf16[256,4096]{1,0:T(8,128)(2,1)} %param.10) | copy-start | bytes 6291460
  7.2 1227.5 %all-reduce.5.cloned.1.call-start = ((), (), s32[]{:S(2)}) async-start(), calls=%async_computation | async-start | bytes 393216 | tf_op jit(solution)/shard_map/psum | solution.py:79
Sparse Core Ops, SparseCore 0:
  1132.8 101.7 all-reduce.4
where the time goes:
time: 1250 us
  blocking collectives  1050 us (84%)
  waiting for transfers between devices  99.9 us (8%)
  other arithmetic  52.1 us (4%)
  between operations  16.7 us (1%)
  matrix products  16.4 us (1%)
    pmax x3, blocking collectives, column_lse(): highest = lax.pmax(jnp.max(values, axis=0), 'dp')  338 us
    psum x3, blocking collectives, column_lse(): totals = lax.psum(jnp.sum(jnp.exp(values - highest[None, :]), axis=0), 'dp')  331 us
    pmax x3, blocking collectives, row_lse(): highest = lax.pmax(jnp.max(values, axis=1), 'proto')  235 us
    psum x1, waiting for transfers between devices, body(): lax.psum(partial_grad.astype(jnp.bfloat16), 'proto').astype(jnp.float32)  99.9 us
    psum x3, blocking collectives, row_lse(): lax.psum(jnp.sum(jnp.exp(values - highest[:, None]), axis=1), 'proto')  70.8 us
  transfers between devices with their start and end apart: 1, of which 1 were waited for; matrix products, arithmetic and copies ran while one was open for 0% of the time, Pallas kernels for 0%

commit v1 on v0

v1 whole, which is shorter than its diff:
```python
import jax
import jax.numpy as jnp
from jax import lax
from jax.sharding import PartitionSpec as P

MASK_DEV = 24
MOST = 72
TEACH = 1.0 / 0.07
STUD = 1.0 / 0.1
F32 = jnp.float32
BF16 = jnp.bfloat16


def lse(values, axis):
    high = jnp.max(values, axis=axis, keepdims=True)
    return jnp.squeeze(high, axis) + jnp.log(jnp.sum(jnp.exp(values - high), axis=axis))


def share(values, axis):
    peers = lax.axis_size(axis)
    return lax.all_to_all(jnp.broadcast_to(values[None], (peers,) + values.shape), axis, 0, 0, tiled=True)


def body(student_patches, teacher_patches, mask_order, counts, student_protos, teacher_protos):
    width = lax.axis_size("proto")
    own_index = lax.axis_index("proto")
    row_total = MASK_DEV * width
    own_count = counts[0, 0]
    order = mask_order[0, :MOST]
    picked_teacher = teacher_patches[0][order]
    picked_student = student_patches[0][order]
    tail = jnp.broadcast_to(own_count.astype(BF16), (8, picked_teacher.shape[1]))
    gathered = lax.all_gather(jnp.concatenate([picked_teacher, tail], axis=0), "proto", axis=0, tiled=False)
    padded = jnp.pad(picked_student, ((0, 64), (0, 0)))
    gathered_student = lax.all_gather(padded, "proto", axis=0, tiled=False)[:, :MOST].reshape(width * MOST, -1)
    sizes = gathered[:, MOST, 0].astype(jnp.int32)
    ends = jnp.cumsum(sizes)
    starts = ends - sizes
    peers = jnp.arange(width, dtype=jnp.int32)
    own_start = jnp.sum(jnp.where(peers == own_index, starts, 0))
    row_index = jnp.arange(row_total, dtype=jnp.int32)
    holder = jnp.sum((row_index[:, None] >= ends[None, :]).astype(jnp.int32), axis=1)
    member = holder[:, None] == peers[None, :]
    within = row_index - jnp.sum(jnp.where(member, starts[None, :], 0), axis=1)
    teacher_rows = gathered[:, :MOST].reshape(width * MOST, -1)[holder * MOST + within]
    student_rows = gathered_student[holder * MOST + within]
    slots = jnp.clip(starts[:, None] + jnp.arange(MOST, dtype=jnp.int32)[None, :], 0, row_total - 1).reshape(-1)

    logits = jnp.dot(teacher_rows, teacher_protos, preferred_element_type=F32) * TEACH
    col = -lse(share(lse(logits, 0), "dp"), 0)

    stud = jnp.dot(student_rows, student_protos, preferred_element_type=F32) * STUD
    stud_high = jnp.max(stud, axis=1)
    stud_exp = jnp.exp(stud - stud_high[:, None])
    stud_lse = stud_high + jnp.log(jnp.sum(stud_exp, axis=1))
    stud_sum = lax.dot_general(stud_exp.astype(BF16), student_protos, (((1,), (1,)), ((), ())), preferred_element_type=F32)

    shifted = logits + col[None, :]
    high = jnp.max(shifted, axis=1)
    exact = jnp.exp(shifted - high[:, None])
    kernel = exact.astype(BF16)
    own_lse = high + jnp.log(jnp.sum(exact, axis=1))
    both = share(jnp.concatenate([own_lse.reshape(-1, 128), stud_lse.reshape(-1, 128)], axis=0), "proto")
    both = lse(both, 0).reshape(2, row_total)
    row_lse, student_lse = both[0], both[1]
    row_scale = jnp.exp(high - row_lse)

    stud_part = (stud_sum * jnp.exp(stud_high - student_lse)[:, None]).astype(BF16)
    stud_back = lax.psum_scatter(stud_part[slots], "proto", scatter_dimension=0, tiled=True)

    def columns(row_scale):
        sums = jnp.sum(kernel.astype(F32) * row_scale[:, None], axis=0)
        return 1.0 / jnp.sum(share(sums.astype(BF16), "dp").astype(F32), axis=0)

    col_scale = columns(row_scale)
    row_sums = row_scale * jnp.sum(kernel.astype(F32) * col_scale[None, :], axis=1)
    row_scale = row_scale / jnp.sum(share(row_sums.reshape(-1, 128), "proto"), axis=0).reshape(-1)
    col_scale = columns(row_scale)
    weights = (kernel.astype(F32) * col_scale[None, :]).astype(BF16)
    teach_sum = lax.dot_general(weights, student_protos, (((1,), (1,)), ((), ())), preferred_element_type=F32)
    total = row_scale * jnp.sum(weights.astype(F32), axis=1)
    teach_part = (teach_sum * row_scale[:, None]).astype(BF16)[slots].reshape(width, MOST, -1)
    total_slots = total[slots].reshape(width, MOST)
    total_high = total_slots.astype(BF16)
    total_low = (total_slots - total_high.astype(F32)).astype(BF16)
    wide = jnp.pad(jnp.stack([total_high, total_low], axis=1), ((0, 0), (0, 6), (0, teach_part.shape[2] - MOST)))
    back = lax.all_to_all(jnp.concatenate([teach_part, wide], axis=1), "proto", 0, 0, tiled=True)
    back = jnp.sum(back.astype(F32), axis=0)
    row_norm = back[MOST, :MOST] + back[MOST + 1, :MOST]
    slot = jnp.arange(MOST, dtype=jnp.int32)
    used = slot < own_count
    mean_proto = back[:MOST] / jnp.where(used, row_norm, 1.0)[:, None]
    own_lse_rows = student_lse[jnp.clip(own_start + slot, 0, row_total - 1)]
    cross = own_lse_rows - STUD * jnp.sum(picked_student.astype(F32) * mean_proto, axis=1)
    own_loss = jnp.sum(jnp.where(used, cross, 0.0)) / own_count.astype(F32)
    own_rows = jnp.where(used[:, None], STUD * (stud_back.astype(F32) - mean_proto), 0.0)
    student_grad = (
        jnp.zeros((student_patches.shape[1], student_patches.shape[2]), BF16).at[order].set(own_rows.astype(BF16))
    )
    return (student_grad[None], own_loss.reshape(1, 1))


def solution(mesh):
    placed = (
        P(("dp", "proto"), None, None),
        P(("dp", "proto"), None, None),
        P(("dp", "proto"), None),
        P("dp", "proto"),
        P(None, "proto"),
        P(None, "proto"),
    )
    return jax.shard_map(
        body,
        mesh=mesh,
        in_specs=placed,
        out_specs=(P(("dp", "proto"), None, None), P("dp", "proto")),
        check_vma=False,
    )
```

time: 1250 us -> 282 us (0.23)
  blocking collectives: 1050 us -> 68.9 us
  local copies, waits for them, and re-layouts: 9.32 us -> 36.5 us
  other arithmetic: 52.1 us -> 31.4 us
  starting transfers between devices: 0.04 us -> 20.2 us
    pmax x6 -> x0, blocking collectives: 573 us -> none  [the longest x3 338 us: column_lse(): highest = lax.pmax(jnp.max(values, axis=0), 'dp')]
    psum x7 -> x0, blocking collectives: 425 us -> none  [the longest x3 331 us: column_lse(): totals = lax.psum(jnp.sum(jnp.exp(values - highest[None, :]), axis=0), 'dp')]
    psum x1 -> x0, waiting for transfers between devices: 99.9 us -> none  [body(): lax.psum(partial_grad.astype(jnp.bfloat16), 'proto').astype(jnp.float32)]
    all_to_all x0 -> x3, blocking collectives: none -> 45.9 us  [share(): lax.all_to_all(jnp.broadcast_to(values[None], (peers,) + values.shape), a...]
    reduce_scatter x0 -> x1, waiting for transfers between devices: none -> 39.2 us  [body(): lax.psum_scatter(stud_part[slots], 'proto', scatter_dimension=0, tiled=True)]
    all_to_all x0 -> x3, waiting for transfers between devices: none -> 36.4 us  [the longest x2 26.9 us: share(): lax.all_to_all(jnp.broadcast_to(values[None], (peers,) + values.shape), a...]
    all_gather x0 -> x1, waiting for transfers between devices: none -> 20.3 us  [body(): lax.all_gather(padded, 'proto', axis=0, tiled=False)[:, :MOST]]
    all_to_all x0 -> x3, starting transfers between devices: none -> 20.1 us  [the longest x2 14.5 us: share(): lax.all_to_all(jnp.broadcast_to(values[None], (peers,) + values.shape), a...]
  transfers between devices with their start and end apart: 1 -> 5, of which waited for: 1 -> 5; matrix products, arithmetic and copies ran while one was open for 0% -> 6% of each run, Pallas kernels for 0% -> 0%
where the time goes in v1:
time: 282 us; the launch traced here: 280 us
  waiting for transfers between devices  95.9 us (34%)
  blocking collectives  68.9 us (24%)
  local copies, waits for them, and re-layouts  36.5 us (13%)
  other arithmetic  31.4 us (11%)
  starting transfers between devices  20.2 us (7%)
  between operations  16.9 us (6%)
  matrix products  10.5 us (4%)
    all_to_all x3, blocking collectives, share(): lax.all_to_all(jnp.broadcast_to(values[None], (peers,) + values.shape), a...  45.9 us
    reduce_scatter x1, waiting for transfers between devices, body(): lax.psum_scatter(stud_part[slots], 'proto', scatter_dimension=0, tiled=True)  39.2 us
    all_to_all x2, waiting for transfers between devices, share(): lax.all_to_all(jnp.broadcast_to(values[None], (peers,) + values.shape), a...  26.9 us
    all_gather x1, blocking collectives, body(): lax.all_gather(jnp.concatenate([picked_teacher, tail], axis=0), 'proto',...  23 us
    all_gather x1, waiting for transfers between devices, body(): lax.all_gather(padded, 'proto', axis=0, tiled=False)[:, :MOST]  20.3 us
    all_to_all x2, starting transfers between devices, share(): lax.all_to_all(jnp.broadcast_to(values[None], (peers,) + values.shape), a...  14.5 us
    all_to_all x1, waiting for transfers between devices, body(): lax.all_to_all(jnp.concatenate([teach_part, wide], axis=1), 'proto', 0, 0...  9.55 us
    unnamed x15, local copies, waits for them, and re-layouts  7.81 us
  transfers between devices with their start and end apart: 5, of which 5 were waited for; matrix products, arithmetic and copies ran while one was open for 6% of the time, Pallas kernels for 0%

profile of v1, /device:TPU:1, one launch (start us, length us, event | category | flops | bytes accessed | tf_op | source)
XLA Modules:
  0.0 280.3 jit_solution(5559329523306388489)
XLA Ops:
  7.2 0.8 fusion.43
  8.7 1.6 gather_fusion.1
  10.3 23.0 %all-gather.1 = bf16[1280,256]{1,0:T(8,128)(2,1)S(1)} all-gather(bf16[80,256]{1,0:T(8,128)(2,1)S(1)} %concatenate.9), channel_id=3, replica_groups=mesh['dp'=32,'proto'=16] {'proto'}, dimensions={0}, use_global_device_ids=true | all-gather | bytes 696320 | tf_op jit(solution)/shard_map/all_gather | solution.py:33
  33.8 0.7 fusion.42
  34.6 2.1 gather_fusion.3
  36.6 2.7 fusion.50
  39.3 2.6 copy-done.1
  42.0 0.9 exponential_reduce_fusion
  42.9 1.3 broadcast_in_dim.48
  44.2 10.6 %all-to-all-start = ((f32[32,1,4096]{2,1,0:T(1,128)}), f32[32,1,4096]{2,1,0:T(1,128)S(1)}, u32[]{:S(2)}, u32[]{:S(2)}) async-start(f32[32,1,4096]{2,1,0:T(1,128)} %broadcast_in_dim.48), calls=%async_computation | async-start | bytes 1048576 | tf_op jit(solution)/shard_map/all_to_all | solution.py:21
  54.8 0.7 gather_fusion
  55.5 0.6 pad.9
  56.2 15.3 %all-to-all-done = f32[32,1,4096]{2,1,0:T(1,128)S(1)} async-done(((f32[32,1,4096]{2,1,0:T(1,128)}), f32[32,1,4096]{2,1,0:T(1,128)S(1)}, u32[]{:S(2)}, u32[]{:S(2)}) %all-to-all-start) | async-done | bytes 524320 | tf_op jit(solution)/shard_map/all_to_all | solution.py:21
  72.2 3.5 %add_reduce_fusion = f32[384]{0:T(512)S(1)} fusion(f32[384,4096]{1,0:T(8,128)} %copy-done.1, f32[4096]{0:T(1024)S(1)} %add_negate_fusion), kind=kLoop, calls=%fused_computation.23 | loop fusion | flops 3145344 | bytes 6309376 | tf_op jit(solution)/shard_map/reduce_max | solution.py:59
  75.7 0.8 copy-done.2
  76.5 1.2 fusion.7
  77.7 20.3 %all-gather.4.cloned.1.call-done = bf16[2176,256]{1,0:T(8,128)(2,1)} async-done(((bf16[136,256]{1,0:T(8,128)(2,1)}), bf16[2176,256]{1,0:T(8,128)(2,1)}) %all-gather.4.cloned.1.call-update) | async-done | bytes 1114128 | tf_op jit(solution)/shard_map/all_gather | solution.py:35
  98.0 1.1 slice.54
  99.1 2.1 gather_fusion.2
  101.1 1.1 fusion.49
  102.2 2.7 copy-done.3
  104.9 1.0 fusion.4
  105.9 12.4 %all_to_all.36 = f32[16,6,128]{2,1,0:T(8,128)S(1)} all-to-all(f32[16,6,128]{2,1,0:T(8,128)S(1)} %broadcast_in_dim.49), channel_id=1, replica_groups=mesh['dp'=32,'proto'=16] {'proto'}, dimensions={0} | all-to-all | bytes 98304 | tf_op jit(solution)/shard_map/all_to_all | solution.py:21
  118.4 4.7 %fusion = (bf16[4096]{0:T(1024)(128)(2,1)S(1)}, bf16[384,4096]{1,0:T(8,128)(2,1)}) fusion(f32[384]{0:T(512)S(1)} %get-tuple-element.10, f32[384]{0:T(512)S(1)} %add_reduce_fusion, f32[384,4096]{1,0:T(8,128)} %copy-done.1, f32[4096]{0:T(1024)S(1)} %add_negate_fusion), kind=kLoop, calls=%fused_computation.13 | loop fusion | flops 9433088 | bytes 9464832 | tf_op jit(solution)/shard_map/reduce_sum | solution.py:72
  123.6 0.5 broadcast.231
  124.1 2.2 reduce.8
  126.5 21.5 %all_to_all.37 = bf16[32,2,2048]{2,1,0:T(2,128)(2,1)S(1)} all-to-all(bf16[32,2,2048]{2,1,0:T(2,128)(2,1)S(1)} %reshape.416), channel_id=1, replica_groups=mesh['dp'=32,'proto'=16] {'dp'}, dimensions={0} | all-to-all | bytes 524288 | tf_op jit(solution)/shard_map/all_to_all | solution.py:21
  148.6 2.6 fusion.1
  151.2 12.0 %all_to_all.38 = f32[16,3,128]{2,1,0:T(4,128)S(1)} all-to-all(f32[16,3,128]{2,1,0:T(4,128)S(1)} %broadcast_in_dim.51), channel_id=1, replica_groups=mesh['dp'=32,'proto'=16] {'proto'}, dimensions={0} | all-to-all | bytes 49152 | tf_op jit(solution)/shard_map/all_to_all | solution.py:21
  163.3 2.8 fusion.2
  166.6 2.2 reduce.9
  168.8 0.9 reshape.418
  169.7 3.9 %all-to-all-start.4 = ((bf16[32,2,2048]{2,1,0:T(2,128)(2,1)}), bf16[32,2,2048]{2,1,0:T(2,128)(2,1)S(1)}, u32[]{:S(2)}, u32[]{:S(2)}) async-start(bf16[32,2,2048]{2,1,0:T(2,128)(2,1)} %reshape.418), calls=%async_computation.5 | async-start | bytes 524288 | tf_op jit(solution)/shard_map/all_to_all | solution.py:21
  173.8 11.6 %all-to-all-done.4 = bf16[32,2,2048]{2,1,0:T(2,128)(2,1)S(1)} async-done(((bf16[32,2,2048]{2,1,0:T(2,128)(2,1)}), bf16[32,2,2048]{2,1,0:T(2,128)(2,1)S(1)}, u32[]{:S(2)}, u32[]{:S(2)}) %all-to-all-start.4) | async-done | bytes 262176 | tf_op jit(solution)/shard_map/all_to_all | solution.py:21
  186.0 2.6 convert_reduce_fusion
  188.6 2.9 %fusion.19 = bf16[384,256]{1,0:T(8,128)(2,1)S(1)} fusion(bf16[256,4096]{1,0:T(8,128)(2,1)S(1)} %copy-done, bf16[384,4096]{1,0:T(8,128)(2,1)} %get-tuple-element.5, f32[4096]{0:T(1024)S(1)} %broadcast_divide_fusion, f32[384]{0:T(512)S(1)} %bitcast_divide_fusion), kind=kOutput, calls=%fused_computation.34 | convolution fusion | flops 810221568 | bytes 5457408 | tf_op jit(solution)/shard_map/dot_general | solution.py:80
  191.5 7.3 %gather_fusion.6 = f32[1152]{0:T(1024)S(1)} fusion(f32[384]{0:T(512)S(1)} %mul.116, s32[2048]{0:T(1024)S(1)} %pad_clamp_fusion), kind=kCustom, calls=%fused_computation.6 | custom fusion | bytes 13824 | tf_op jit(solution)/shard_map/gather | solution.py:83
  198.9 4.2 %gather_fusion.5 = bf16[1152,256]{1,0:T(8,128)(2,1)S(1)} fusion(bf16[384,256]{1,0:T(8,128)(2,1)S(1)} %fusion.19, s32[2048]{0:T(1024)S(1)} %pad_clamp_fusion), kind=kCustom, calls=%fused_computation.5 | custom fusion | bytes 1184256 | tf_op jit(solution)/shard_map/gather | solution.py:82
  203.2 0.9 pad_maximum_fusion
  204.1 5.7 %all-to-all-start.5 = ((bf16[16,80,256]{2,1,0:T(8,128)(2,1)}), bf16[16,80,256]{2,1,0:T(8,128)(2,1)S(1)}, u32[]{:S(2)}, u32[]{:S(2)}) async-start(bf16[16,80,256]{2,1,0:T(8,128)(2,1)} %pad_maximum_fusion), calls=%async_computation.6 | async-start | bytes 1310720 | tf_op jit(solution)/shard_map/all_to_all | solution.py:87
  209.8 3.8 %fusion.22 = bf16[384,256]{1,0:T(8,128)(2,1)S(1)} fusion(bf16[256,4096]{1,0:T(8,128)(2,1)S(1)} %copy-done, f32[384,4096]{1,0:T(8,128)} %copy-done.3, f32[384]{0:T(512)S(1)} %get-tuple-element.12, f32[384]{0:T(512)S(1)} %get-tuple-element.11), kind=kOutput, calls=%fused_computation.35 | convolution fusion | flops 808648704 | bytes 8588288 | tf_op jit(solution)/shard_map/dot_general | solution.py:56
  213.7 4.6 %gather_fusion.4 = bf16[1152,256]{1,0:T(8,128)(2,1)} fusion(bf16[384,256]{1,0:T(8,128)(2,1)S(1)} %fusion.22, s32[2048]{0:T(1024)S(1)} %pad_clamp_fusion), kind=kCustom, calls=%fused_computation.4 | custom fusion | bytes 1184256 | tf_op jit(solution)/shard_map/gather | solution.py:69
  218.3 0.6 fusion.44
  219.0 1.3 gather_fusion.7
  220.3 9.5 %all-to-all-done.5 = bf16[16,80,256]{2,1,0:T(8,128)(2,1)S(1)} async-done(((bf16[16,80,256]{2,1,0:T(8,128)(2,1)}), bf16[16,80,256]{2,1,0:T(8,128)(2,1)S(1)}, u32[]{:S(2)}, u32[]{:S(2)}) %all-to-all-start.5) | async-done | bytes 655392 | tf_op jit(solution)/shard_map/all_to_all | solution.py:87
  230.1 0.6 select_reduce_fusion.1
  231.4 39.2 %reduce-scatter.2.cloned.1.call-done = bf16[72,256]{1,0:T(8,128)(2,1)} async-done(((bf16[1152,256]{1,0:T(8,128)(2,1)}), bf16[72,256]{1,0:T(8,128)(2,1)}) %reduce-scatter.2.cloned.1.call-update) | async-done | bytes 36880 | tf_op jit(solution)/shard_map/reduce_scatter | solution.py:69
  270.6 1.8 scatter_custom_fusion
  (63 shorter events, 4.5 us)
Async XLA Ops:
  7.2 94.0 %copy-start = (bf16[256,4096]{1,0:T(8,128)(2,1)S(1)}, bf16[256,4096]{1,0:T(8,128)(2,1)}, u32[]{:S(2)}) copy-start(bf16[256,4096]{1,0:T(8,128)(2,1)} %param.10) | copy-start | bytes 6291460
  36.6 18.2 %copy-start.4 = (bf16[1,256,256]{2,1,0:T(8,128)(2,1)S(1)}, bf16[1,256,256]{2,1,0:T(8,128)(2,1)}, u32[]{:S(2)}) copy-start(bf16[1,256,256]{2,1,0:T(8,128)(2,1)} %param.6) | copy-start | bytes 393220
  39.3 2.7 copy-start.1
  44.2 27.3 %all-to-all-start = ((f32[32,1,4096]{2,1,0:T(1,128)}), f32[32,1,4096]{2,1,0:T(1,128)S(1)}, u32[]{:S(2)}, u32[]{:S(2)}) async-start(f32[32,1,4096]{2,1,0:T(1,128)} %broadcast_in_dim.48), calls=%async_computation | async-start | bytes 1048576 | tf_op jit(solution)/shard_map/all_to_all | solution.py:21
  54.8 43.2 %all-gather.4.cloned.1.call-start = ((), (), s32[]{:S(2)}) async-start(), calls=%async_computation.8 | async-start | bytes 1183744 | tf_op jit(solution)/shard_map/all_gather | solution.py:35
  71.8 4.6 %copy-start.2 = (f32[384,4096]{1,0:T(8,128)S(1)}, f32[384,4096]{1,0:T(8,128)}, u32[]{:S(2)}) copy-start(f32[384,4096]{1,0:T(8,128)} %copy-done.1) | copy-start | bytes 18874372
  102.2 2.7 copy-start.3
  169.7 15.7 %all-to-all-start.4 = ((bf16[32,2,2048]{2,1,0:T(2,128)(2,1)}), bf16[32,2,2048]{2,1,0:T(2,128)(2,1)S(1)}, u32[]{:S(2)}, u32[]{:S(2)}) async-start(bf16[32,2,2048]{2,1,0:T(2,128)(2,1)} %reshape.418), calls=%async_computation.5 | async-start | bytes 524288 | tf_op jit(solution)/shard_map/all_to_all | solution.py:21
  204.1 25.7 %all-to-all-start.5 = ((bf16[16,80,256]{2,1,0:T(8,128)(2,1)}), bf16[16,80,256]{2,1,0:T(8,128)(2,1)S(1)}, u32[]{:S(2)}, u32[]{:S(2)}) async-start(bf16[16,80,256]{2,1,0:T(8,128)(2,1)} %pad_maximum_fusion), calls=%async_computation.6 | async-start | bytes 1310720 | tf_op jit(solution)/shard_map/all_to_all | solution.py:87
  209.8 60.8 %reduce-scatter.2.cloned.1.call-start = ((), (), s32[]{:S(2)}) async-start(), calls=%async_computation.7 | async-start | bytes 626688 | tf_op jit(solution)/shard_map/reduce_scatter | solution.py:69
Sparse Core Ops, SparseCore 0:
  58.3 39.6 all-gather.3
  218.4 52.0 reduce-scatter.1

commit v2 on v0

v2 whole, which is shorter than its diff:
```python
import functools

import jax
import jax.numpy as jnp
from jax import lax
from jax.experimental import pallas as pl
from jax.experimental.pallas import tpu as pltpu
from jax.sharding import PartitionSpec as P

MASK_DEV = 24
MOST = 72
SLOT = 80
TEACH = 1.0 / 0.07
STUD = 1.0 / 0.1
F32 = jnp.float32
BF16 = jnp.bfloat16
LANES = 128
BLOCK = 1024
LIMIT = 40 << 20
VMEM = pl.BlockSpec(memory_space=pltpu.VMEM)
SMEM = pl.BlockSpec(memory_space=pltpu.SMEM)


def call(kernel, out_shape, *args, grid=None, in_specs=None, out_specs=None, scratch=(), flops=0, moved=0):
    out_shape = [jax.ShapeDtypeStruct(s, d) for s, d in out_shape]
    extra = {} if grid is None else {"grid": grid}
    return pl.pallas_call(
        kernel,
        out_shape=out_shape,
        in_specs=[VMEM] * len(args) if in_specs is None else in_specs,
        out_specs=[VMEM] * len(out_shape) if out_specs is None else out_specs,
        scratch_shapes=list(scratch),
        compiler_params=pltpu.CompilerParams(vmem_limit_bytes=LIMIT),
        cost_estimate=pl.CostEstimate(flops=flops, bytes_accessed=moved, transcendentals=0),
        **extra,
    )(*args)


def iota(shape, dim):
    return lax.broadcasted_iota(jnp.int32, shape, dim)


def eye():
    return iota((LANES, LANES), 0) == iota((LANES, LANES), 1)


def to_lanes(column):
    parts = []
    for b in range(column.shape[0] // LANES):
        part = jnp.broadcast_to(column[b * LANES : (b + 1) * LANES], (LANES, LANES))
        parts.append(jnp.sum(jnp.where(eye(), part, 0.0), axis=0, keepdims=True))
    return jnp.concatenate(parts, axis=0)


def to_column(lanes):
    parts = []
    for b in range(lanes.shape[0]):
        part = jnp.broadcast_to(lanes[b : b + 1], (LANES, LANES))
        parts.append(jnp.sum(jnp.where(eye(), part, 0.0), axis=1, keepdims=True))
    return jnp.concatenate(parts, axis=0)


def pick_kernel(teacher_ref, student_ref, order_ref, count_ref, teacher_out, student_out):
    patches, width = teacher_ref.shape
    order = jnp.broadcast_to(order_ref[:, :LANES], (patches, LANES))
    chosen = (iota((patches, LANES), 0) == order).astype(BF16)
    dims = (((0,), (0,)), ((), ()))
    picked = lax.dot_general(chosen, teacher_ref[...], dims, preferred_element_type=F32)
    count = jnp.full((SLOT - MOST, width), count_ref[0, 0], jnp.int32).astype(F32)
    teacher_out[...] = jnp.concatenate([picked[:MOST], count], axis=0).astype(BF16)
    picked = lax.dot_general(chosen, student_ref[...], dims, preferred_element_type=F32)
    student_out[...] = picked.astype(BF16)


def compact(gathered, starts, counts, rows):
    total = gathered.shape[0]
    images = starts.shape[0]
    slots = total // images
    lane, image = iota((images, total), 1), iota((images, total), 0)
    within = lane - image * slots
    member = jnp.logical_and(within >= 0, within < slots)
    used = jnp.logical_and(member, within.astype(F32) < counts[:, :1])
    row = jnp.sum(jnp.where(used, starts[:, :1] + within.astype(F32) + 1.0, 0.0), axis=0, keepdims=True) - 1.0
    chosen = (iota((rows, total), 0).astype(F32) == row).astype(BF16)
    return jnp.dot(chosen, gathered, preferred_element_type=F32).astype(BF16)


def spread(starts, counts, slots, rows):
    images = starts.shape[0]
    shape = (images, slots, rows)
    within = iota(shape, 1)
    row = (iota(shape, 2) - within).astype(F32) - starts[:, :1].reshape(images, 1, 1)
    used = jnp.logical_and(row == 0.0, within.astype(F32) < counts[:, :1].reshape(images, 1, 1))
    return used.astype(F32).astype(BF16).reshape(images * slots, rows)


def column_kernel(gathered_ref, protos_ref, share_ref, rows_ref, places_ref):
    images = gathered_ref.shape[0]
    rows = rows_ref.shape[0]

    @pl.when(pl.program_id(0) == 0)
    def _():
        counts = gathered_ref[:, MOST:MOST + 8, :LANES].astype(F32)[:, 0]
        before = (iota((images, images), 1) < iota((images, images), 0)).astype(BF16)
        starts = jnp.dot(before, counts.astype(BF16), preferred_element_type=F32)
        places_ref[0] = starts
        places_ref[1] = counts
        flat = gathered_ref[...].reshape(images * SLOT, gathered_ref.shape[2])
        rows_ref[...] = compact(flat, starts, counts, rows)

    logits = jnp.dot(rows_ref[...], protos_ref[...], preferred_element_type=F32) * TEACH
    high = jnp.max(logits, axis=0, keepdims=True)
    total = jnp.sum(jnp.exp(logits - high), axis=0, keepdims=True)
    share_ref[...] = jnp.broadcast_to(high + jnp.log(total), share_ref.shape)


def row_kernel(shares_ref, rows_ref, protos_ref, student_lse_ref, matrix_ref, high_ref, share_ref, sums):
    step = pl.program_id(0)
    shares = shares_ref[...]
    top = jnp.max(shares, axis=0, keepdims=True)
    column = top + jnp.log(jnp.sum(jnp.exp(shares - top), axis=0, keepdims=True))
    logits = jnp.dot(rows_ref[...], protos_ref[...], preferred_element_type=F32) * TEACH
    shifted = logits - column
    high = jnp.max(shifted, axis=1, keepdims=True)
    exact = jnp.exp(shifted - high)
    matrix_ref[...] = exact.astype(BF16)
    high_ref[step] = high
    sums[step] = jnp.sum(exact, axis=1, keepdims=True)

    @pl.when(step == pl.num_programs(0) - 1)
    def _():
        highs = high_ref[...]
        top = jnp.max(highs, axis=0)
        total = jnp.sum(jnp.exp(highs - top[None]) * sums[...], axis=0)
        own = to_lanes(top + jnp.log(total))
        peers, depth = share_ref.shape[0], share_ref.shape[1]
        chunk = jnp.concatenate([own, student_lse_ref[...], jnp.zeros((depth - 2 * own.shape[0], LANES), F32)], axis=0)
        share_ref[...] = jnp.broadcast_to(chunk[None], share_ref.shape)


def merged(shares):
    top = jnp.max(shares, axis=0)
    return top + jnp.log(jnp.sum(jnp.exp(shares - top[None]), axis=0))


def column_sums(matrix_ref, scale, share_ref):
    sums = jnp.sum(matrix_ref[...].astype(F32) * scale, axis=0, keepdims=True)
    share_ref[...] = jnp.broadcast_to(sums, share_ref.shape).astype(share_ref.dtype)


def first_column_kernel(shares_ref, high_ref, matrix_ref, share_ref, scale_ref, student_lse_ref):
    step = pl.program_id(0)
    lines = student_lse_ref.shape[0]

    @pl.when(step == 0)
    def _():
        both = merged(shares_ref[...][:, : 2 * lines])
        student_lse_ref[...] = both[lines:]
        scale_ref[...] = jnp.exp(high_ref[...] - to_column(both[:lines])[None])

    column_sums(matrix_ref, scale_ref[step], share_ref)


def later_column_kernel(shares_ref, scale_in_ref, matrix_ref, share_ref, scale_ref):
    step = pl.program_id(0)

    @pl.when(step == 0)
    def _():
        lines = scale_ref.shape[1] // LANES
        total = to_column(jnp.sum(shares_ref[...][:, :lines], axis=0))
        scale_ref[...] = scale_in_ref[...] / total[None]

    column_sums(matrix_ref, scale_ref[step], share_ref)


def later_row_kernel(shares_ref, scale_ref, matrix_ref, share_ref, sums):
    step = pl.program_id(0)
    inverse = 1.0 / jnp.sum(shares_ref[...].astype(F32), axis=0, keepdims=True)
    part = scale_ref[step] * jnp.sum(matrix_ref[...].astype(F32) * inverse, axis=1, keepdims=True)

    @pl.when(step == 0)
    def _():
        sums[...] = part

    @pl.when(step > 0)
    def _():
        sums[...] += part

    @pl.when(step == pl.num_programs(0) - 1)
    def _():
        own = to_lanes(sums[...])
        chunk = jnp.concatenate([own, jnp.zeros((share_ref.shape[1] - own.shape[0], LANES), F32)], axis=0)
        share_ref[...] = jnp.broadcast_to(chunk[None], share_ref.shape)


def target_kernel(shares_ref, scale_ref, matrix_ref, protos_ref, places_ref, out_ref, sums, total):
    step = pl.program_id(0)
    scale = scale_ref[step]
    inverse = 1.0 / jnp.sum(shares_ref[...].astype(F32), axis=0, keepdims=True)
    weights = matrix_ref[...].astype(F32) * inverse
    narrow = weights.astype(BF16)
    part = scale * lax.dot_general(narrow, protos_ref[...], (((1,), (1,)), ((), ())), preferred_element_type=F32)
    mass = scale * jnp.sum(narrow.astype(F32), axis=1, keepdims=True)

    @pl.when(step == 0)
    def _():
        sums[...] = part
        total[...] = mass

    @pl.when(step > 0)
    def _():
        sums[...] += part
        total[...] += mass

    @pl.when(step == pl.num_programs(0) - 1)
    def _():
        rows, width = sums.shape
        mass_high = jnp.broadcast_to(total[...], (rows, LANES)).astype(BF16)
        mass_low = (jnp.broadcast_to(total[...], (rows, LANES)) - mass_high.astype(F32)).astype(BF16)
        sent = jnp.concatenate([sums[...].astype(BF16), mass_high, mass_low], axis=1)
        images = out_ref.shape[0]
        chosen = spread(places_ref[0], places_ref[1], SLOT, rows)
        packed = jnp.dot(chosen, sent, preferred_element_type=F32).reshape(images, SLOT, width + 2 * LANES)
        same = iota((1, SLOT, LANES), 1) == iota((1, SLOT, LANES), 2)
        high = jnp.sum(jnp.where(same, packed[:, :, width : width + LANES], 0.0), axis=1, keepdims=True)
        low = jnp.sum(jnp.where(same, packed[:, :, width + LANES :], 0.0), axis=1, keepdims=True)
        filler = jnp.zeros((images, 1, width - LANES), F32)
        out_ref[:, :MOST] = packed[:, :MOST, :width].astype(BF16)
        numbers = jnp.concatenate(
            [
                jnp.concatenate([high, filler], axis=2),
                jnp.concatenate([low, filler], axis=2),
                jnp.zeros((images, SLOT - MOST - 2, width), F32),
            ],
            axis=1,
        )
        out_ref[:, MOST:] = numbers.astype(BF16)


def student_kernel(gathered_ref, places_ref, protos_ref, sums_ref, high_ref, lse_ref, rows_ref, total):
    step = pl.program_id(0)
    rows = rows_ref.shape[0]

    @pl.when(step == 0)
    def _():
        images, slots, width = gathered_ref.shape
        flat = gathered_ref[...].reshape(images * slots, width)
        rows_ref[...] = compact(flat, places_ref[0], places_ref[1], rows)
        high_ref[...] = jnp.full(high_ref.shape, -1e30, F32)
        total[...] = jnp.zeros(total.shape, F32)
        sums_ref[...] = jnp.zeros(sums_ref.shape, F32)

    protos = protos_ref[...]
    logits = jnp.dot(rows_ref[...], protos, preferred_element_type=F32) * STUD
    before = high_ref[...]
    high = jnp.maximum(before, jnp.max(logits, axis=1, keepdims=True))
    shrink = jnp.exp(before - high)
    exact = jnp.exp(logits - high)
    total[...] = total[...] * shrink + jnp.sum(exact, axis=1, keepdims=True)
    part = lax.dot_general(exact.astype(BF16), protos, (((1,), (1,)), ((), ())), preferred_element_type=F32)
    sums_ref[...] = sums_ref[...] * shrink + part
    high_ref[...] = high

    @pl.when(step == pl.num_programs(0) - 1)
    def _():
        lse_ref[...] = to_lanes(high_ref[...] + jnp.log(total[...]))


def student_pack_kernel(sums_ref, high_ref, lse_ref, places_ref, out_ref):
    rows = sums_ref.shape[0]
    images = places_ref.shape[1]
    sent = (sums_ref[...] * jnp.exp(high_ref[...] - to_column(lse_ref[...]))).astype(BF16)
    chosen = spread(places_ref[0], places_ref[1], out_ref.shape[0] // images, rows)
    out_ref[...] = jnp.dot(chosen, sent, preferred_element_type=F32).astype(BF16)


def finish_kernel(back_ref, student_ref, picked_ref, lse_ref, places_ref, order_ref, index_ref, grad_ref, loss_ref):
    patches, width = grad_ref.shape
    lines = lse_ref.shape[0]
    back = jnp.sum(back_ref[...].astype(F32), axis=0)
    images = places_ref.shape[1]
    own = iota((images, LANES), 0) == index_ref[0, 0]
    start = jnp.sum(jnp.where(own, places_ref[0], 0.0), axis=0, keepdims=True)
    count = jnp.sum(jnp.where(own, places_ref[1], 0.0), axis=0, keepdims=True)
    mass = to_column((back[MOST : MOST + 1] + back[MOST + 1 : MOST + 2])[:, :LANES])[:MOST]
    used = iota((MOST, 1), 0).astype(F32) < count[:, :1]
    mean = back[:MOST] / jnp.where(used, mass, 1.0)
    lse_row = jnp.concatenate([lse_ref[b : b + 1] for b in range(lines)], axis=1)
    shape = (MOST, lines * LANES)
    here = (iota(shape, 1) - iota(shape, 0)).astype(F32) == start[:, :1]
    own_lse = jnp.sum(jnp.where(here, lse_row, 0.0), axis=1, keepdims=True)
    cross = own_lse - STUD * jnp.sum(picked_ref[:MOST].astype(F32) * mean, axis=1, keepdims=True)
    cross = jnp.sum(jnp.where(used, cross, 0.0), axis=0, keepdims=True)
    loss_ref[...] = cross / count[:, :1]
    rows = jnp.where(used, STUD * (student_ref[...].astype(F32) - mean), 0.0)
    rows = jnp.concatenate([rows, jnp.zeros((LANES - MOST, width), F32)], axis=0).astype(BF16)
    order = jnp.broadcast_to(order_ref[:, :LANES], (patches, LANES))
    chosen = (iota((patches, LANES), 0) == order).astype(BF16)
    grad_ref[...] = jnp.dot(chosen, rows, preferred_element_type=F32).astype(BF16)


def body(student_patches, teacher_patches, mask_order, counts, student_protos, teacher_protos):
    width = lax.axis_size("proto")
    groups = lax.axis_size("dp")
    rows = MASK_DEV * width
    lines = rows // LANES
    patches, bot = student_patches.shape[1:]
    protos = student_protos.shape[1]
    steps = protos // BLOCK
    depth = 8
    index = lax.axis_index("proto").astype(jnp.int32).reshape(1, 1)
    over = functools.partial(lax.all_to_all, split_axis=0, concat_axis=0, tiled=True)
    wide = pl.BlockSpec((bot, BLOCK), lambda k: (0, k))
    peer = pl.BlockSpec((groups, BLOCK), lambda k: (0, k))
    square = pl.BlockSpec((rows, BLOCK), lambda k: (0, k))
    grid = (steps,)
    dot = 2 * rows * protos * bot
    column = pltpu.VMEM((rows, 1), F32)

    teacher_sent, student_sent = call(
        pick_kernel,
        [((SLOT, bot), BF16), ((LANES, bot), BF16)],
        teacher_patches[0],
        student_patches[0],
        mask_order,
        counts,
        in_specs=[VMEM, VMEM, VMEM, SMEM],
        moved=4 * patches * bot,
    )
    gathered_student = lax.all_gather(student_sent, "proto", axis=0, tiled=False)
    gathered = lax.all_gather(teacher_sent, "proto", axis=0, tiled=False)
    share, teacher_rows, places = call(
        column_kernel,
        [((groups, protos), F32), ((rows, bot), BF16), ((2, width, LANES), F32)],
        gathered,
        teacher_protos,
        grid=grid,
        in_specs=[VMEM, wide],
        out_specs=[peer, VMEM, VMEM],
        flops=dot,
        moved=2 * bot * protos,
    )
    shares = over(share, "dp")
    student_sum, student_high, student_lse = call(
        student_kernel,
        [((rows, bot), F32), ((rows, 1), F32), ((lines, LANES), F32)],
        gathered_student,
        places,
        student_protos,
        grid=grid,
        in_specs=[VMEM, VMEM, wide],
        scratch=[pltpu.VMEM((rows, bot), BF16), column],
        flops=2 * dot,
        moved=2 * bot * protos,
    )
    matrix, high, share = call(
        row_kernel,
        [((rows, protos), BF16), ((steps, rows, 1), F32), ((width, depth, LANES), F32)],
        shares,
        teacher_rows,
        teacher_protos,
        student_lse,
        grid=grid,
        in_specs=[peer, VMEM, wide, VMEM],
        out_specs=[square, VMEM, VMEM],
        scratch=[pltpu.VMEM((steps, rows, 1), F32)],
        flops=dot,
        moved=2 * bot * protos + 2 * rows * protos,
    )
    shares = over(share, "proto")
    share, scale, student_lse = call(
        first_column_kernel,
        [((groups, protos), BF16), ((steps, rows, 1), F32), ((lines, LANES), F32)],
        shares,
        high,
        matrix,
        grid=grid,
        in_specs=[VMEM, VMEM, square],
        out_specs=[peer, VMEM, VMEM],
        moved=2 * rows * protos,
    )
    student_part = call(
        student_pack_kernel,
        [((width * MOST, bot), BF16)],
        student_sum,
        student_high,
        student_lse,
        places,
        flops=2 * width * MOST * rows * bot,
    )[0]
    student_back = lax.psum_scatter(student_part, "proto", scatter_dimension=0, tiled=True)
    shares = over(share, "dp")
    share = call(
        later_row_kernel,
        [((width, depth, LANES), F32)],
        shares,
        scale,
        matrix,
        grid=grid,
        in_specs=[peer, VMEM, square],
        scratch=[column],
        moved=2 * rows * protos,
    )[0]
    shares = over(share, "proto")
    share, scale = call(
        later_column_kernel,
        [((groups, protos), BF16), ((steps, rows, 1), F32)],
        shares,
        scale,
        matrix,
        grid=grid,
        in_specs=[VMEM, VMEM, square],
        out_specs=[peer, VMEM],
        moved=2 * rows * protos,
    )
    shares = over(share, "dp")
    sent = call(
        target_kernel,
        [((width, SLOT, bot), BF16)],
        shares,
        scale,
        matrix,
        student_protos,
        places,
        grid=grid,
        in_specs=[peer, VMEM, square, wide, VMEM],
        scratch=[pltpu.VMEM((rows, bot), F32), column],
        flops=dot,
        moved=2 * rows * protos,
    )[0]
    back = over(sent, "proto")
    student_grad, image_loss = call(
        finish_kernel,
        [((patches, bot), BF16), ((1, 1), F32)],
        back,
        student_back,
        student_sent,
        student_lse,
        places,
        mask_order,
        index,
        in_specs=[VMEM, VMEM, VMEM, VMEM, VMEM, VMEM, SMEM],
        moved=2 * patches * bot,
    )
    return (student_grad[None], image_loss)


def solution(mesh):
    placed = (
        P(("dp", "proto"), None, None),
        P(("dp", "proto"), None, None),
        P(("dp", "proto"), None),
        P("dp", "proto"),
        P(None, "proto"),
        P(None, "proto"),
    )
    return jax.shard_map(
        body,
        mesh=mesh,
        in_specs=placed,
        out_specs=(P(("dp", "proto"), None, None), P("dp", "proto")),
        check_vma=False,
    )
```

time: 1250 us -> 247 us (0.20)
  blocking collectives: 1050 us -> 110 us
  other arithmetic: 52.1 us -> 4.85 us
  waiting for transfers between devices: 99.9 us -> 52.8 us
  Pallas kernels: 0 us -> 24.9 us
  local copies, waits for them, and re-layouts: 9.32 us -> 31.2 us
  matrix products: 16.4 us -> 0 us
    pmax x6 -> x0, blocking collectives: 573 us -> none  [the longest x3 338 us: column_lse(): highest = lax.pmax(jnp.max(values, axis=0), 'dp')]
    psum x7 -> x0, blocking collectives: 425 us -> none  [the longest x3 331 us: column_lse(): totals = lax.psum(jnp.sum(jnp.exp(values - highest[None, :]), axis=0), 'dp')]
    psum x1 -> x0, waiting for transfers between devices: 99.9 us -> none  [body(): lax.psum(partial_grad.astype(jnp.bfloat16), 'proto').astype(jnp.float32)]
    all_to_all x0 -> x5, blocking collectives: none -> 86.8 us  [the longest x3 60.6 us: body(): shares = over(share, 'dp')]
    reduce_scatter x0 -> x1, waiting for transfers between devices: none -> 52.8 us  [body(): lax.psum_scatter(student_part, 'proto', scatter_dimension=0, tiled=True)]
    reduce_sum x11 -> x0, other arithmetic: 30.8 us -> none  [the longest x3 11.8 us: row_lse(): jnp.sum(jnp.exp(values - highest[:, None]), axis=1)]
    unnamed x5 -> x55, local copies, waits for them, and re-layouts: 1.95 us -> 30.1 us
    pallas_call x0 -> x10, Pallas kernels: none -> 24.9 us  [call(): pl.pallas_call(kernel, out_shape=out_shape, in_specs=[VMEM] * len(args) i...]
  transfers between devices with their start and end apart: 1 -> 3, of which waited for: 1 -> 1; matrix products, arithmetic and copies ran while one was open for 0% -> 1% of each run, Pallas kernels for 0% -> 2%
where the time goes in v2:
time: 247 us; the launch traced here: 244 us
  blocking collectives  110 us (45%)
  waiting for transfers between devices  52.8 us (21%)
  local copies, waits for them, and re-layouts  31.2 us (13%)
  Pallas kernels  24.9 us (10%)
  between operations  14.9 us (6%)
  starting transfers between devices  5.37 us (2%)
  other arithmetic  4.85 us (2%)
    all_to_all x3, blocking collectives, body(): shares = over(share, 'dp')  60.6 us
    reduce_scatter x1, waiting for transfers between devices, body(): lax.psum_scatter(student_part, 'proto', scatter_dimension=0, tiled=True)  52.8 us
    unnamed x55, local copies, waits for them, and re-layouts  30.1 us
    all_to_all x2, blocking collectives, body(): shares = over(share, 'proto')  26.2 us
    pallas_call x10, Pallas kernels, call(): pl.pallas_call(kernel, out_shape=out_shape, in_specs=[VMEM] * len(args) i...  24.9 us
    all_gather x1, blocking collectives, body(): gathered = lax.all_gather(teacher_sent, 'proto', axis=0, tiled=False)  23 us
    all_to_all x1, starting transfers between devices, body(): back = over(sent, 'proto')  5.3 us
  transfers between devices with their start and end apart: 3, of which 1 were waited for; matrix products, arithmetic and copies ran while one was open for 1% of the time, Pallas kernels for 2%

profile of v2, /device:TPU:1, one launch (start us, length us, event | category | flops | bytes accessed | tf_op | source)
XLA Modules:
  0.0 243.8 jit_solution(15940583735511346719)
XLA Ops:
  7.9 0.9 copy-done.12
  8.8 0.9 copy-done.13
  9.7 0.7 copy-done.17
  10.3 0.8 shard_map.77
  11.2 23.0 %all-gather = bf16[1280,256]{1,0:T(8,128)(2,1)S(1)} all-gather(bf16[80,256]{1,0:T(8,128)(2,1)S(1)} %get-tuple-element.20), channel_id=2, replica_groups=mesh['dp'=32,'proto'=16] {'proto'}, dimensions={0}, use_global_device_ids=true | all-gather | bytes 696320 | tf_op jit(solution)/shard_map/all_gather | solution.py:331
  34.2 1.6 copy-done.19
  35.8 3.5 %shard_map.78 = (f32[32,4096]{1,0:T(8,128)S(1)}, bf16[384,256]{1,0:T(8,128)(2,1)S(1)}, f32[2,16,128]{2,1,0:T(8,128)S(1)}) custom-call(bf16[16,80,256]{2,1,0:T(8,128)(2,1)S(1)} %bitcast.20, bf16[256,4096]{1,0:T(8,128)(2,1)S(1)} %copy-done.19), custom_call_target="tpu_custom_call" | custom-call | flops 805306368 | bytes 2097152 | tf_op jit(solution)/shard_map/pallas_call | solution.py:27
  39.4 0.5 copy.11
  40.0 0.1 copy-done.22
  40.1 27.6 %all_to_all.48 = f32[32,1,4096]{2,1,0:T(1,128)S(1)} all-to-all(f32[32,1,4096]{2,1,0:T(1,128)S(1)} %copy.11), channel_id=1, replica_groups=mesh['dp'=32,'proto'=16] {'dp'}, dimensions={0} | all-to-all | bytes 1048576 | tf_op jit(solution)/shard_map/all_to_all | solution.py:343
  67.7 1.1 copy.20
  68.8 1.2 copy-done.21
  70.0 5.9 %shard_map.79 = (f32[384,256]{1,0:T(8,128)S(1)}, f32[384,1]{1,0:T(8,128)S(1)}, f32[3,128]{1,0:T(4,128)S(1)}) custom-call(bf16[16,128,256]{2,1,0:T(8,128)(2,1)S(1)} %bitcast.27, f32[2,16,128]{2,1,0:T(8,128)S(1)} %get-tuple-element.24.places_ref, bf16[256,4096]{1,0:T(8,128)(2,1)S(1)} %copy-done.3), custom_call_target="tpu_custom_call" | custom-call | flops 1610612736 | bytes 2097152 | tf_op jit(solution)/shard_map/pallas_call | solution.py:27
  76.0 0.7 copy-done.10
  76.7 3.6 %shard_map.80 = (bf16[384,4096]{1,0:T(8,128)(2,1)S(1)}, f32[4,384,1]{2,1,0:T(8,128)S(1)}, f32[16,8,128]{2,1,0:T(8,128)S(1)}) custom-call(f32[32,4096]{1,0:T(8,128)S(1)} %bitcast.21, bf16[384,256]{1,0:T(8,128)(2,1)S(1)} %copy-done.23, bf16[256,4096]{1,0:T(8,128)(2,1)S(1)} %copy-done.20, f32[3,128]{1,0:T(4,128)S(1)} %get-tuple-element.25.student_lse_ref), custom_call_target="tpu_custom_call" | custom-call | flops 805306368 | bytes 5242880 | tf_op jit(solution)/shard_map/pallas_call | solution.py:27
  80.3 13.8 %all_to_all.49.shares_ref = f32[16,8,128]{2,1,0:T(8,128)S(1)} all-to-all(f32[16,8,128]{2,1,0:T(8,128)S(1)} %get-tuple-element.26), channel_id=1, replica_groups=mesh['dp'=32,'proto'=16] {'proto'}, dimensions={0} | all-to-all | bytes 131072 | tf_op jit(solution)/shard_map/all_to_all | solution.py:370
  94.1 1.5 shard_map.81
  95.6 0.9 copy-done
  96.5 0.7 copy-done.8
  97.2 0.6 copy-done.15
  97.7 0.5 broadcast
  98.3 2.4 reduce
  100.7 1.9 reshape.16
  102.5 16.4 %all_to_all.50 = bf16[32,2,2048]{2,1,0:T(2,128)(2,1)} all-to-all(bf16[32,2,2048]{2,1,0:T(2,128)(2,1)} %reshape.16), channel_id=1, replica_groups=mesh['dp'=32,'proto'=16] {'dp'}, dimensions={0} | all-to-all | bytes 524288 | tf_op jit(solution)/shard_map/all_to_all | solution.py:392
  118.9 2.8 %reshape.17 = bf16[32,1,4096]{2,1,0:T(2,128)(2,1)} reshape(bf16[32,2,2048]{2,1,0:T(2,128)(2,1)} %all_to_all.50) | data formatting | bytes 524288
  121.7 1.3 copy.22
  123.1 1.1 copy-done.1
  124.2 1.4 shard_map.82
  125.6 12.4 %all_to_all.51.shares_ref = f32[16,8,128]{2,1,0:T(8,128)S(1)} all-to-all(f32[16,8,128]{2,1,0:T(8,128)S(1)} %shard_map.82), channel_id=1, replica_groups=mesh['dp'=32,'proto'=16] {'proto'}, dimensions={0} | all-to-all | bytes 131072 | tf_op jit(solution)/shard_map/all_to_all | solution.py:404
  138.0 1.4 shard_map.83
  139.4 0.9 copy-done.5
  140.3 0.7 copy-done.9
  141.0 2.4 reduce.1
  143.5 1.9 reshape.18
  145.3 16.7 %all_to_all.52 = bf16[32,2,2048]{2,1,0:T(2,128)(2,1)} all-to-all(bf16[32,2,2048]{2,1,0:T(2,128)(2,1)} %reshape.18), channel_id=1, replica_groups=mesh['dp'=32,'proto'=16] {'dp'}, dimensions={0} | all-to-all | bytes 524288 | tf_op jit(solution)/shard_map/all_to_all | solution.py:416
  162.0 2.8 %reshape.19 = bf16[32,1,4096]{2,1,0:T(2,128)(2,1)} reshape(bf16[32,2,2048]{2,1,0:T(2,128)(2,1)} %all_to_all.52) | data formatting | bytes 524288
  164.8 1.3 copy.21
  166.1 1.6 copy-done.4
  167.7 1.1 copy-done.6
  168.8 3.3 %shard_map.84 = bf16[16,80,256]{2,1,0:T(8,128)(2,1)S(1)} custom-call(bf16[32,4096]{1,0:T(8,128)(2,1)S(1)} %bitcast.19, f32[4,384,1]{2,1,0:T(8,128)S(1)} %copy-done.6, bf16[384,4096]{1,0:T(8,128)(2,1)S(1)} %get-tuple-element.28.matrix_ref, bf16[256,4096]{1,0:T(8,128)(2,1)S(1)} %copy-done.4, f32[2,16,128]{2,1,0:T(8,128)S(1)} %get-tuple-element.24.places_ref), custom_call_target="tpu_custom_call" | custom-call | flops 805306368 | bytes 3145728 | tf_op jit(solution)/shard_map/pallas_call | solution.py:27
  172.2 0.8 copy-done.2
  173.0 5.3 %all-to-all-start.5 = ((bf16[16,80,256]{2,1,0:T(8,128)(2,1)}), bf16[16,80,256]{2,1,0:T(8,128)(2,1)S(1)}, u32[]{:S(2)}, u32[]{:S(2)}) async-start(bf16[16,80,256]{2,1,0:T(8,128)(2,1)} %copy-done.2), calls=%async_computation.5 | async-start | bytes 1310720 | tf_op jit(solution)/shard_map/all_to_all | solution.py:431
  178.4 0.9 copy-done.11
  179.3 0.7 copy-done.16
  180.0 1.6 shard_map.85
  181.6 52.8 %reduce-scatter.2.cloned.1.call-done.student_ref = bf16[72,256]{1,0:T(8,128)(2,1)} async-done(((bf16[1152,256]{1,0:T(8,128)(2,1)}), bf16[72,256]{1,0:T(8,128)(2,1)}) %reduce-scatter.2.cloned.1.call-update) | async-done | bytes 36880 | tf_op jit(solution)/shard_map/reduce_scatter | solution.py:391
  234.4 0.8 copy-done.14
  235.1 1.9 shard_map.86
  (35 shorter events, 0.2 us)
Async XLA Ops:
  7.2 61.6 %all-gather.4.cloned.1.call-start = ((), (), s32[]{:S(2)}) async-start(), calls=%async_computation.8 | async-start | bytes 1114112 | tf_op jit(solution)/shard_map/all_gather | solution.py:330
  7.9 0.9 copy-start.12
  8.8 0.9 copy-start.13
  9.7 0.7 copy-start.17
  34.2 1.6 copy-start.19
  39.4 0.7 copy-start.22
  39.4 29.4 %copy-start.3 = (bf16[256,4096]{1,0:T(8,128)(2,1)S(1)}, bf16[256,4096]{1,0:T(8,128)(2,1)}, u32[]{:S(2)}) copy-start(bf16[256,4096]{1,0:T(8,128)(2,1)} %protos_ref.7) | copy-start | bytes 6291460
  68.8 1.2 copy-start.21
  70.0 6.6 %copy-start.7 = (f32[32,1,4096]{2,0,1:T(8,128)S(1)}, f32[32,1,4096]{2,0,1:T(8,128)}, u32[]{:S(2)}) copy-start(f32[32,1,4096]{2,0,1:T(8,128)} %copy.20) | copy-start | bytes 1572868
  70.0 6.6 %copy-start.20 = (bf16[256,4096]{1,0:T(8,128)(2,1)S(1)}, bf16[256,4096]{1,0:T(8,128)(2,1)}, u32[]{:S(2)}) copy-start(bf16[256,4096]{1,0:T(8,128)(2,1)} %protos_ref.6) | copy-start | bytes 6291460
  70.0 6.6 %copy-start.23 = (bf16[384,256]{1,0:T(8,128)(2,1)S(1)}, bf16[384,256]{1,0:T(8,128)(2,1)}, u32[]{:S(2)}) copy-start(bf16[384,256]{1,0:T(8,128)(2,1)} %copy-done.22) | copy-start | bytes 589828
  76.0 0.7 copy-start.10
  95.6 0.9 copy-start
  96.5 0.7 copy-start.8
  97.2 0.6 copy-start.15
  123.1 1.1 copy-start.1
  139.4 0.9 copy-start.5
  140.3 0.7 copy-start.9
  166.1 1.6 copy-start.4
  167.7 1.1 copy-start.6
  172.2 0.8 copy-start.2
  173.0 61.3 %copy-start.18 = (s32[1,256]{1,0:T(1,128)S(1)}, s32[1,256]{1,0:T(1,128)}, u32[]{:S(2)}) copy-start(s32[1,256]{1,0:T(1,128)} %order_ref.3) | copy-start | bytes 3076
  173.0 61.3 %all-to-all-start.5 = ((bf16[16,80,256]{2,1,0:T(8,128)(2,1)}), bf16[16,80,256]{2,1,0:T(8,128)(2,1)S(1)}, u32[]{:S(2)}, u32[]{:S(2)}) async-start(bf16[16,80,256]{2,1,0:T(8,128)(2,1)} %copy-done.2), calls=%async_computation.5 | async-start | bytes 1310720 | tf_op jit(solution)/shard_map/all_to_all | solution.py:431
  178.3 56.0 %reduce-scatter.2.cloned.1.call-start = ((), (), s32[]{:S(2)}) async-start(), calls=%async_computation.7 | async-start | bytes 626688 | tf_op jit(solution)/shard_map/reduce_scatter | solution.py:391
  178.4 0.9 copy-start.11
  179.3 0.7 copy-start.16
  234.4 0.8 copy-start.14
Sparse Core Ops, SparseCore 0:
  11.3 46.6 all-gather.3
  182.0 52.3 reduce-scatter.1

commit v3 on v2

--- a/solution.py
+++ b/solution.py
@@ -15,8 +15,8 @@
 F32 = jnp.float32
 BF16 = jnp.bfloat16
 LANES = 128
-BLOCK = 1024
-LIMIT = 40 << 20
+BLOCK = 2048
+LIMIT = 20 << 20
 VMEM = pl.BlockSpec(memory_space=pltpu.VMEM)
 SMEM = pl.BlockSpec(memory_space=pltpu.SMEM)
 
@@ -60,6 +60,19 @@
     return jnp.concatenate(parts, axis=0)
 
 
+def to_lines(row):
+    return jnp.concatenate([row[:, b * LANES : (b + 1) * LANES] for b in range(row.shape[1] // LANES)], axis=0)
+
+
+def to_row(lines):
+    return jnp.concatenate([lines[b : b + 1] for b in range(lines.shape[0])], axis=1)
+
+
+def merged(shares):
+    top = jnp.max(shares, axis=0)
+    return top + jnp.log(jnp.sum(jnp.exp(shares - top[None]), axis=0))
+
+
 def pick_kernel(teacher_ref, student_ref, order_ref, count_ref, teacher_out, student_out):
     patches, width = teacher_ref.shape
     order = jnp.broadcast_to(order_ref[:, :LANES], (patches, LANES))
@@ -111,14 +124,12 @@
     logits = jnp.dot(rows_ref[...], protos_ref[...], preferred_element_type=F32) * TEACH
     high = jnp.max(logits, axis=0, keepdims=True)
     total = jnp.sum(jnp.exp(logits - high), axis=0, keepdims=True)
-    share_ref[...] = jnp.broadcast_to(high + jnp.log(total), share_ref.shape)
+    share_ref[...] = jnp.broadcast_to(to_lines(high + jnp.log(total))[None], share_ref.shape)
 
 
 def row_kernel(shares_ref, rows_ref, protos_ref, student_lse_ref, matrix_ref, high_ref, share_ref, sums):
     step = pl.program_id(0)
-    shares = shares_ref[...]
-    top = jnp.max(shares, axis=0, keepdims=True)
-    column = top + jnp.log(jnp.sum(jnp.exp(shares - top), axis=0, keepdims=True))
+    column = to_row(merged(shares_ref[...]))
     logits = jnp.dot(rows_ref[...], protos_ref[...], preferred_element_type=F32) * TEACH
     shifted = logits - column
     high = jnp.max(shifted, axis=1, keepdims=True)
@@ -138,14 +149,9 @@
         share_ref[...] = jnp.broadcast_to(chunk[None], share_ref.shape)
 
 
-def merged(shares):
-    top = jnp.max(shares, axis=0)
-    return top + jnp.log(jnp.sum(jnp.exp(shares - top[None]), axis=0))
-
-
 def column_sums(matrix_ref, scale, share_ref):
     sums = jnp.sum(matrix_ref[...].astype(F32) * scale, axis=0, keepdims=True)
-    share_ref[...] = jnp.broadcast_to(sums, share_ref.shape).astype(share_ref.dtype)
+    share_ref[...] = jnp.broadcast_to(to_lines(sums)[None], share_ref.shape).astype(share_ref.dtype)
 
 
 def first_column_kernel(shares_ref, high_ref, matrix_ref, share_ref, scale_ref, student_lse_ref):
@@ -175,7 +181,7 @@
 
 def later_row_kernel(shares_ref, scale_ref, matrix_ref, share_ref, sums):
     step = pl.program_id(0)
-    inverse = 1.0 / jnp.sum(shares_ref[...].astype(F32), axis=0, keepdims=True)
+    inverse = to_row(1.0 / jnp.sum(shares_ref[...].astype(F32), axis=0))
     part = scale_ref[step] * jnp.sum(matrix_ref[...].astype(F32) * inverse, axis=1, keepdims=True)
 
     @pl.when(step == 0)
@@ -196,7 +202,7 @@
 def target_kernel(shares_ref, scale_ref, matrix_ref, protos_ref, places_ref, out_ref, sums, total):
     step = pl.program_id(0)
     scale = scale_ref[step]
-    inverse = 1.0 / jnp.sum(shares_ref[...].astype(F32), axis=0, keepdims=True)
+    inverse = to_row(1.0 / jnp.sum(shares_ref[...].astype(F32), axis=0))
     weights = matrix_ref[...].astype(F32) * inverse
     narrow = weights.astype(BF16)
     part = scale * lax.dot_general(narrow, protos_ref[...], (((1,), (1,)), ((), ())), preferred_element_type=F32)
@@ -285,7 +291,7 @@
     mass = to_column((back[MOST : MOST + 1] + back[MOST + 1 : MOST + 2])[:, :LANES])[:MOST]
     used = iota((MOST, 1), 0).astype(F32) < count[:, :1]
     mean = back[:MOST] / jnp.where(used, mass, 1.0)
-    lse_row = jnp.concatenate([lse_ref[b : b + 1] for b in range(lines)], axis=1)
+    lse_row = to_row(lse_ref[...])
     shape = (MOST, lines * LANES)
     here = (iota(shape, 1) - iota(shape, 0)).astype(F32) == start[:, :1]
     own_lse = jnp.sum(jnp.where(here, lse_row, 0.0), axis=1, keepdims=True)
@@ -311,7 +317,7 @@
     index = lax.axis_index("proto").astype(jnp.int32).reshape(1, 1)
     over = functools.partial(lax.all_to_all, split_axis=0, concat_axis=0, tiled=True)
     wide = pl.BlockSpec((bot, BLOCK), lambda k: (0, k))
-    peer = pl.BlockSpec((groups, BLOCK), lambda k: (0, k))
+    peer = pl.BlockSpec((groups, BLOCK // LANES, LANES), lambda k: (0, k, 0))
     square = pl.BlockSpec((rows, BLOCK), lambda k: (0, k))
     grid = (steps,)
     dot = 2 * rows * protos * bot
@@ -331,7 +337,7 @@
     gathered = lax.all_gather(teacher_sent, "proto", axis=0, tiled=False)
     share, teacher_rows, places = call(
         column_kernel,
-        [((groups, protos), F32), ((rows, bot), BF16), ((2, width, LANES), F32)],
+        [((groups, protos // LANES, LANES), F32), ((rows, bot), BF16), ((2, width, LANES), F32)],
         gathered,
         teacher_protos,
         grid=grid,
@@ -370,7 +376,7 @@
     shares = over(share, "proto")
     share, scale, student_lse = call(
         first_column_kernel,
-        [((groups, protos), BF16), ((steps, rows, 1), F32), ((lines, LANES), F32)],
+        [((groups, protos // LANES, LANES), BF16), ((steps, rows, 1), F32), ((lines, LANES), F32)],
         shares,
         high,
         matrix,
@@ -388,8 +394,8 @@
         places,
         flops=2 * width * MOST * rows * bot,
     )[0]
+    shares, student_part = lax.optimization_barrier((over(share, "dp"), student_part))
     student_back = lax.psum_scatter(student_part, "proto", scatter_dimension=0, tiled=True)
-    shares = over(share, "dp")
     share = call(
         later_row_kernel,
         [((width, depth, LANES), F32)],
@@ -404,7 +410,7 @@
     shares = over(share, "proto")
     share, scale = call(
         later_column_kernel,
-        [((groups, protos), BF16), ((steps, rows, 1), F32)],
+        [((groups, protos // LANES, LANES), BF16), ((steps, rows, 1), F32)],
         shares,
         scale,
         matrix,

time: 247 us -> 217 us (0.88)
  blocking collectives: 110 us -> 64.3 us
  waiting for transfers between devices: 52.8 us -> 72.2 us
  starting transfers between devices: 5.37 us -> 23.8 us
  local copies, waits for them, and re-layouts: 31.2 us -> 16.7 us
  other arithmetic: 4.85 us -> 0 us
    all_to_all x3 -> x1, blocking collectives: 60.6 us -> 15.1 us  [body(): shares = over(share, 'dp')]
    all_to_all x0 -> x2, starting transfers between devices: none -> 18.2 us  [the longest x1 11 us: body(): shares = over(share, 'dp')]
    unnamed x55 -> x44, local copies, waits for them, and re-layouts: 30.1 us -> 16.7 us
    all_to_all x0 -> x2, waiting for transfers between devices: none -> 9.05 us  [the longest x1 7.65 us: body(): over(share, 'dp')]
    all_gather x1, waiting for transfers between devices: 0.01 us -> 7.25 us  [body(): lax.all_gather(student_sent, 'proto', axis=0, tiled=False)]
    all_to_all x2 -> x0, other arithmetic: 4.85 us -> none  [body(): shares = over(share, 'dp')]
  transfers between devices with their start and end apart: 3 -> 5, of which waited for: 1 -> 4; matrix products, arithmetic and copies ran while one was open for 1% -> 0% of each run, Pallas kernels for 2% -> 5%
where the time goes in v3:
time: 217 us; the launch traced here: 215 us
  waiting for transfers between devices  72.2 us (33%)
  blocking collectives  64.3 us (30%)
  starting transfers between devices  23.8 us (11%)
  Pallas kernels  22.9 us (11%)
  local copies, waits for them, and re-layouts  16.7 us (8%)
  between operations  14.8 us (7%)
    reduce_scatter x1, waiting for transfers between devices, body(): lax.psum_scatter(student_part, 'proto', scatter_dimension=0, tiled=True)  55.2 us
    all_to_all x2, blocking collectives, body(): shares = over(share, 'proto')  26.2 us
    all_gather x1, blocking collectives, body(): gathered = lax.all_gather(teacher_sent, 'proto', axis=0, tiled=False)  23 us
    pallas_call x10, Pallas kernels, call(): pl.pallas_call(kernel, out_shape=out_shape, in_specs=[VMEM] * len(args) i...  22.9 us
    unnamed x44, local copies, waits for them, and re-layouts  16.7 us
    all_to_all x1, blocking collectives, body(): shares = over(share, 'dp')  15.1 us
    all_to_all x1, starting transfers between devices, body(): shares = over(share, 'dp')  11 us
    all_to_all x1, waiting for transfers between devices, body(): over(share, 'dp')  7.65 us
  transfers between devices with their start and end apart: 5, of which 4 were waited for; matrix products, arithmetic and copies ran while one was open for 0% of the time, Pallas kernels for 5%

profile of v3, /device:TPU:1, one launch (start us, length us, event | category | flops | bytes accessed | tf_op | source)
XLA Modules:
  0.0 214.7 jit_solution(3443907316272679528)
XLA Ops:
  7.2 0.0 all-gather.4.cloned.1.call-start
  7.9 0.0 copy-start.11
  7.9 0.9 copy-done.11
  8.8 0.9 copy-done.12
  9.7 0.7 copy-done.17
  10.3 0.8 shard_map.77
  11.2 0.0 all-gather.4.cloned.1.call-update
  11.2 23.0 %all-gather = bf16[1280,256]{1,0:T(8,128)(2,1)S(1)} all-gather(bf16[80,256]{1,0:T(8,128)(2,1)S(1)} %get-tuple-element.22), channel_id=2, replica_groups=mesh['dp'=32,'proto'=16] {'proto'}, dimensions={0}, use_global_device_ids=true | all-gather | bytes 696320 | tf_op jit(solution)/shard_map/all_gather | solution.py:337
  34.2 1.8 copy-done.19
  36.0 3.8 %shard_map.78 = (f32[32,32,128]{2,1,0:T(8,128)}, bf16[384,256]{1,0:T(8,128)(2,1)S(1)}, f32[2,16,128]{2,1,0:T(8,128)S(1)}) custom-call(bf16[16,80,256]{2,1,0:T(8,128)(2,1)S(1)} %bitcast.6, bf16[256,4096]{1,0:T(8,128)(2,1)S(1)} %copy-done.19), custom_call_target="tpu_custom_call" | custom-call | flops 805306368 | bytes 2097152 | tf_op jit(solution)/shard_map/pallas_call | solution.py:27
  39.9 11.0 %all-to-all-start = ((f32[32,32,128]{2,1,0:T(8,128)}), f32[32,32,128]{2,1,0:T(8,128)S(1)}, u32[]{:S(2)}, u32[]{:S(2)}) async-start(f32[32,32,128]{2,1,0:T(8,128)} %get-tuple-element.23), calls=%async_computation | async-start | bytes 1048576 | tf_op jit(solution)/shard_map/all_to_all | solution.py:349
  50.8 7.3 %all-gather.4.cloned.1.call-done = bf16[2048,256]{1,0:T(8,128)(2,1)} async-done(((bf16[128,256]{1,0:T(8,128)(2,1)}), bf16[2048,256]{1,0:T(8,128)(2,1)}) %all-gather.4.cloned.1.call-update) | async-done | bytes 1048592 | tf_op jit(solution)/shard_map/all_gather | solution.py:336
  58.1 0.0 copy-done.2
  58.1 1.2 copy-done.21
  59.3 5.4 %shard_map.79 = (f32[384,256]{1,0:T(8,128)S(1)}, f32[384,1]{1,0:T(8,128)S(1)}, f32[3,128]{1,0:T(4,128)S(1)}) custom-call(bf16[16,128,256]{2,1,0:T(8,128)(2,1)S(1)} %bitcast.9, f32[2,16,128]{2,1,0:T(8,128)S(1)} %get-tuple-element.26.places_ref, bf16[256,4096]{1,0:T(8,128)(2,1)S(1)} %copy-done.2), custom_call_target="tpu_custom_call" | custom-call | flops 1610612736 | bytes 2097152 | tf_op jit(solution)/shard_map/pallas_call | solution.py:27
  64.7 0.8 copy-done.6
  65.5 0.7 copy-done.9
  66.1 1.4 all-to-all-done.shares_ref
  67.5 0.8 copy-done.4
  68.3 1.0 copy-done.5
  69.4 1.6 copy-done.20
  71.0 3.0 %shard_map.80 = (bf16[384,4096]{1,0:T(8,128)(2,1)S(1)}, f32[2,384,1]{2,1,0:T(8,128)S(1)}, f32[16,8,128]{2,1,0:T(8,128)S(1)}) custom-call(f32[32,32,128]{2,1,0:T(8,128)S(1)} %copy-done.5, bf16[384,256]{1,0:T(8,128)(2,1)S(1)} %get-tuple-element.24.rows_ref, bf16[256,4096]{1,0:T(8,128)(2,1)S(1)} %copy-done.20, f32[3,128]{1,0:T(4,128)S(1)} %get-tuple-element.27.student_lse_ref), custom_call_target="tpu_custom_call" | custom-call | flops 805306368 | bytes 5242880 | tf_op jit(solution)/shard_map/pallas_call | solution.py:27
  74.0 13.8 %all_to_all.30.shares_ref = f32[16,8,128]{2,1,0:T(8,128)S(1)} all-to-all(f32[16,8,128]{2,1,0:T(8,128)S(1)} %get-tuple-element.28), channel_id=1, replica_groups=mesh['dp'=32,'proto'=16] {'proto'}, dimensions={0} | all-to-all | bytes 131072 | tf_op jit(solution)/shard_map/all_to_all | solution.py:376
  87.8 1.2 shard_map.81
  89.1 0.7 copy-done.8
  89.8 0.6 copy-done.14
  90.4 7.2 %all-to-all-start.2 = ((bf16[32,32,128]{2,1,0:T(8,128)(2,1)}), bf16[32,32,128]{2,1,0:T(8,128)(2,1)}, u32[]{:S(2)}, u32[]{:S(2)}) async-start(bf16[32,32,128]{2,1,0:T(8,128)(2,1)} %copy-done.8), calls=%async_computation.2 | async-start | bytes 524288 | tf_op jit(solution)/shard_map/all_to_all | solution.py:397
  97.6 0.0 copy-start.7
  97.6 1.0 copy-done.7
  98.6 0.9 copy-done.10
  99.5 0.7 copy-done.15
  100.2 0.7 shard_map.82
  100.9 0.8 copy-done.1
  101.7 7.6 %all-to-all-done.2.shares_ref = bf16[32,32,128]{2,1,0:T(8,128)(2,1)} async-done(((bf16[32,32,128]{2,1,0:T(8,128)(2,1)}), bf16[32,32,128]{2,1,0:T(8,128)(2,1)}, u32[]{:S(2)}, u32[]{:S(2)}) %all-to-all-start.2) | async-done | bytes 262176 | tf_op jit(solution)/shard_map/all_to_all | solution.py:397
  109.4 1.9 shard_map.83
  111.3 12.4 %all_to_all.31.shares_ref = f32[16,8,128]{2,1,0:T(8,128)S(1)} all-to-all(f32[16,8,128]{2,1,0:T(8,128)S(1)} %shard_map.83), channel_id=1, replica_groups=mesh['dp'=32,'proto'=16] {'proto'}, dimensions={0} | all-to-all | bytes 131072 | tf_op jit(solution)/shard_map/all_to_all | solution.py:410
  123.7 1.2 shard_map.84
  125.0 15.1 %all_to_all.32.shares_ref = bf16[32,32,128]{2,1,0:T(8,128)(2,1)S(1)} all-to-all(bf16[32,32,128]{2,1,0:T(8,128)(2,1)S(1)} %get-tuple-element.37), channel_id=1, replica_groups=mesh['dp'=32,'proto'=16] {'dp'}, dimensions={0} | all-to-all | bytes 524288 | tf_op jit(solution)/shard_map/all_to_all | solution.py:422
  140.1 0.0 copy-done.3
  140.1 2.8 %shard_map.85 = bf16[16,80,256]{2,1,0:T(8,128)(2,1)S(1)} custom-call(bf16[32,32,128]{2,1,0:T(8,128)(2,1)S(1)} %all_to_all.32.shares_ref, f32[2,384,1]{2,1,0:T(8,128)S(1)} %get-tuple-element.38.scale_ref, bf16[384,4096]{1,0:T(8,128)(2,1)S(1)} %get-tuple-element.30.matrix_ref, bf16[256,4096]{1,0:T(8,128)(2,1)S(1)} %copy-done.3, ...), custom_call_target="tpu_custom_call" | custom-call | flops 805306368 | bytes 3145728 | tf_op jit(solution)/shard_map/pallas_call | solution.py:27
  142.9 0.9 copy-done
  143.7 5.5 %all-to-all-start.5 = ((bf16[16,80,256]{2,1,0:T(8,128)(2,1)}), bf16[16,80,256]{2,1,0:T(8,128)(2,1)S(1)}, u32[]{:S(2)}, u32[]{:S(2)}) async-start(bf16[16,80,256]{2,1,0:T(8,128)(2,1)} %copy-done), calls=%async_computation.5 | async-start | bytes 1310720 | tf_op jit(solution)/shard_map/all_to_all | solution.py:437
  149.3 0.0 reduce-scatter.2.cloned.1.call-start
  149.3 0.7 reduce-scatter.2.cloned.1.call-update
  150.0 55.2 %reduce-scatter.2.cloned.1.call-done.student_ref = bf16[72,256]{1,0:T(8,128)(2,1)} async-done(((bf16[1152,256]{1,0:T(8,128)(2,1)}), bf16[72,256]{1,0:T(8,128)(2,1)}) %reduce-scatter.2.cloned.1.call-update) | async-done | bytes 36880 | tf_op jit(solution)/shard_map/reduce_scatter | solution.py:398
  205.2 0.0 all-to-all-done.5.back_ref
  205.2 0.8 copy-done.13
  206.0 1.9 shard_map.86
  (22 shorter events, 0.0 us)
Async XLA Ops:
  7.2 50.9 %all-gather.4.cloned.1.call-start = ((), (), s32[]{:S(2)}) async-start(), calls=%async_computation.8 | async-start | bytes 1114112 | tf_op jit(solution)/shard_map/all_gather | solution.py:336
  7.9 0.9 copy-start.11
  8.8 0.9 copy-start.12
  9.7 0.7 copy-start.17
  34.2 23.9 %copy-start.2 = (bf16[256,4096]{1,0:T(8,128)(2,1)S(1)}, bf16[256,4096]{1,0:T(8,128)(2,1)}, u32[]{:S(2)}) copy-start(bf16[256,4096]{1,0:T(8,128)(2,1)} %protos_ref.7) | copy-start | bytes 6291460
  34.2 1.8 copy-start.19
  39.9 27.7 %all-to-all-start = ((f32[32,32,128]{2,1,0:T(8,128)}), f32[32,32,128]{2,1,0:T(8,128)S(1)}, u32[]{:S(2)}, u32[]{:S(2)}) async-start(f32[32,32,128]{2,1,0:T(8,128)} %get-tuple-element.23), calls=%async_computation | async-start | bytes 1048576 | tf_op jit(solution)/shard_map/all_to_all | solution.py:349
  58.1 1.2 copy-start.21
  64.7 0.8 copy-start.6
  65.5 0.7 copy-start.9
  67.5 0.8 copy-start.4
  68.3 1.0 copy-start.5
  69.4 1.6 copy-start.20
  89.1 0.7 copy-start.8
  89.8 0.6 copy-start.14
  90.4 19.0 %all-to-all-start.2 = ((bf16[32,32,128]{2,1,0:T(8,128)(2,1)}), bf16[32,32,128]{2,1,0:T(8,128)(2,1)}, u32[]{:S(2)}, u32[]{:S(2)}) async-start(bf16[32,32,128]{2,1,0:T(8,128)(2,1)} %copy-done.8), calls=%async_computation.2 | async-start | bytes 524288 | tf_op jit(solution)/shard_map/all_to_all | solution.py:397
  97.6 1.0 copy-start.7
  98.6 0.9 copy-start.10
  99.5 0.7 copy-start.15
  100.9 0.9 copy-start.1
  123.7 16.3 %copy-start.3 = (bf16[256,4096]{1,0:T(8,128)(2,1)S(1)}, bf16[256,4096]{1,0:T(8,128)(2,1)}, u32[]{:S(2)}) copy-start(bf16[256,4096]{1,0:T(8,128)(2,1)} %protos_ref.7) | copy-start | bytes 6291460
  140.1 65.2 %copy-start.16 = (f32[3,128]{1,0:T(4,128)S(1)}, f32[3,128]{1,0:T(4,128)}, u32[]{:S(2)}) copy-start(f32[3,128]{1,0:T(4,128)} %copy-done.14) | copy-start | bytes 4612
  140.1 65.2 %copy-start.18 = (s32[1,256]{1,0:T(1,128)S(1)}, s32[1,256]{1,0:T(1,128)}, u32[]{:S(2)}) copy-start(s32[1,256]{1,0:T(1,128)} %order_ref.3) | copy-start | bytes 3076
  142.9 0.9 copy-start
  143.7 61.5 %all-to-all-start.5 = ((bf16[16,80,256]{2,1,0:T(8,128)(2,1)}), bf16[16,80,256]{2,1,0:T(8,128)(2,1)S(1)}, u32[]{:S(2)}, u32[]{:S(2)}) async-start(bf16[16,80,256]{2,1,0:T(8,128)(2,1)} %copy-done), calls=%async_computation.5 | async-start | bytes 1310720 | tf_op jit(solution)/shard_map/all_to_all | solution.py:437
  149.3 55.9 %reduce-scatter.2.cloned.1.call-start = ((), (), s32[]{:S(2)}) async-start(), calls=%async_computation.7 | async-start | bytes 626688 | tf_op jit(solution)/shard_map/reduce_scatter | solution.py:398
  205.2 0.8 copy-start.13
Sparse Core Ops, SparseCore 0:
  11.3 46.6 all-gather.3
  152.9 52.2 reduce-scatter.1

commit v4 on v3

--- a/solution.py
+++ b/solution.py
@@ -107,7 +107,7 @@
     return used.astype(F32).astype(BF16).reshape(images * slots, rows)
 
 
-def column_kernel(gathered_ref, protos_ref, share_ref, rows_ref, places_ref):
+def column_kernel(gathered_ref, index_ref, protos_ref, share_ref, rows_ref, places_ref):
     images = gathered_ref.shape[0]
     rows = rows_ref.shape[0]
 
@@ -116,8 +116,14 @@
         counts = gathered_ref[:, MOST:MOST + 8, :LANES].astype(F32)[:, 0]
         before = (iota((images, images), 1) < iota((images, images), 0)).astype(BF16)
         starts = jnp.dot(before, counts.astype(BF16), preferred_element_type=F32)
-        places_ref[0] = starts
-        places_ref[1] = counts
+        half, core = images // 2, index_ref[0, 0] % 2
+        place = iota((images, images), 0)
+        image = jnp.where(place < half, 2 * place + core, 2 * (place - half) + 1 - core)
+        other = iota((images, images), 1)
+        places_ref[0] = jnp.dot((other < image).astype(BF16), counts.astype(BF16), preferred_element_type=F32)
+        places_ref[1] = jnp.dot((other == image).astype(BF16), counts.astype(BF16), preferred_element_type=F32)
+        places_ref[2] = starts
+        places_ref[3] = counts
         flat = gathered_ref[...].reshape(images * SLOT, gathered_ref.shape[2])
         rows_ref[...] = compact(flat, starts, counts, rows)
 
@@ -127,7 +133,12 @@
     share_ref[...] = jnp.broadcast_to(to_lines(high + jnp.log(total))[None], share_ref.shape)
 
 
-def row_kernel(shares_ref, rows_ref, protos_ref, student_lse_ref, matrix_ref, high_ref, share_ref, sums):
+def fill_share(share_ref, lines):
+    blank = jnp.zeros((share_ref.shape[1] - lines.shape[0], LANES), F32)
+    share_ref[...] = jnp.broadcast_to(jnp.concatenate([lines, blank], axis=0)[None], share_ref.shape)
+
+
+def row_kernel(shares_ref, rows_ref, protos_ref, matrix_ref, high_ref, share_ref, sums):
     step = pl.program_id(0)
     column = to_row(merged(shares_ref[...]))
     logits = jnp.dot(rows_ref[...], protos_ref[...], preferred_element_type=F32) * TEACH
@@ -143,10 +154,7 @@
         highs = high_ref[...]
         top = jnp.max(highs, axis=0)
         total = jnp.sum(jnp.exp(highs - top[None]) * sums[...], axis=0)
-        own = to_lanes(top + jnp.log(total))
-        peers, depth = share_ref.shape[0], share_ref.shape[1]
-        chunk = jnp.concatenate([own, student_lse_ref[...], jnp.zeros((depth - 2 * own.shape[0], LANES), F32)], axis=0)
-        share_ref[...] = jnp.broadcast_to(chunk[None], share_ref.shape)
+        fill_share(share_ref, to_lanes(top + jnp.log(total)))
 
 
 def column_sums(matrix_ref, scale, share_ref):
@@ -154,15 +162,14 @@
     share_ref[...] = jnp.broadcast_to(to_lines(sums)[None], share_ref.shape).astype(share_ref.dtype)
 
 
-def first_column_kernel(shares_ref, high_ref, matrix_ref, share_ref, scale_ref, student_lse_ref):
+def first_column_kernel(shares_ref, high_ref, matrix_ref, share_ref, scale_ref):
     step = pl.program_id(0)
-    lines = student_lse_ref.shape[0]
 
     @pl.when(step == 0)
     def _():
-        both = merged(shares_ref[...][:, : 2 * lines])
-        student_lse_ref[...] = both[lines:]
-        scale_ref[...] = jnp.exp(high_ref[...] - to_column(both[:lines])[None])
+        lines = scale_ref.shape[1] // LANES
+        row_lse = merged(shares_ref[...][:, :lines])
+        scale_ref[...] = jnp.exp(high_ref[...] - to_column(row_lse)[None])
 
     column_sums(matrix_ref, scale_ref[step], share_ref)
 
@@ -194,12 +201,59 @@
 
     @pl.when(step == pl.num_programs(0) - 1)
     def _():
-        own = to_lanes(sums[...])
-        chunk = jnp.concatenate([own, jnp.zeros((share_ref.shape[1] - own.shape[0], LANES), F32)], axis=0)
-        share_ref[...] = jnp.broadcast_to(chunk[None], share_ref.shape)
-
-
-def target_kernel(shares_ref, scale_ref, matrix_ref, protos_ref, places_ref, out_ref, sums, total):
+        fill_share(share_ref, to_lanes(sums[...]))
+
+
+def split(values, parts):
+    out = []
+    for _ in range(parts):
+        part = values.astype(BF16)
+        out.append(part)
+        values = values - part.astype(F32)
+    return out
+
+
+def pack(sums, numbers, parts, starts, counts):
+    rows, width = sums.shape
+    images = starts.shape[0]
+    wide = jnp.broadcast_to(numbers, (rows, LANES))
+    sent = jnp.concatenate([sums.astype(BF16)] + split(wide, parts), axis=1)
+    chosen = spread(starts, counts, SLOT, rows)
+    packed = jnp.dot(chosen, sent, preferred_element_type=F32).reshape(images, SLOT, width + parts * LANES)
+    same = iota((1, SLOT, LANES), 1) == iota((1, SLOT, LANES), 2)
+    tail = []
+    for k in range(parts):
+        part = packed[:, :, width + k * LANES : width + (k + 1) * LANES]
+        tail.append(jnp.sum(jnp.where(same, part, 0.0), axis=1, keepdims=True))
+    return packed[:, :MOST, :width].astype(BF16), join(tail, width)
+
+
+def join(tail, width):
+    images = tail[0].shape[0]
+    filler = jnp.zeros((images, 1, width - LANES), F32)
+    rows = [jnp.concatenate([part.astype(F32), filler], axis=2) for part in tail]
+    rows.append(jnp.zeros((images, SLOT - MOST - len(tail), width), F32))
+    return jnp.concatenate(rows, axis=1).astype(BF16)
+
+
+def numbers_of(chunk, parts):
+    tail = chunk[:, MOST:SLOT, :LANES].astype(F32)
+    return sum(tail[:, k] for k in range(parts))
+
+
+def put(own_ref, other_ref, rows, tail):
+    half = own_ref.shape[0]
+    own_ref[:, :MOST], own_ref[:, MOST:] = rows[:half], tail[:half]
+    other_ref[:, :MOST], other_ref[:, MOST:] = rows[half:], tail[half:]
+
+
+def slots_of(lanes):
+    images = lanes.shape[0]
+    same = iota((1, MOST, LANES), 1) == iota((1, MOST, LANES), 2)
+    return jnp.sum(jnp.where(same, lanes.reshape(images, 1, LANES), 0.0), axis=2, keepdims=True)
+
+
+def target_kernel(shares_ref, scale_ref, matrix_ref, protos_ref, places_ref, own_ref, other_ref, sums, total):
     step = pl.program_id(0)
     scale = scale_ref[step]
     inverse = to_row(1.0 / jnp.sum(shares_ref[...].astype(F32), axis=0))
@@ -220,30 +274,18 @@
 
     @pl.when(step == pl.num_programs(0) - 1)
     def _():
-        rows, width = sums.shape
-        mass_high = jnp.broadcast_to(total[...], (rows, LANES)).astype(BF16)
-        mass_low = (jnp.broadcast_to(total[...], (rows, LANES)) - mass_high.astype(F32)).astype(BF16)
-        sent = jnp.concatenate([sums[...].astype(BF16), mass_high, mass_low], axis=1)
-        images = out_ref.shape[0]
-        chosen = spread(places_ref[0], places_ref[1], SLOT, rows)
-        packed = jnp.dot(chosen, sent, preferred_element_type=F32).reshape(images, SLOT, width + 2 * LANES)
-        same = iota((1, SLOT, LANES), 1) == iota((1, SLOT, LANES), 2)
-        high = jnp.sum(jnp.where(same, packed[:, :, width : width + LANES], 0.0), axis=1, keepdims=True)
-        low = jnp.sum(jnp.where(same, packed[:, :, width + LANES :], 0.0), axis=1, keepdims=True)
-        filler = jnp.zeros((images, 1, width - LANES), F32)
-        out_ref[:, :MOST] = packed[:, :MOST, :width].astype(BF16)
-        numbers = jnp.concatenate(
-            [
-                jnp.concatenate([high, filler], axis=2),
-                jnp.concatenate([low, filler], axis=2),
-                jnp.zeros((images, SLOT - MOST - 2, width), F32),
-            ],
-            axis=1,
-        )
-        out_ref[:, MOST:] = numbers.astype(BF16)
-
-
-def student_kernel(gathered_ref, places_ref, protos_ref, sums_ref, high_ref, lse_ref, rows_ref, total):
+        put(own_ref, other_ref, *pack(sums[...], total[...], 2, places_ref[0], places_ref[1]))
+
+
+def target_merge_kernel(own_ref, came_ref, student_ref, out_ref):
+    width = own_ref.shape[2]
+    out_ref[:, :MOST] = (own_ref[:, :MOST].astype(F32) + came_ref[:, :MOST].astype(F32)).astype(BF16)
+    total = numbers_of(own_ref, 2) + numbers_of(came_ref, 2)
+    out_ref[:, MOST:SLOT] = join([part[:, None] for part in split(total, 2)], width)
+    out_ref[:, SLOT:] = student_ref[...]
+
+
+def student_kernel(gathered_ref, places_ref, protos_ref, own_ref, other_ref, rows_ref, sums, top, total):
     step = pl.program_id(0)
     rows = rows_ref.shape[0]
 
@@ -251,54 +293,58 @@
     def _():
         images, slots, width = gathered_ref.shape
         flat = gathered_ref[...].reshape(images * slots, width)
-        rows_ref[...] = compact(flat, places_ref[0], places_ref[1], rows)
-        high_ref[...] = jnp.full(high_ref.shape, -1e30, F32)
+        rows_ref[...] = compact(flat, places_ref[2], places_ref[3], rows)
+        top[...] = jnp.full(top.shape, -1e30, F32)
         total[...] = jnp.zeros(total.shape, F32)
-        sums_ref[...] = jnp.zeros(sums_ref.shape, F32)
+        sums[...] = jnp.zeros(sums.shape, F32)
 
     protos = protos_ref[...]
     logits = jnp.dot(rows_ref[...], protos, preferred_element_type=F32) * STUD
-    before = high_ref[...]
+    before = top[...]
     high = jnp.maximum(before, jnp.max(logits, axis=1, keepdims=True))
     shrink = jnp.exp(before - high)
     exact = jnp.exp(logits - high)
     total[...] = total[...] * shrink + jnp.sum(exact, axis=1, keepdims=True)
     part = lax.dot_general(exact.astype(BF16), protos, (((1,), (1,)), ((), ())), preferred_element_type=F32)
-    sums_ref[...] = sums_ref[...] * shrink + part
-    high_ref[...] = high
+    sums[...] = sums[...] * shrink + part
+    top[...] = high
 
     @pl.when(step == pl.num_programs(0) - 1)
     def _():
-        lse_ref[...] = to_lanes(high_ref[...] + jnp.log(total[...]))
-
-
-def student_pack_kernel(sums_ref, high_ref, lse_ref, places_ref, out_ref):
-    rows = sums_ref.shape[0]
-    images = places_ref.shape[1]
-    sent = (sums_ref[...] * jnp.exp(high_ref[...] - to_column(lse_ref[...]))).astype(BF16)
-    chosen = spread(places_ref[0], places_ref[1], out_ref.shape[0] // images, rows)
-    out_ref[...] = jnp.dot(chosen, sent, preferred_element_type=F32).astype(BF16)
-
-
-def finish_kernel(back_ref, student_ref, picked_ref, lse_ref, places_ref, order_ref, index_ref, grad_ref, loss_ref):
+        mean, own_lse = sums[...] / total[...], top[...] + jnp.log(total[...])
+        put(own_ref, other_ref, *pack(mean, own_lse, 3, places_ref[0], places_ref[1]))
+
+
+def blend(chunk, lse):
+    joint = merged(lse)
+    weights = slots_of(jnp.exp(lse - joint[None]))
+    return jnp.sum(chunk * weights, axis=0), joint
+
+
+def student_merge_kernel(own_ref, came_ref, out_ref):
+    width = own_ref.shape[2]
+    own, came = numbers_of(own_ref, 3), numbers_of(came_ref, 3)
+    high = jnp.maximum(own, came)
+    joint = high + jnp.log(jnp.exp(own - high) + jnp.exp(came - high))
+    mean = own_ref[:, :MOST].astype(F32) * slots_of(jnp.exp(own - joint))
+    mean = mean + came_ref[:, :MOST].astype(F32) * slots_of(jnp.exp(came - joint))
+    out_ref[:, :MOST] = mean.astype(BF16)
+    out_ref[:, MOST:] = join([part[:, None] for part in split(joint, 3)], width)
+
+
+def finish_kernel(back_ref, picked_ref, order_ref, count_ref, grad_ref, loss_ref):
     patches, width = grad_ref.shape
-    lines = lse_ref.shape[0]
-    back = jnp.sum(back_ref[...].astype(F32), axis=0)
-    images = places_ref.shape[1]
-    own = iota((images, LANES), 0) == index_ref[0, 0]
-    start = jnp.sum(jnp.where(own, places_ref[0], 0.0), axis=0, keepdims=True)
-    count = jnp.sum(jnp.where(own, places_ref[1], 0.0), axis=0, keepdims=True)
-    mass = to_column((back[MOST : MOST + 1] + back[MOST + 1 : MOST + 2])[:, :LANES])[:MOST]
-    used = iota((MOST, 1), 0).astype(F32) < count[:, :1]
-    mean = back[:MOST] / jnp.where(used, mass, 1.0)
-    lse_row = to_row(lse_ref[...])
-    shape = (MOST, lines * LANES)
-    here = (iota(shape, 1) - iota(shape, 0)).astype(F32) == start[:, :1]
-    own_lse = jnp.sum(jnp.where(here, lse_row, 0.0), axis=1, keepdims=True)
+    target = jnp.sum(back_ref[:, :SLOT].astype(F32), axis=0)
+    mass = to_column((target[MOST : MOST + 1] + target[MOST + 1 : MOST + 2])[:, :LANES])[:MOST]
+    tail = back_ref[:, SLOT + MOST : 2 * SLOT, :LANES].astype(F32)
+    soft, lse_lanes = blend(back_ref[:, SLOT : SLOT + MOST].astype(F32), sum(tail[:, k] for k in range(3)))
+    used = iota((MOST, 1), 0) < count_ref[0, 0]
+    mean = target[:MOST] / jnp.where(used, mass, 1.0)
+    own_lse = to_column(lse_lanes.reshape(1, LANES))[:MOST]
     cross = own_lse - STUD * jnp.sum(picked_ref[:MOST].astype(F32) * mean, axis=1, keepdims=True)
     cross = jnp.sum(jnp.where(used, cross, 0.0), axis=0, keepdims=True)
-    loss_ref[...] = cross / count[:, :1]
-    rows = jnp.where(used, STUD * (student_ref[...].astype(F32) - mean), 0.0)
+    loss_ref[...] = cross / jnp.full((1, 1), count_ref[0, 0], jnp.int32).astype(F32)
+    rows = jnp.where(used, STUD * (soft - mean), 0.0)
     rows = jnp.concatenate([rows, jnp.zeros((LANES - MOST, width), F32)], axis=0).astype(BF16)
     order = jnp.broadcast_to(order_ref[:, :LANES], (patches, LANES))
     chosen = (iota((patches, LANES), 0) == order).astype(BF16)
@@ -337,65 +383,43 @@
     gathered = lax.all_gather(teacher_sent, "proto", axis=0, tiled=False)
     share, teacher_rows, places = call(
         column_kernel,
-        [((groups, protos // LANES, LANES), F32), ((rows, bot), BF16), ((2, width, LANES), F32)],
+        [((groups, protos // LANES, LANES), F32), ((rows, bot), BF16), ((4, width, LANES), F32)],
         gathered,
+        index,
         teacher_protos,
         grid=grid,
-        in_specs=[VMEM, wide],
+        in_specs=[VMEM, SMEM, wide],
         out_specs=[peer, VMEM, VMEM],
         flops=dot,
         moved=2 * bot * protos,
     )
     shares = over(share, "dp")
-    student_sum, student_high, student_lse = call(
-        student_kernel,
-        [((rows, bot), F32), ((rows, 1), F32), ((lines, LANES), F32)],
-        gathered_student,
-        places,
-        student_protos,
-        grid=grid,
-        in_specs=[VMEM, VMEM, wide],
-        scratch=[pltpu.VMEM((rows, bot), BF16), column],
-        flops=2 * dot,
-        moved=2 * bot * protos,
-    )
     matrix, high, share = call(
         row_kernel,
         [((rows, protos), BF16), ((steps, rows, 1), F32), ((width, depth, LANES), F32)],
         shares,
         teacher_rows,
         teacher_protos,
-        student_lse,
-        grid=grid,
-        in_specs=[peer, VMEM, wide, VMEM],
+        grid=grid,
+        in_specs=[peer, VMEM, wide],
         out_specs=[square, VMEM, VMEM],
         scratch=[pltpu.VMEM((steps, rows, 1), F32)],
         flops=dot,
         moved=2 * bot * protos + 2 * rows * protos,
     )
     shares = over(share, "proto")
-    share, scale, student_lse = call(
+    share, scale = call(
         first_column_kernel,
-        [((groups, protos // LANES, LANES), BF16), ((steps, rows, 1), F32), ((lines, LANES), F32)],
+        [((groups, protos // LANES, LANES), BF16), ((steps, rows, 1), F32)],
         shares,
         high,
         matrix,
         grid=grid,
         in_specs=[VMEM, VMEM, square],
-        out_specs=[peer, VMEM, VMEM],
+        out_specs=[peer, VMEM],
         moved=2 * rows * protos,
     )
-    student_part = call(
-        student_pack_kernel,
-        [((width * MOST, bot), BF16)],
-        student_sum,
-        student_high,
-        student_lse,
-        places,
-        flops=2 * width * MOST * rows * bot,
-    )[0]
-    shares, student_part = lax.optimization_barrier((over(share, "dp"), student_part))
-    student_back = lax.psum_scatter(student_part, "proto", scatter_dimension=0, tiled=True)
+    shares = over(share, "dp")
     share = call(
         later_row_kernel,
         [((width, depth, LANES), F32)],
@@ -420,9 +444,25 @@
         moved=2 * rows * protos,
     )
     shares = over(share, "dp")
-    sent = call(
+    packed = ((width // 2, SLOT, bot), BF16)
+    student_own, student_other = call(
+        student_kernel,
+        [packed, packed],
+        gathered_student,
+        places,
+        student_protos,
+        grid=grid,
+        in_specs=[VMEM, VMEM, wide],
+        scratch=[pltpu.VMEM((rows, bot), BF16), pltpu.VMEM((rows, bot), F32), column, column],
+        flops=2 * dot,
+        moved=2 * bot * protos,
+    )
+    swap = [(p, p ^ 1) for p in range(width)]
+    student_came = lax.ppermute(student_other, "proto", swap)
+    student_sum = call(student_merge_kernel, [packed], student_own, student_came)[0]
+    own, other = call(
         target_kernel,
-        [((width, SLOT, bot), BF16)],
+        [packed, packed],
         shares,
         scale,
         matrix,
@@ -433,19 +473,19 @@
         scratch=[pltpu.VMEM((rows, bot), F32), column],
         flops=dot,
         moved=2 * rows * protos,
-    )[0]
-    back = over(sent, "proto")
+    )
+    came = lax.ppermute(other, "proto", swap)
+    sent = call(target_merge_kernel, [((width // 2, 2 * SLOT, bot), BF16)], own, came, student_sum)[0]
+    same_core = [list(range(core, width, 2)) for core in range(2)]
+    back = over(sent, "proto", axis_index_groups=same_core)
     student_grad, image_loss = call(
         finish_kernel,
         [((patches, bot), BF16), ((1, 1), F32)],
         back,
-        student_back,
         student_sent,
-        student_lse,
-        places,
         mask_order,
-        index,
-        in_specs=[VMEM, VMEM, VMEM, VMEM, VMEM, VMEM, SMEM],
+        counts,
+        in_specs=[VMEM, VMEM, VMEM, SMEM],
         moved=2 * patches * bot,
     )
     return (student_grad[None], image_loss)

time: 217 us -> 180 us (0.83)
  waiting for transfers between devices: 72.2 us -> 16.7 us
  blocking collectives: 64.3 us -> 88.5 us
  starting transfers between devices: 23.8 us -> 19.5 us
    reduce_scatter x1 -> x0, waiting for transfers between devices: 55.2 us -> none  [body(): lax.psum_scatter(student_part, 'proto', scatter_dimension=0, tiled=True)]
    all_to_all x0 -> x1, blocking collectives: none -> 23.2 us  [body(): back = over(sent, 'proto', axis_index_groups=same_core)]
    all_to_all x1 -> x2, waiting for transfers between devices: 1.4 us -> 16 us  [body(): shares = over(share, 'dp')]
    all_to_all x2 -> x0, starting transfers between devices: 12.7 us -> none  [the longest x1 7.21 us: body(): over(share, 'dp')]
    all_to_all x2 -> x0, waiting for transfers between devices: 7.65 us -> none  [the longest x1 7.65 us: body(): over(share, 'dp')]
    all_gather x1, waiting for transfers between devices: 7.25 us -> 0.02 us  [body(): lax.all_gather(student_sent, 'proto', axis=0, tiled=False)]
    ppermute x0 -> x2, starting transfers between devices: none -> 4.98 us  [the longest x1 2.76 us: body(): came = lax.ppermute(other, 'proto', swap)]
    all_to_all x1 -> x2, starting transfers between devices: 11 us -> 14.5 us  [body(): shares = over(share, 'dp')]
  transfers between devices with their start and end apart: 5 -> 5, of which waited for: 4 -> 1; matrix products, arithmetic and copies ran while one was open for 0% -> 0% of each run, Pallas kernels for 5% -> 10%
where the time goes in v4:
time: 180 us; the launch traced here: 179 us
  blocking collectives  88.5 us (49%)
  Pallas kernels  24.7 us (14%)
  starting transfers between devices  19.5 us (11%)
  waiting for transfers between devices  16.7 us (9%)
  local copies, waits for them, and re-layouts  15.1 us (8%)
  between operations  14.9 us (8%)
    all_to_all x2, blocking collectives, body(): shares = over(share, 'proto')  26.8 us
    pallas_call x11, Pallas kernels, call(): pl.pallas_call(kernel, out_shape=out_shape, in_specs=[VMEM] * len(args) i...  24.7 us
    all_to_all x1, blocking collectives, body(): back = over(sent, 'proto', axis_index_groups=same_core)  23.2 us
    all_gather x1, blocking collectives, body(): gathered = lax.all_gather(teacher_sent, 'proto', axis=0, tiled=False)  23 us
    all_to_all x2, waiting for transfers between devices, body(): shares = over(share, 'dp')  16 us
    all_to_all x1, blocking collectives, body(): shares = over(share, 'dp')  15.6 us
    unnamed x32, local copies, waits for them, and re-layouts  15.1 us
    all_to_all x2, starting transfers between devices, body(): shares = over(share, 'dp')  14.5 us
  transfers between devices with their start and end apart: 5, of which 1 were waited for; matrix products, arithmetic and copies ran while one was open for 0% of the time, Pallas kernels for 10%

profile of v4, /device:TPU:1, one launch (start us, length us, event | category | flops | bytes accessed | tf_op | source)
XLA Modules:
  0.0 179.4 jit_solution(10467997082152881661)
XLA Ops:
  7.8 0.0 copy-start.9
  7.8 0.9 copy-done.9
  8.7 0.9 copy-done.10
  9.6 0.7 copy-done.11
  10.3 0.8 shard_map.77
  11.1 23.0 %all-gather = bf16[1280,256]{1,0:T(8,128)(2,1)S(1)} all-gather(bf16[80,256]{1,0:T(8,128)(2,1)S(1)} %get-tuple-element.20), channel_id=2, replica_groups=mesh['dp'=32,'proto'=16] {'proto'}, dimensions={0}, use_global_device_ids=true | all-gather | bytes 696320 | tf_op jit(solution)/shard_map/all_gather | solution.py:383
  34.1 1.6 copy-done.13
  35.7 3.8 %shard_map.78 = (f32[32,32,128]{2,1,0:T(8,128)}, bf16[384,256]{1,0:T(8,128)(2,1)S(1)}, f32[4,16,128]{2,1,0:T(8,128)S(1)}) custom-call(bf16[16,80,256]{2,1,0:T(8,128)(2,1)S(1)} %bitcast.6, s32[1,1]{1,0:T(1,128)} %bitcast.3.index_ref, bf16[256,4096]{1,0:T(8,128)(2,1)S(1)} %copy-done.13), custom_call_target="tpu_custom_call" | custom-call | flops 805306368 | bytes 2097152 | tf_op jit(solution)/shard_map/pallas_call | solution.py:27
  39.6 10.6 %all-to-all-start = ((f32[32,32,128]{2,1,0:T(8,128)}), f32[32,32,128]{2,1,0:T(8,128)S(1)}, u32[]{:S(2)}, u32[]{:S(2)}) async-start(f32[32,32,128]{2,1,0:T(8,128)} %get-tuple-element.21), calls=%async_computation | async-start | bytes 1048576 | tf_op jit(solution)/shard_map/all_to_all | solution.py:396
  50.2 0.0 all-gather.4.cloned.1.call-start
  50.2 0.7 all-gather.4.cloned.1.call-update
  50.9 16.0 %all-to-all-done.shares_ref = f32[32,32,128]{2,1,0:T(8,128)S(1)} async-done(((f32[32,32,128]{2,1,0:T(8,128)}), f32[32,32,128]{2,1,0:T(8,128)S(1)}, u32[]{:S(2)}, u32[]{:S(2)}) %all-to-all-start) | async-done | bytes 524320 | tf_op jit(solution)/shard_map/all_to_all | solution.py:396
  66.9 0.8 copy-done.2
  67.7 1.0 copy-done.3
  68.7 1.6 copy-done.14
  70.4 3.0 %shard_map.79 = (bf16[384,4096]{1,0:T(8,128)(2,1)S(1)}, f32[2,384,1]{2,1,0:T(8,128)S(1)}, f32[16,8,128]{2,1,0:T(8,128)S(1)}) custom-call(f32[32,32,128]{2,1,0:T(8,128)S(1)} %copy-done.3, bf16[384,256]{1,0:T(8,128)(2,1)S(1)} %get-tuple-element.22.rows_ref, bf16[256,4096]{1,0:T(8,128)(2,1)S(1)} %copy-done.14), custom_call_target="tpu_custom_call" | custom-call | flops 805306368 | bytes 5242880 | tf_op jit(solution)/shard_map/pallas_call | solution.py:27
  73.4 14.3 %all_to_all.30.shares_ref = f32[16,8,128]{2,1,0:T(8,128)S(1)} all-to-all(f32[16,8,128]{2,1,0:T(8,128)S(1)} %get-tuple-element.23), channel_id=1, replica_groups=mesh['dp'=32,'proto'=16] {'proto'}, dimensions={0} | all-to-all | bytes 131072 | tf_op jit(solution)/shard_map/all_to_all | solution.py:410
  87.7 1.2 shard_map.80
  88.9 15.6 %all_to_all.31.shares_ref = bf16[32,32,128]{2,1,0:T(8,128)(2,1)S(1)} all-to-all(bf16[32,32,128]{2,1,0:T(8,128)(2,1)S(1)} %get-tuple-element.26), channel_id=1, replica_groups=mesh['dp'=32,'proto'=16] {'dp'}, dimensions={0} | all-to-all | bytes 524288 | tf_op jit(solution)/shard_map/all_to_all | solution.py:422
  104.5 1.3 shard_map.81
  105.8 12.5 %all_to_all.32.shares_ref = f32[16,8,128]{2,1,0:T(8,128)S(1)} all-to-all(f32[16,8,128]{2,1,0:T(8,128)S(1)} %shard_map.81), channel_id=1, replica_groups=mesh['dp'=32,'proto'=16] {'proto'}, dimensions={0} | all-to-all | bytes 131072 | tf_op jit(solution)/shard_map/all_to_all | solution.py:434
  118.3 1.2 shard_map.82
  119.5 0.0 copy-start.4
  119.5 0.7 copy-done.4
  120.3 0.7 copy-done.8
  121.0 3.9 %all-to-all-start.4 = ((bf16[32,32,128]{2,1,0:T(8,128)(2,1)}), bf16[32,32,128]{2,1,0:T(8,128)(2,1)S(1)}, u32[]{:S(2)}, u32[]{:S(2)}) async-start(bf16[32,32,128]{2,1,0:T(8,128)(2,1)} %copy-done.8), calls=%async_computation.4 | async-start | bytes 524288 | tf_op jit(solution)/shard_map/all_to_all | solution.py:446
  124.8 0.0 all-gather.4.cloned.1.call-done
  124.9 0.0 copy-start
  124.9 1.6 copy-done
  126.5 1.2 copy-done.15
  127.7 7.2 %shard_map.84 = (bf16[8,80,256]{2,1,0:T(8,128)(2,1)S(1)}, bf16[8,80,256]{2,1,0:T(8,128)(2,1)}) custom-call(bf16[16,128,256]{2,1,0:T(8,128)(2,1)S(1)} %bitcast.9, f32[4,16,128]{2,1,0:T(8,128)S(1)} %get-tuple-element.30.places_ref, bf16[256,4096]{1,0:T(8,128)(2,1)S(1)} %copy-done), custom_call_target="tpu_custom_call" | custom-call | flops 1610612736 | bytes 2097152 | tf_op jit(solution)/shard_map/pallas_call | solution.py:27
  134.9 0.7 copy-done.6
  135.7 2.2 %collective-permute-start.1 = (bf16[8,80,256]{2,1,0:T(8,128)(2,1)}, bf16[8,80,256]{2,1,0:T(8,128)(2,1)}, u32[]{:S(2)}, u32[]{:S(2)}) collective-permute-start(bf16[8,80,256]{2,1,0:T(8,128)(2,1)} %get-tuple-element.35), channel_id=1, source_target_pairs={{0,1},{1,0},{2,3},{3,2},{4,5},{5,4},{6,7},{7,6},{8,9},{9,8},{10,11... | collective-permute-start | bytes 983048 | tf_op jit(solution)/shard_map/ppermute | solution.py:461
  137.9 0.0 all-to-all-done.4.shares_ref
  137.9 0.0 copy-start.1
  137.9 1.6 copy-done.1
  139.5 1.0 copy-done.5
  140.5 2.8 %shard_map.83 = (bf16[8,80,256]{2,1,0:T(8,128)(2,1)S(1)}, bf16[8,80,256]{2,1,0:T(8,128)(2,1)S(1)}) custom-call(bf16[32,32,128]{2,1,0:T(8,128)(2,1)S(1)} %all-to-all-done.4.shares_ref, f32[2,384,1]{2,1,0:T(8,128)S(1)} %copy-done.5, bf16[384,4096]{1,0:T(8,128)(2,1)S(1)} %get-tuple-element.25.matrix_ref, bf16[256,4096]{1,0:T(8,128)(2,1)S(1)} %copy-done.1, ...), custom_call_target="tpu_custom_call" | custom-call | flops 805306368 | bytes 3145728 | tf_op jit(solution)/shard_map/pallas_call | solution.py:27
  143.3 0.0 copy-start.12
  143.3 2.8 %collective-permute-start = (bf16[8,80,256]{2,1,0:T(8,128)(2,1)S(1)}, bf16[8,80,256]{2,1,0:T(8,128)(2,1)S(1)}, u32[]{:S(2)}, u32[]{:S(2)}) collective-permute-start(bf16[8,80,256]{2,1,0:T(8,128)(2,1)S(1)} %get-tuple-element.32), channel_id=1, source_target_pairs={{0,1},{1,0},{2,3},{3,2},{4,5},{5,4},{6,7},{7,6},{8,9},{9,8},{10,11... | collective-permute-start | bytes 983048 | tf_op jit(solution)/shard_map/ppermute | solution.py:477
  146.1 0.0 collective-permute-done.1.came_ref
  146.1 0.0 copy-done.7
  146.1 1.3 shard_map.85.student_ref
  147.4 0.0 collective-permute-done.came_ref
  147.4 0.1 shard_map.86
  147.5 23.2 %all_to_all.33.back_ref = bf16[8,160,256]{2,1,0:T(8,128)(2,1)S(1)} all-to-all(bf16[8,160,256]{2,1,0:T(8,128)(2,1)S(1)} %shard_map.86), channel_id=1, replica_groups={{0,2,4,6,8,10,12,14},{1,3,5,7,9,11,13,15},{16,18,20,22,24,26,28,30},{17..., dimensions={0} | all-to-all | bytes 1310720 | tf_op jit(solution)/shard_map/all_to_all | solution.py:480
  170.7 0.0 copy-done.12
  170.7 1.9 %shard_map.87 = (bf16[256,256]{1,0:T(8,128)(2,1)}, f32[1,1]{1,0:T(1,128)}) custom-call(bf16[8,160,256]{2,1,0:T(8,128)(2,1)S(1)} %all_to_all.33.back_ref, bf16[128,256]{1,0:T(8,128)(2,1)} %get-tuple-element.33.picked_ref, s32[1,256]{1,0:T(1,128)S(1)} %copy-done.12, s32[1,1]{1,0:T(1,128)S(6)} %copy.8.count_ref), custom_call_target="tpu_custom_call" | custom-call | bytes 131072 | tf_op jit(solution)/shard_map/pallas_call | solution.py:27
  (11 shorter events, 0.0 us)
Async XLA Ops:
  7.8 0.9 copy-start.9
  8.7 0.9 copy-start.10
  9.6 0.7 copy-start.11
  34.1 1.6 copy-start.13
  39.6 27.3 %all-to-all-start = ((f32[32,32,128]{2,1,0:T(8,128)}), f32[32,32,128]{2,1,0:T(8,128)S(1)}, u32[]{:S(2)}, u32[]{:S(2)}) async-start(f32[32,32,128]{2,1,0:T(8,128)} %get-tuple-element.21), calls=%async_computation | async-start | bytes 1048576 | tf_op jit(solution)/shard_map/all_to_all | solution.py:396
  50.2 74.7 %all-gather.4.cloned.1.call-start = ((), (), s32[]{:S(2)}) async-start(), calls=%async_computation.6 | async-start | bytes 1114112 | tf_op jit(solution)/shard_map/all_gather | solution.py:382
  66.9 0.8 copy-start.2
  67.7 1.0 copy-start.3
  68.7 1.6 copy-start.14
  119.5 0.7 copy-start.4
  120.3 0.7 copy-start.8
  121.0 16.9 %all-to-all-start.4 = ((bf16[32,32,128]{2,1,0:T(8,128)(2,1)}), bf16[32,32,128]{2,1,0:T(8,128)(2,1)S(1)}, u32[]{:S(2)}, u32[]{:S(2)}) async-start(bf16[32,32,128]{2,1,0:T(8,128)(2,1)} %copy-done.8), calls=%async_computation.4 | async-start | bytes 524288 | tf_op jit(solution)/shard_map/all_to_all | solution.py:446
  124.9 1.6 copy-start
  126.5 1.2 copy-start.15
  134.9 0.7 copy-start.6
  135.7 10.4 %collective-permute-start.1 = (bf16[8,80,256]{2,1,0:T(8,128)(2,1)}, bf16[8,80,256]{2,1,0:T(8,128)(2,1)}, u32[]{:S(2)}, u32[]{:S(2)}) collective-permute-start(bf16[8,80,256]{2,1,0:T(8,128)(2,1)} %get-tuple-element.35), channel_id=1, source_target_pairs={{0,1},{1,0},{2,3},{3,2},{4,5},{5,4},{6,7},{7,6},{8,9},{9,8},{10,11... | collective-permute-start | bytes 983048 | tf_op jit(solution)/shard_map/ppermute | solution.py:461
  137.9 1.6 copy-start.1
  139.5 1.0 copy-start.5
  140.5 5.6 %copy-start.7 = (bf16[8,80,256]{2,1,0:T(8,128)(2,1)S(1)}, bf16[8,80,256]{2,1,0:T(8,128)(2,1)}, u32[]{:S(2)}) copy-start(bf16[8,80,256]{2,1,0:T(8,128)(2,1)} %copy-done.6) | copy-start | bytes 983044
  143.3 27.4 %copy-start.12 = (s32[1,256]{1,0:T(1,128)S(1)}, s32[1,256]{1,0:T(1,128)}, u32[]{:S(2)}) copy-start(s32[1,256]{1,0:T(1,128)} %order_ref.3) | copy-start | bytes 3076
  143.3 4.1 %collective-permute-start = (bf16[8,80,256]{2,1,0:T(8,128)(2,1)S(1)}, bf16[8,80,256]{2,1,0:T(8,128)(2,1)S(1)}, u32[]{:S(2)}, u32[]{:S(2)}) collective-permute-start(bf16[8,80,256]{2,1,0:T(8,128)(2,1)S(1)} %get-tuple-element.32), channel_id=1, source_target_pairs={{0,1},{1,0},{2,3},{3,2},{4,5},{5,4},{6,7},{7,6},{8,9},{9,8},{10,11... | collective-permute-start | bytes 983048 | tf_op jit(solution)/shard_map/ppermute | solution.py:477
Sparse Core Ops, SparseCore 0:
  53.1 39.5 all-gather.3

commit v5 on v4

--- a/solution.py
+++ b/solution.py
@@ -366,14 +366,18 @@
     peer = pl.BlockSpec((groups, BLOCK // LANES, LANES), lambda k: (0, k, 0))
     square = pl.BlockSpec((rows, BLOCK), lambda k: (0, k))
     grid = (steps,)
+    student_patches, teacher_patches, mask_order, student_protos, teacher_protos = (
+        pltpu.with_memory_space_constraint(a, pltpu.HBM)
+        for a in (student_patches[0], teacher_patches[0], mask_order, student_protos, teacher_protos)
+    )
     dot = 2 * rows * protos * bot
     column = pltpu.VMEM((rows, 1), F32)
 
     teacher_sent, student_sent = call(
         pick_kernel,
         [((SLOT, bot), BF16), ((LANES, bot), BF16)],
-        teacher_patches[0],
-        student_patches[0],
+        teacher_patches,
+        student_patches,
         mask_order,
         counts,
         in_specs=[VMEM, VMEM, VMEM, SMEM],

time: 180 us -> 177 us (0.983)
  local copies, waits for them, and re-layouts: 15.1 us -> 6.23 us
  Pallas kernels: 24.7 us -> 29.9 us
    unnamed x32 -> x16, local copies, waits for them, and re-layouts: 15.1 us -> 6.23 us
    pallas_call x11, Pallas kernels: 24.7 us -> 29.9 us  [call(): pl.pallas_call(kernel, out_shape=out_shape, in_specs=[VMEM] * len(args) i...]
  transfers between devices with their start and end apart: 5 -> 5, of which waited for: 1 -> 1; matrix products, arithmetic and copies ran while one was open for 0% -> 0% of each run, Pallas kernels for 10% -> 12%
where the time goes in v5:
time: 177 us; the launch traced here: 176 us
  blocking collectives  88.4 us (50%)
  Pallas kernels  29.9 us (17%)
  starting transfers between devices  20 us (11%)
  waiting for transfers between devices  16.7 us (9%)
  between operations  14.8 us (8%)
  local copies, waits for them, and re-layouts  6.23 us (4%)
    pallas_call x11, Pallas kernels, call(): pl.pallas_call(kernel, out_shape=out_shape, in_specs=[VMEM] * len(args) i...  29.9 us
    all_to_all x2, blocking collectives, body(): shares = over(share, 'proto')  26.8 us
    all_to_all x1, blocking collectives, body(): back = over(sent, 'proto', axis_index_groups=same_core)  23.2 us
    all_gather x1, blocking collectives, body(): gathered = lax.all_gather(teacher_sent, 'proto', axis=0, tiled=False)  23 us
    all_to_all x2, waiting for transfers between devices, body(): shares = over(share, 'dp')  16 us
    all_to_all x1, blocking collectives, body(): shares = over(share, 'dp')  15.4 us
    all_to_all x2, starting transfers between devices, body(): shares = over(share, 'dp')  14.5 us
    unnamed x16, local copies, waits for them, and re-layouts  6.23 us
  transfers between devices with their start and end apart: 5, of which 1 were waited for; matrix products, arithmetic and copies ran while one was open for 0% of the time, Pallas kernels for 12%

profile of v5, /device:TPU:1, one launch (start us, length us, event | category | flops | bytes accessed | tf_op | source)
XLA Modules:
  0.0 176.0 jit_solution(9942209580218492527)
XLA Ops:
  7.8 1.8 %shard_map.77 = (bf16[80,256]{1,0:T(8,128)(2,1)S(1)}, bf16[128,256]{1,0:T(8,128)(2,1)}) custom-call(bf16[256,256]{1,0:T(8,128)(2,1)} %bitcast.8, bf16[256,256]{1,0:T(8,128)(2,1)} %bitcast.9, s32[1,256]{1,0:T(1,128)} %order_ref.3, s32[1,1]{1,0:T(1,128)S(6)} %copy.8.count_ref), custom_call_target="tpu_custom_call" | custom-call | bytes 262144 | tf_op jit(solution)/shard_map/pallas_call | solution.py:27
  9.6 23.0 %all-gather = bf16[1280,256]{1,0:T(8,128)(2,1)S(1)} all-gather(bf16[80,256]{1,0:T(8,128)(2,1)S(1)} %get-tuple-element.20), channel_id=2, replica_groups=mesh['dp'=32,'proto'=16] {'proto'}, dimensions={0}, use_global_device_ids=true | all-gather | bytes 696320 | tf_op jit(solution)/shard_map/all_gather | solution.py:387
  32.6 4.9 %shard_map.78 = (f32[32,32,128]{2,1,0:T(8,128)}, bf16[384,256]{1,0:T(8,128)(2,1)S(1)}, f32[4,16,128]{2,1,0:T(8,128)S(1)}) custom-call(bf16[16,80,256]{2,1,0:T(8,128)(2,1)S(1)} %bitcast.6, s32[1,1]{1,0:T(1,128)} %bitcast.3.index_ref, bf16[256,4096]{1,0:T(8,128)(2,1)} %protos_ref.5), custom_call_target="tpu_custom_call" | custom-call | flops 805306368 | bytes 2097152 | tf_op jit(solution)/shard_map/pallas_call | solution.py:27
  37.6 10.6 %all-to-all-start = ((f32[32,32,128]{2,1,0:T(8,128)}), f32[32,32,128]{2,1,0:T(8,128)S(1)}, u32[]{:S(2)}, u32[]{:S(2)}) async-start(f32[32,32,128]{2,1,0:T(8,128)} %get-tuple-element.21), calls=%async_computation | async-start | bytes 1048576 | tf_op jit(solution)/shard_map/all_to_all | solution.py:400
  48.2 0.0 all-gather.4.cloned.1.call-start
  48.2 0.7 all-gather.4.cloned.1.call-update
  48.9 16.0 %all-to-all-done.shares_ref = f32[32,32,128]{2,1,0:T(8,128)S(1)} async-done(((f32[32,32,128]{2,1,0:T(8,128)}), f32[32,32,128]{2,1,0:T(8,128)S(1)}, u32[]{:S(2)}, u32[]{:S(2)}) %all-to-all-start) | async-done | bytes 524320 | tf_op jit(solution)/shard_map/all_to_all | solution.py:400
  64.9 0.0 copy-start
  64.9 0.8 copy-done
  65.7 0.0 copy-start.1
  65.7 1.0 copy-done.1
  66.7 4.1 %shard_map.79 = (bf16[384,4096]{1,0:T(8,128)(2,1)S(1)}, f32[2,384,1]{2,1,0:T(8,128)S(1)}, f32[16,8,128]{2,1,0:T(8,128)S(1)}) custom-call(f32[32,32,128]{2,1,0:T(8,128)S(1)} %copy-done.1, bf16[384,256]{1,0:T(8,128)(2,1)S(1)} %get-tuple-element.22.rows_ref, bf16[256,4096]{1,0:T(8,128)(2,1)} %protos_ref.5), custom_call_target="tpu_custom_call" | custom-call | flops 805306368 | bytes 5242880 | tf_op jit(solution)/shard_map/pallas_call | solution.py:27
  70.8 14.2 %all_to_all.30.shares_ref = f32[16,8,128]{2,1,0:T(8,128)S(1)} all-to-all(f32[16,8,128]{2,1,0:T(8,128)S(1)} %get-tuple-element.23), channel_id=1, replica_groups=mesh['dp'=32,'proto'=16] {'proto'}, dimensions={0} | all-to-all | bytes 131072 | tf_op jit(solution)/shard_map/all_to_all | solution.py:414
  85.1 1.2 shard_map.80
  86.3 15.4 %all_to_all.31.shares_ref = bf16[32,32,128]{2,1,0:T(8,128)(2,1)S(1)} all-to-all(bf16[32,32,128]{2,1,0:T(8,128)(2,1)S(1)} %get-tuple-element.26), channel_id=1, replica_groups=mesh['dp'=32,'proto'=16] {'dp'}, dimensions={0} | all-to-all | bytes 524288 | tf_op jit(solution)/shard_map/all_to_all | solution.py:426
  101.8 1.3 shard_map.81
  103.0 12.6 %all_to_all.32.shares_ref = f32[16,8,128]{2,1,0:T(8,128)S(1)} all-to-all(f32[16,8,128]{2,1,0:T(8,128)S(1)} %shard_map.81), channel_id=1, replica_groups=mesh['dp'=32,'proto'=16] {'proto'}, dimensions={0} | all-to-all | bytes 131072 | tf_op jit(solution)/shard_map/all_to_all | solution.py:438
  115.6 1.2 shard_map.82
  116.8 0.0 copy-start.2
  116.8 0.8 copy-done.2
  117.6 0.0 copy-start.6
  117.6 0.7 copy-done.6
  118.3 3.9 %all-to-all-start.4 = ((bf16[32,32,128]{2,1,0:T(8,128)(2,1)}), bf16[32,32,128]{2,1,0:T(8,128)(2,1)S(1)}, u32[]{:S(2)}, u32[]{:S(2)}) async-start(bf16[32,32,128]{2,1,0:T(8,128)(2,1)} %copy-done.6), calls=%async_computation.4 | async-start | bytes 524288 | tf_op jit(solution)/shard_map/all_to_all | solution.py:450
  122.2 0.0 all-gather.4.cloned.1.call-done
  122.2 0.0 copy-start.7
  122.2 1.2 copy-done.7
  123.4 8.3 %shard_map.84 = (bf16[8,80,256]{2,1,0:T(8,128)(2,1)S(1)}, bf16[8,80,256]{2,1,0:T(8,128)(2,1)}) custom-call(bf16[16,128,256]{2,1,0:T(8,128)(2,1)S(1)} %bitcast.7, f32[4,16,128]{2,1,0:T(8,128)S(1)} %get-tuple-element.30.places_ref, bf16[256,4096]{1,0:T(8,128)(2,1)} %protos_ref.7), custom_call_target="tpu_custom_call" | custom-call | flops 1610612736 | bytes 2097152 | tf_op jit(solution)/shard_map/pallas_call | solution.py:27
  131.7 0.0 copy-start.4
  131.7 0.7 copy-done.4
  132.5 2.2 %collective-permute-start.1 = (bf16[8,80,256]{2,1,0:T(8,128)(2,1)}, bf16[8,80,256]{2,1,0:T(8,128)(2,1)}, u32[]{:S(2)}, u32[]{:S(2)}) collective-permute-start(bf16[8,80,256]{2,1,0:T(8,128)(2,1)} %get-tuple-element.35), channel_id=1, source_target_pairs={{0,1},{1,0},{2,3},{3,2},{4,5},{5,4},{6,7},{7,6},{8,9},{9,8},{10,11... | collective-permute-start | bytes 983048 | tf_op jit(solution)/shard_map/ppermute | solution.py:465
  134.7 0.0 all-to-all-done.4.shares_ref
  134.7 0.0 copy-start.3
  134.7 1.0 copy-done.3
  135.7 0.0 copy-start.5
  135.7 3.8 %shard_map.83 = (bf16[8,80,256]{2,1,0:T(8,128)(2,1)S(1)}, bf16[8,80,256]{2,1,0:T(8,128)(2,1)S(1)}) custom-call(bf16[32,32,128]{2,1,0:T(8,128)(2,1)S(1)} %all-to-all-done.4.shares_ref, f32[2,384,1]{2,1,0:T(8,128)S(1)} %copy-done.3, bf16[384,4096]{1,0:T(8,128)(2,1)S(1)} %get-tuple-element.25.matrix_ref, bf16[256,4096]{1,0:T(8,128)(2,1)} %protos_ref.7, ...), custom_call_target="tpu_custom_call" | custom-call | flops 805306368 | bytes 3145728 | tf_op jit(solution)/shard_map/pallas_call | solution.py:27
  139.5 3.3 %collective-permute-start = (bf16[8,80,256]{2,1,0:T(8,128)(2,1)S(1)}, bf16[8,80,256]{2,1,0:T(8,128)(2,1)S(1)}, u32[]{:S(2)}, u32[]{:S(2)}) collective-permute-start(bf16[8,80,256]{2,1,0:T(8,128)(2,1)S(1)} %get-tuple-element.32), channel_id=1, source_target_pairs={{0,1},{1,0},{2,3},{3,2},{4,5},{5,4},{6,7},{7,6},{8,9},{9,8},{10,11... | collective-permute-start | bytes 983048 | tf_op jit(solution)/shard_map/ppermute | solution.py:481
  142.7 0.0 collective-permute-done.1.came_ref
  142.8 0.0 copy-done.5
  142.8 1.3 shard_map.85.student_ref
  144.0 0.0 collective-permute-done.came_ref
  144.0 0.1 shard_map.86
  144.1 23.2 %all_to_all.33.back_ref = bf16[8,160,256]{2,1,0:T(8,128)(2,1)S(1)} all-to-all(bf16[8,160,256]{2,1,0:T(8,128)(2,1)S(1)} %shard_map.86), channel_id=1, replica_groups={{0,2,4,6,8,10,12,14},{1,3,5,7,9,11,13,15},{16,18,20,22,24,26,28,30},{17..., dimensions={0} | all-to-all | bytes 1310720 | tf_op jit(solution)/shard_map/all_to_all | solution.py:484
  167.3 1.9 %shard_map.87 = (bf16[256,256]{1,0:T(8,128)(2,1)}, f32[1,1]{1,0:T(1,128)}) custom-call(bf16[8,160,256]{2,1,0:T(8,128)(2,1)S(1)} %all_to_all.33.back_ref, bf16[128,256]{1,0:T(8,128)(2,1)} %get-tuple-element.33.picked_ref, s32[1,256]{1,0:T(1,128)} %order_ref.3, s32[1,1]{1,0:T(1,128)S(6)} %copy.8.count_ref), custom_call_target="tpu_custom_call" | custom-call | bytes 131072 | tf_op jit(solution)/shard_map/pallas_call | solution.py:27
Async XLA Ops:
  37.6 27.3 %all-to-all-start = ((f32[32,32,128]{2,1,0:T(8,128)}), f32[32,32,128]{2,1,0:T(8,128)S(1)}, u32[]{:S(2)}, u32[]{:S(2)}) async-start(f32[32,32,128]{2,1,0:T(8,128)} %get-tuple-element.21), calls=%async_computation | async-start | bytes 1048576 | tf_op jit(solution)/shard_map/all_to_all | solution.py:400
  48.2 74.0 %all-gather.4.cloned.1.call-start = ((), (), s32[]{:S(2)}) async-start(), calls=%async_computation.6 | async-start | bytes 1114112 | tf_op jit(solution)/shard_map/all_gather | solution.py:386
  64.9 0.8 copy-start
  65.7 1.0 copy-start.1
  116.8 0.8 copy-start.2
  117.6 0.7 copy-start.6
  118.3 16.4 %all-to-all-start.4 = ((bf16[32,32,128]{2,1,0:T(8,128)(2,1)}), bf16[32,32,128]{2,1,0:T(8,128)(2,1)S(1)}, u32[]{:S(2)}, u32[]{:S(2)}) async-start(bf16[32,32,128]{2,1,0:T(8,128)(2,1)} %copy-done.6), calls=%async_computation.4 | async-start | bytes 524288 | tf_op jit(solution)/shard_map/all_to_all | solution.py:450
  122.2 1.2 copy-start.7
  131.7 0.7 copy-start.4
  132.5 10.3 %collective-permute-start.1 = (bf16[8,80,256]{2,1,0:T(8,128)(2,1)}, bf16[8,80,256]{2,1,0:T(8,128)(2,1)}, u32[]{:S(2)}, u32[]{:S(2)}) collective-permute-start(bf16[8,80,256]{2,1,0:T(8,128)(2,1)} %get-tuple-element.35), channel_id=1, source_target_pairs={{0,1},{1,0},{2,3},{3,2},{4,5},{5,4},{6,7},{7,6},{8,9},{9,8},{10,11... | collective-permute-start | bytes 983048 | tf_op jit(solution)/shard_map/ppermute | solution.py:465
  134.7 1.0 copy-start.3
  135.7 7.1 %copy-start.5 = (bf16[8,80,256]{2,1,0:T(8,128)(2,1)S(1)}, bf16[8,80,256]{2,1,0:T(8,128)(2,1)}, u32[]{:S(2)}) copy-start(bf16[8,80,256]{2,1,0:T(8,128)(2,1)} %copy-done.4) | copy-start | bytes 983044
  139.5 4.5 %collective-permute-start = (bf16[8,80,256]{2,1,0:T(8,128)(2,1)S(1)}, bf16[8,80,256]{2,1,0:T(8,128)(2,1)S(1)}, u32[]{:S(2)}, u32[]{:S(2)}) collective-permute-start(bf16[8,80,256]{2,1,0:T(8,128)(2,1)S(1)} %get-tuple-element.32), channel_id=1, source_target_pairs={{0,1},{1,0},{2,3},{3,2},{4,5},{5,4},{6,7},{7,6},{8,9},{9,8},{10,11... | collective-permute-start | bytes 983048 | tf_op jit(solution)/shard_map/ppermute | solution.py:481
Sparse Core Ops, SparseCore 0:
  51.1 39.5 all-gather.3

commit v6 on v5

--- a/solution.py
+++ b/solution.py
@@ -9,6 +9,8 @@
 
 MASK_DEV = 24
 MOST = 72
+EARLY = 40
+LATE = (MOST - EARLY) // 2
 SLOT = 80
 TEACH = 1.0 / 0.07
 STUD = 1.0 / 0.1
@@ -73,29 +75,32 @@
     return top + jnp.log(jnp.sum(jnp.exp(shares - top[None]), axis=0))
 
 
-def pick_kernel(teacher_ref, student_ref, order_ref, count_ref, teacher_out, student_out):
+def pick_kernel(teacher_ref, student_ref, order_ref, count_ref, sent_ref, late_ref, picked_ref):
     patches, width = teacher_ref.shape
     order = jnp.broadcast_to(order_ref[:, :LANES], (patches, LANES))
     chosen = (iota((patches, LANES), 0) == order).astype(BF16)
     dims = (((0,), (0,)), ((), ()))
-    picked = lax.dot_general(chosen, teacher_ref[...], dims, preferred_element_type=F32)
+    teacher = lax.dot_general(chosen, teacher_ref[...], dims, preferred_element_type=F32)
+    student = lax.dot_general(chosen, student_ref[...], dims, preferred_element_type=F32)
     count = jnp.full((SLOT - MOST, width), count_ref[0, 0], jnp.int32).astype(F32)
-    teacher_out[...] = jnp.concatenate([picked[:MOST], count], axis=0).astype(BF16)
-    picked = lax.dot_general(chosen, student_ref[...], dims, preferred_element_type=F32)
-    student_out[...] = picked.astype(BF16)
-
-
-def compact(gathered, starts, counts, rows):
-    total = gathered.shape[0]
-    images = starts.shape[0]
-    slots = total // images
+    sent_ref[...] = jnp.concatenate([teacher[:MOST], count, student[:EARLY]], axis=0).astype(BF16)
+    for half in range(2):
+        late = student[EARLY + half * LATE : EARLY + (half + 1) * LATE]
+        late_ref[half] = jnp.concatenate([late[:, :LANES], late[:, LANES:]], axis=0).astype(BF16)
+    picked_ref[...] = student[:SLOT].astype(BF16)
+
+
+def compact(gathered, starts, counts, rows, first, length, shift):
+    images, slots, width = gathered.shape
+    total = images * slots
     lane, image = iota((images, total), 1), iota((images, total), 0)
-    within = lane - image * slots
-    member = jnp.logical_and(within >= 0, within < slots)
-    used = jnp.logical_and(member, within.astype(F32) < counts[:, :1])
-    row = jnp.sum(jnp.where(used, starts[:, :1] + within.astype(F32) + 1.0, 0.0), axis=0, keepdims=True) - 1.0
+    within = lane - image * slots - first
+    member = jnp.logical_and(within >= 0, within < length)
+    place = (within + shift).astype(F32)
+    used = jnp.logical_and(member, place < counts[:, :1])
+    row = jnp.sum(jnp.where(used, starts[:, :1] + place + 1.0, 0.0), axis=0, keepdims=True) - 1.0
     chosen = (iota((rows, total), 0).astype(F32) == row).astype(BF16)
-    return jnp.dot(chosen, gathered, preferred_element_type=F32).astype(BF16)
+    return jnp.dot(chosen, gathered.reshape(total, width), preferred_element_type=F32)
 
 
 def spread(starts, counts, slots, rows):
@@ -124,8 +129,7 @@
         places_ref[1] = jnp.dot((other == image).astype(BF16), counts.astype(BF16), preferred_element_type=F32)
         places_ref[2] = starts
         places_ref[3] = counts
-        flat = gathered_ref[...].reshape(images * SLOT, gathered_ref.shape[2])
-        rows_ref[...] = compact(flat, starts, counts, rows)
+        rows_ref[...] = compact(gathered_ref[...], starts, counts, rows, 0, MOST, 0).astype(BF16)
 
     logits = jnp.dot(rows_ref[...], protos_ref[...], preferred_element_type=F32) * TEACH
     high = jnp.max(logits, axis=0, keepdims=True)
@@ -133,12 +137,21 @@
     share_ref[...] = jnp.broadcast_to(to_lines(high + jnp.log(total))[None], share_ref.shape)
 
 
+def split(values, parts):
+    out = []
+    for _ in range(parts):
+        part = values.astype(BF16)
+        out.append(part)
+        values = values - part.astype(F32)
+    return out
+
+
 def fill_share(share_ref, lines):
     blank = jnp.zeros((share_ref.shape[1] - lines.shape[0], LANES), F32)
     share_ref[...] = jnp.broadcast_to(jnp.concatenate([lines, blank], axis=0)[None], share_ref.shape)
 
 
-def row_kernel(shares_ref, rows_ref, protos_ref, matrix_ref, high_ref, share_ref, sums):
+def row_kernel(shares_ref, rows_ref, protos_ref, late_ref, matrix_ref, high_ref, share_ref, sums):
     step = pl.program_id(0)
     column = to_row(merged(shares_ref[...]))
     logits = jnp.dot(rows_ref[...], protos_ref[...], preferred_element_type=F32) * TEACH
@@ -154,7 +167,12 @@
         highs = high_ref[...]
         top = jnp.max(highs, axis=0)
         total = jnp.sum(jnp.exp(highs - top[None]) * sums[...], axis=0)
-        fill_share(share_ref, to_lanes(top + jnp.log(total)))
+        own = jnp.concatenate([part.astype(F32) for part in split(to_lanes(top + jnp.log(total)), 3)], axis=0)
+        blank = jnp.zeros((share_ref.shape[2] - 2 * LATE - own.shape[0], LANES), F32)
+        numbers = jnp.concatenate([own, blank], axis=0).astype(BF16)
+        for half in range(2):
+            chunk = jnp.concatenate([late_ref[half], numbers], axis=0)
+            share_ref[:, half] = jnp.broadcast_to(chunk[None], (share_ref.shape[0],) + chunk.shape)
 
 
 def column_sums(matrix_ref, scale, share_ref):
@@ -168,7 +186,8 @@
     @pl.when(step == 0)
     def _():
         lines = scale_ref.shape[1] // LANES
-        row_lse = merged(shares_ref[...][:, :lines])
+        numbers = shares_ref[:, 2 * LATE :].astype(F32)
+        row_lse = merged(sum(numbers[:, k * lines : (k + 1) * lines] for k in range(3)))
         scale_ref[...] = jnp.exp(high_ref[...] - to_column(row_lse)[None])
 
     column_sums(matrix_ref, scale_ref[step], share_ref)
@@ -202,15 +221,6 @@
     @pl.when(step == pl.num_programs(0) - 1)
     def _():
         fill_share(share_ref, to_lanes(sums[...]))
-
-
-def split(values, parts):
-    out = []
-    for _ in range(parts):
-        part = values.astype(BF16)
-        out.append(part)
-        values = values - part.astype(F32)
-    return out
 
 
 def pack(sums, numbers, parts, starts, counts):
@@ -285,15 +295,20 @@
     out_ref[:, SLOT:] = student_ref[...]
 
 
-def student_kernel(gathered_ref, places_ref, protos_ref, own_ref, other_ref, rows_ref, sums, top, total):
+def student_kernel(
+    gathered_ref, late_ref, came_ref, index_ref, places_ref, protos_ref, own_ref, other_ref, rows_ref, sums, top, total
+):
     step = pl.program_id(0)
     rows = rows_ref.shape[0]
 
     @pl.when(step == 0)
     def _():
-        images, slots, width = gathered_ref.shape
-        flat = gathered_ref[...].reshape(images * slots, width)
-        rows_ref[...] = compact(flat, places_ref[2], places_ref[3], rows)
+        starts, counts, core = places_ref[2], places_ref[3], index_ref[0, 0] % 2
+        found = compact(gathered_ref[...], starts, counts, rows, SLOT, EARLY, 0)
+        for ref, half in ((late_ref, core), (came_ref, 1 - core)):
+            late = jnp.concatenate([ref[:, :LATE], ref[:, LATE : 2 * LATE]], axis=2)
+            found += compact(late, starts, counts, rows, 0, LATE, EARLY + half * LATE)
+        rows_ref[...] = found.astype(BF16)
         top[...] = jnp.full(top.shape, -1e30, F32)
         total[...] = jnp.zeros(total.shape, F32)
         sums[...] = jnp.zeros(sums.shape, F32)
@@ -373,9 +388,9 @@
     dot = 2 * rows * protos * bot
     column = pltpu.VMEM((rows, 1), F32)
 
-    teacher_sent, student_sent = call(
+    sent, late, picked = call(
         pick_kernel,
-        [((SLOT, bot), BF16), ((LANES, bot), BF16)],
+        [((SLOT + EARLY, bot), BF16), ((2, 2 * LATE, LANES), BF16), ((SLOT, bot), BF16)],
         teacher_patches,
         student_patches,
         mask_order,
@@ -383,8 +398,7 @@
         in_specs=[VMEM, VMEM, VMEM, SMEM],
         moved=4 * patches * bot,
     )
-    gathered_student = lax.all_gather(student_sent, "proto", axis=0, tiled=False)
-    gathered = lax.all_gather(teacher_sent, "proto", axis=0, tiled=False)
+    gathered = lax.all_gather(sent, "proto", axis=0, tiled=False)
     share, teacher_rows, places = call(
         column_kernel,
         [((groups, protos // LANES, LANES), F32), ((rows, bot), BF16), ((4, width, LANES), F32)],
@@ -400,18 +414,22 @@
     shares = over(share, "dp")
     matrix, high, share = call(
         row_kernel,
-        [((rows, protos), BF16), ((steps, rows, 1), F32), ((width, depth, LANES), F32)],
+        [((rows, protos), BF16), ((steps, rows, 1), F32), ((width // 2, 2, 2 * LATE + 16, LANES), BF16)],
         shares,
         teacher_rows,
         teacher_protos,
-        grid=grid,
-        in_specs=[peer, VMEM, wide],
+        late,
+        grid=grid,
+        in_specs=[peer, VMEM, wide, VMEM],
         out_specs=[square, VMEM, VMEM],
         scratch=[pltpu.VMEM((steps, rows, 1), F32)],
         flops=dot,
         moved=2 * bot * protos + 2 * rows * protos,
     )
-    shares = over(share, "proto")
+    swap = [(p, p ^ 1) for p in range(width)]
+    shares = over(share.reshape((width,) + share.shape[2:]), "proto")
+    late = shares
+    late_came = lax.ppermute(late, "proto", swap)
     share, scale = call(
         first_column_kernel,
         [((groups, protos // LANES, LANES), BF16), ((steps, rows, 1), F32)],
@@ -452,16 +470,18 @@
     student_own, student_other = call(
         student_kernel,
         [packed, packed],
-        gathered_student,
+        gathered,
+        late,
+        late_came,
+        index,
         places,
         student_protos,
         grid=grid,
-        in_specs=[VMEM, VMEM, wide],
+        in_specs=[VMEM, VMEM, VMEM, SMEM, VMEM, wide],
         scratch=[pltpu.VMEM((rows, bot), BF16), pltpu.VMEM((rows, bot), F32), column, column],
         flops=2 * dot,
         moved=2 * bot * protos,
     )
-    swap = [(p, p ^ 1) for p in range(width)]
     student_came = lax.ppermute(student_other, "proto", swap)
     student_sum = call(student_merge_kernel, [packed], student_own, student_came)[0]
     own, other = call(
@@ -486,7 +506,7 @@
         finish_kernel,
         [((patches, bot), BF16), ((1, 1), F32)],
         back,
-        student_sent,
+        picked,
         mask_order,
         counts,
         in_specs=[VMEM, VMEM, VMEM, SMEM],

time: 177 us -> 167 us (0.944)
  blocking collectives: 88.4 us -> 119 us
  waiting for transfers between devices: 16.7 us -> 1.47 us
  between operations: 14.8 us -> 1.44 us
  starting transfers between devices: 20 us -> 10.4 us
    all_to_all x1 -> x2, blocking collectives: 15.4 us -> 43.2 us  [body(): shares = over(share, 'dp')]
    all_to_all x0 -> x1, blocking collectives: none -> 16.4 us  [body(): shares = over(share.reshape((width,) + share.shape[2:]), 'proto')]
    all_to_all x2 -> x1, waiting for transfers between devices: 16 us -> 0.01 us  [body(): shares = over(share, 'dp')]
    all_to_all x2 -> x1, blocking collectives: 26.8 us -> 11.8 us  [body(): shares = over(share, 'proto')]
    all_to_all x2 -> x1, starting transfers between devices: 14.5 us -> 3.87 us  [body(): shares = over(share, 'dp')]
    ppermute x0 -> x1, starting transfers between devices: none -> 2.08 us  [body(): late_came = lax.ppermute(late, 'proto', swap)]
    unnamed x16 -> x18, local copies, waits for them, and re-layouts: 6.23 us -> 5.3 us
  transfers between devices with their start and end apart: 5 -> 4, of which waited for: 1 -> 1; matrix products, arithmetic and copies ran while one was open for 0% -> 0% of each run, Pallas kernels for 12% -> 8%
where the time goes in v6:
time: 167 us
  blocking collectives  119 us (71%)
  Pallas kernels  29 us (17%)
  starting transfers between devices  10.4 us (6%)
  local copies, waits for them, and re-layouts  5.3 us (3%)
    all_to_all x2, blocking collectives, body(): shares = over(share, 'dp')  43.2 us
    pallas_call x11, Pallas kernels, call(): pl.pallas_call(kernel, out_shape=out_shape, in_specs=[VMEM] * len(args) i...  29 us
    all_gather x1, blocking collectives, body(): gathered = lax.all_gather(sent, 'proto', axis=0, tiled=False)  24.3 us
    all_to_all x1, blocking collectives, body(): back = over(sent, 'proto', axis_index_groups=same_core)  23.2 us
    all_to_all x1, blocking collectives, body(): shares = over(share.reshape((width,) + share.shape[2:]), 'proto')  16.4 us
    all_to_all x1, blocking collectives, body(): shares = over(share, 'proto')  11.8 us
    unnamed x18, local copies, waits for them, and re-layouts  5.3 us
    all_to_all x1, starting transfers between devices, body(): shares = over(share, 'dp')  3.87 us
  transfers between devices with their start and end apart: 4, of which 1 were waited for; matrix products, arithmetic and copies ran while one was open for 0% of the time, Pallas kernels for 8%

profile of v6, /device:TPU:1, one launch (start us, length us, event | category | flops | bytes accessed | tf_op | source)
XLA Modules:
  0.0 166.6 jit_solution(1717751406995690105)
XLA Ops:
  1.3 1.2 shard_map.77
  2.5 24.3 %all-gather = bf16[1920,256]{1,0:T(8,128)(2,1)S(1)} all-gather(bf16[120,256]{1,0:T(8,128)(2,1)S(1)} %get-tuple-element.21), channel_id=2, replica_groups=mesh['dp'=32,'proto'=16] {'proto'}, dimensions={0}, use_global_device_ids=true | all-gather | bytes 1044480 | tf_op jit(solution)/shard_map/all_gather | solution.py:401
  26.8 0.0 copy-start
  26.8 4.8 %shard_map.78 = (f32[32,32,128]{2,1,0:T(8,128)S(1)}, bf16[384,256]{1,0:T(8,128)(2,1)S(1)}, f32[4,16,128]{2,1,0:T(8,128)S(1)}) custom-call(bf16[16,120,256]{2,1,0:T(8,128)(2,1)S(1)} %bitcast.6, s32[1,1]{1,0:T(1,128)} %bitcast.3.index_ref, bf16[256,4096]{1,0:T(8,128)(2,1)} %protos_ref.5), custom_call_target="tpu_custom_call" | custom-call | flops 805306368 | bytes 2097152 | tf_op jit(solution)/shard_map/pallas_call | solution.py:29
  31.5 26.7 %all_to_all.30.shares_ref = f32[32,32,128]{2,1,0:T(8,128)S(1)} all-to-all(f32[32,32,128]{2,1,0:T(8,128)S(1)} %get-tuple-element.22), channel_id=1, replica_groups=mesh['dp'=32,'proto'=16] {'dp'}, dimensions={0} | all-to-all | bytes 1048576 | tf_op jit(solution)/shard_map/all_to_all | solution.py:414
  58.3 0.0 copy-done
  58.3 4.1 %shard_map.79 = (bf16[384,4096]{1,0:T(8,128)(2,1)S(1)}, f32[2,384,1]{2,1,0:T(8,128)S(1)}, bf16[8,2,48,128]{3,2,1,0:T(8,128)(2,1)S(1)}) custom-call(f32[32,32,128]{2,1,0:T(8,128)S(1)} %all_to_all.30.shares_ref, bf16[384,256]{1,0:T(8,128)(2,1)S(1)} %get-tuple-element.23.rows_ref, bf16[256,4096]{1,0:T(8,128)(2,1)} %protos_ref.5, ...), custom_call_target="tpu_custom_call" | custom-call | flops 805306368 | bytes 5242880 | tf_op jit(solution)/shard_map/pallas_call | solution.py:29
  62.4 16.4 %all_to_all.31.shares_ref.late_ref = bf16[16,48,128]{2,1,0:T(8,128)(2,1)S(1)} all-to-all(bf16[16,48,128]{2,1,0:T(8,128)(2,1)S(1)} %bitcast.8), channel_id=1, replica_groups=mesh['dp'=32,'proto'=16] {'proto'}, dimensions={0} | all-to-all | bytes 393216 | tf_op jit(solution)/shard_map/all_to_all | solution.py:430
  78.8 0.0 copy-start.2
  78.8 1.3 shard_map.80
  80.0 16.5 %all_to_all.32.shares_ref = bf16[32,32,128]{2,1,0:T(8,128)(2,1)S(1)} all-to-all(bf16[32,32,128]{2,1,0:T(8,128)(2,1)S(1)} %get-tuple-element.28), channel_id=1, replica_groups=mesh['dp'=32,'proto'=16] {'dp'}, dimensions={0} | all-to-all | bytes 524288 | tf_op jit(solution)/shard_map/all_to_all | solution.py:444
  96.5 0.0 copy-done.2
  96.5 1.3 shard_map.81
  97.8 11.8 %all_to_all.33.shares_ref = f32[16,8,128]{2,1,0:T(8,128)S(1)} all-to-all(f32[16,8,128]{2,1,0:T(8,128)S(1)} %shard_map.81), channel_id=1, replica_groups=mesh['dp'=32,'proto'=16] {'proto'}, dimensions={0} | all-to-all | bytes 131072 | tf_op jit(solution)/shard_map/all_to_all | solution.py:456
  109.6 1.2 shard_map.82
  110.8 0.0 copy-start.4
  110.8 0.8 copy-done.4
  111.6 0.0 copy-start.8
  111.6 0.7 copy-done.8
  112.3 3.9 %all-to-all-start.4 = ((bf16[32,32,128]{2,1,0:T(8,128)(2,1)}), bf16[32,32,128]{2,1,0:T(8,128)(2,1)S(1)}, u32[]{:S(2)}, u32[]{:S(2)}) async-start(bf16[32,32,128]{2,1,0:T(8,128)(2,1)} %copy-done.8), calls=%async_computation.4 | async-start | bytes 524288 | tf_op jit(solution)/shard_map/all_to_all | solution.py:468
  116.2 2.1 %collective-permute-start.1 = (bf16[16,48,128]{2,1,0:T(8,128)(2,1)}, bf16[16,48,128]{2,1,0:T(8,128)(2,1)S(1)}, u32[]{:S(2)}, u32[]{:S(2)}) collective-permute-start(bf16[16,48,128]{2,1,0:T(8,128)(2,1)} %copy-done.2), channel_id=1, source_target_pairs={{0,1},{1,0},{2,3},{3,2},{4,5},{5,4},{6,7},{7,6},{8,9},{9,8},{10,11... | collective-permute-start | bytes 589832 | tf_op jit(solution)/shard_map/ppermute | solution.py:432
  118.3 1.5 collective-permute-done.1.came_ref
  119.7 0.0 copy-start.1
  119.7 1.2 copy-done.1
  120.9 0.0 copy-start.3
  120.9 0.9 copy-done.3
  121.8 8.4 %shard_map.84 = (bf16[8,80,256]{2,1,0:T(8,128)(2,1)S(1)}, bf16[8,80,256]{2,1,0:T(8,128)(2,1)}) custom-call(bf16[16,120,256]{2,1,0:T(8,128)(2,1)S(1)} %bitcast.7, bf16[16,48,128]{2,1,0:T(8,128)(2,1)S(1)} %copy-done.3, bf16[16,48,128]{2,1,0:T(8,128)(2,1)S(1)} %collective-permute-done.1.came_ref, s32[1,1]{1,0:T(1,128)} %bitcast.3.index_ref, ...), custom_call_target="tpu_custom_call" | custom-call | flops 1610612736 | bytes 2097152 | tf_op jit(solution)/shard_map/pallas_call | solution.py:29
  130.3 0.0 copy-start.6
  130.3 0.7 copy-done.6
  131.0 2.3 %collective-permute-start.2 = (bf16[8,80,256]{2,1,0:T(8,128)(2,1)}, bf16[8,80,256]{2,1,0:T(8,128)(2,1)}, u32[]{:S(2)}, u32[]{:S(2)}) collective-permute-start(bf16[8,80,256]{2,1,0:T(8,128)(2,1)} %get-tuple-element.36), channel_id=1, source_target_pairs={{0,1},{1,0},{2,3},{3,2},{4,5},{5,4},{6,7},{7,6},{8,9},{9,8},{10,11... | collective-permute-start | bytes 983048 | tf_op jit(solution)/shard_map/ppermute | solution.py:485
  133.3 0.0 all-to-all-done.4.shares_ref
  133.3 0.0 copy-start.5
  133.3 1.0 copy-done.5
  134.3 0.0 copy-start.7
  134.3 3.8 %shard_map.83 = (bf16[8,80,256]{2,1,0:T(8,128)(2,1)S(1)}, bf16[8,80,256]{2,1,0:T(8,128)(2,1)S(1)}) custom-call(bf16[32,32,128]{2,1,0:T(8,128)(2,1)S(1)} %all-to-all-done.4.shares_ref, f32[2,384,1]{2,1,0:T(8,128)S(1)} %copy-done.5, bf16[384,4096]{1,0:T(8,128)(2,1)S(1)} %get-tuple-element.27.matrix_ref, bf16[256,4096]{1,0:T(8,128)(2,1)} %protos_ref.7, ...), custom_call_target="tpu_custom_call" | custom-call | flops 805306368 | bytes 3145728 | tf_op jit(solution)/shard_map/pallas_call | solution.py:29
  138.1 2.2 %collective-permute-start = (bf16[8,80,256]{2,1,0:T(8,128)(2,1)S(1)}, bf16[8,80,256]{2,1,0:T(8,128)(2,1)S(1)}, u32[]{:S(2)}, u32[]{:S(2)}) collective-permute-start(bf16[8,80,256]{2,1,0:T(8,128)(2,1)S(1)} %get-tuple-element.34), channel_id=1, source_target_pairs={{0,1},{1,0},{2,3},{3,2},{4,5},{5,4},{6,7},{7,6},{8,9},{9,8},{10,11... | collective-permute-start | bytes 983048 | tf_op jit(solution)/shard_map/ppermute | solution.py:501
  140.3 0.0 collective-permute-done.2.came_ref
  140.3 0.0 copy-done.7
  140.3 1.3 shard_map.85.student_ref
  141.6 0.0 collective-permute-done.came_ref
  141.6 0.1 shard_map.86
  141.7 23.2 %all_to_all.34.back_ref = bf16[8,160,256]{2,1,0:T(8,128)(2,1)S(1)} all-to-all(bf16[8,160,256]{2,1,0:T(8,128)(2,1)S(1)} %shard_map.86), channel_id=1, replica_groups={{0,2,4,6,8,10,12,14},{1,3,5,7,9,11,13,15},{16,18,20,22,24,26,28,30},{17..., dimensions={0} | all-to-all | bytes 1310720 | tf_op jit(solution)/shard_map/all_to_all | solution.py:504
  164.9 1.7 %shard_map.87 = (bf16[256,256]{1,0:T(8,128)(2,1)}, f32[1,1]{1,0:T(1,128)}) custom-call(bf16[8,160,256]{2,1,0:T(8,128)(2,1)S(1)} %all_to_all.34.back_ref, bf16[80,256]{1,0:T(8,128)(2,1)S(1)} %get-tuple-element.37.picked_ref, s32[1,256]{1,0:T(1,128)} %order_ref.3, s32[1,1]{1,0:T(1,128)S(6)} %copy.8.count_ref), custom_call_target="tpu_custom_call" | custom-call | bytes 131072 | tf_op jit(solution)/shard_map/pallas_call | solution.py:29
Async XLA Ops:
  26.8 31.5 %copy-start = (bf16[1920,256]{1,0:T(8,128)(2,1)}, bf16[1920,256]{1,0:T(8,128)(2,1)S(1)}, u32[]{:S(2)}) copy-start(bf16[1920,256]{1,0:T(8,128)(2,1)S(1)} %all-gather) | copy-start | bytes 2949124
  78.8 17.8 %copy-start.2 = (bf16[16,48,128]{2,1,0:T(8,128)(2,1)}, bf16[16,48,128]{2,1,0:T(8,128)(2,1)S(1)}, u32[]{:S(2)}) copy-start(bf16[16,48,128]{2,1,0:T(8,128)(2,1)S(1)} %all_to_all.31.shares_ref.late_ref) | copy-start | bytes 589828
  110.8 0.8 copy-start.4
  111.6 0.7 copy-start.8
  112.3 21.0 %all-to-all-start.4 = ((bf16[32,32,128]{2,1,0:T(8,128)(2,1)}), bf16[32,32,128]{2,1,0:T(8,128)(2,1)S(1)}, u32[]{:S(2)}, u32[]{:S(2)}) async-start(bf16[32,32,128]{2,1,0:T(8,128)(2,1)} %copy-done.8), calls=%async_computation.4 | async-start | bytes 524288 | tf_op jit(solution)/shard_map/all_to_all | solution.py:468
  116.2 3.5 %collective-permute-start.1 = (bf16[16,48,128]{2,1,0:T(8,128)(2,1)}, bf16[16,48,128]{2,1,0:T(8,128)(2,1)S(1)}, u32[]{:S(2)}, u32[]{:S(2)}) collective-permute-start(bf16[16,48,128]{2,1,0:T(8,128)(2,1)} %copy-done.2), channel_id=1, source_target_pairs={{0,1},{1,0},{2,3},{3,2},{4,5},{5,4},{6,7},{7,6},{8,9},{9,8},{10,11... | collective-permute-start | bytes 589832 | tf_op jit(solution)/shard_map/ppermute | solution.py:432
  119.7 1.2 copy-start.1
  120.9 0.9 copy-start.3
  130.3 0.7 copy-start.6
  131.0 9.3 %collective-permute-start.2 = (bf16[8,80,256]{2,1,0:T(8,128)(2,1)}, bf16[8,80,256]{2,1,0:T(8,128)(2,1)}, u32[]{:S(2)}, u32[]{:S(2)}) collective-permute-start(bf16[8,80,256]{2,1,0:T(8,128)(2,1)} %get-tuple-element.36), channel_id=1, source_target_pairs={{0,1},{1,0},{2,3},{3,2},{4,5},{5,4},{6,7},{7,6},{8,9},{9,8},{10,11... | collective-permute-start | bytes 983048 | tf_op jit(solution)/shard_map/ppermute | solution.py:485
  133.3 1.0 copy-start.5
  134.3 6.0 %copy-start.7 = (bf16[8,80,256]{2,1,0:T(8,128)(2,1)S(1)}, bf16[8,80,256]{2,1,0:T(8,128)(2,1)}, u32[]{:S(2)}) copy-start(bf16[8,80,256]{2,1,0:T(8,128)(2,1)} %copy-done.6) | copy-start | bytes 983044
  138.1 3.5 %collective-permute-start = (bf16[8,80,256]{2,1,0:T(8,128)(2,1)S(1)}, bf16[8,80,256]{2,1,0:T(8,128)(2,1)S(1)}, u32[]{:S(2)}, u32[]{:S(2)}) collective-permute-start(bf16[8,80,256]{2,1,0:T(8,128)(2,1)S(1)} %get-tuple-element.34), channel_id=1, source_target_pairs={{0,1},{1,0},{2,3},{3,2},{4,5},{5,4},{6,7},{7,6},{8,9},{9,8},{10,11... | collective-permute-start | bytes 983048 | tf_op jit(solution)/shard_map/ppermute | solution.py:501

commit v7 on v6

--- a/solution.py
+++ b/solution.py
@@ -24,7 +24,7 @@
 
 
 def call(kernel, out_shape, *args, grid=None, in_specs=None, out_specs=None, scratch=(), flops=0, moved=0):
-    out_shape = [jax.ShapeDtypeStruct(s, d) for s, d in out_shape]
+    out_shape = [jax.ShapeDtypeStruct(*o) if isinstance(o, tuple) else o for o in out_shape]
     extra = {} if grid is None else {"grid": grid}
     return pl.pallas_call(
         kernel,
@@ -129,7 +129,7 @@
         places_ref[1] = jnp.dot((other == image).astype(BF16), counts.astype(BF16), preferred_element_type=F32)
         places_ref[2] = starts
         places_ref[3] = counts
-        rows_ref[...] = compact(gathered_ref[...], starts, counts, rows, 0, MOST, 0).astype(BF16)
+        rows_ref[...] = compact(gathered_ref[:, :SLOT], starts, counts, rows, 0, MOST, 0).astype(BF16)
 
     logits = jnp.dot(rows_ref[...], protos_ref[...], preferred_element_type=F32) * TEACH
     high = jnp.max(logits, axis=0, keepdims=True)
@@ -432,7 +432,7 @@
     late_came = lax.ppermute(late, "proto", swap)
     share, scale = call(
         first_column_kernel,
-        [((groups, protos // LANES, LANES), BF16), ((steps, rows, 1), F32)],
+        [pltpu.HBM((groups, protos // LANES, LANES), BF16), pltpu.HBM((steps, rows, 1), F32)],
         shares,
         high,
         matrix,
@@ -441,7 +441,25 @@
         out_specs=[peer, VMEM],
         moved=2 * rows * protos,
     )
-    shares = over(share, "dp")
+    packed = ((width // 2, SLOT, bot), BF16)
+    student_own, student_other = call(
+        student_kernel,
+        [packed, packed],
+        gathered,
+        late,
+        late_came,
+        index,
+        places,
+        student_protos,
+        grid=grid,
+        in_specs=[VMEM, VMEM, VMEM, SMEM, VMEM, wide],
+        scratch=[pltpu.VMEM((rows, bot), BF16), pltpu.VMEM((rows, bot), F32), column, column],
+        flops=2 * dot,
+        moved=2 * bot * protos,
+    )
+    student_came = lax.ppermute(student_other, "proto", swap)
+    student_sum = call(student_merge_kernel, [packed], student_own, student_came)[0]
+    shares, student_sum = lax.optimization_barrier((over(share, "dp"), student_sum))
     share = call(
         later_row_kernel,
         [((width, depth, LANES), F32)],
@@ -466,24 +484,6 @@
         moved=2 * rows * protos,
     )
     shares = over(share, "dp")
-    packed = ((width // 2, SLOT, bot), BF16)
-    student_own, student_other = call(
-        student_kernel,
-        [packed, packed],
-        gathered,
-        late,
-        late_came,
-        index,
-        places,
-        student_protos,
-        grid=grid,
-        in_specs=[VMEM, VMEM, VMEM, SMEM, VMEM, wide],
-        scratch=[pltpu.VMEM((rows, bot), BF16), pltpu.VMEM((rows, bot), F32), column, column],
-        flops=2 * dot,
-        moved=2 * bot * protos,
-    )
-    student_came = lax.ppermute(student_other, "proto", swap)
-    student_sum = call(student_merge_kernel, [packed], student_own, student_came)[0]
     own, other = call(
         target_kernel,
         [packed, packed],

time: 167 us -> 175 us (1.048)
  blocking collectives: 119 us -> 122 us
  starting transfers between devices: 10.4 us -> 13.2 us
    all_to_all x2, blocking collectives: 43.2 us -> 47.8 us  [body(): shares = over(share, 'dp')]
    ppermute x1, starting transfers between devices: 2.24 us -> 4.06 us  [body(): came = lax.ppermute(other, 'proto', swap)]
    unnamed x18 -> x28, local copies, waits for them, and re-layouts: 5.3 us -> 5.86 us
  transfers between devices with their start and end apart: 4 -> 4, of which waited for: 1 -> 2; matrix products, arithmetic and copies ran while one was open for 0% -> 0% of each run, Pallas kernels for 8% -> 6%
where the time goes in v7:
time: 175 us; the launch traced here: 174 us
  blocking collectives  122 us (70%)
  Pallas kernels  28.7 us (16%)
  starting transfers between devices  13.2 us (8%)
  local copies, waits for them, and re-layouts  5.86 us (3%)
  waiting for transfers between devices  2.47 us (1%)
    all_to_all x2, blocking collectives, body(): shares = over(share, 'dp')  47.8 us
    pallas_call x11, Pallas kernels, call(): pl.pallas_call(kernel, out_shape=out_shape, in_specs=[VMEM] * len(args) i...  28.7 us
    all_gather x1, blocking collectives, body(): gathered = lax.all_gather(sent, 'proto', axis=0, tiled=False)  24.3 us
    all_to_all x1, blocking collectives, body(): back = over(sent, 'proto', axis_index_groups=same_core)  23.2 us
    all_to_all x1, blocking collectives, body(): shares = over(share.reshape((width,) + share.shape[2:]), 'proto')  16.4 us
    all_to_all x1, blocking collectives, body(): shares = over(share, 'proto')  10.6 us
    unnamed x28, local copies, waits for them, and re-layouts  5.86 us
    all_to_all x1, starting transfers between devices, body(): over(share, 'dp')  4.59 us
  transfers between devices with their start and end apart: 4, of which 2 were waited for; matrix products, arithmetic and copies ran while one was open for 0% of the time, Pallas kernels for 6%

profile of v7, /device:TPU:1, one launch (start us, length us, event | category | flops | bytes accessed | tf_op | source)
XLA Modules:
  0.0 173.9 jit_solution(1584797436933837759)
XLA Ops:
  1.3 1.2 shard_map.77
  2.5 0.0 copy-start.7
  2.5 0.6 copy-done.7
  3.1 24.3 %all-gather = bf16[1920,256]{1,0:T(8,128)(2,1)S(1)} all-gather(bf16[120,256]{1,0:T(8,128)(2,1)S(1)} %get-tuple-element.23), channel_id=2, replica_groups=mesh['dp'=32,'proto'=16] {'proto'}, dimensions={0}, use_global_device_ids=true | all-gather | bytes 1044480 | tf_op jit(solution)/shard_map/all_gather | solution.py:401
  27.4 0.0 copy-start
  27.4 4.6 %shard_map.78 = (f32[32,32,128]{2,1,0:T(8,128)S(1)}, bf16[384,256]{1,0:T(8,128)(2,1)S(1)}, f32[4,16,128]{2,1,0:T(8,128)S(1)}) custom-call(bf16[16,120,256]{2,1,0:T(8,128)(2,1)S(1)} %bitcast.6, s32[1,1]{1,0:T(1,128)} %bitcast.3.index_ref, bf16[256,4096]{1,0:T(8,128)(2,1)} %protos_ref.5), custom_call_target="tpu_custom_call" | custom-call | flops 805306368 | bytes 2097152 | tf_op jit(solution)/shard_map/pallas_call | solution.py:29
  32.0 0.0 copy-start.9
  32.0 26.8 %all_to_all.30.shares_ref = f32[32,32,128]{2,1,0:T(8,128)S(1)} all-to-all(f32[32,32,128]{2,1,0:T(8,128)S(1)} %get-tuple-element.24), channel_id=1, replica_groups=mesh['dp'=32,'proto'=16] {'dp'}, dimensions={0} | all-to-all | bytes 1048576 | tf_op jit(solution)/shard_map/all_to_all | solution.py:414
  58.7 0.0 copy-done
  58.7 4.1 %shard_map.79 = (bf16[384,4096]{1,0:T(8,128)(2,1)S(1)}, f32[2,384,1]{2,1,0:T(8,128)S(1)}, bf16[8,2,48,128]{3,2,1,0:T(8,128)(2,1)S(1)}) custom-call(f32[32,32,128]{2,1,0:T(8,128)S(1)} %all_to_all.30.shares_ref, bf16[384,256]{1,0:T(8,128)(2,1)S(1)} %get-tuple-element.25.rows_ref, bf16[256,4096]{1,0:T(8,128)(2,1)} %protos_ref.5, ...), custom_call_target="tpu_custom_call" | custom-call | flops 805306368 | bytes 5242880 | tf_op jit(solution)/shard_map/pallas_call | solution.py:29
  62.8 16.4 %all_to_all.31.shares_ref.late_ref = bf16[16,48,128]{2,1,0:T(8,128)(2,1)S(1)} all-to-all(bf16[16,48,128]{2,1,0:T(8,128)(2,1)S(1)} %bitcast.8), channel_id=1, replica_groups=mesh['dp'=32,'proto'=16] {'proto'}, dimensions={0} | all-to-all | bytes 393216 | tf_op jit(solution)/shard_map/all_to_all | solution.py:430
  79.2 0.0 copy-done.9
  79.2 0.0 copy-start.5
  79.2 1.9 %collective-permute-start = (bf16[16,48,128]{2,1,0:T(8,128)(2,1)S(1)}, bf16[16,48,128]{2,1,0:T(8,128)(2,1)S(1)}, u32[]{:S(2)}, u32[]{:S(2)}) collective-permute-start(bf16[16,48,128]{2,1,0:T(8,128)(2,1)S(1)} %all_to_all.31.shares_ref.late_ref), channel_id=1, source_target_pairs={{0,1},{1,0},{2,3},{3,2},{4,5},{5,4},{6,7},{7,6},{8,9},{9,8},{10,11... | collective-permute-start | bytes 589832 | tf_op jit(solution)/shard_map/ppermute | solution.py:432
  81.1 2.1 %shard_map.80 = (bf16[32,32,128]{2,1,0:T(8,128)(2,1)}, f32[2,384,1]{2,1,0:T(8,128)}) custom-call(bf16[16,48,128]{2,1,0:T(8,128)(2,1)S(1)} %all_to_all.31.shares_ref.late_ref, f32[2,384,1]{2,1,0:T(8,128)S(1)} %get-tuple-element.28.high_ref, bf16[384,4096]{1,0:T(8,128)(2,1)S(1)} %get-tuple-element.29.matrix_ref), custom_call_target="tpu_custom_call" | custom-call | bytes 3145728 | tf_op jit(solution)/shard_map/pallas_call | solution.py:29
  83.2 0.0 copy-done.5
  83.2 4.6 %all-to-all-start.2 = ((bf16[32,32,128]{2,1,0:T(8,128)(2,1)}), bf16[32,32,128]{2,1,0:T(8,128)(2,1)}, u32[]{:S(2)}, u32[]{:S(2)}) async-start(bf16[32,32,128]{2,1,0:T(8,128)(2,1)} %get-tuple-element.30), calls=%async_computation.2 | async-start | bytes 524288 | tf_op jit(solution)/shard_map/all_to_all | solution.py:462
  87.8 0.0 collective-permute-done.came_ref
  87.8 0.0 copy-start.12
  87.8 0.7 copy-done.12
  88.5 0.0 copy-start.1
  88.5 1.2 copy-done.1
  89.7 0.0 copy-start.6
  89.7 0.9 copy-done.6
  90.6 0.8 copy-done.10
  91.4 0.9 copy-done.13
  92.3 7.8 %shard_map.81 = (bf16[8,80,256]{2,1,0:T(8,128)(2,1)S(1)}, bf16[8,80,256]{2,1,0:T(8,128)(2,1)S(1)}) custom-call(bf16[16,120,256]{2,1,0:T(8,128)(2,1)S(1)} %bitcast.7, bf16[16,48,128]{2,1,0:T(8,128)(2,1)S(1)} %copy-done.6, bf16[16,48,128]{2,1,0:T(8,128)(2,1)S(1)} %copy-done.13, s32[1,1]{1,0:T(1,128)} %bitcast.3.index_ref, f32[4,16,128]{2,1,0:T(8,128)S(1)} %copy-done.10, ...), custom_call_target="tpu_custom_call" | custom-call | flops 1610612736 | bytes 2097152 | tf_op jit(solution)/shard_map/pallas_call | solution.py:29
  100.1 2.6 %collective-permute-start.1 = (bf16[8,80,256]{2,1,0:T(8,128)(2,1)S(1)}, bf16[8,80,256]{2,1,0:T(8,128)(2,1)S(1)}, u32[]{:S(2)}, u32[]{:S(2)}) collective-permute-start(bf16[8,80,256]{2,1,0:T(8,128)(2,1)S(1)} %get-tuple-element.33), channel_id=1, source_target_pairs={{0,1},{1,0},{2,3},{3,2},{4,5},{5,4},{6,7},{7,6},{8,9},{9,8},{10,11... | collective-permute-start | bytes 983048 | tf_op jit(solution)/shard_map/ppermute | solution.py:460
  102.7 1.2 collective-permute-done.1.came_ref
  104.0 0.3 shard_map.82.student_ref
  104.3 0.0 copy-start.3
  104.3 0.7 copy-done.3
  105.0 0.0 all-to-all-done.2.shares_ref
  105.0 0.0 copy-done.2
  105.0 1.9 %shard_map.83 = f32[16,8,128]{2,1,0:T(8,128)S(1)} custom-call(bf16[32,32,128]{2,1,0:T(8,128)(2,1)} %all-to-all-done.2.shares_ref, f32[2,384,1]{2,1,0:T(8,128)S(1)} %copy-done.2, bf16[384,4096]{1,0:T(8,128)(2,1)S(1)} %get-tuple-element.29.matrix_ref), custom_call_target="tpu_custom_call" | custom-call | bytes 3145728 | tf_op jit(solution)/shard_map/pallas_call | solution.py:29
  106.9 10.6 %all_to_all.32.shares_ref = f32[16,8,128]{2,1,0:T(8,128)S(1)} all-to-all(f32[16,8,128]{2,1,0:T(8,128)S(1)} %shard_map.83), channel_id=1, replica_groups=mesh['dp'=32,'proto'=16] {'proto'}, dimensions={0} | all-to-all | bytes 131072 | tf_op jit(solution)/shard_map/all_to_all | solution.py:474
  117.5 1.2 shard_map.84
  118.8 21.1 %all_to_all.33.shares_ref = bf16[32,32,128]{2,1,0:T(8,128)(2,1)S(1)} all-to-all(bf16[32,32,128]{2,1,0:T(8,128)(2,1)S(1)} %get-tuple-element.36), channel_id=1, replica_groups=mesh['dp'=32,'proto'=16] {'dp'}, dimensions={0} | all-to-all | bytes 524288 | tf_op jit(solution)/shard_map/all_to_all | solution.py:486
  139.8 0.0 copy-done.11
  139.8 3.8 %shard_map.85 = (bf16[8,80,256]{2,1,0:T(8,128)(2,1)S(1)}, bf16[8,80,256]{2,1,0:T(8,128)(2,1)S(1)}) custom-call(bf16[32,32,128]{2,1,0:T(8,128)(2,1)S(1)} %all_to_all.33.shares_ref, f32[2,384,1]{2,1,0:T(8,128)S(1)} %get-tuple-element.37.scale_ref, bf16[384,4096]{1,0:T(8,128)(2,1)S(1)} %get-tuple-element.29.matrix_ref, bf16[256,4096]{1,0:T(8,128)(2,1)} %protos_ref.7, ...), custom_call_target="tpu_custom_call" | custom-call | flops 805306368 | bytes 3145728 | tf_op jit(solution)/shard_map/pallas_call | solution.py:29
  143.6 0.0 copy-start.8
  143.6 4.1 %collective-permute-start.2 = (bf16[8,80,256]{2,1,0:T(8,128)(2,1)S(1)}, bf16[8,80,256]{2,1,0:T(8,128)(2,1)S(1)}, u32[]{:S(2)}, u32[]{:S(2)}) collective-permute-start(bf16[8,80,256]{2,1,0:T(8,128)(2,1)S(1)} %get-tuple-element.39), channel_id=1, source_target_pairs={{0,1},{1,0},{2,3},{3,2},{4,5},{5,4},{6,7},{7,6},{8,9},{9,8},{10,11... | collective-permute-start | bytes 983048 | tf_op jit(solution)/shard_map/ppermute | solution.py:501
  147.7 1.2 collective-permute-done.2.came_ref
  148.9 0.0 copy-done.4
  148.9 0.1 shard_map.86
  149.0 23.2 %all_to_all.34.back_ref = bf16[8,160,256]{2,1,0:T(8,128)(2,1)S(1)} all-to-all(bf16[8,160,256]{2,1,0:T(8,128)(2,1)S(1)} %shard_map.86), channel_id=1, replica_groups={{0,2,4,6,8,10,12,14},{1,3,5,7,9,11,13,15},{16,18,20,22,24,26,28,30},{17..., dimensions={0} | all-to-all | bytes 1310720 | tf_op jit(solution)/shard_map/all_to_all | solution.py:504
  172.2 0.0 copy-done.8
  172.2 1.7 shard_map.87
  (5 shorter events, 0.0 us)
Async XLA Ops:
  2.5 0.6 copy-start.7
  27.4 31.4 %copy-start = (bf16[1920,256]{1,0:T(8,128)(2,1)}, bf16[1920,256]{1,0:T(8,128)(2,1)S(1)}, u32[]{:S(2)}) copy-start(bf16[1920,256]{1,0:T(8,128)(2,1)S(1)} %all-gather) | copy-start | bytes 2949124
  32.0 47.3 %copy-start.9 = (f32[4,16,128]{2,1,0:T(8,128)}, f32[4,16,128]{2,1,0:T(8,128)S(1)}, u32[]{:S(2)}) copy-start(f32[4,16,128]{2,1,0:T(8,128)S(1)} %get-tuple-element.31.places_ref) | copy-start | bytes 98308
  79.2 4.0 %copy-start.5 = (bf16[16,48,128]{2,1,0:T(8,128)(2,1)}, bf16[16,48,128]{2,1,0:T(8,128)(2,1)S(1)}, u32[]{:S(2)}) copy-start(bf16[16,48,128]{2,1,0:T(8,128)(2,1)S(1)} %all_to_all.31.shares_ref.late_ref) | copy-start | bytes 589828
  79.2 8.6 %collective-permute-start = (bf16[16,48,128]{2,1,0:T(8,128)(2,1)S(1)}, bf16[16,48,128]{2,1,0:T(8,128)(2,1)S(1)}, u32[]{:S(2)}, u32[]{:S(2)}) collective-permute-start(bf16[16,48,128]{2,1,0:T(8,128)(2,1)S(1)} %all_to_all.31.shares_ref.late_ref), channel_id=1, source_target_pairs={{0,1},{1,0},{2,3},{3,2},{4,5},{5,4},{6,7},{7,6},{8,9},{9,8},{10,11... | collective-permute-start | bytes 589832 | tf_op jit(solution)/shard_map/ppermute | solution.py:432
  83.2 21.8 %all-to-all-start.2 = ((bf16[32,32,128]{2,1,0:T(8,128)(2,1)}), bf16[32,32,128]{2,1,0:T(8,128)(2,1)}, u32[]{:S(2)}, u32[]{:S(2)}) async-start(bf16[32,32,128]{2,1,0:T(8,128)(2,1)} %get-tuple-element.30), calls=%async_computation.2 | async-start | bytes 524288 | tf_op jit(solution)/shard_map/all_to_all | solution.py:462
  87.8 0.7 copy-start.12
  88.5 1.2 copy-start.1
  89.7 0.9 copy-start.6
  90.6 0.8 copy-start.10
  91.4 0.9 copy-start.13
  92.3 12.7 %copy-start.2 = (f32[2,384,1]{2,1,0:T(8,128)S(1)}, f32[2,384,1]{2,1,0:T(8,128)}, u32[]{:S(2)}) copy-start(f32[2,384,1]{2,1,0:T(8,128)} %get-tuple-element.35.scale_ref.scale_in_ref) | copy-start | bytes 9220
  100.1 3.9 %collective-permute-start.1 = (bf16[8,80,256]{2,1,0:T(8,128)(2,1)S(1)}, bf16[8,80,256]{2,1,0:T(8,128)(2,1)S(1)}, u32[]{:S(2)}, u32[]{:S(2)}) collective-permute-start(bf16[8,80,256]{2,1,0:T(8,128)(2,1)S(1)} %get-tuple-element.33), channel_id=1, source_target_pairs={{0,1},{1,0},{2,3},{3,2},{4,5},{5,4},{6,7},{7,6},{8,9},{9,8},{10,11... | collective-permute-start | bytes 983048 | tf_op jit(solution)/shard_map/ppermute | solution.py:460
  104.3 0.7 copy-start.3
  117.5 22.3 %copy-start.11 = (f32[4,16,128]{2,1,0:T(8,128)S(1)}, f32[4,16,128]{2,1,0:T(8,128)}, u32[]{:S(2)}) copy-start(f32[4,16,128]{2,1,0:T(8,128)} %copy-done.9) | copy-start | bytes 98308
  139.8 9.1 %copy-start.4 = (bf16[8,80,256]{2,1,0:T(8,128)(2,1)S(1)}, bf16[8,80,256]{2,1,0:T(8,128)(2,1)}, u32[]{:S(2)}) copy-start(bf16[8,80,256]{2,1,0:T(8,128)(2,1)} %copy-done.3) | copy-start | bytes 983044
  143.6 28.6 %copy-start.8 = (bf16[80,256]{1,0:T(8,128)(2,1)S(1)}, bf16[80,256]{1,0:T(8,128)(2,1)}, u32[]{:S(2)}) copy-start(bf16[80,256]{1,0:T(8,128)(2,1)} %copy-done.7) | copy-start | bytes 122884
  143.6 5.3 %collective-permute-start.2 = (bf16[8,80,256]{2,1,0:T(8,128)(2,1)S(1)}, bf16[8,80,256]{2,1,0:T(8,128)(2,1)S(1)}, u32[]{:S(2)}, u32[]{:S(2)}) collective-permute-start(bf16[8,80,256]{2,1,0:T(8,128)(2,1)S(1)} %get-tuple-element.39), channel_id=1, source_target_pairs={{0,1},{1,0},{2,3},{3,2},{4,5},{5,4},{6,7},{7,6},{8,9},{9,8},{10,11... | collective-permute-start | bytes 983048 | tf_op jit(solution)/shard_map/ppermute | solution.py:501

commit v8 on v7

--- a/solution.py
+++ b/solution.py
@@ -287,12 +287,18 @@
         put(own_ref, other_ref, *pack(sums[...], total[...], 2, places_ref[0], places_ref[1]))
 
 
-def target_merge_kernel(own_ref, came_ref, student_ref, out_ref):
+def merge_kernel(own_ref, came_ref, student_own_ref, student_came_ref, out_ref):
     width = own_ref.shape[2]
     out_ref[:, :MOST] = (own_ref[:, :MOST].astype(F32) + came_ref[:, :MOST].astype(F32)).astype(BF16)
     total = numbers_of(own_ref, 2) + numbers_of(came_ref, 2)
     out_ref[:, MOST:SLOT] = join([part[:, None] for part in split(total, 2)], width)
-    out_ref[:, SLOT:] = student_ref[...]
+    own, came = numbers_of(student_own_ref, 3), numbers_of(student_came_ref, 3)
+    high = jnp.maximum(own, came)
+    joint = high + jnp.log(jnp.exp(own - high) + jnp.exp(came - high))
+    mean = student_own_ref[:, :MOST].astype(F32) * slots_of(jnp.exp(own - joint))
+    mean = mean + student_came_ref[:, :MOST].astype(F32) * slots_of(jnp.exp(came - joint))
+    out_ref[:, SLOT : SLOT + MOST] = mean.astype(BF16)
+    out_ref[:, SLOT + MOST :] = join([part[:, None] for part in split(joint, 3)], width)
 
 
 def student_kernel(
@@ -304,7 +310,7 @@
     @pl.when(step == 0)
     def _():
         starts, counts, core = places_ref[2], places_ref[3], index_ref[0, 0] % 2
-        found = compact(gathered_ref[...], starts, counts, rows, SLOT, EARLY, 0)
+        found = compact(gathered_ref[:, SLOT:], starts, counts, rows, 0, EARLY, 0)
         for ref, half in ((late_ref, core), (came_ref, 1 - core)):
             late = jnp.concatenate([ref[:, :LATE], ref[:, LATE : 2 * LATE]], axis=2)
             found += compact(late, starts, counts, rows, 0, LATE, EARLY + half * LATE)
@@ -334,17 +340,6 @@
     joint = merged(lse)
     weights = slots_of(jnp.exp(lse - joint[None]))
     return jnp.sum(chunk * weights, axis=0), joint
-
-
-def student_merge_kernel(own_ref, came_ref, out_ref):
-    width = own_ref.shape[2]
-    own, came = numbers_of(own_ref, 3), numbers_of(came_ref, 3)
-    high = jnp.maximum(own, came)
-    joint = high + jnp.log(jnp.exp(own - high) + jnp.exp(came - high))
-    mean = own_ref[:, :MOST].astype(F32) * slots_of(jnp.exp(own - joint))
-    mean = mean + came_ref[:, :MOST].astype(F32) * slots_of(jnp.exp(came - joint))
-    out_ref[:, :MOST] = mean.astype(BF16)
-    out_ref[:, MOST:] = join([part[:, None] for part in split(joint, 3)], width)
 
 
 def finish_kernel(back_ref, picked_ref, order_ref, count_ref, grad_ref, loss_ref):
@@ -381,16 +376,15 @@
     peer = pl.BlockSpec((groups, BLOCK // LANES, LANES), lambda k: (0, k, 0))
     square = pl.BlockSpec((rows, BLOCK), lambda k: (0, k))
     grid = (steps,)
-    student_patches, teacher_patches, mask_order, student_protos, teacher_protos = (
-        pltpu.with_memory_space_constraint(a, pltpu.HBM)
-        for a in (student_patches[0], teacher_patches[0], mask_order, student_protos, teacher_protos)
-    )
+    far = functools.partial(pltpu.with_memory_space_constraint, memory_space=pltpu.HBM)
+    student_patches, teacher_patches, mask_order = far(student_patches[0]), far(teacher_patches[0]), far(mask_order)
+    student_protos, teacher_protos = far(student_protos), far(teacher_protos)
     dot = 2 * rows * protos * bot
     column = pltpu.VMEM((rows, 1), F32)
 
     sent, late, picked = call(
         pick_kernel,
-        [((SLOT + EARLY, bot), BF16), ((2, 2 * LATE, LANES), BF16), ((SLOT, bot), BF16)],
+        [((SLOT + EARLY, bot), BF16), ((2, 2 * LATE, LANES), BF16), pltpu.HBM((SLOT, bot), BF16)],
         teacher_patches,
         student_patches,
         mask_order,
@@ -401,7 +395,7 @@
     gathered = lax.all_gather(sent, "proto", axis=0, tiled=False)
     share, teacher_rows, places = call(
         column_kernel,
-        [((groups, protos // LANES, LANES), F32), ((rows, bot), BF16), ((4, width, LANES), F32)],
+        [((groups, protos // LANES, LANES), F32), ((rows, bot), BF16), pltpu.HBM((4, width, LANES), F32)],
         gathered,
         index,
         teacher_protos,
@@ -428,8 +422,6 @@
     )
     swap = [(p, p ^ 1) for p in range(width)]
     shares = over(share.reshape((width,) + share.shape[2:]), "proto")
-    late = shares
-    late_came = lax.ppermute(late, "proto", swap)
     share, scale = call(
         first_column_kernel,
         [pltpu.HBM((groups, protos // LANES, LANES), BF16), pltpu.HBM((steps, rows, 1), F32)],
@@ -441,15 +433,17 @@
         out_specs=[peer, VMEM],
         moved=2 * rows * protos,
     )
+    late, share = lax.optimization_barrier((shares, share))
+    late_came = lax.ppermute(late, "proto", swap)
     packed = ((width // 2, SLOT, bot), BF16)
     student_own, student_other = call(
         student_kernel,
-        [packed, packed],
-        gathered,
-        late,
-        late_came,
+        [pltpu.HBM(*packed), pltpu.HBM(*packed)],
+        far(gathered),
+        far(late),
+        far(late_came),
         index,
-        places,
+        far(places),
         student_protos,
         grid=grid,
         in_specs=[VMEM, VMEM, VMEM, SMEM, VMEM, wide],
@@ -458,8 +452,7 @@
         moved=2 * bot * protos,
     )
     student_came = lax.ppermute(student_other, "proto", swap)
-    student_sum = call(student_merge_kernel, [packed], student_own, student_came)[0]
-    shares, student_sum = lax.optimization_barrier((over(share, "dp"), student_sum))
+    shares, student_came = lax.optimization_barrier((over(share, "dp"), student_came))
     share = call(
         later_row_kernel,
         [((width, depth, LANES), F32)],
@@ -491,7 +484,7 @@
         scale,
         matrix,
         student_protos,
-        places,
+        far(places),
         grid=grid,
         in_specs=[peer, VMEM, square, wide, VMEM],
         scratch=[pltpu.VMEM((rows, bot), F32), column],
@@ -499,7 +492,9 @@
         moved=2 * rows * protos,
     )
     came = lax.ppermute(other, "proto", swap)
-    sent = call(target_merge_kernel, [((width // 2, 2 * SLOT, bot), BF16)], own, came, student_sum)[0]
+    sent = call(
+        merge_kernel, [((width // 2, 2 * SLOT, bot), BF16)], own, came, student_own, student_came
+    )[0]
     same_core = [list(range(core, width, 2)) for core in range(2)]
     back = over(sent, "proto", axis_index_groups=same_core)
     student_grad, image_loss = call(

time: 175 us -> 173 us (0.989)
  local copies, waits for them, and re-layouts: 5.86 us -> 0.7 us
  Pallas kernels: 28.7 us -> 31.9 us
    unnamed x28 -> x12, local copies, waits for them, and re-layouts: 5.86 us -> 0.7 us
    pallas_call x11 -> x10, Pallas kernels: 28.7 us -> 31.9 us  [call(): pl.pallas_call(kernel, out_shape=out_shape, in_specs=[VMEM] * len(args) i...]
  transfers between devices with their start and end apart: 4 -> 4, of which waited for: 2 -> 2; matrix products, arithmetic and copies ran while one was open for 0% -> 0% of each run, Pallas kernels for 6% -> 5%
where the time goes in v8:
time: 173 us; the launch traced here: 172 us
  blocking collectives  122 us (71%)
  Pallas kernels  31.9 us (18%)
  starting transfers between devices  13.2 us (8%)
  waiting for transfers between devices  2.8 us (2%)
    all_to_all x2, blocking collectives, body(): shares = over(share, 'dp')  47.7 us
    pallas_call x10, Pallas kernels, call(): pl.pallas_call(kernel, out_shape=out_shape, in_specs=[VMEM] * len(args) i...  31.9 us
    all_gather x1, blocking collectives, body(): gathered = lax.all_gather(sent, 'proto', axis=0, tiled=False)  24.3 us
    all_to_all x1, blocking collectives, body(): back = over(sent, 'proto', axis_index_groups=same_core)  23.2 us
    all_to_all x1, blocking collectives, body(): shares = over(share.reshape((width,) + share.shape[2:]), 'proto')  16.4 us
    all_to_all x1, blocking collectives, body(): shares = over(share, 'proto')  10.7 us
    all_to_all x1, starting transfers between devices, body(): over(share, 'dp')  4.6 us
    ppermute x1, starting transfers between devices, body(): came = lax.ppermute(other, 'proto', swap)  4.06 us
  transfers between devices with their start and end apart: 4, of which 2 were waited for; matrix products, arithmetic and copies ran while one was open for 0% of the time, Pallas kernels for 5%

profile of v8, /device:TPU:1, one launch (start us, length us, event | category | flops | bytes accessed | tf_op | source)
XLA Modules:
  0.0 172.2 jit_solution(1102904513641673069)
XLA Ops:
  1.3 1.8 %shard_map.77 = (bf16[120,256]{1,0:T(8,128)(2,1)S(1)}, bf16[2,32,128]{2,1,0:T(8,128)(2,1)S(1)}, bf16[80,256]{1,0:T(8,128)(2,1)}) custom-call(bf16[256,256]{1,0:T(8,128)(2,1)} %bitcast.9, bf16[256,256]{1,0:T(8,128)(2,1)} %bitcast.10, s32[1,256]{1,0:T(1,128)} %order_ref.3, s32[1,1]{1,0:T(1,128)S(6)} %copy.8.count_ref), custom_call_target="tpu_custom_call" | custom-call | bytes 262144 | tf_op jit(solution)/shard_map/pallas_call | solution.py:29
  3.1 24.3 %all-gather = bf16[1920,256]{1,0:T(8,128)(2,1)S(1)} all-gather(bf16[120,256]{1,0:T(8,128)(2,1)S(1)} %get-tuple-element.25), channel_id=2, replica_groups=mesh['dp'=32,'proto'=16] {'proto'}, dimensions={0}, use_global_device_ids=true | all-gather | bytes 1044480 | tf_op jit(solution)/shard_map/all_gather | solution.py:395
  27.4 0.0 copy-start
  27.4 5.2 %shard_map.78 = (f32[32,32,128]{2,1,0:T(8,128)S(1)}, bf16[384,256]{1,0:T(8,128)(2,1)S(1)}, f32[4,16,128]{2,1,0:T(8,128)}) custom-call(bf16[16,120,256]{2,1,0:T(8,128)(2,1)S(1)} %bitcast.6, s32[1,1]{1,0:T(1,128)} %bitcast.3.index_ref, bf16[256,4096]{1,0:T(8,128)(2,1)} %protos_ref.5), custom_call_target="tpu_custom_call" | custom-call | flops 805306368 | bytes 2097152 | tf_op jit(solution)/shard_map/pallas_call | solution.py:29
  32.5 26.7 %all_to_all.30.shares_ref = f32[32,32,128]{2,1,0:T(8,128)S(1)} all-to-all(f32[32,32,128]{2,1,0:T(8,128)S(1)} %get-tuple-element.26), channel_id=1, replica_groups=mesh['dp'=32,'proto'=16] {'dp'}, dimensions={0} | all-to-all | bytes 1048576 | tf_op jit(solution)/shard_map/all_to_all | solution.py:408
  59.3 0.0 copy-done
  59.3 4.1 %shard_map.79 = (bf16[384,4096]{1,0:T(8,128)(2,1)S(1)}, f32[2,384,1]{2,1,0:T(8,128)S(1)}, bf16[8,2,48,128]{3,2,1,0:T(8,128)(2,1)S(1)}) custom-call(f32[32,32,128]{2,1,0:T(8,128)S(1)} %all_to_all.30.shares_ref, bf16[384,256]{1,0:T(8,128)(2,1)S(1)} %get-tuple-element.27.rows_ref, bf16[256,4096]{1,0:T(8,128)(2,1)} %protos_ref.5, ...), custom_call_target="tpu_custom_call" | custom-call | flops 805306368 | bytes 5242880 | tf_op jit(solution)/shard_map/pallas_call | solution.py:29
  63.4 16.4 %all_to_all.31.shares_ref.late_ref = bf16[16,48,128]{2,1,0:T(8,128)(2,1)S(1)} all-to-all(bf16[16,48,128]{2,1,0:T(8,128)(2,1)S(1)} %bitcast.8), channel_id=1, replica_groups=mesh['dp'=32,'proto'=16] {'proto'}, dimensions={0} | all-to-all | bytes 393216 | tf_op jit(solution)/shard_map/all_to_all | solution.py:424
  79.8 0.0 copy-start.2
  79.8 2.0 %shard_map.80 = (bf16[32,32,128]{2,1,0:T(8,128)(2,1)}, f32[2,384,1]{2,1,0:T(8,128)}) custom-call(bf16[16,48,128]{2,1,0:T(8,128)(2,1)S(1)} %all_to_all.31.shares_ref.late_ref, f32[2,384,1]{2,1,0:T(8,128)S(1)} %get-tuple-element.30.high_ref, bf16[384,4096]{1,0:T(8,128)(2,1)S(1)} %get-tuple-element.31.matrix_ref), custom_call_target="tpu_custom_call" | custom-call | bytes 3145728 | tf_op jit(solution)/shard_map/pallas_call | solution.py:29
  81.8 1.9 %collective-permute-start = (bf16[16,48,128]{2,1,0:T(8,128)(2,1)S(1)}, bf16[16,48,128]{2,1,0:T(8,128)(2,1)S(1)}, u32[]{:S(2)}, u32[]{:S(2)}) collective-permute-start(bf16[16,48,128]{2,1,0:T(8,128)(2,1)S(1)} %all_to_all.31.shares_ref.late_ref), channel_id=1, source_target_pairs={{0,1},{1,0},{2,3},{3,2},{4,5},{5,4},{6,7},{7,6},{8,9},{9,8},{10,11... | collective-permute-start | bytes 589832 | tf_op jit(solution)/shard_map/ppermute | solution.py:437
  83.7 0.0 copy-done.2
  83.7 4.6 %all-to-all-start.2 = ((bf16[32,32,128]{2,1,0:T(8,128)(2,1)}), bf16[32,32,128]{2,1,0:T(8,128)(2,1)}, u32[]{:S(2)}, u32[]{:S(2)}) async-start(bf16[32,32,128]{2,1,0:T(8,128)(2,1)} %get-tuple-element.33), calls=%async_computation.2 | async-start | bytes 524288 | tf_op jit(solution)/shard_map/all_to_all | solution.py:455
  88.3 0.0 collective-permute-done.came_ref
  88.4 0.0 copy-start.5
  88.4 0.7 copy-done.5
  89.0 0.0 copy-start.1
  89.1 8.7 %shard_map.81 = (bf16[8,80,256]{2,1,0:T(8,128)(2,1)}, bf16[8,80,256]{2,1,0:T(8,128)(2,1)}) custom-call(bf16[16,120,256]{2,1,0:T(8,128)(2,1)} %bitcast.7, bf16[16,48,128]{2,1,0:T(8,128)(2,1)} %copy-done.2, bf16[16,48,128]{2,1,0:T(8,128)(2,1)} %copy-done.5, s32[1,1]{1,0:T(1,128)} %bitcast.3.index_ref, f32[4,16,128]{2,1,0:T(8,128)} %get-tuple-element.35.places_ref, ...), custom_call_target="tpu_custom_call" | custom-call | flops 1610612736 | bytes 2097152 | tf_op jit(solution)/shard_map/pallas_call | solution.py:29
  97.8 2.6 %collective-permute-start.1 = (bf16[8,80,256]{2,1,0:T(8,128)(2,1)}, bf16[8,80,256]{2,1,0:T(8,128)(2,1)}, u32[]{:S(2)}, u32[]{:S(2)}) collective-permute-start(bf16[8,80,256]{2,1,0:T(8,128)(2,1)} %get-tuple-element.36), channel_id=1, source_target_pairs={{0,1},{1,0},{2,3},{3,2},{4,5},{5,4},{6,7},{7,6},{8,9},{9,8},{10,11... | collective-permute-start | bytes 983048 | tf_op jit(solution)/shard_map/ppermute | solution.py:454
  100.4 0.0 all-to-all-done.2.shares_ref
  100.4 1.6 collective-permute-done.1.student_came_ref
  102.0 0.0 copy-done.1
  102.0 1.9 %shard_map.82 = f32[16,8,128]{2,1,0:T(8,128)S(1)} custom-call(bf16[32,32,128]{2,1,0:T(8,128)(2,1)} %all-to-all-done.2.shares_ref, f32[2,384,1]{2,1,0:T(8,128)S(1)} %copy-done.1, bf16[384,4096]{1,0:T(8,128)(2,1)S(1)} %get-tuple-element.31.matrix_ref), custom_call_target="tpu_custom_call" | custom-call | bytes 3145728 | tf_op jit(solution)/shard_map/pallas_call | solution.py:29
  103.9 10.7 %all_to_all.32.shares_ref = f32[16,8,128]{2,1,0:T(8,128)S(1)} all-to-all(f32[16,8,128]{2,1,0:T(8,128)S(1)} %shard_map.82), channel_id=1, replica_groups=mesh['dp'=32,'proto'=16] {'proto'}, dimensions={0} | all-to-all | bytes 131072 | tf_op jit(solution)/shard_map/all_to_all | solution.py:467
  114.7 1.2 shard_map.83
  115.9 20.9 %all_to_all.33.shares_ref = bf16[32,32,128]{2,1,0:T(8,128)(2,1)S(1)} all-to-all(bf16[32,32,128]{2,1,0:T(8,128)(2,1)S(1)} %get-tuple-element.39), channel_id=1, replica_groups=mesh['dp'=32,'proto'=16] {'dp'}, dimensions={0} | all-to-all | bytes 524288 | tf_op jit(solution)/shard_map/all_to_all | solution.py:479
  136.8 0.0 copy-start.3
  136.8 3.8 %shard_map.84 = (bf16[8,80,256]{2,1,0:T(8,128)(2,1)S(1)}, bf16[8,80,256]{2,1,0:T(8,128)(2,1)S(1)}) custom-call(bf16[32,32,128]{2,1,0:T(8,128)(2,1)S(1)} %all_to_all.33.shares_ref, f32[2,384,1]{2,1,0:T(8,128)S(1)} %get-tuple-element.40.scale_ref, bf16[384,4096]{1,0:T(8,128)(2,1)S(1)} %get-tuple-element.31.matrix_ref, bf16[256,4096]{1,0:T(8,128)(2,1)} %protos_ref.7, ...), custom_call_target="tpu_custom_call" | custom-call | flops 805306368 | bytes 3145728 | tf_op jit(solution)/shard_map/pallas_call | solution.py:29
  140.6 0.0 copy-start.4
  140.6 4.1 %collective-permute-start.2 = (bf16[8,80,256]{2,1,0:T(8,128)(2,1)S(1)}, bf16[8,80,256]{2,1,0:T(8,128)(2,1)S(1)}, u32[]{:S(2)}, u32[]{:S(2)}) collective-permute-start(bf16[8,80,256]{2,1,0:T(8,128)(2,1)S(1)} %get-tuple-element.42), channel_id=1, source_target_pairs={{0,1},{1,0},{2,3},{3,2},{4,5},{5,4},{6,7},{7,6},{8,9},{9,8},{10,11... | collective-permute-start | bytes 983048 | tf_op jit(solution)/shard_map/ppermute | solution.py:494
  144.7 1.2 collective-permute-done.2.came_ref
  145.9 0.0 copy-done.3
  145.9 1.4 shard_map.85
  147.3 23.2 %all_to_all.34.back_ref = bf16[8,160,256]{2,1,0:T(8,128)(2,1)S(1)} all-to-all(bf16[8,160,256]{2,1,0:T(8,128)(2,1)S(1)} %shard_map.85), channel_id=1, replica_groups={{0,2,4,6,8,10,12,14},{1,3,5,7,9,11,13,15},{16,18,20,22,24,26,28,30},{17..., dimensions={0} | all-to-all | bytes 1310720 | tf_op jit(solution)/shard_map/all_to_all | solution.py:499
  170.5 0.0 copy-done.4
  170.5 1.7 shard_map.86
Async XLA Ops:
  27.4 31.9 %copy-start = (bf16[1920,256]{1,0:T(8,128)(2,1)}, bf16[1920,256]{1,0:T(8,128)(2,1)S(1)}, u32[]{:S(2)}) copy-start(bf16[1920,256]{1,0:T(8,128)(2,1)S(1)} %all-gather) | copy-start | bytes 2949124
  79.8 4.0 %copy-start.2 = (bf16[16,48,128]{2,1,0:T(8,128)(2,1)}, bf16[16,48,128]{2,1,0:T(8,128)(2,1)S(1)}, u32[]{:S(2)}) copy-start(bf16[16,48,128]{2,1,0:T(8,128)(2,1)S(1)} %all_to_all.31.shares_ref.late_ref) | copy-start | bytes 589828
  81.8 6.5 %collective-permute-start = (bf16[16,48,128]{2,1,0:T(8,128)(2,1)S(1)}, bf16[16,48,128]{2,1,0:T(8,128)(2,1)S(1)}, u32[]{:S(2)}, u32[]{:S(2)}) collective-permute-start(bf16[16,48,128]{2,1,0:T(8,128)(2,1)S(1)} %all_to_all.31.shares_ref.late_ref), channel_id=1, source_target_pairs={{0,1},{1,0},{2,3},{3,2},{4,5},{5,4},{6,7},{7,6},{8,9},{9,8},{10,11... | collective-permute-start | bytes 589832 | tf_op jit(solution)/shard_map/ppermute | solution.py:437
  83.7 16.7 %all-to-all-start.2 = ((bf16[32,32,128]{2,1,0:T(8,128)(2,1)}), bf16[32,32,128]{2,1,0:T(8,128)(2,1)}, u32[]{:S(2)}, u32[]{:S(2)}) async-start(bf16[32,32,128]{2,1,0:T(8,128)(2,1)} %get-tuple-element.33), calls=%async_computation.2 | async-start | bytes 524288 | tf_op jit(solution)/shard_map/all_to_all | solution.py:455
  88.4 0.7 copy-start.5
  89.0 12.9 %copy-start.1 = (f32[2,384,1]{2,1,0:T(8,128)S(1)}, f32[2,384,1]{2,1,0:T(8,128)}, u32[]{:S(2)}) copy-start(f32[2,384,1]{2,1,0:T(8,128)} %get-tuple-element.38.scale_ref.scale_in_ref) | copy-start | bytes 9220
  97.8 4.2 %collective-permute-start.1 = (bf16[8,80,256]{2,1,0:T(8,128)(2,1)}, bf16[8,80,256]{2,1,0:T(8,128)(2,1)}, u32[]{:S(2)}, u32[]{:S(2)}) collective-permute-start(bf16[8,80,256]{2,1,0:T(8,128)(2,1)} %get-tuple-element.36), channel_id=1, source_target_pairs={{0,1},{1,0},{2,3},{3,2},{4,5},{5,4},{6,7},{7,6},{8,9},{9,8},{10,11... | collective-permute-start | bytes 983048 | tf_op jit(solution)/shard_map/ppermute | solution.py:454
  136.8 9.1 %copy-start.3 = (bf16[8,80,256]{2,1,0:T(8,128)(2,1)S(1)}, bf16[8,80,256]{2,1,0:T(8,128)(2,1)}, u32[]{:S(2)}) copy-start(bf16[8,80,256]{2,1,0:T(8,128)(2,1)} %get-tuple-element.43.student_own_ref) | copy-start | bytes 983044
  140.6 29.9 %copy-start.4 = (bf16[80,256]{1,0:T(8,128)(2,1)S(1)}, bf16[80,256]{1,0:T(8,128)(2,1)}, u32[]{:S(2)}) copy-start(bf16[80,256]{1,0:T(8,128)(2,1)} %get-tuple-element.45.picked_ref) | copy-start | bytes 122884
  140.6 5.3 %collective-permute-start.2 = (bf16[8,80,256]{2,1,0:T(8,128)(2,1)S(1)}, bf16[8,80,256]{2,1,0:T(8,128)(2,1)S(1)}, u32[]{:S(2)}, u32[]{:S(2)}) collective-permute-start(bf16[8,80,256]{2,1,0:T(8,128)(2,1)S(1)} %get-tuple-element.42), channel_id=1, source_target_pairs={{0,1},{1,0},{2,3},{3,2},{4,5},{5,4},{6,7},{7,6},{8,9},{9,8},{10,11... | collective-permute-start | bytes 983048 | tf_op jit(solution)/shard_map/ppermute | solution.py:494

commit v9 on v8

--- a/solution.py
+++ b/solution.py
@@ -422,9 +422,10 @@
     )
     swap = [(p, p ^ 1) for p in range(width)]
     shares = over(share.reshape((width,) + share.shape[2:]), "proto")
+    late = shares
     share, scale = call(
         first_column_kernel,
-        [pltpu.HBM((groups, protos // LANES, LANES), BF16), pltpu.HBM((steps, rows, 1), F32)],
+        [((groups, protos // LANES, LANES), BF16), ((steps, rows, 1), F32)],
         shares,
         high,
         matrix,
@@ -433,7 +434,30 @@
         out_specs=[peer, VMEM],
         moved=2 * rows * protos,
     )
-    late, share = lax.optimization_barrier((shares, share))
+    shares = over(share, "dp")
+    share = call(
+        later_row_kernel,
+        [((width, depth, LANES), F32)],
+        shares,
+        scale,
+        matrix,
+        grid=grid,
+        in_specs=[peer, VMEM, square],
+        scratch=[column],
+        moved=2 * rows * protos,
+    )[0]
+    shares = over(share, "proto")
+    share, scale = call(
+        later_column_kernel,
+        [pltpu.HBM((groups, protos // LANES, LANES), BF16), pltpu.HBM((steps, rows, 1), F32)],
+        shares,
+        scale,
+        matrix,
+        grid=grid,
+        in_specs=[VMEM, VMEM, square],
+        out_specs=[peer, VMEM],
+        moved=2 * rows * protos,
+    )
     late_came = lax.ppermute(late, "proto", swap)
     packed = ((width // 2, SLOT, bot), BF16)
     student_own, student_other = call(
@@ -452,30 +476,6 @@
         moved=2 * bot * protos,
     )
     student_came = lax.ppermute(student_other, "proto", swap)
-    shares, student_came = lax.optimization_barrier((over(share, "dp"), student_came))
-    share = call(
-        later_row_kernel,
-        [((width, depth, LANES), F32)],
-        shares,
-        scale,
-        matrix,
-        grid=grid,
-        in_specs=[peer, VMEM, square],
-        scratch=[column],
-        moved=2 * rows * protos,
-    )[0]
-    shares = over(share, "proto")
-    share, scale = call(
-        later_column_kernel,
-        [((groups, protos // LANES, LANES), BF16), ((steps, rows, 1), F32)],
-        shares,
-        scale,
-        matrix,
-        grid=grid,
-        in_specs=[VMEM, VMEM, square],
-        out_specs=[peer, VMEM],
-        moved=2 * rows * protos,
-    )
     shares = over(share, "dp")
     own, other = call(
         target_kernel,

time: 173 us -> 167 us (0.965)
  blocking collectives: 122 us -> 119 us
  starting transfers between devices: 13.2 us -> 10.4 us
    all_to_all x2, blocking collectives: 47.7 us -> 43.2 us  [body(): shares = over(share, 'dp')]
    ppermute x1, starting transfers between devices: 4.06 us -> 2.25 us  [body(): came = lax.ppermute(other, 'proto', swap)]
  transfers between devices with their start and end apart: 4 -> 4, of which waited for: 2 -> 2; matrix products, arithmetic and copies ran while one was open for 0% -> 0% of each run, Pallas kernels for 5% -> 8%
where the time goes in v9:
time: 167 us; the launch traced here: 166 us
  blocking collectives  119 us (71%)
  Pallas kernels  31.2 us (19%)
  starting transfers between devices  10.4 us (6%)
  waiting for transfers between devices  2.72 us (2%)
  local copies, waits for them, and re-layouts  1.68 us (1%)
    all_to_all x2, blocking collectives, body(): shares = over(share, 'dp')  43.2 us
    pallas_call x10, Pallas kernels, call(): pl.pallas_call(kernel, out_shape=out_shape, in_specs=[VMEM] * len(args) i...  31.2 us
    all_gather x1, blocking collectives, body(): gathered = lax.all_gather(sent, 'proto', axis=0, tiled=False)  24.3 us
    all_to_all x1, blocking collectives, body(): back = over(sent, 'proto', axis_index_groups=same_core)  23.2 us
    all_to_all x1, blocking collectives, body(): shares = over(share.reshape((width,) + share.shape[2:]), 'proto')  16.4 us
    all_to_all x1, blocking collectives, body(): shares = over(share, 'proto')  11.8 us
    all_to_all x1, starting transfers between devices, body(): shares = over(share, 'dp')  3.87 us
  transfers between devices with their start and end apart: 4, of which 2 were waited for; matrix products, arithmetic and copies ran while one was open for 0% of the time, Pallas kernels for 8%

profile of v9, /device:TPU:1, one launch (start us, length us, event | category | flops | bytes accessed | tf_op | source)
XLA Modules:
  0.0 166.3 jit_solution(16630977272377839290)
XLA Ops:
  1.3 1.8 %shard_map.77 = (bf16[120,256]{1,0:T(8,128)(2,1)S(1)}, bf16[2,32,128]{2,1,0:T(8,128)(2,1)S(1)}, bf16[80,256]{1,0:T(8,128)(2,1)}) custom-call(bf16[256,256]{1,0:T(8,128)(2,1)} %bitcast.9, bf16[256,256]{1,0:T(8,128)(2,1)} %bitcast.10, s32[1,256]{1,0:T(1,128)} %order_ref.3, s32[1,1]{1,0:T(1,128)S(6)} %copy.8.count_ref), custom_call_target="tpu_custom_call" | custom-call | bytes 262144 | tf_op jit(solution)/shard_map/pallas_call | solution.py:29
  3.1 24.3 %all-gather = bf16[1920,256]{1,0:T(8,128)(2,1)S(1)} all-gather(bf16[120,256]{1,0:T(8,128)(2,1)S(1)} %get-tuple-element.21), channel_id=2, replica_groups=mesh['dp'=32,'proto'=16] {'proto'}, dimensions={0}, use_global_device_ids=true | all-gather | bytes 1044480 | tf_op jit(solution)/shard_map/all_gather | solution.py:395
  27.4 0.0 copy-start
  27.4 5.2 %shard_map.78 = (f32[32,32,128]{2,1,0:T(8,128)S(1)}, bf16[384,256]{1,0:T(8,128)(2,1)S(1)}, f32[4,16,128]{2,1,0:T(8,128)}) custom-call(bf16[16,120,256]{2,1,0:T(8,128)(2,1)S(1)} %bitcast.6, s32[1,1]{1,0:T(1,128)} %bitcast.3.index_ref, bf16[256,4096]{1,0:T(8,128)(2,1)} %protos_ref.5), custom_call_target="tpu_custom_call" | custom-call | flops 805306368 | bytes 2097152 | tf_op jit(solution)/shard_map/pallas_call | solution.py:29
  32.5 26.7 %all_to_all.30.shares_ref = f32[32,32,128]{2,1,0:T(8,128)S(1)} all-to-all(f32[32,32,128]{2,1,0:T(8,128)S(1)} %get-tuple-element.22), channel_id=1, replica_groups=mesh['dp'=32,'proto'=16] {'dp'}, dimensions={0} | all-to-all | bytes 1048576 | tf_op jit(solution)/shard_map/all_to_all | solution.py:408
  59.3 0.0 copy-done
  59.3 4.1 %shard_map.79 = (bf16[384,4096]{1,0:T(8,128)(2,1)S(1)}, f32[2,384,1]{2,1,0:T(8,128)S(1)}, bf16[8,2,48,128]{3,2,1,0:T(8,128)(2,1)S(1)}) custom-call(f32[32,32,128]{2,1,0:T(8,128)S(1)} %all_to_all.30.shares_ref, bf16[384,256]{1,0:T(8,128)(2,1)S(1)} %get-tuple-element.23.rows_ref, bf16[256,4096]{1,0:T(8,128)(2,1)} %protos_ref.5, ...), custom_call_target="tpu_custom_call" | custom-call | flops 805306368 | bytes 5242880 | tf_op jit(solution)/shard_map/pallas_call | solution.py:29
  63.4 16.4 %all_to_all.31.shares_ref.late_ref = bf16[16,48,128]{2,1,0:T(8,128)(2,1)S(1)} all-to-all(bf16[16,48,128]{2,1,0:T(8,128)(2,1)S(1)} %bitcast.8), channel_id=1, replica_groups=mesh['dp'=32,'proto'=16] {'proto'}, dimensions={0} | all-to-all | bytes 393216 | tf_op jit(solution)/shard_map/all_to_all | solution.py:424
  79.8 0.0 copy-start.1
  79.8 1.3 shard_map.80
  81.0 16.5 %all_to_all.32.shares_ref = bf16[32,32,128]{2,1,0:T(8,128)(2,1)S(1)} all-to-all(bf16[32,32,128]{2,1,0:T(8,128)(2,1)S(1)} %get-tuple-element.28), channel_id=1, replica_groups=mesh['dp'=32,'proto'=16] {'dp'}, dimensions={0} | all-to-all | bytes 524288 | tf_op jit(solution)/shard_map/all_to_all | solution.py:437
  97.5 0.0 copy-done.1
  97.5 1.3 shard_map.81
  98.8 11.8 %all_to_all.33.shares_ref = f32[16,8,128]{2,1,0:T(8,128)S(1)} all-to-all(f32[16,8,128]{2,1,0:T(8,128)S(1)} %shard_map.81), channel_id=1, replica_groups=mesh['dp'=32,'proto'=16] {'proto'}, dimensions={0} | all-to-all | bytes 131072 | tf_op jit(solution)/shard_map/all_to_all | solution.py:449
  110.6 2.0 %shard_map.82 = (bf16[32,32,128]{2,1,0:T(8,128)(2,1)}, f32[2,384,1]{2,1,0:T(8,128)}) custom-call(f32[16,8,128]{2,1,0:T(8,128)S(1)} %all_to_all.33.shares_ref, f32[2,384,1]{2,1,0:T(8,128)S(1)} %get-tuple-element.29.scale_ref.scale_in_ref, bf16[384,4096]{1,0:T(8,128)(2,1)S(1)} %get-tuple-element.27.matrix_ref), custom_call_target="tpu_custom_call" | custom-call | bytes 3145728 | tf_op jit(solution)/shard_map/pallas_call | solution.py:29
  112.6 3.9 %all-to-all-start.4 = ((bf16[32,32,128]{2,1,0:T(8,128)(2,1)}), bf16[32,32,128]{2,1,0:T(8,128)(2,1)S(1)}, u32[]{:S(2)}, u32[]{:S(2)}) async-start(bf16[32,32,128]{2,1,0:T(8,128)(2,1)} %get-tuple-element.30), calls=%async_computation.4 | async-start | bytes 524288 | tf_op jit(solution)/shard_map/all_to_all | solution.py:479
  116.5 2.1 %collective-permute-start.1 = (bf16[16,48,128]{2,1,0:T(8,128)(2,1)}, bf16[16,48,128]{2,1,0:T(8,128)(2,1)S(1)}, u32[]{:S(2)}, u32[]{:S(2)}) collective-permute-start(bf16[16,48,128]{2,1,0:T(8,128)(2,1)} %copy-done.1), channel_id=1, source_target_pairs={{0,1},{1,0},{2,3},{3,2},{4,5},{5,4},{6,7},{7,6},{8,9},{9,8},{10,11... | collective-permute-start | bytes 589832 | tf_op jit(solution)/shard_map/ppermute | solution.py:461
  118.6 1.5 collective-permute-done.1.came_ref
  120.0 0.0 copy-start.5
  120.1 0.7 copy-done.5
  120.7 8.7 %shard_map.84 = (bf16[8,80,256]{2,1,0:T(8,128)(2,1)}, bf16[8,80,256]{2,1,0:T(8,128)(2,1)}) custom-call(bf16[16,120,256]{2,1,0:T(8,128)(2,1)} %bitcast.7, bf16[16,48,128]{2,1,0:T(8,128)(2,1)} %copy-done.1, bf16[16,48,128]{2,1,0:T(8,128)(2,1)} %copy-done.5, s32[1,1]{1,0:T(1,128)} %bitcast.3.index_ref, f32[4,16,128]{2,1,0:T(8,128)} %get-tuple-element.32.places_ref, ...), custom_call_target="tpu_custom_call" | custom-call | flops 1610612736 | bytes 2097152 | tf_op jit(solution)/shard_map/pallas_call | solution.py:29
  129.4 2.2 %collective-permute-start.2 = (bf16[8,80,256]{2,1,0:T(8,128)(2,1)}, bf16[8,80,256]{2,1,0:T(8,128)(2,1)}, u32[]{:S(2)}, u32[]{:S(2)}) collective-permute-start(bf16[8,80,256]{2,1,0:T(8,128)(2,1)} %get-tuple-element.36), channel_id=1, source_target_pairs={{0,1},{1,0},{2,3},{3,2},{4,5},{5,4},{6,7},{7,6},{8,9},{9,8},{10,11... | collective-permute-start | bytes 983048 | tf_op jit(solution)/shard_map/ppermute | solution.py:478
  131.7 0.0 all-to-all-done.4.shares_ref
  131.7 0.0 copy-start.2
  131.7 1.0 copy-done.2
  132.7 0.0 copy-start.3
  132.7 3.8 %shard_map.83 = (bf16[8,80,256]{2,1,0:T(8,128)(2,1)S(1)}, bf16[8,80,256]{2,1,0:T(8,128)(2,1)S(1)}) custom-call(bf16[32,32,128]{2,1,0:T(8,128)(2,1)S(1)} %all-to-all-done.4.shares_ref, f32[2,384,1]{2,1,0:T(8,128)S(1)} %copy-done.2, bf16[384,4096]{1,0:T(8,128)(2,1)S(1)} %get-tuple-element.27.matrix_ref, bf16[256,4096]{1,0:T(8,128)(2,1)} %protos_ref.7, ...), custom_call_target="tpu_custom_call" | custom-call | flops 805306368 | bytes 3145728 | tf_op jit(solution)/shard_map/pallas_call | solution.py:29
  136.5 0.0 copy-start.4
  136.5 2.2 %collective-permute-start = (bf16[8,80,256]{2,1,0:T(8,128)(2,1)S(1)}, bf16[8,80,256]{2,1,0:T(8,128)(2,1)S(1)}, u32[]{:S(2)}, u32[]{:S(2)}) collective-permute-start(bf16[8,80,256]{2,1,0:T(8,128)(2,1)S(1)} %get-tuple-element.34), channel_id=1, source_target_pairs={{0,1},{1,0},{2,3},{3,2},{4,5},{5,4},{6,7},{7,6},{8,9},{9,8},{10,11... | collective-permute-start | bytes 983048 | tf_op jit(solution)/shard_map/ppermute | solution.py:494
  138.8 0.0 collective-permute-done.2.student_came_ref
  138.8 1.3 collective-permute-done.came_ref
  140.0 0.0 copy-done.3
  140.0 1.4 shard_map.85
  141.4 23.2 %all_to_all.34.back_ref = bf16[8,160,256]{2,1,0:T(8,128)(2,1)S(1)} all-to-all(bf16[8,160,256]{2,1,0:T(8,128)(2,1)S(1)} %shard_map.85), channel_id=1, replica_groups={{0,2,4,6,8,10,12,14},{1,3,5,7,9,11,13,15},{16,18,20,22,24,26,28,30},{17..., dimensions={0} | all-to-all | bytes 1310720 | tf_op jit(solution)/shard_map/all_to_all | solution.py:499
  164.6 0.0 copy-done.4
  164.6 1.7 %shard_map.86 = (bf16[256,256]{1,0:T(8,128)(2,1)}, f32[1,1]{1,0:T(1,128)}) custom-call(bf16[8,160,256]{2,1,0:T(8,128)(2,1)S(1)} %all_to_all.34.back_ref, bf16[80,256]{1,0:T(8,128)(2,1)S(1)} %copy-done.4, s32[1,256]{1,0:T(1,128)} %order_ref.3, s32[1,1]{1,0:T(1,128)S(6)} %copy.8.count_ref), custom_call_target="tpu_custom_call" | custom-call | bytes 131072 | tf_op jit(solution)/shard_map/pallas_call | solution.py:29
Async XLA Ops:
  27.4 31.9 %copy-start = (bf16[1920,256]{1,0:T(8,128)(2,1)}, bf16[1920,256]{1,0:T(8,128)(2,1)S(1)}, u32[]{:S(2)}) copy-start(bf16[1920,256]{1,0:T(8,128)(2,1)S(1)} %all-gather) | copy-start | bytes 2949124
  79.8 17.8 %copy-start.1 = (bf16[16,48,128]{2,1,0:T(8,128)(2,1)}, bf16[16,48,128]{2,1,0:T(8,128)(2,1)S(1)}, u32[]{:S(2)}) copy-start(bf16[16,48,128]{2,1,0:T(8,128)(2,1)S(1)} %all_to_all.31.shares_ref.late_ref) | copy-start | bytes 589828
  112.6 19.0 %all-to-all-start.4 = ((bf16[32,32,128]{2,1,0:T(8,128)(2,1)}), bf16[32,32,128]{2,1,0:T(8,128)(2,1)S(1)}, u32[]{:S(2)}, u32[]{:S(2)}) async-start(bf16[32,32,128]{2,1,0:T(8,128)(2,1)} %get-tuple-element.30), calls=%async_computation.4 | async-start | bytes 524288 | tf_op jit(solution)/shard_map/all_to_all | solution.py:479
  116.5 3.5 %collective-permute-start.1 = (bf16[16,48,128]{2,1,0:T(8,128)(2,1)}, bf16[16,48,128]{2,1,0:T(8,128)(2,1)S(1)}, u32[]{:S(2)}, u32[]{:S(2)}) collective-permute-start(bf16[16,48,128]{2,1,0:T(8,128)(2,1)} %copy-done.1), channel_id=1, source_target_pairs={{0,1},{1,0},{2,3},{3,2},{4,5},{5,4},{6,7},{7,6},{8,9},{9,8},{10,11... | collective-permute-start | bytes 589832 | tf_op jit(solution)/shard_map/ppermute | solution.py:461
  120.0 0.7 copy-start.5
  129.4 9.3 %collective-permute-start.2 = (bf16[8,80,256]{2,1,0:T(8,128)(2,1)}, bf16[8,80,256]{2,1,0:T(8,128)(2,1)}, u32[]{:S(2)}, u32[]{:S(2)}) collective-permute-start(bf16[8,80,256]{2,1,0:T(8,128)(2,1)} %get-tuple-element.36), channel_id=1, source_target_pairs={{0,1},{1,0},{2,3},{3,2},{4,5},{5,4},{6,7},{7,6},{8,9},{9,8},{10,11... | collective-permute-start | bytes 983048 | tf_op jit(solution)/shard_map/ppermute | solution.py:478
  131.7 1.0 copy-start.2
  132.7 7.3 %copy-start.3 = (bf16[8,80,256]{2,1,0:T(8,128)(2,1)S(1)}, bf16[8,80,256]{2,1,0:T(8,128)(2,1)}, u32[]{:S(2)}) copy-start(bf16[8,80,256]{2,1,0:T(8,128)(2,1)} %get-tuple-element.35.student_own_ref) | copy-start | bytes 983044
  136.5 28.1 %copy-start.4 = (bf16[80,256]{1,0:T(8,128)(2,1)S(1)}, bf16[80,256]{1,0:T(8,128)(2,1)}, u32[]{:S(2)}) copy-start(bf16[80,256]{1,0:T(8,128)(2,1)} %get-tuple-element.37.picked_ref) | copy-start | bytes 122884
  136.5 3.5 %collective-permute-start = (bf16[8,80,256]{2,1,0:T(8,128)(2,1)S(1)}, bf16[8,80,256]{2,1,0:T(8,128)(2,1)S(1)}, u32[]{:S(2)}, u32[]{:S(2)}) collective-permute-start(bf16[8,80,256]{2,1,0:T(8,128)(2,1)S(1)} %get-tuple-element.34), channel_id=1, source_target_pairs={{0,1},{1,0},{2,3},{3,2},{4,5},{5,4},{6,7},{7,6},{8,9},{9,8},{10,11... | collective-permute-start | bytes 983048 | tf_op jit(solution)/shard_map/ppermute | solution.py:494

commit v10 on v9

v10 whole, which is shorter than its diff:
```python
import functools

import jax
import jax.numpy as jnp
from jax import lax
from jax.experimental import pallas as pl
from jax.experimental.pallas import tpu as pltpu
from jax.sharding import PartitionSpec as P

MASK_DEV = 24
MOST = 72
EARLY = 40
LATE = (MOST - EARLY) // 2
SLOT = 80
TEACH = 1.0 / 0.07
STUD = 1.0 / 0.1
F32 = jnp.float32
BF16 = jnp.bfloat16
LANES = 128
BLOCK = 2048
PIECE = 1024
LIMIT = 24 << 20
VMEM = pl.BlockSpec(memory_space=pltpu.VMEM)
SMEM = pl.BlockSpec(memory_space=pltpu.SMEM)


HBM = pl.BlockSpec(memory_space=pl.ANY)


def call(kernel, out_shape, *args, in_specs=None, scratch=(), flops=0, moved=0):
    out_shape = [jax.ShapeDtypeStruct(*o) if isinstance(o, tuple) else o for o in out_shape]
    return pl.pallas_call(
        kernel,
        out_shape=out_shape,
        in_specs=[VMEM] * len(args) if in_specs is None else in_specs,
        out_specs=[VMEM] * len(out_shape),
        scratch_shapes=list(scratch),
        compiler_params=pltpu.CompilerParams(vmem_limit_bytes=LIMIT),
        cost_estimate=pl.CostEstimate(flops=flops, bytes_accessed=moved, transcendentals=0),
    )(*args)


def fetch(far_ref, near_ref, sems):
    copies = []
    for k in range(near_ref.shape[1] // PIECE):
        piece = slice(k * PIECE, (k + 1) * PIECE)
        copies.append(pltpu.make_async_copy(far_ref.at[:, piece], near_ref.at[:, piece], sems.at[k]))
        copies[-1].start()

    def block(b):
        for copy in copies[b * BLOCK // PIECE : (b + 1) * BLOCK // PIECE]:
            copy.wait()
        return near_ref[:, b * BLOCK : (b + 1) * BLOCK]

    return block, range(near_ref.shape[1] // BLOCK)


def columns(b):
    return slice(b * BLOCK, (b + 1) * BLOCK)


def lines_of(b):
    return slice(b * BLOCK // LANES, (b + 1) * BLOCK // LANES)


def iota(shape, dim):
    return lax.broadcasted_iota(jnp.int32, shape, dim)


def eye():
    return iota((LANES, LANES), 0) == iota((LANES, LANES), 1)


def to_lanes(column):
    parts = []
    for b in range(column.shape[0] // LANES):
        part = jnp.broadcast_to(column[b * LANES : (b + 1) * LANES], (LANES, LANES))
        parts.append(jnp.sum(jnp.where(eye(), part, 0.0), axis=0, keepdims=True))
    return jnp.concatenate(parts, axis=0)


def to_column(lanes):
    parts = []
    for b in range(lanes.shape[0]):
        part = jnp.broadcast_to(lanes[b : b + 1], (LANES, LANES))
        parts.append(jnp.sum(jnp.where(eye(), part, 0.0), axis=1, keepdims=True))
    return jnp.concatenate(parts, axis=0)


def to_lines(row):
    return jnp.concatenate([row[:, b * LANES : (b + 1) * LANES] for b in range(row.shape[1] // LANES)], axis=0)


def to_row(lines):
    return jnp.concatenate([lines[b : b + 1] for b in range(lines.shape[0])], axis=1)


def merged(shares):
    top = jnp.max(shares, axis=0)
    return top + jnp.log(jnp.sum(jnp.exp(shares - top[None]), axis=0))


def pick_kernel(teacher_ref, student_ref, order_ref, count_ref, sent_ref, late_ref, picked_ref):
    patches, width = teacher_ref.shape
    order = jnp.broadcast_to(order_ref[:, :LANES], (patches, LANES))
    chosen = (iota((patches, LANES), 0) == order).astype(BF16)
    dims = (((0,), (0,)), ((), ()))
    teacher = lax.dot_general(chosen, teacher_ref[...], dims, preferred_element_type=F32)
    student = lax.dot_general(chosen, student_ref[...], dims, preferred_element_type=F32)
    count = jnp.full((SLOT - MOST, width), count_ref[0, 0], jnp.int32).astype(F32)
    sent_ref[...] = jnp.concatenate([teacher[:MOST], count, student[:EARLY]], axis=0).astype(BF16)
    for half in range(2):
        late = student[EARLY + half * LATE : EARLY + (half + 1) * LATE]
        late_ref[half] = jnp.concatenate([late[:, :LANES], late[:, LANES:]], axis=0).astype(BF16)
    picked_ref[...] = student[:SLOT].astype(BF16)


def compact(gathered, starts, counts, rows, first, length, shift):
    images, slots, width = gathered.shape
    total = images * slots
    lane, image = iota((images, total), 1), iota((images, total), 0)
    within = lane - image * slots - first
    member = jnp.logical_and(within >= 0, within < length)
    place = (within + shift).astype(F32)
    used = jnp.logical_and(member, place < counts[:, :1])
    row = jnp.sum(jnp.where(used, starts[:, :1] + place + 1.0, 0.0), axis=0, keepdims=True) - 1.0
    chosen = (iota((rows, total), 0).astype(F32) == row).astype(BF16)
    return jnp.dot(chosen, gathered.reshape(total, width), preferred_element_type=F32)


def spread(starts, counts, slots, rows):
    images = starts.shape[0]
    shape = (images, slots, rows)
    within = iota(shape, 1)
    row = (iota(shape, 2) - within).astype(F32) - starts[:, :1].reshape(images, 1, 1)
    used = jnp.logical_and(row == 0.0, within.astype(F32) < counts[:, :1].reshape(images, 1, 1))
    return used.astype(F32).astype(BF16).reshape(images * slots, rows)


def column_kernel(gathered_ref, index_ref, far_ref, share_ref, rows_ref, places_ref, near_ref, sems):
    block, blocks = fetch(far_ref, near_ref, sems)
    images = gathered_ref.shape[0]
    counts = gathered_ref[:, MOST:SLOT, :LANES].astype(F32)[:, 0]
    before = (iota((images, images), 1) < iota((images, images), 0)).astype(BF16)
    starts = jnp.dot(before, counts.astype(BF16), preferred_element_type=F32)
    half, core = images // 2, index_ref[0, 0] % 2
    place = iota((images, images), 0)
    image = jnp.where(place < half, 2 * place + core, 2 * (place - half) + 1 - core)
    other = iota((images, images), 1)
    places_ref[0] = jnp.dot((other < image).astype(BF16), counts.astype(BF16), preferred_element_type=F32)
    places_ref[1] = jnp.dot((other == image).astype(BF16), counts.astype(BF16), preferred_element_type=F32)
    places_ref[2] = starts
    places_ref[3] = counts
    rows = compact(gathered_ref[:, :SLOT], starts, counts, rows_ref.shape[0], 0, MOST, 0).astype(BF16)
    rows_ref[...] = rows
    for b in blocks:
        logits = jnp.dot(rows, block(b), preferred_element_type=F32) * TEACH
        high = jnp.max(logits, axis=0, keepdims=True)
        total = jnp.sum(jnp.exp(logits - high), axis=0, keepdims=True)
        lines = to_lines(high + jnp.log(total))
        share_ref[:, lines_of(b)] = jnp.broadcast_to(lines[None], (share_ref.shape[0],) + lines.shape)


def split(values, parts):
    out = []
    for _ in range(parts):
        part = values.astype(BF16)
        out.append(part)
        values = values - part.astype(F32)
    return out


def fill_share(share_ref, lines):
    blank = jnp.zeros((share_ref.shape[1] - lines.shape[0], LANES), F32)
    share_ref[...] = jnp.broadcast_to(jnp.concatenate([lines, blank], axis=0)[None], share_ref.shape)


def row_kernel(shares_ref, rows_ref, protos_ref, late_ref, matrix_ref, high_ref, share_ref):
    column = merged(shares_ref[...])
    rows = rows_ref[...]
    highs, sums = [], []
    for b in range(high_ref.shape[0]):
        logits = jnp.dot(rows, protos_ref[:, columns(b)], preferred_element_type=F32) * TEACH
        shifted = logits - to_row(column[lines_of(b)])
        high = jnp.max(shifted, axis=1, keepdims=True)
        exact = jnp.exp(shifted - high)
        matrix_ref[:, columns(b)] = exact.astype(BF16)
        high_ref[b] = high
        highs.append(high)
        sums.append(jnp.sum(exact, axis=1, keepdims=True))
    top = functools.reduce(jnp.maximum, highs)
    total = sum(jnp.exp(high - top) * part for high, part in zip(highs, sums))
    own = jnp.concatenate([part.astype(F32) for part in split(to_lanes(top + jnp.log(total)), 3)], axis=0)
    blank = jnp.zeros((share_ref.shape[2] - 2 * LATE - own.shape[0], LANES), F32)
    numbers = jnp.concatenate([own, blank], axis=0).astype(BF16)
    for half in range(2):
        chunk = jnp.concatenate([late_ref[half], numbers], axis=0)
        share_ref[:, half] = jnp.broadcast_to(chunk[None], (share_ref.shape[0],) + chunk.shape)


def column_sums(matrix_ref, scale, share_ref):
    for b in range(scale.shape[0]):
        sums = jnp.sum(matrix_ref[:, columns(b)].astype(F32) * scale[b], axis=0, keepdims=True)
        lines = to_lines(sums)
        shape = (share_ref.shape[0],) + lines.shape
        share_ref[:, lines_of(b)] = jnp.broadcast_to(lines[None], shape).astype(share_ref.dtype)


def first_column_kernel(shares_ref, high_ref, matrix_ref, share_ref, scale_ref):
    lines = scale_ref.shape[1] // LANES
    numbers = shares_ref[:, 2 * LATE :].astype(F32)
    row_lse = merged(sum(numbers[:, k * lines : (k + 1) * lines] for k in range(3)))
    scale = jnp.exp(high_ref[...] - to_column(row_lse)[None])
    scale_ref[...] = scale
    column_sums(matrix_ref, scale, share_ref)


def later_column_kernel(shares_ref, scale_in_ref, matrix_ref, share_ref, scale_ref):
    lines = scale_ref.shape[1] // LANES
    total = to_column(jnp.sum(shares_ref[...][:, :lines], axis=0))
    scale = scale_in_ref[...] / total[None]
    scale_ref[...] = scale
    column_sums(matrix_ref, scale, share_ref)


def inverse_of(shares_ref):
    return 1.0 / jnp.sum(shares_ref[...].astype(F32), axis=0)


def later_row_kernel(shares_ref, scale_ref, matrix_ref, share_ref):
    inverse = inverse_of(shares_ref)
    sums = 0.0
    for b in range(scale_ref.shape[0]):
        scaled = matrix_ref[:, columns(b)].astype(F32) * to_row(inverse[lines_of(b)])
        sums += scale_ref[b] * jnp.sum(scaled, axis=1, keepdims=True)
    fill_share(share_ref, to_lanes(sums))


def pack(sums, numbers, parts, starts, counts):
    rows, width = sums.shape
    images = starts.shape[0]
    chosen = spread(starts, counts, SLOT, rows)
    packed = jnp.dot(chosen, sums.astype(BF16), preferred_element_type=F32).astype(BF16)
    row = split(to_row(to_lanes(numbers)), parts)
    row = jnp.concatenate([part.astype(F32) for part in row] + [jnp.zeros((SLOT - MOST - parts, rows), F32)], axis=0)
    tail = lax.dot_general(row.astype(BF16), chosen, (((1,), (1,)), ((), ())), preferred_element_type=F32)
    tail = jnp.concatenate([tail, jnp.zeros((SLOT - MOST, LANES), F32)], axis=1)
    blank = jnp.zeros((SLOT - MOST, width - LANES), F32)
    tail = [jnp.concatenate([tail[:, j * SLOT : j * SLOT + LANES], blank], axis=1)[None] for j in range(images)]
    return packed.reshape(images, SLOT, width)[:, :MOST], jnp.concatenate(tail, axis=0).astype(BF16)


def join(tail, width):
    images = tail[0].shape[0]
    filler = jnp.zeros((images, 1, width - LANES), F32)
    rows = [jnp.concatenate([part.astype(F32), filler], axis=2) for part in tail]
    rows.append(jnp.zeros((images, SLOT - MOST - len(tail), width), F32))
    return jnp.concatenate(rows, axis=1).astype(BF16)


def numbers_of(chunk, parts):
    tail = chunk[:, MOST:SLOT, :LANES].astype(F32)
    return sum(tail[:, k] for k in range(parts))


def put(own_ref, other_ref, rows, tail):
    half = own_ref.shape[0]
    own_ref[:, :MOST], own_ref[:, MOST:] = rows[:half], tail[:half]
    other_ref[:, :MOST], other_ref[:, MOST:] = rows[half:], tail[half:]


def slots_of(lanes):
    images = lanes.shape[0]
    same = iota((1, MOST, LANES), 1) == iota((1, MOST, LANES), 2)
    return jnp.sum(jnp.where(same, lanes.reshape(images, 1, LANES), 0.0), axis=2, keepdims=True)


def target_kernel(shares_ref, scale_ref, matrix_ref, protos_ref, places_ref, own_ref, other_ref):
    inverse = inverse_of(shares_ref)
    sums, total = 0.0, 0.0
    for b in range(scale_ref.shape[0]):
        weights = (matrix_ref[:, columns(b)].astype(F32) * to_row(inverse[lines_of(b)])).astype(BF16)
        part = lax.dot_general(weights, protos_ref[:, columns(b)], (((1,), (1,)), ((), ())), preferred_element_type=F32)
        sums += scale_ref[b] * part
        total += scale_ref[b] * jnp.sum(weights.astype(F32), axis=1, keepdims=True)
    put(own_ref, other_ref, *pack(sums, total, 2, places_ref[0], places_ref[1]))


def merge_kernel(own_ref, came_ref, student_own_ref, student_came_ref, out_ref):
    width = own_ref.shape[2]
    out_ref[:, :MOST] = (own_ref[:, :MOST].astype(F32) + came_ref[:, :MOST].astype(F32)).astype(BF16)
    total = numbers_of(own_ref, 2) + numbers_of(came_ref, 2)
    out_ref[:, MOST:SLOT] = join([part[:, None] for part in split(total, 2)], width)
    own, came = numbers_of(student_own_ref, 3), numbers_of(student_came_ref, 3)
    high = jnp.maximum(own, came)
    joint = high + jnp.log(jnp.exp(own - high) + jnp.exp(came - high))
    mean = student_own_ref[:, :MOST].astype(F32) * slots_of(jnp.exp(own - joint))
    mean = mean + student_came_ref[:, :MOST].astype(F32) * slots_of(jnp.exp(came - joint))
    out_ref[:, SLOT : SLOT + MOST] = mean.astype(BF16)
    out_ref[:, SLOT + MOST :] = join([part[:, None] for part in split(joint, 3)], width)


def student_kernel(
    gathered_ref, late_ref, came_ref, index_ref, places_ref, far_ref, own_ref, other_ref, near_ref, sems
):
    block, blocks = fetch(far_ref, near_ref, sems)
    rows = places_ref.shape[1] * MASK_DEV
    starts, counts, core = places_ref[2], places_ref[3], index_ref[0, 0] % 2
    found = compact(gathered_ref[:, SLOT:], starts, counts, rows, 0, EARLY, 0)
    for ref, half in ((late_ref, core), (came_ref, 1 - core)):
        late = jnp.concatenate([ref[:, :LATE], ref[:, LATE : 2 * LATE]], axis=2)
        found += compact(late, starts, counts, rows, 0, LATE, EARLY + half * LATE)
    found = found.astype(BF16)
    top, total, sums = -1e30, 0.0, 0.0
    for b in blocks:
        protos = block(b)
        logits = jnp.dot(found, protos, preferred_element_type=F32) * STUD
        high = jnp.maximum(top, jnp.max(logits, axis=1, keepdims=True))
        shrink = jnp.exp(top - high)
        exact = jnp.exp(logits - high)
        total = total * shrink + jnp.sum(exact, axis=1, keepdims=True)
        part = lax.dot_general(exact.astype(BF16), protos, (((1,), (1,)), ((), ())), preferred_element_type=F32)
        sums = sums * shrink + part
        top = high
    put(own_ref, other_ref, *pack(sums / total, top + jnp.log(total), 3, places_ref[0], places_ref[1]))


def blend(chunk, lse):
    joint = merged(lse)
    weights = slots_of(jnp.exp(lse - joint[None]))
    return jnp.sum(chunk * weights, axis=0), joint


def finish_kernel(back_ref, picked_ref, order_ref, count_ref, grad_ref, loss_ref):
    patches, width = grad_ref.shape
    target = jnp.sum(back_ref[:, :SLOT].astype(F32), axis=0)
    mass = to_column((target[MOST : MOST + 1] + target[MOST + 1 : MOST + 2])[:, :LANES])[:MOST]
    tail = back_ref[:, SLOT + MOST : 2 * SLOT, :LANES].astype(F32)
    soft, lse_lanes = blend(back_ref[:, SLOT : SLOT + MOST].astype(F32), sum(tail[:, k] for k in range(3)))
    used = iota((MOST, 1), 0) < count_ref[0, 0]
    mean = target[:MOST] / jnp.where(used, mass, 1.0)
    own_lse = to_column(lse_lanes.reshape(1, LANES))[:MOST]
    cross = own_lse - STUD * jnp.sum(picked_ref[:MOST].astype(F32) * mean, axis=1, keepdims=True)
    cross = jnp.sum(jnp.where(used, cross, 0.0), axis=0, keepdims=True)
    loss_ref[...] = cross / jnp.full((1, 1), count_ref[0, 0], jnp.int32).astype(F32)
    rows = jnp.where(used, STUD * (soft - mean), 0.0)
    rows = jnp.concatenate([rows, jnp.zeros((LANES - MOST, width), F32)], axis=0).astype(BF16)
    order = jnp.broadcast_to(order_ref[:, :LANES], (patches, LANES))
    chosen = (iota((patches, LANES), 0) == order).astype(BF16)
    grad_ref[...] = jnp.dot(chosen, rows, preferred_element_type=F32).astype(BF16)


def body(student_patches, teacher_patches, mask_order, counts, student_protos, teacher_protos):
    width = lax.axis_size("proto")
    groups = lax.axis_size("dp")
    rows = MASK_DEV * width
    lines = rows // LANES
    patches, bot = student_patches.shape[1:]
    protos = student_protos.shape[1]
    steps = protos // BLOCK
    depth = 8
    index = lax.axis_index("proto").astype(jnp.int32).reshape(1, 1)
    over = functools.partial(lax.all_to_all, split_axis=0, concat_axis=0, tiled=True)
    near = ((bot, protos), BF16)
    sems = [pltpu.SemaphoreType.DMA((protos // PIECE,))]
    far = functools.partial(pltpu.with_memory_space_constraint, memory_space=pltpu.HBM)
    student_patches, teacher_patches, mask_order = far(student_patches[0]), far(teacher_patches[0]), far(mask_order)
    student_protos, teacher_protos = far(student_protos), far(teacher_protos)
    dot = 2 * rows * protos * bot

    sent, late, picked = call(
        pick_kernel,
        [((SLOT + EARLY, bot), BF16), ((2, 2 * LATE, LANES), BF16), pltpu.HBM((SLOT, bot), BF16)],
        teacher_patches,
        student_patches,
        mask_order,
        counts,
        in_specs=[VMEM, VMEM, VMEM, SMEM],
        moved=4 * patches * bot,
    )
    gathered = lax.all_gather(sent, "proto", axis=0, tiled=False)
    share, teacher_rows, places, near_teacher = call(
        column_kernel,
        [((groups, protos // LANES, LANES), F32), ((rows, bot), BF16), pltpu.HBM((4, width, LANES), F32), near],
        gathered,
        index,
        teacher_protos,
        in_specs=[VMEM, SMEM, HBM],
        scratch=sems,
        flops=dot,
        moved=2 * bot * protos,
    )
    shares = over(share, "dp")
    matrix, high, share = call(
        row_kernel,
        [((rows, protos), BF16), ((steps, rows, 1), F32), ((width // 2, 2, 2 * LATE + 16, LANES), BF16)],
        shares,
        teacher_rows,
        near_teacher,
        late,
        flops=dot,
        moved=2 * bot * protos + 2 * rows * protos,
    )
    swap = [(p, p ^ 1) for p in range(width)]
    shares = over(share.reshape((width,) + share.shape[2:]), "proto")
    late = shares
    share, scale = call(
        first_column_kernel,
        [((groups, protos // LANES, LANES), BF16), ((steps, rows, 1), F32)],
        shares,
        high,
        matrix,
        moved=2 * rows * protos,
    )
    shares = over(share, "dp")
    share = call(
        later_row_kernel,
        [((width, depth, LANES), F32)],
        shares,
        scale,
        matrix,
        moved=2 * rows * protos,
    )[0]
    shares = over(share, "proto")
    share, scale = call(
        later_column_kernel,
        [pltpu.HBM((groups, protos // LANES, LANES), BF16), pltpu.HBM((steps, rows, 1), F32)],
        shares,
        scale,
        matrix,
        moved=2 * rows * protos,
    )
    late_came = lax.ppermute(late, "proto", swap)
    packed = ((width // 2, SLOT, bot), BF16)
    student_own, student_other, near_student = call(
        student_kernel,
        [pltpu.HBM(*packed), pltpu.HBM(*packed), near],
        far(gathered),
        far(late),
        far(late_came),
        index,
        far(places),
        student_protos,
        in_specs=[VMEM, VMEM, VMEM, SMEM, VMEM, HBM],
        scratch=sems,
        flops=2 * dot,
        moved=2 * bot * protos,
    )
    student_came = lax.ppermute(student_other, "proto", swap)
    shares = over(share, "dp")
    own, other = call(
        target_kernel,
        [packed, packed],
        shares,
        scale,
        matrix,
        near_student,
        far(places),
        flops=dot,
        moved=2 * rows * protos,
    )
    came = lax.ppermute(other, "proto", swap)
    sent = call(
        merge_kernel, [((width // 2, 2 * SLOT, bot), BF16)], own, came, student_own, student_came
    )[0]
    same_core = [list(range(core, width, 2)) for core in range(2)]
    back = over(sent, "proto", axis_index_groups=same_core)
    student_grad, image_loss = call(
        finish_kernel,
        [((patches, bot), BF16), ((1, 1), F32)],
        back,
        picked,
        mask_order,
        counts,
        in_specs=[VMEM, VMEM, VMEM, SMEM],
        moved=2 * patches * bot,
    )
    return (student_grad[None], image_loss)


def solution(mesh):
    placed = (
        P(("dp", "proto"), None, None),
        P(("dp", "proto"), None, None),
        P(("dp", "proto"), None),
        P("dp", "proto"),
        P(None, "proto"),
        P(None, "proto"),
    )
    return jax.shard_map(
        body,
        mesh=mesh,
        in_specs=placed,
        out_specs=(P(("dp", "proto"), None, None), P("dp", "proto")),
        check_vma=False,
    )
```

time: 167 us -> 165 us (0.988)
  Pallas kernels: 31.2 us -> 26.2 us
  local copies, waits for them, and re-layouts: 1.68 us -> 4.62 us
    pallas_call x10, Pallas kernels: 31.2 us -> 26.2 us  [call(): pl.pallas_call(kernel, out_shape=out_shape, in_specs=[VMEM] * len(args) i...]
    unnamed x12 -> x16, local copies, waits for them, and re-layouts: 1.68 us -> 4.62 us
  transfers between devices with their start and end apart: 4 -> 4, of which waited for: 2 -> 2; matrix products, arithmetic and copies ran while one was open for 0% -> 0% of each run, Pallas kernels for 8% -> 7%
where the time goes in v10:
time: 165 us; the launch traced here: 164 us
  blocking collectives  119 us (72%)
  Pallas kernels  26.2 us (16%)
  starting transfers between devices  10.6 us (6%)
  local copies, waits for them, and re-layouts  4.62 us (3%)
  waiting for transfers between devices  2.54 us (2%)
    all_to_all x2, blocking collectives, body(): shares = over(share, 'dp')  43.2 us
    pallas_call x10, Pallas kernels, call(): pl.pallas_call(kernel, out_shape=out_shape, in_specs=[VMEM] * len(args) i...  26.2 us
    all_gather x1, blocking collectives, body(): gathered = lax.all_gather(sent, 'proto', axis=0, tiled=False)  24.3 us
    all_to_all x1, blocking collectives, body(): back = over(sent, 'proto', axis_index_groups=same_core)  23.2 us
    all_to_all x1, blocking collectives, body(): shares = over(share.reshape((width,) + share.shape[2:]), 'proto')  16.4 us
    all_to_all x1, blocking collectives, body(): shares = over(share, 'proto')  11.8 us
    unnamed x16, local copies, waits for them, and re-layouts  4.62 us
    all_to_all x1, starting transfers between devices, body(): shares = over(share, 'dp')  3.87 us
  transfers between devices with their start and end apart: 4, of which 2 were waited for; matrix products, arithmetic and copies ran while one was open for 0% of the time, Pallas kernels for 7%

profile of v10, /device:TPU:1, one launch (start us, length us, event | category | flops | bytes accessed | tf_op | source)
XLA Modules:
  0.0 164.3 jit_solution(6385517823830987601)
XLA Ops:
  1.3 1.8 %shard_map.77 = (bf16[120,256]{1,0:T(8,128)(2,1)S(1)}, bf16[2,32,128]{2,1,0:T(8,128)(2,1)S(1)}, bf16[80,256]{1,0:T(8,128)(2,1)}) custom-call(bf16[256,256]{1,0:T(8,128)(2,1)} %bitcast.9, bf16[256,256]{1,0:T(8,128)(2,1)} %bitcast.10, s32[1,256]{1,0:T(1,128)} %order_ref.3, s32[1,1]{1,0:T(1,128)S(6)} %copy.8.count_ref), custom_call_target="tpu_custom_call" | custom-call | bytes 262144 | tf_op jit(solution)/shard_map/pallas_call | solution.py:32
  3.1 24.3 %all-gather = bf16[1920,256]{1,0:T(8,128)(2,1)S(1)} all-gather(bf16[120,256]{1,0:T(8,128)(2,1)S(1)} %get-tuple-element.23), channel_id=2, replica_groups=mesh['dp'=32,'proto'=16] {'proto'}, dimensions={0}, use_global_device_ids=true | all-gather | bytes 1044480 | tf_op jit(solution)/shard_map/all_gather | solution.py:381
  27.4 0.0 copy-start
  27.4 3.9 %shard_map.78 = (f32[32,32,128]{2,1,0:T(8,128)S(1)}, bf16[384,256]{1,0:T(8,128)(2,1)S(1)}, f32[4,16,128]{2,1,0:T(8,128)}, bf16[256,4096]{1,0:T(8,128)(2,1)S(1)}) custom-call(bf16[16,120,256]{2,1,0:T(8,128)(2,1)S(1)} %bitcast.6, s32[1,1]{1,0:T(1,128)} %bitcast.3.index_ref, bf16[256,4096]{1,0:T(8,128)(2,1)} %far_ref.2), custom_call_target="tpu_custom_call" | custom-call | flops 805306368 | bytes 2097152 | tf_op jit(solution)/shard_map/pallas_call | solution.py:32
  31.3 26.7 %all_to_all.30.shares_ref = f32[32,32,128]{2,1,0:T(8,128)S(1)} all-to-all(f32[32,32,128]{2,1,0:T(8,128)S(1)} %get-tuple-element.24), channel_id=1, replica_groups=mesh['dp'=32,'proto'=16] {'dp'}, dimensions={0} | all-to-all | bytes 1048576 | tf_op jit(solution)/shard_map/all_to_all | solution.py:393
  58.0 0.0 copy-done
  58.0 2.2 %shard_map.79 = (bf16[384,4096]{1,0:T(8,128)(2,1)S(1)}, f32[2,384,1]{2,1,0:T(8,128)S(1)}, bf16[8,2,48,128]{3,2,1,0:T(8,128)(2,1)S(1)}) custom-call(f32[32,32,128]{2,1,0:T(8,128)S(1)} %all_to_all.30.shares_ref, bf16[384,256]{1,0:T(8,128)(2,1)S(1)} %get-tuple-element.25.rows_ref, bf16[256,4096]{1,0:T(8,128)(2,1)S(1)} %get-tuple-element.26.protos_ref, ...), custom_call_target="tpu_custom_call" | custom-call | flops 805306368 | bytes 5242880 | tf_op jit(solution)/shard_map/pallas_call | solution.py:32
  60.2 16.4 %all_to_all.31.shares_ref.late_ref = bf16[16,48,128]{2,1,0:T(8,128)(2,1)S(1)} all-to-all(bf16[16,48,128]{2,1,0:T(8,128)(2,1)S(1)} %bitcast.8), channel_id=1, replica_groups=mesh['dp'=32,'proto'=16] {'proto'}, dimensions={0} | all-to-all | bytes 393216 | tf_op jit(solution)/shard_map/all_to_all | solution.py:405
  76.6 0.0 copy-start.3
  76.6 0.9 shard_map.80
  77.5 16.5 %all_to_all.32.shares_ref = bf16[32,32,128]{2,1,0:T(8,128)(2,1)S(1)} all-to-all(bf16[32,32,128]{2,1,0:T(8,128)(2,1)S(1)} %get-tuple-element.31), channel_id=1, replica_groups=mesh['dp'=32,'proto'=16] {'dp'}, dimensions={0} | all-to-all | bytes 524288 | tf_op jit(solution)/shard_map/all_to_all | solution.py:415
  94.0 0.0 copy-done.3
  94.0 0.9 shard_map.81
  94.8 11.8 %all_to_all.33.shares_ref = f32[16,8,128]{2,1,0:T(8,128)S(1)} all-to-all(f32[16,8,128]{2,1,0:T(8,128)S(1)} %shard_map.81), channel_id=1, replica_groups=mesh['dp'=32,'proto'=16] {'proto'}, dimensions={0} | all-to-all | bytes 131072 | tf_op jit(solution)/shard_map/all_to_all | solution.py:424
  106.7 1.5 shard_map.82
  108.2 3.9 %all-to-all-start.4 = ((bf16[32,32,128]{2,1,0:T(8,128)(2,1)}), bf16[32,32,128]{2,1,0:T(8,128)(2,1)S(1)}, u32[]{:S(2)}, u32[]{:S(2)}) async-start(bf16[32,32,128]{2,1,0:T(8,128)(2,1)} %get-tuple-element.33), calls=%async_computation.4 | async-start | bytes 524288 | tf_op jit(solution)/shard_map/all_to_all | solution.py:450
  112.1 2.3 %collective-permute-start = (bf16[16,48,128]{2,1,0:T(8,128)(2,1)}, bf16[16,48,128]{2,1,0:T(8,128)(2,1)S(1)}, u32[]{:S(2)}, u32[]{:S(2)}) collective-permute-start(bf16[16,48,128]{2,1,0:T(8,128)(2,1)} %copy-done.3), channel_id=1, source_target_pairs={{0,1},{1,0},{2,3},{3,2},{4,5},{5,4},{6,7},{7,6},{8,9},{9,8},{10,11... | collective-permute-start | bytes 589832 | tf_op jit(solution)/shard_map/ppermute | solution.py:433
  114.3 1.3 collective-permute-done.came_ref
  115.6 0.0 copy-start.7
  115.6 0.7 copy-done.7
  116.3 8.8 %shard_map.83 = (bf16[8,80,256]{2,1,0:T(8,128)(2,1)}, bf16[8,80,256]{2,1,0:T(8,128)(2,1)}, bf16[256,4096]{1,0:T(8,128)(2,1)S(1)}) custom-call(bf16[16,120,256]{2,1,0:T(8,128)(2,1)} %bitcast.7, bf16[16,48,128]{2,1,0:T(8,128)(2,1)} %copy-done.3, bf16[16,48,128]{2,1,0:T(8,128)(2,1)} %copy-done.7, s32[1,1]{1,0:T(1,128)} %bitcast.3.index_ref, ...), custom_call_target="tpu_custom_call" | custom-call | flops 1610612736 | bytes 2097152 | tf_op jit(solution)/shard_map/pallas_call | solution.py:32
  125.1 0.0 copy-start.1
  125.1 1.3 copy-done.1
  126.5 2.1 %collective-permute-start.2 = (bf16[8,80,256]{2,1,0:T(8,128)(2,1)}, bf16[8,80,256]{2,1,0:T(8,128)(2,1)}, u32[]{:S(2)}, u32[]{:S(2)}) collective-permute-start(bf16[8,80,256]{2,1,0:T(8,128)(2,1)} %get-tuple-element.40), channel_id=1, source_target_pairs={{0,1},{1,0},{2,3},{3,2},{4,5},{5,4},{6,7},{7,6},{8,9},{9,8},{10,11... | collective-permute-start | bytes 983048 | tf_op jit(solution)/shard_map/ppermute | solution.py:449
  128.5 0.0 all-to-all-done.4.shares_ref
  128.6 0.0 copy-start.2
  128.6 1.6 copy-done.2
  130.2 0.0 copy-start.4
  130.2 1.0 copy-done.4
  131.1 0.0 copy-start.5
  131.2 3.1 %shard_map.84 = (bf16[8,80,256]{2,1,0:T(8,128)(2,1)S(1)}, bf16[8,80,256]{2,1,0:T(8,128)(2,1)S(1)}) custom-call(bf16[32,32,128]{2,1,0:T(8,128)(2,1)S(1)} %all-to-all-done.4.shares_ref, f32[2,384,1]{2,1,0:T(8,128)S(1)} %copy-done.4, bf16[384,4096]{1,0:T(8,128)(2,1)S(1)} %get-tuple-element.30.matrix_ref, bf16[256,4096]{1,0:T(8,128)(2,1)S(1)} %copy-done.2, ...), custom_call_target="tpu_custom_call" | custom-call | flops 805306368 | bytes 3145728 | tf_op jit(solution)/shard_map/pallas_call | solution.py:32
  134.3 0.0 copy-start.6
  134.3 2.4 %collective-permute-start.1 = (bf16[8,80,256]{2,1,0:T(8,128)(2,1)S(1)}, bf16[8,80,256]{2,1,0:T(8,128)(2,1)S(1)}, u32[]{:S(2)}, u32[]{:S(2)}) collective-permute-start(bf16[8,80,256]{2,1,0:T(8,128)(2,1)S(1)} %get-tuple-element.38), channel_id=1, source_target_pairs={{0,1},{1,0},{2,3},{3,2},{4,5},{5,4},{6,7},{7,6},{8,9},{9,8},{10,11... | collective-permute-start | bytes 983048 | tf_op jit(solution)/shard_map/ppermute | solution.py:462
  136.7 0.0 collective-permute-done.2.student_came_ref
  136.7 1.3 collective-permute-done.1.came_ref
  138.0 0.0 copy-done.5
  138.0 1.4 shard_map.85
  139.4 23.2 %all_to_all.34.back_ref = bf16[8,160,256]{2,1,0:T(8,128)(2,1)S(1)} all-to-all(bf16[8,160,256]{2,1,0:T(8,128)(2,1)S(1)} %shard_map.85), channel_id=1, replica_groups={{0,2,4,6,8,10,12,14},{1,3,5,7,9,11,13,15},{16,18,20,22,24,26,28,30},{17..., dimensions={0} | all-to-all | bytes 1310720 | tf_op jit(solution)/shard_map/all_to_all | solution.py:467
  162.5 0.0 copy-done.6
  162.5 1.7 %shard_map.86 = (bf16[256,256]{1,0:T(8,128)(2,1)}, f32[1,1]{1,0:T(1,128)}) custom-call(bf16[8,160,256]{2,1,0:T(8,128)(2,1)S(1)} %all_to_all.34.back_ref, bf16[80,256]{1,0:T(8,128)(2,1)S(1)} %copy-done.6, s32[1,256]{1,0:T(1,128)} %order_ref.3, s32[1,1]{1,0:T(1,128)S(6)} %copy.8.count_ref), custom_call_target="tpu_custom_call" | custom-call | bytes 131072 | tf_op jit(solution)/shard_map/pallas_call | solution.py:32
Async XLA Ops:
  27.4 30.7 %copy-start = (bf16[1920,256]{1,0:T(8,128)(2,1)}, bf16[1920,256]{1,0:T(8,128)(2,1)S(1)}, u32[]{:S(2)}) copy-start(bf16[1920,256]{1,0:T(8,128)(2,1)S(1)} %all-gather) | copy-start | bytes 2949124
  76.6 17.4 %copy-start.3 = (bf16[16,48,128]{2,1,0:T(8,128)(2,1)}, bf16[16,48,128]{2,1,0:T(8,128)(2,1)S(1)}, u32[]{:S(2)}) copy-start(bf16[16,48,128]{2,1,0:T(8,128)(2,1)S(1)} %all_to_all.31.shares_ref.late_ref) | copy-start | bytes 589828
  108.2 20.4 %all-to-all-start.4 = ((bf16[32,32,128]{2,1,0:T(8,128)(2,1)}), bf16[32,32,128]{2,1,0:T(8,128)(2,1)S(1)}, u32[]{:S(2)}, u32[]{:S(2)}) async-start(bf16[32,32,128]{2,1,0:T(8,128)(2,1)} %get-tuple-element.33), calls=%async_computation.4 | async-start | bytes 524288 | tf_op jit(solution)/shard_map/all_to_all | solution.py:450
  112.1 3.5 %collective-permute-start = (bf16[16,48,128]{2,1,0:T(8,128)(2,1)}, bf16[16,48,128]{2,1,0:T(8,128)(2,1)S(1)}, u32[]{:S(2)}, u32[]{:S(2)}) collective-permute-start(bf16[16,48,128]{2,1,0:T(8,128)(2,1)} %copy-done.3), channel_id=1, source_target_pairs={{0,1},{1,0},{2,3},{3,2},{4,5},{5,4},{6,7},{7,6},{8,9},{9,8},{10,11... | collective-permute-start | bytes 589832 | tf_op jit(solution)/shard_map/ppermute | solution.py:433
  115.6 0.7 copy-start.7
  125.1 1.3 copy-start.1
  126.5 10.2 %collective-permute-start.2 = (bf16[8,80,256]{2,1,0:T(8,128)(2,1)}, bf16[8,80,256]{2,1,0:T(8,128)(2,1)}, u32[]{:S(2)}, u32[]{:S(2)}) collective-permute-start(bf16[8,80,256]{2,1,0:T(8,128)(2,1)} %get-tuple-element.40), channel_id=1, source_target_pairs={{0,1},{1,0},{2,3},{3,2},{4,5},{5,4},{6,7},{7,6},{8,9},{9,8},{10,11... | collective-permute-start | bytes 983048 | tf_op jit(solution)/shard_map/ppermute | solution.py:449
  128.6 1.6 copy-start.2
  130.2 1.0 copy-start.4
  131.1 6.8 %copy-start.5 = (bf16[8,80,256]{2,1,0:T(8,128)(2,1)S(1)}, bf16[8,80,256]{2,1,0:T(8,128)(2,1)}, u32[]{:S(2)}) copy-start(bf16[8,80,256]{2,1,0:T(8,128)(2,1)} %get-tuple-element.39.student_own_ref) | copy-start | bytes 983044
  134.3 28.2 %copy-start.6 = (bf16[80,256]{1,0:T(8,128)(2,1)S(1)}, bf16[80,256]{1,0:T(8,128)(2,1)}, u32[]{:S(2)}) copy-start(bf16[80,256]{1,0:T(8,128)(2,1)} %get-tuple-element.41.picked_ref) | copy-start | bytes 122884
  134.3 3.7 %collective-permute-start.1 = (bf16[8,80,256]{2,1,0:T(8,128)(2,1)S(1)}, bf16[8,80,256]{2,1,0:T(8,128)(2,1)S(1)}, u32[]{:S(2)}, u32[]{:S(2)}) collective-permute-start(bf16[8,80,256]{2,1,0:T(8,128)(2,1)S(1)} %get-tuple-element.38), channel_id=1, source_target_pairs={{0,1},{1,0},{2,3},{3,2},{4,5},{5,4},{6,7},{7,6},{8,9},{9,8},{10,11... | collective-permute-start | bytes 983048 | tf_op jit(solution)/shard_map/ppermute | solution.py:462

commit v11 on v10

--- a/solution.py
+++ b/solution.py
@@ -27,8 +27,9 @@
 HBM = pl.BlockSpec(memory_space=pl.ANY)
 
 
-def call(kernel, out_shape, *args, in_specs=None, scratch=(), flops=0, moved=0):
+def call(kernel, out_shape, *args, in_specs=None, scratch=(), grid=None, flops=0, moved=0):
     out_shape = [jax.ShapeDtypeStruct(*o) if isinstance(o, tuple) else o for o in out_shape]
+    extra = {} if grid is None else {"grid": grid}
     return pl.pallas_call(
         kernel,
         out_shape=out_shape,
@@ -37,6 +38,7 @@
         scratch_shapes=list(scratch),
         compiler_params=pltpu.CompilerParams(vmem_limit_bytes=LIMIT),
         cost_estimate=pl.CostEstimate(flops=flops, bytes_accessed=moved, transcendentals=0),
+        **extra,
     )(*args)
 
 
@@ -275,15 +277,26 @@
     return jnp.sum(jnp.where(same, lanes.reshape(images, 1, LANES), 0.0), axis=2, keepdims=True)
 
 
-def target_kernel(shares_ref, scale_ref, matrix_ref, protos_ref, places_ref, own_ref, other_ref):
-    inverse = inverse_of(shares_ref)
-    sums, total = 0.0, 0.0
-    for b in range(scale_ref.shape[0]):
-        weights = (matrix_ref[:, columns(b)].astype(F32) * to_row(inverse[lines_of(b)])).astype(BF16)
-        part = lax.dot_general(weights, protos_ref[:, columns(b)], (((1,), (1,)), ((), ())), preferred_element_type=F32)
-        sums += scale_ref[b] * part
-        total += scale_ref[b] * jnp.sum(weights.astype(F32), axis=1, keepdims=True)
-    put(own_ref, other_ref, *pack(sums, total, 2, places_ref[0], places_ref[1]))
+def target_kernel(shares_ref, scale_ref, matrix_ref, protos_ref, places_ref, own_ref, other_ref, sums, total):
+    step = pl.program_id(0)
+    scale = scale_ref[step]
+    weights = (matrix_ref[...].astype(F32) * to_row(inverse_of(shares_ref))).astype(BF16)
+    part = scale * lax.dot_general(weights, protos_ref[...], (((1,), (1,)), ((), ())), preferred_element_type=F32)
+    mass = scale * jnp.sum(weights.astype(F32), axis=1, keepdims=True)
+
+    @pl.when(step == 0)
+    def _():
+        sums[...] = part
+        total[...] = mass
+
+    @pl.when(step > 0)
+    def _():
+        sums[...] += part
+        total[...] += mass
+
+    @pl.when(step == pl.num_programs(0) - 1)
+    def _():
+        put(own_ref, other_ref, *pack(sums[...], total[...], 2, places_ref[0], places_ref[1]))
 
 
 def merge_kernel(own_ref, came_ref, student_own_ref, student_came_ref, out_ref):
@@ -301,28 +314,38 @@
 
 
 def student_kernel(
-    gathered_ref, late_ref, came_ref, index_ref, places_ref, far_ref, own_ref, other_ref, near_ref, sems
+    gathered_ref, late_ref, came_ref, index_ref, places_ref, protos_ref, own_ref, other_ref, rows_ref, sums, top, total
 ):
-    block, blocks = fetch(far_ref, near_ref, sems)
-    rows = places_ref.shape[1] * MASK_DEV
-    starts, counts, core = places_ref[2], places_ref[3], index_ref[0, 0] % 2
-    found = compact(gathered_ref[:, SLOT:], starts, counts, rows, 0, EARLY, 0)
-    for ref, half in ((late_ref, core), (came_ref, 1 - core)):
-        late = jnp.concatenate([ref[:, :LATE], ref[:, LATE : 2 * LATE]], axis=2)
-        found += compact(late, starts, counts, rows, 0, LATE, EARLY + half * LATE)
-    found = found.astype(BF16)
-    top, total, sums = -1e30, 0.0, 0.0
-    for b in blocks:
-        protos = block(b)
-        logits = jnp.dot(found, protos, preferred_element_type=F32) * STUD
-        high = jnp.maximum(top, jnp.max(logits, axis=1, keepdims=True))
-        shrink = jnp.exp(top - high)
-        exact = jnp.exp(logits - high)
-        total = total * shrink + jnp.sum(exact, axis=1, keepdims=True)
-        part = lax.dot_general(exact.astype(BF16), protos, (((1,), (1,)), ((), ())), preferred_element_type=F32)
-        sums = sums * shrink + part
-        top = high
-    put(own_ref, other_ref, *pack(sums / total, top + jnp.log(total), 3, places_ref[0], places_ref[1]))
+    step = pl.program_id(0)
+
+    @pl.when(step == 0)
+    def _():
+        starts, counts, core = places_ref[2], places_ref[3], index_ref[0, 0] % 2
+        rows = rows_ref.shape[0]
+        found = compact(gathered_ref[:, SLOT:], starts, counts, rows, 0, EARLY, 0)
+        for ref, half in ((late_ref, core), (came_ref, 1 - core)):
+            late = jnp.concatenate([ref[:, :LATE], ref[:, LATE : 2 * LATE]], axis=2)
+            found += compact(late, starts, counts, rows, 0, LATE, EARLY + half * LATE)
+        rows_ref[...] = found.astype(BF16)
+        top[...] = jnp.full(top.shape, -1e30, F32)
+        total[...] = jnp.zeros(total.shape, F32)
+        sums[...] = jnp.zeros(sums.shape, F32)
+
+    protos = protos_ref[...]
+    logits = jnp.dot(rows_ref[...], protos, preferred_element_type=F32) * STUD
+    before = top[...]
+    high = jnp.maximum(before, jnp.max(logits, axis=1, keepdims=True))
+    shrink = jnp.exp(before - high)
+    exact = jnp.exp(logits - high)
+    total[...] = total[...] * shrink + jnp.sum(exact, axis=1, keepdims=True)
+    part = lax.dot_general(exact.astype(BF16), protos, (((1,), (1,)), ((), ())), preferred_element_type=F32)
+    sums[...] = sums[...] * shrink + part
+    top[...] = high
+
+    @pl.when(step == pl.num_programs(0) - 1)
+    def _():
+        mean, own_lse = sums[...] / total[...], top[...] + jnp.log(total[...])
+        put(own_ref, other_ref, *pack(mean, own_lse, 3, places_ref[0], places_ref[1]))
 
 
 def blend(chunk, lse):
@@ -362,6 +385,11 @@
     index = lax.axis_index("proto").astype(jnp.int32).reshape(1, 1)
     over = functools.partial(lax.all_to_all, split_axis=0, concat_axis=0, tiled=True)
     near = ((bot, protos), BF16)
+    grid = (steps,)
+    wide = pl.BlockSpec((bot, BLOCK), lambda k: (0, k))
+    peer = pl.BlockSpec((groups, BLOCK // LANES, LANES), lambda k: (0, k, 0))
+    square = pl.BlockSpec((rows, BLOCK), lambda k: (0, k))
+    column = pltpu.VMEM((rows, 1), F32)
     sems = [pltpu.SemaphoreType.DMA((protos // PIECE,))]
     far = functools.partial(pltpu.with_memory_space_constraint, memory_space=pltpu.HBM)
     student_patches, teacher_patches, mask_order = far(student_patches[0]), far(teacher_patches[0]), far(mask_order)
@@ -406,8 +434,8 @@
     late = shares
     share, scale = call(
         first_column_kernel,
-        [((groups, protos // LANES, LANES), BF16), ((steps, rows, 1), F32)],
-        shares,
+        [pltpu.HBM((groups, protos // LANES, LANES), BF16), ((steps, rows, 1), F32)],
+        far(shares),
         high,
         matrix,
         moved=2 * rows * protos,
@@ -432,30 +460,35 @@
     )
     late_came = lax.ppermute(late, "proto", swap)
     packed = ((width // 2, SLOT, bot), BF16)
-    student_own, student_other, near_student = call(
+    student_own, student_other = call(
         student_kernel,
-        [pltpu.HBM(*packed), pltpu.HBM(*packed), near],
+        [pltpu.HBM(*packed), pltpu.HBM(*packed)],
         far(gathered),
         far(late),
-        far(late_came),
+        late_came,
         index,
         far(places),
         student_protos,
-        in_specs=[VMEM, VMEM, VMEM, SMEM, VMEM, HBM],
-        scratch=sems,
+        grid=grid,
+        in_specs=[VMEM, VMEM, VMEM, SMEM, VMEM, wide],
+        scratch=[pltpu.VMEM((rows, bot), BF16), pltpu.VMEM((rows, bot), F32), column, column],
         flops=2 * dot,
         moved=2 * bot * protos,
     )
     student_came = lax.ppermute(student_other, "proto", swap)
     shares = over(share, "dp")
+    shares, student_came = lax.optimization_barrier((shares, student_came))
     own, other = call(
         target_kernel,
         [packed, packed],
         shares,
-        scale,
+        far(scale),
         matrix,
-        near_student,
+        student_protos,
         far(places),
+        grid=grid,
+        in_specs=[peer, VMEM, square, wide, VMEM],
+        scratch=[pltpu.VMEM((rows, bot), F32), column],
         flops=dot,
         moved=2 * rows * protos,
     )

time: 165 us -> 162 us (0.982)
  blocking collectives: 119 us -> 103 us
  waiting for transfers between devices: 2.54 us -> 13.1 us
  starting transfers between devices: 10.6 us -> 15.4 us
  local copies, waits for them, and re-layouts: 4.62 us -> 0.74 us
  Pallas kernels: 26.2 us -> 28.1 us
    all_to_all x2 -> x1, blocking collectives: 43.2 us -> 26.8 us  [body(): shares = over(share, 'dp')]
    all_to_all x1 -> x2, waiting for transfers between devices: 0.01 us -> 10.2 us  [body(): shares = over(share, 'dp')]
    all_to_all x1 -> x2, starting transfers between devices: 3.87 us -> 8.65 us  [body(): shares = over(share, 'dp')]
    unnamed x16 -> x10, local copies, waits for them, and re-layouts: 4.62 us -> 0.74 us
    pallas_call x10, Pallas kernels: 26.2 us -> 28.1 us  [call(): pl.pallas_call(kernel, out_shape=out_shape, in_specs=[VMEM] * len(args) i...]
    ppermute x1, waiting for transfers between devices: 0.01 us -> 1.65 us  [body(): student_came = lax.ppermute(student_other, 'proto', swap)]
  transfers between devices with their start and end apart: 4 -> 5, of which waited for: 2 -> 3; matrix products, arithmetic and copies ran while one was open for 0% -> 0% of each run, Pallas kernels for 7% -> 7%
where the time goes in v11:
time: 162 us; the launch traced here: 161 us
  blocking collectives  103 us (64%)
  Pallas kernels  28.1 us (17%)
  starting transfers between devices  15.4 us (10%)
  waiting for transfers between devices  13.1 us (8%)
    pallas_call x10, Pallas kernels, call(): pl.pallas_call(kernel, out_shape=out_shape, in_specs=[VMEM] * len(args) i...  28.1 us
    all_to_all x1, blocking collectives, body(): shares = over(share, 'dp')  26.8 us
    all_gather x1, blocking collectives, body(): gathered = lax.all_gather(sent, 'proto', axis=0, tiled=False)  24.3 us
    all_to_all x1, blocking collectives, body(): back = over(sent, 'proto', axis_index_groups=same_core)  23.2 us
    all_to_all x1, blocking collectives, body(): shares = over(share.reshape((width,) + share.shape[2:]), 'proto')  16.5 us
    all_to_all x1, blocking collectives, body(): shares = over(share, 'proto')  11.9 us
    all_to_all x2, waiting for transfers between devices, body(): shares = over(share, 'dp')  10.2 us
    all_to_all x2, starting transfers between devices, body(): shares = over(share, 'dp')  8.65 us
  transfers between devices with their start and end apart: 5, of which 3 were waited for; matrix products, arithmetic and copies ran while one was open for 0% of the time, Pallas kernels for 7%

profile of v11, /device:TPU:1, one launch (start us, length us, event | category | flops | bytes accessed | tf_op | source)
XLA Modules:
  0.0 161.4 jit_solution(13599370182614141583)
XLA Ops:
  1.3 1.8 %shard_map.77 = (bf16[120,256]{1,0:T(8,128)(2,1)S(1)}, bf16[2,32,128]{2,1,0:T(8,128)(2,1)S(1)}, bf16[80,256]{1,0:T(8,128)(2,1)}) custom-call(bf16[256,256]{1,0:T(8,128)(2,1)} %bitcast.9, bf16[256,256]{1,0:T(8,128)(2,1)} %bitcast.10, s32[1,256]{1,0:T(1,128)} %order_ref.3, s32[1,1]{1,0:T(1,128)S(6)} %copy.8.count_ref), custom_call_target="tpu_custom_call" | custom-call | bytes 262144 | tf_op jit(solution)/shard_map/pallas_call | solution.py:33
  3.1 24.3 %all-gather = bf16[1920,256]{1,0:T(8,128)(2,1)S(1)} all-gather(bf16[120,256]{1,0:T(8,128)(2,1)S(1)} %get-tuple-element.24), channel_id=2, replica_groups=mesh['dp'=32,'proto'=16] {'proto'}, dimensions={0}, use_global_device_ids=true | all-gather | bytes 1044480 | tf_op jit(solution)/shard_map/all_gather | solution.py:409
  27.4 0.0 copy-start
  27.4 3.9 %shard_map.78 = (f32[32,32,128]{2,1,0:T(8,128)S(1)}, bf16[384,256]{1,0:T(8,128)(2,1)S(1)}, f32[4,16,128]{2,1,0:T(8,128)}, bf16[256,4096]{1,0:T(8,128)(2,1)S(1)}) custom-call(bf16[16,120,256]{2,1,0:T(8,128)(2,1)S(1)} %bitcast.6, s32[1,1]{1,0:T(1,128)} %bitcast.3.index_ref, bf16[256,4096]{1,0:T(8,128)(2,1)} %far_ref.1), custom_call_target="tpu_custom_call" | custom-call | flops 805306368 | bytes 2097152 | tf_op jit(solution)/shard_map/pallas_call | solution.py:33
  31.3 26.8 %all_to_all.30.shares_ref = f32[32,32,128]{2,1,0:T(8,128)S(1)} all-to-all(f32[32,32,128]{2,1,0:T(8,128)S(1)} %get-tuple-element.25), channel_id=1, replica_groups=mesh['dp'=32,'proto'=16] {'dp'}, dimensions={0} | all-to-all | bytes 1048576 | tf_op jit(solution)/shard_map/all_to_all | solution.py:421
  58.0 0.0 copy-done
  58.0 2.2 %shard_map.79 = (bf16[384,4096]{1,0:T(8,128)(2,1)S(1)}, f32[2,384,1]{2,1,0:T(8,128)S(1)}, bf16[8,2,48,128]{3,2,1,0:T(8,128)(2,1)S(1)}) custom-call(f32[32,32,128]{2,1,0:T(8,128)S(1)} %all_to_all.30.shares_ref, bf16[384,256]{1,0:T(8,128)(2,1)S(1)} %get-tuple-element.26.rows_ref, bf16[256,4096]{1,0:T(8,128)(2,1)S(1)} %get-tuple-element.27.protos_ref, ...), custom_call_target="tpu_custom_call" | custom-call | flops 805306368 | bytes 5242880 | tf_op jit(solution)/shard_map/pallas_call | solution.py:33
  60.2 16.5 %all_to_all.31.shares_ref.late_ref = bf16[16,48,128]{2,1,0:T(8,128)(2,1)} all-to-all(bf16[16,48,128]{2,1,0:T(8,128)(2,1)S(1)} %bitcast.8), channel_id=1, replica_groups=mesh['dp'=32,'proto'=16] {'proto'}, dimensions={0} | all-to-all | bytes 393216 | tf_op jit(solution)/shard_map/all_to_all | solution.py:433
  76.7 2.5 %shard_map.80 = (bf16[32,32,128]{2,1,0:T(8,128)(2,1)}, f32[2,384,1]{2,1,0:T(8,128)S(1)}) custom-call(bf16[16,48,128]{2,1,0:T(8,128)(2,1)} %all_to_all.31.shares_ref.late_ref, f32[2,384,1]{2,1,0:T(8,128)S(1)} %get-tuple-element.30.high_ref, bf16[384,4096]{1,0:T(8,128)(2,1)S(1)} %get-tuple-element.31.matrix_ref), custom_call_target="tpu_custom_call" | custom-call | bytes 3145728 | tf_op jit(solution)/shard_map/pallas_call | solution.py:33
  79.2 4.6 %all-to-all-start.2 = ((bf16[32,32,128]{2,1,0:T(8,128)(2,1)}), bf16[32,32,128]{2,1,0:T(8,128)(2,1)}, u32[]{:S(2)}, u32[]{:S(2)}) async-start(bf16[32,32,128]{2,1,0:T(8,128)(2,1)} %get-tuple-element.32), calls=%async_computation.2 | async-start | bytes 524288 | tf_op jit(solution)/shard_map/all_to_all | solution.py:443
  83.8 1.9 %collective-permute-start = (bf16[16,48,128]{2,1,0:T(8,128)(2,1)}, bf16[16,48,128]{2,1,0:T(8,128)(2,1)}, u32[]{:S(2)}, u32[]{:S(2)}) collective-permute-start(bf16[16,48,128]{2,1,0:T(8,128)(2,1)} %all_to_all.31.shares_ref.late_ref), channel_id=1, source_target_pairs={{0,1},{1,0},{2,3},{3,2},{4,5},{5,4},{6,7},{7,6},{8,9},{9,8},{10,11... | collective-permute-start | bytes 589832 | tf_op jit(solution)/shard_map/ppermute | solution.py:461
  85.7 10.2 %all-to-all-done.2.shares_ref = bf16[32,32,128]{2,1,0:T(8,128)(2,1)} async-done(((bf16[32,32,128]{2,1,0:T(8,128)(2,1)}), bf16[32,32,128]{2,1,0:T(8,128)(2,1)}, u32[]{:S(2)}, u32[]{:S(2)}) %all-to-all-start.2) | async-done | bytes 262176 | tf_op jit(solution)/shard_map/all_to_all | solution.py:443
  96.0 1.8 %shard_map.81 = f32[16,8,128]{2,1,0:T(8,128)S(1)} custom-call(bf16[32,32,128]{2,1,0:T(8,128)(2,1)} %all-to-all-done.2.shares_ref, f32[2,384,1]{2,1,0:T(8,128)S(1)} %get-tuple-element.33.scale_ref.scale_in_ref, bf16[384,4096]{1,0:T(8,128)(2,1)S(1)} %get-tuple-element.31.matrix_ref), custom_call_target="tpu_custom_call" | custom-call | bytes 3145728 | tf_op jit(solution)/shard_map/pallas_call | solution.py:33
  97.8 11.9 %all_to_all.32.shares_ref = f32[16,8,128]{2,1,0:T(8,128)S(1)} all-to-all(f32[16,8,128]{2,1,0:T(8,128)S(1)} %shard_map.81), channel_id=1, replica_groups=mesh['dp'=32,'proto'=16] {'proto'}, dimensions={0} | all-to-all | bytes 131072 | tf_op jit(solution)/shard_map/all_to_all | solution.py:452
  109.7 1.5 shard_map.82
  111.3 4.1 %all-to-all-start.4 = ((bf16[32,32,128]{2,1,0:T(8,128)(2,1)}), bf16[32,32,128]{2,1,0:T(8,128)(2,1)S(1)}, u32[]{:S(2)}, u32[]{:S(2)}) async-start(bf16[32,32,128]{2,1,0:T(8,128)(2,1)} %get-tuple-element.34), calls=%async_computation.4 | async-start | bytes 524288 | tf_op jit(solution)/shard_map/all_to_all | solution.py:479
  115.3 0.0 collective-permute-done.came_ref
  115.3 8.4 %shard_map.83 = (bf16[8,80,256]{2,1,0:T(8,128)(2,1)}, bf16[8,80,256]{2,1,0:T(8,128)(2,1)}) custom-call(bf16[16,120,256]{2,1,0:T(8,128)(2,1)} %bitcast.7, bf16[16,48,128]{2,1,0:T(8,128)(2,1)} %all_to_all.31.shares_ref.late_ref, bf16[16,48,128]{2,1,0:T(8,128)(2,1)} %collective-permute-done.came_ref, s32[1,1]{1,0:T(1,128)} %bitcast.3.index_ref, ...), custom_call_target="tpu_custom_call" | custom-call | flops 1610612736 | bytes 2097152 | tf_op jit(solution)/shard_map/pallas_call | solution.py:33
  123.7 2.1 %collective-permute-start.1 = (bf16[8,80,256]{2,1,0:T(8,128)(2,1)}, bf16[8,80,256]{2,1,0:T(8,128)(2,1)S(1)}, u32[]{:S(2)}, u32[]{:S(2)}) collective-permute-start(bf16[8,80,256]{2,1,0:T(8,128)(2,1)} %get-tuple-element.36), channel_id=1, source_target_pairs={{0,1},{1,0},{2,3},{3,2},{4,5},{5,4},{6,7},{7,6},{8,9},{9,8},{10,11... | collective-permute-start | bytes 983048 | tf_op jit(solution)/shard_map/ppermute | solution.py:478
  125.8 1.7 %collective-permute-done.1.student_came_ref = bf16[8,80,256]{2,1,0:T(8,128)(2,1)S(1)} collective-permute-done((bf16[8,80,256]{2,1,0:T(8,128)(2,1)}, bf16[8,80,256]{2,1,0:T(8,128)(2,1)S(1)}, u32[]{:S(2)}, u32[]{:S(2)}) %collective-permute-start.1) | collective-permute-done | bytes 327712 | tf_op jit(solution)/shard_map/ppermute | solution.py:478
  127.4 0.0 copy-start.2
  127.4 0.7 copy-done.2
  128.2 0.0 all-to-all-done.4.shares_ref
  128.2 0.0 copy-start.1
  128.2 0.0 copy-start.3
  128.2 3.9 %shard_map.84 = (bf16[8,80,256]{2,1,0:T(8,128)(2,1)S(1)}, bf16[8,80,256]{2,1,0:T(8,128)(2,1)S(1)}) custom-call(bf16[32,32,128]{2,1,0:T(8,128)(2,1)S(1)} %all-to-all-done.4.shares_ref, f32[2,384,1]{2,1,0:T(8,128)} %get-tuple-element.38.scale_ref, bf16[384,4096]{1,0:T(8,128)(2,1)S(1)} %get-tuple-element.31.matrix_ref, bf16[256,4096]{1,0:T(8,128)(2,1)} %protos_ref.3, ...), custom_call_target="tpu_custom_call" | custom-call | flops 805306368 | bytes 3145728 | tf_op jit(solution)/shard_map/pallas_call | solution.py:33
  132.0 0.0 copy-start.4
  132.0 2.8 %collective-permute-start.2 = (bf16[8,80,256]{2,1,0:T(8,128)(2,1)S(1)}, bf16[8,80,256]{2,1,0:T(8,128)(2,1)S(1)}, u32[]{:S(2)}, u32[]{:S(2)}) collective-permute-start(bf16[8,80,256]{2,1,0:T(8,128)(2,1)S(1)} %get-tuple-element.40), channel_id=1, source_target_pairs={{0,1},{1,0},{2,3},{3,2},{4,5},{5,4},{6,7},{7,6},{8,9},{9,8},{10,11... | collective-permute-start | bytes 983048 | tf_op jit(solution)/shard_map/ppermute | solution.py:495
  134.8 1.2 collective-permute-done.2.came_ref
  136.1 0.0 copy-done.1
  136.1 0.0 copy-done.3
  136.1 0.4 shard_map.85
  136.5 23.2 %all_to_all.33.back_ref = bf16[8,160,256]{2,1,0:T(8,128)(2,1)S(1)} all-to-all(bf16[8,160,256]{2,1,0:T(8,128)(2,1)S(1)} %shard_map.85), channel_id=1, replica_groups={{0,2,4,6,8,10,12,14},{1,3,5,7,9,11,13,15},{16,18,20,22,24,26,28,30},{17..., dimensions={0} | all-to-all | bytes 1310720 | tf_op jit(solution)/shard_map/all_to_all | solution.py:500
  159.7 0.0 copy-done.4
  159.7 1.7 %shard_map.86 = (bf16[256,256]{1,0:T(8,128)(2,1)}, f32[1,1]{1,0:T(1,128)}) custom-call(bf16[8,160,256]{2,1,0:T(8,128)(2,1)S(1)} %all_to_all.33.back_ref, bf16[80,256]{1,0:T(8,128)(2,1)S(1)} %copy-done.4, s32[1,256]{1,0:T(1,128)} %order_ref.3, s32[1,1]{1,0:T(1,128)S(6)} %copy.8.count_ref), custom_call_target="tpu_custom_call" | custom-call | bytes 131072 | tf_op jit(solution)/shard_map/pallas_call | solution.py:33
Async XLA Ops:
  27.4 30.7 %copy-start = (bf16[1920,256]{1,0:T(8,128)(2,1)}, bf16[1920,256]{1,0:T(8,128)(2,1)S(1)}, u32[]{:S(2)}) copy-start(bf16[1920,256]{1,0:T(8,128)(2,1)S(1)} %all-gather) | copy-start | bytes 2949124
  79.2 16.8 %all-to-all-start.2 = ((bf16[32,32,128]{2,1,0:T(8,128)(2,1)}), bf16[32,32,128]{2,1,0:T(8,128)(2,1)}, u32[]{:S(2)}, u32[]{:S(2)}) async-start(bf16[32,32,128]{2,1,0:T(8,128)(2,1)} %get-tuple-element.32), calls=%async_computation.2 | async-start | bytes 524288 | tf_op jit(solution)/shard_map/all_to_all | solution.py:443
  83.8 31.5 %collective-permute-start = (bf16[16,48,128]{2,1,0:T(8,128)(2,1)}, bf16[16,48,128]{2,1,0:T(8,128)(2,1)}, u32[]{:S(2)}, u32[]{:S(2)}) collective-permute-start(bf16[16,48,128]{2,1,0:T(8,128)(2,1)} %all_to_all.31.shares_ref.late_ref), channel_id=1, source_target_pairs={{0,1},{1,0},{2,3},{3,2},{4,5},{5,4},{6,7},{7,6},{8,9},{9,8},{10,11... | collective-permute-start | bytes 589832 | tf_op jit(solution)/shard_map/ppermute | solution.py:461
  111.3 16.9 %all-to-all-start.4 = ((bf16[32,32,128]{2,1,0:T(8,128)(2,1)}), bf16[32,32,128]{2,1,0:T(8,128)(2,1)S(1)}, u32[]{:S(2)}, u32[]{:S(2)}) async-start(bf16[32,32,128]{2,1,0:T(8,128)(2,1)} %get-tuple-element.34), calls=%async_computation.4 | async-start | bytes 524288 | tf_op jit(solution)/shard_map/all_to_all | solution.py:479
  123.7 3.7 %collective-permute-start.1 = (bf16[8,80,256]{2,1,0:T(8,128)(2,1)}, bf16[8,80,256]{2,1,0:T(8,128)(2,1)S(1)}, u32[]{:S(2)}, u32[]{:S(2)}) collective-permute-start(bf16[8,80,256]{2,1,0:T(8,128)(2,1)} %get-tuple-element.36), channel_id=1, source_target_pairs={{0,1},{1,0},{2,3},{3,2},{4,5},{5,4},{6,7},{7,6},{8,9},{9,8},{10,11... | collective-permute-start | bytes 983048 | tf_op jit(solution)/shard_map/ppermute | solution.py:478
  127.4 0.7 copy-start.2
  128.2 7.9 %copy-start.1 = (bf16[8,80,256]{2,1,0:T(8,128)(2,1)S(1)}, bf16[8,80,256]{2,1,0:T(8,128)(2,1)}, u32[]{:S(2)}) copy-start(bf16[8,80,256]{2,1,0:T(8,128)(2,1)} %get-tuple-element.41.student_own_ref) | copy-start | bytes 983044
  128.2 7.9 %copy-start.3 = (bf16[8,80,256]{2,1,0:T(8,128)(2,1)S(1)}, bf16[8,80,256]{2,1,0:T(8,128)(2,1)}, u32[]{:S(2)}) copy-start(bf16[8,80,256]{2,1,0:T(8,128)(2,1)} %copy-done.2) | copy-start | bytes 983044
  132.0 27.6 %copy-start.4 = (bf16[80,256]{1,0:T(8,128)(2,1)S(1)}, bf16[80,256]{1,0:T(8,128)(2,1)}, u32[]{:S(2)}) copy-start(bf16[80,256]{1,0:T(8,128)(2,1)} %get-tuple-element.43.picked_ref) | copy-start | bytes 122884
  132.0 4.0 %collective-permute-start.2 = (bf16[8,80,256]{2,1,0:T(8,128)(2,1)S(1)}, bf16[8,80,256]{2,1,0:T(8,128)(2,1)S(1)}, u32[]{:S(2)}, u32[]{:S(2)}) collective-permute-start(bf16[8,80,256]{2,1,0:T(8,128)(2,1)S(1)} %get-tuple-element.40), channel_id=1, source_target_pairs={{0,1},{1,0},{2,3},{3,2},{4,5},{5,4},{6,7},{7,6},{8,9},{9,8},{10,11... | collective-permute-start | bytes 983048 | tf_op jit(solution)/shard_map/ppermute | solution.py:495

commit v12 on v11

--- a/solution.py
+++ b/solution.py
@@ -208,7 +208,8 @@
         share_ref[:, lines_of(b)] = jnp.broadcast_to(lines[None], shape).astype(share_ref.dtype)
 
 
-def first_column_kernel(shares_ref, high_ref, matrix_ref, share_ref, scale_ref):
+def first_column_kernel(shares_ref, high_ref, matrix_ref, share_ref, scale_ref, late_ref):
+    late_ref[...] = shares_ref[:, : 2 * LATE]
     lines = scale_ref.shape[1] // LANES
     numbers = shares_ref[:, 2 * LATE :].astype(F32)
     row_lse = merged(sum(numbers[:, k * lines : (k + 1) * lines] for k in range(3)))
@@ -218,10 +219,11 @@
 
 
 def later_column_kernel(shares_ref, scale_in_ref, matrix_ref, share_ref, scale_ref):
-    lines = scale_ref.shape[1] // LANES
+    lines = scale_in_ref.shape[1] // LANES
     total = to_column(jnp.sum(shares_ref[...][:, :lines], axis=0))
     scale = scale_in_ref[...] / total[None]
-    scale_ref[...] = scale
+    for b in range(scale.shape[0]):
+        scale_ref[b] = to_lanes(scale[b])
     column_sums(matrix_ref, scale, share_ref)
 
 
@@ -279,7 +281,7 @@
 
 def target_kernel(shares_ref, scale_ref, matrix_ref, protos_ref, places_ref, own_ref, other_ref, sums, total):
     step = pl.program_id(0)
-    scale = scale_ref[step]
+    scale = to_column(scale_ref[step])
     weights = (matrix_ref[...].astype(F32) * to_row(inverse_of(shares_ref))).astype(BF16)
     part = scale * lax.dot_general(weights, protos_ref[...], (((1,), (1,)), ((), ())), preferred_element_type=F32)
     mass = scale * jnp.sum(weights.astype(F32), axis=1, keepdims=True)
@@ -303,14 +305,13 @@
     width = own_ref.shape[2]
     out_ref[:, :MOST] = (own_ref[:, :MOST].astype(F32) + came_ref[:, :MOST].astype(F32)).astype(BF16)
     total = numbers_of(own_ref, 2) + numbers_of(came_ref, 2)
-    out_ref[:, MOST:SLOT] = join([part[:, None] for part in split(total, 2)], width)
     own, came = numbers_of(student_own_ref, 3), numbers_of(student_came_ref, 3)
     high = jnp.maximum(own, came)
     joint = high + jnp.log(jnp.exp(own - high) + jnp.exp(came - high))
     mean = student_own_ref[:, :MOST].astype(F32) * slots_of(jnp.exp(own - joint))
     mean = mean + student_came_ref[:, :MOST].astype(F32) * slots_of(jnp.exp(came - joint))
-    out_ref[:, SLOT : SLOT + MOST] = mean.astype(BF16)
-    out_ref[:, SLOT + MOST :] = join([part[:, None] for part in split(joint, 3)], width)
+    out_ref[:, MOST : 2 * MOST] = mean.astype(BF16)
+    out_ref[:, 2 * MOST :] = join([part[:, None] for part in split(total, 2) + split(joint, 3)], width)
 
 
 def student_kernel(
@@ -356,12 +357,12 @@
 
 def finish_kernel(back_ref, picked_ref, order_ref, count_ref, grad_ref, loss_ref):
     patches, width = grad_ref.shape
-    target = jnp.sum(back_ref[:, :SLOT].astype(F32), axis=0)
-    mass = to_column((target[MOST : MOST + 1] + target[MOST + 1 : MOST + 2])[:, :LANES])[:MOST]
-    tail = back_ref[:, SLOT + MOST : 2 * SLOT, :LANES].astype(F32)
-    soft, lse_lanes = blend(back_ref[:, SLOT : SLOT + MOST].astype(F32), sum(tail[:, k] for k in range(3)))
+    target = jnp.sum(back_ref[:, :MOST].astype(F32), axis=0)
+    tail = back_ref[:, 2 * MOST :, :LANES].astype(F32)
+    mass = to_column(jnp.sum(tail[:, 0] + tail[:, 1], axis=0, keepdims=True))[:MOST]
+    soft, lse_lanes = blend(back_ref[:, MOST : 2 * MOST].astype(F32), tail[:, 2] + tail[:, 3] + tail[:, 4])
     used = iota((MOST, 1), 0) < count_ref[0, 0]
-    mean = target[:MOST] / jnp.where(used, mass, 1.0)
+    mean = target / jnp.where(used, mass, 1.0)
     own_lse = to_column(lse_lanes.reshape(1, LANES))[:MOST]
     cross = own_lse - STUD * jnp.sum(picked_ref[:MOST].astype(F32) * mean, axis=1, keepdims=True)
     cross = jnp.sum(jnp.where(used, cross, 0.0), axis=0, keepdims=True)
@@ -431,11 +432,14 @@
     )
     swap = [(p, p ^ 1) for p in range(width)]
     shares = over(share.reshape((width,) + share.shape[2:]), "proto")
-    late = shares
-    share, scale = call(
+    share, scale, late = call(
         first_column_kernel,
-        [pltpu.HBM((groups, protos // LANES, LANES), BF16), ((steps, rows, 1), F32)],
-        far(shares),
+        [
+            ((groups, protos // LANES, LANES), BF16),
+            ((steps, rows, 1), F32),
+            pltpu.HBM((width, 2 * LATE, LANES), BF16),
+        ],
+        shares,
         high,
         matrix,
         moved=2 * rows * protos,
@@ -443,7 +447,7 @@
     shares = over(share, "dp")
     share = call(
         later_row_kernel,
-        [((width, depth, LANES), F32)],
+        [pltpu.HBM((width, depth, LANES), F32)],
         shares,
         scale,
         matrix,
@@ -452,7 +456,7 @@
     shares = over(share, "proto")
     share, scale = call(
         later_column_kernel,
-        [pltpu.HBM((groups, protos // LANES, LANES), BF16), pltpu.HBM((steps, rows, 1), F32)],
+        [pltpu.HBM((groups, protos // LANES, LANES), BF16), pltpu.HBM((steps, rows // LANES, LANES), F32)],
         shares,
         scale,
         matrix,
@@ -494,7 +498,7 @@
     )
     came = lax.ppermute(other, "proto", swap)
     sent = call(
-        merge_kernel, [((width // 2, 2 * SLOT, bot), BF16)], own, came, student_own, student_came
+        merge_kernel, [((width // 2, MOST + SLOT, bot), BF16)], own, came, student_own, student_came
     )[0]
     same_core = [list(range(core, width, 2)) for core in range(2)]
     back = over(sent, "proto", axis_index_groups=same_core)

time: 162 us -> 162 us (level)
  waiting for transfers between devices: 13.1 us -> 8.64 us
  blocking collectives: 103 us -> 106 us
    all_to_all x1 -> x2, blocking collectives: 26.8 us -> 43.2 us  [body(): shares = over(share, 'dp')]
    all_to_all x1 -> x0, blocking collectives: 11.9 us -> none  [body(): shares = over(share, 'proto')]
    all_to_all x2 -> x1, waiting for transfers between devices: 10.2 us -> 0.01 us  [body(): shares = over(share, 'dp')]
    all_to_all x0 -> x1, waiting for transfers between devices: none -> 5.74 us  [body(): shares = over(share, 'proto')]
    all_to_all x0 -> x1, starting transfers between devices: none -> 5.45 us  [body(): shares = over(share, 'proto')]
    all_to_all x2 -> x1, starting transfers between devices: 8.65 us -> 4.05 us  [body(): shares = over(share, 'dp')]
where the time goes in v12:
time: 162 us; the launch traced here: 161 us
  blocking collectives  106 us (65%)
  Pallas kernels  27.7 us (17%)
  starting transfers between devices  16.7 us (10%)
  waiting for transfers between devices  8.64 us (5%)
    all_to_all x2, blocking collectives, body(): shares = over(share, 'dp')  43.2 us
    pallas_call x10, Pallas kernels, call(): pl.pallas_call(kernel, out_shape=out_shape, in_specs=[VMEM] * len(args) i...  27.7 us
    all_gather x1, blocking collectives, body(): gathered = lax.all_gather(sent, 'proto', axis=0, tiled=False)  24.3 us
    all_to_all x1, blocking collectives, body(): back = over(sent, 'proto', axis_index_groups=same_core)  22.5 us
    all_to_all x1, blocking collectives, body(): shares = over(share.reshape((width,) + share.shape[2:]), 'proto')  16.4 us
    all_to_all x1, waiting for transfers between devices, body(): shares = over(share, 'proto')  5.74 us
    all_to_all x1, starting transfers between devices, body(): shares = over(share, 'proto')  5.45 us
    all_to_all x1, starting transfers between devices, body(): shares = over(share, 'dp')  4.05 us
  transfers between devices with their start and end apart: 5, of which 3 were waited for; matrix products, arithmetic and copies ran while one was open for 0% of the time, Pallas kernels for 7%

profile of v12, /device:TPU:1, one launch (start us, length us, event | category | flops | bytes accessed | tf_op | source)
XLA Modules:
  0.0 161.5 jit_solution(7961474283419661308)
XLA Ops:
  1.3 1.8 %shard_map.77 = (bf16[120,256]{1,0:T(8,128)(2,1)S(1)}, bf16[2,32,128]{2,1,0:T(8,128)(2,1)S(1)}, bf16[80,256]{1,0:T(8,128)(2,1)}) custom-call(bf16[256,256]{1,0:T(8,128)(2,1)} %bitcast.9, bf16[256,256]{1,0:T(8,128)(2,1)} %bitcast.10, s32[1,256]{1,0:T(1,128)} %order_ref.3, s32[1,1]{1,0:T(1,128)S(6)} %copy.8.count_ref), custom_call_target="tpu_custom_call" | custom-call | bytes 262144 | tf_op jit(solution)/shard_map/pallas_call | solution.py:33
  3.1 24.3 %all-gather = bf16[1920,256]{1,0:T(8,128)(2,1)S(1)} all-gather(bf16[120,256]{1,0:T(8,128)(2,1)S(1)} %get-tuple-element.25), channel_id=2, replica_groups=mesh['dp'=32,'proto'=16] {'proto'}, dimensions={0}, use_global_device_ids=true | all-gather | bytes 1044480 | tf_op jit(solution)/shard_map/all_gather | solution.py:410
  27.3 0.0 copy-start
  27.3 3.9 %shard_map.78 = (f32[32,32,128]{2,1,0:T(8,128)S(1)}, bf16[384,256]{1,0:T(8,128)(2,1)S(1)}, f32[4,16,128]{2,1,0:T(8,128)}, bf16[256,4096]{1,0:T(8,128)(2,1)S(1)}) custom-call(bf16[16,120,256]{2,1,0:T(8,128)(2,1)S(1)} %bitcast.6, s32[1,1]{1,0:T(1,128)} %bitcast.3.index_ref, bf16[256,4096]{1,0:T(8,128)(2,1)} %far_ref.1), custom_call_target="tpu_custom_call" | custom-call | flops 805306368 | bytes 2097152 | tf_op jit(solution)/shard_map/pallas_call | solution.py:33
  31.3 26.7 %all_to_all.30.shares_ref = f32[32,32,128]{2,1,0:T(8,128)S(1)} all-to-all(f32[32,32,128]{2,1,0:T(8,128)S(1)} %get-tuple-element.26), channel_id=1, replica_groups=mesh['dp'=32,'proto'=16] {'dp'}, dimensions={0} | all-to-all | bytes 1048576 | tf_op jit(solution)/shard_map/all_to_all | solution.py:422
  58.0 0.0 copy-done
  58.0 2.2 %shard_map.79 = (bf16[384,4096]{1,0:T(8,128)(2,1)S(1)}, f32[2,384,1]{2,1,0:T(8,128)S(1)}, bf16[8,2,48,128]{3,2,1,0:T(8,128)(2,1)S(1)}) custom-call(f32[32,32,128]{2,1,0:T(8,128)S(1)} %all_to_all.30.shares_ref, bf16[384,256]{1,0:T(8,128)(2,1)S(1)} %get-tuple-element.27.rows_ref, bf16[256,4096]{1,0:T(8,128)(2,1)S(1)} %get-tuple-element.28.protos_ref, ...), custom_call_target="tpu_custom_call" | custom-call | flops 805306368 | bytes 5242880 | tf_op jit(solution)/shard_map/pallas_call | solution.py:33
  60.2 16.4 %all_to_all.31.shares_ref = bf16[16,48,128]{2,1,0:T(8,128)(2,1)S(1)} all-to-all(bf16[16,48,128]{2,1,0:T(8,128)(2,1)S(1)} %bitcast.8), channel_id=1, replica_groups=mesh['dp'=32,'proto'=16] {'proto'}, dimensions={0} | all-to-all | bytes 393216 | tf_op jit(solution)/shard_map/all_to_all | solution.py:434
  76.6 1.5 shard_map.80
  78.0 16.5 %all_to_all.32.shares_ref = bf16[32,32,128]{2,1,0:T(8,128)(2,1)S(1)} all-to-all(bf16[32,32,128]{2,1,0:T(8,128)(2,1)S(1)} %get-tuple-element.33), channel_id=1, replica_groups=mesh['dp'=32,'proto'=16] {'dp'}, dimensions={0} | all-to-all | bytes 524288 | tf_op jit(solution)/shard_map/all_to_all | solution.py:447
  94.5 1.5 shard_map.81
  96.0 5.5 %all-to-all-start.3 = ((f32[16,8,128]{2,1,0:T(8,128)}), f32[16,8,128]{2,1,0:T(8,128)}, u32[]{:S(2)}, u32[]{:S(2)}) async-start(f32[16,8,128]{2,1,0:T(8,128)} %shard_map.81), calls=%async_computation.3 | async-start | bytes 131072 | tf_op jit(solution)/shard_map/all_to_all | solution.py:456
  101.5 2.2 %collective-permute-start = (bf16[16,32,128]{2,1,0:T(8,128)(2,1)}, bf16[16,32,128]{2,1,0:T(8,128)(2,1)}, u32[]{:S(2)}, u32[]{:S(2)}) collective-permute-start(bf16[16,32,128]{2,1,0:T(8,128)(2,1)} %get-tuple-element.36.late_ref), channel_id=1, source_target_pairs={{0,1},{1,0},{2,3},{3,2},{4,5},{5,4},{6,7},{7,6},{8,9},{9,8},{10,11... | collective-permute-start | bytes 393224 | tf_op jit(solution)/shard_map/ppermute | solution.py:465
  103.7 5.7 %all-to-all-done.3.shares_ref = f32[16,8,128]{2,1,0:T(8,128)} async-done(((f32[16,8,128]{2,1,0:T(8,128)}), f32[16,8,128]{2,1,0:T(8,128)}, u32[]{:S(2)}, u32[]{:S(2)}) %all-to-all-start.3) | async-done | bytes 65568 | tf_op jit(solution)/shard_map/all_to_all | solution.py:456
  109.4 2.4 %shard_map.82 = (bf16[32,32,128]{2,1,0:T(8,128)(2,1)}, f32[2,3,128]{2,1,0:T(4,128)}) custom-call(f32[16,8,128]{2,1,0:T(8,128)} %all-to-all-done.3.shares_ref, f32[2,384,1]{2,1,0:T(8,128)S(1)} %get-tuple-element.34.scale_ref.scale_in_ref, bf16[384,4096]{1,0:T(8,128)(2,1)S(1)} %get-tuple-element.32.matrix_ref), custom_call_target="tpu_custom_call" | custom-call | bytes 3145728 | tf_op jit(solution)/shard_map/pallas_call | solution.py:33
  111.8 4.0 %all-to-all-start.4 = ((bf16[32,32,128]{2,1,0:T(8,128)(2,1)}), bf16[32,32,128]{2,1,0:T(8,128)(2,1)S(1)}, u32[]{:S(2)}, u32[]{:S(2)}) async-start(bf16[32,32,128]{2,1,0:T(8,128)(2,1)} %get-tuple-element.35), calls=%async_computation.4 | async-start | bytes 524288 | tf_op jit(solution)/shard_map/all_to_all | solution.py:483
  115.8 0.0 collective-permute-done.came_ref
  115.8 8.4 %shard_map.83 = (bf16[8,80,256]{2,1,0:T(8,128)(2,1)}, bf16[8,80,256]{2,1,0:T(8,128)(2,1)}) custom-call(bf16[16,120,256]{2,1,0:T(8,128)(2,1)} %bitcast.7, bf16[16,32,128]{2,1,0:T(8,128)(2,1)} %get-tuple-element.36.late_ref, bf16[16,32,128]{2,1,0:T(8,128)(2,1)} %collective-permute-done.came_ref, s32[1,1]{1,0:T(1,128)} %bitcast.3.index_ref, ...), custom_call_target="tpu_custom_call" | custom-call | flops 1610612736 | bytes 2097152 | tf_op jit(solution)/shard_map/pallas_call | solution.py:33
  124.2 2.1 %collective-permute-start.1 = (bf16[8,80,256]{2,1,0:T(8,128)(2,1)}, bf16[8,80,256]{2,1,0:T(8,128)(2,1)S(1)}, u32[]{:S(2)}, u32[]{:S(2)}) collective-permute-start(bf16[8,80,256]{2,1,0:T(8,128)(2,1)} %get-tuple-element.38), channel_id=1, source_target_pairs={{0,1},{1,0},{2,3},{3,2},{4,5},{5,4},{6,7},{7,6},{8,9},{9,8},{10,11... | collective-permute-start | bytes 983048 | tf_op jit(solution)/shard_map/ppermute | solution.py:482
  126.3 1.7 %collective-permute-done.1.student_came_ref = bf16[8,80,256]{2,1,0:T(8,128)(2,1)S(1)} collective-permute-done((bf16[8,80,256]{2,1,0:T(8,128)(2,1)}, bf16[8,80,256]{2,1,0:T(8,128)(2,1)S(1)}, u32[]{:S(2)}, u32[]{:S(2)}) %collective-permute-start.1) | collective-permute-done | bytes 327712 | tf_op jit(solution)/shard_map/ppermute | solution.py:482
  127.9 0.0 copy-start.2
  127.9 0.7 copy-done.2
  128.7 0.0 all-to-all-done.4.shares_ref
  128.7 0.0 copy-start.1
  128.7 0.0 copy-start.3
  128.7 4.0 %shard_map.84 = (bf16[8,80,256]{2,1,0:T(8,128)(2,1)S(1)}, bf16[8,80,256]{2,1,0:T(8,128)(2,1)S(1)}) custom-call(bf16[32,32,128]{2,1,0:T(8,128)(2,1)S(1)} %all-to-all-done.4.shares_ref, f32[2,3,128]{2,1,0:T(4,128)} %get-tuple-element.40.scale_ref, bf16[384,4096]{1,0:T(8,128)(2,1)S(1)} %get-tuple-element.32.matrix_ref, bf16[256,4096]{1,0:T(8,128)(2,1)} %protos_ref.3, ...), custom_call_target="tpu_custom_call" | custom-call | flops 805306368 | bytes 3145728 | tf_op jit(solution)/shard_map/pallas_call | solution.py:33
  132.7 0.0 copy-start.4
  132.7 2.9 %collective-permute-start.2 = (bf16[8,80,256]{2,1,0:T(8,128)(2,1)S(1)}, bf16[8,80,256]{2,1,0:T(8,128)(2,1)S(1)}, u32[]{:S(2)}, u32[]{:S(2)}) collective-permute-start(bf16[8,80,256]{2,1,0:T(8,128)(2,1)S(1)} %get-tuple-element.42), channel_id=1, source_target_pairs={{0,1},{1,0},{2,3},{3,2},{4,5},{5,4},{6,7},{7,6},{8,9},{9,8},{10,11... | collective-permute-start | bytes 983048 | tf_op jit(solution)/shard_map/ppermute | solution.py:499
  135.6 1.2 collective-permute-done.2.came_ref
  136.9 0.0 copy-done.1
  136.9 0.0 copy-done.3
  136.9 0.4 shard_map.85
  137.3 22.5 %all_to_all.33.back_ref = bf16[8,152,256]{2,1,0:T(8,128)(2,1)S(1)} all-to-all(bf16[8,152,256]{2,1,0:T(8,128)(2,1)S(1)} %shard_map.85), channel_id=1, replica_groups={{0,2,4,6,8,10,12,14},{1,3,5,7,9,11,13,15},{16,18,20,22,24,26,28,30},{17..., dimensions={0} | all-to-all | bytes 1245184 | tf_op jit(solution)/shard_map/all_to_all | solution.py:504
  159.8 0.0 copy-done.4
  159.8 1.7 %shard_map.86 = (bf16[256,256]{1,0:T(8,128)(2,1)}, f32[1,1]{1,0:T(1,128)}) custom-call(bf16[8,152,256]{2,1,0:T(8,128)(2,1)S(1)} %all_to_all.33.back_ref, bf16[80,256]{1,0:T(8,128)(2,1)S(1)} %copy-done.4, s32[1,256]{1,0:T(1,128)} %order_ref.3, s32[1,1]{1,0:T(1,128)S(6)} %copy.8.count_ref), custom_call_target="tpu_custom_call" | custom-call | bytes 131072 | tf_op jit(solution)/shard_map/pallas_call | solution.py:33
Async XLA Ops:
  27.3 30.7 %copy-start = (bf16[1920,256]{1,0:T(8,128)(2,1)}, bf16[1920,256]{1,0:T(8,128)(2,1)S(1)}, u32[]{:S(2)}) copy-start(bf16[1920,256]{1,0:T(8,128)(2,1)S(1)} %all-gather) | copy-start | bytes 2949124
  96.0 13.4 %all-to-all-start.3 = ((f32[16,8,128]{2,1,0:T(8,128)}), f32[16,8,128]{2,1,0:T(8,128)}, u32[]{:S(2)}, u32[]{:S(2)}) async-start(f32[16,8,128]{2,1,0:T(8,128)} %shard_map.81), calls=%async_computation.3 | async-start | bytes 131072 | tf_op jit(solution)/shard_map/all_to_all | solution.py:456
  101.5 14.4 %collective-permute-start = (bf16[16,32,128]{2,1,0:T(8,128)(2,1)}, bf16[16,32,128]{2,1,0:T(8,128)(2,1)}, u32[]{:S(2)}, u32[]{:S(2)}) collective-permute-start(bf16[16,32,128]{2,1,0:T(8,128)(2,1)} %get-tuple-element.36.late_ref), channel_id=1, source_target_pairs={{0,1},{1,0},{2,3},{3,2},{4,5},{5,4},{6,7},{7,6},{8,9},{9,8},{10,11... | collective-permute-start | bytes 393224 | tf_op jit(solution)/shard_map/ppermute | solution.py:465
  111.8 16.9 %all-to-all-start.4 = ((bf16[32,32,128]{2,1,0:T(8,128)(2,1)}), bf16[32,32,128]{2,1,0:T(8,128)(2,1)S(1)}, u32[]{:S(2)}, u32[]{:S(2)}) async-start(bf16[32,32,128]{2,1,0:T(8,128)(2,1)} %get-tuple-element.35), calls=%async_computation.4 | async-start | bytes 524288 | tf_op jit(solution)/shard_map/all_to_all | solution.py:483
  124.2 3.7 %collective-permute-start.1 = (bf16[8,80,256]{2,1,0:T(8,128)(2,1)}, bf16[8,80,256]{2,1,0:T(8,128)(2,1)S(1)}, u32[]{:S(2)}, u32[]{:S(2)}) collective-permute-start(bf16[8,80,256]{2,1,0:T(8,128)(2,1)} %get-tuple-element.38), channel_id=1, source_target_pairs={{0,1},{1,0},{2,3},{3,2},{4,5},{5,4},{6,7},{7,6},{8,9},{9,8},{10,11... | collective-permute-start | bytes 983048 | tf_op jit(solution)/shard_map/ppermute | solution.py:482
  127.9 0.7 copy-start.2
  128.7 8.2 %copy-start.1 = (bf16[8,80,256]{2,1,0:T(8,128)(2,1)S(1)}, bf16[8,80,256]{2,1,0:T(8,128)(2,1)}, u32[]{:S(2)}) copy-start(bf16[8,80,256]{2,1,0:T(8,128)(2,1)} %get-tuple-element.43.student_own_ref) | copy-start | bytes 983044
  128.7 8.2 %copy-start.3 = (bf16[8,80,256]{2,1,0:T(8,128)(2,1)S(1)}, bf16[8,80,256]{2,1,0:T(8,128)(2,1)}, u32[]{:S(2)}) copy-start(bf16[8,80,256]{2,1,0:T(8,128)(2,1)} %copy-done.2) | copy-start | bytes 983044
  132.7 27.1 %copy-start.4 = (bf16[80,256]{1,0:T(8,128)(2,1)S(1)}, bf16[80,256]{1,0:T(8,128)(2,1)}, u32[]{:S(2)}) copy-start(bf16[80,256]{1,0:T(8,128)(2,1)} %get-tuple-element.45.picked_ref) | copy-start | bytes 122884
  132.7 4.2 %collective-permute-start.2 = (bf16[8,80,256]{2,1,0:T(8,128)(2,1)S(1)}, bf16[8,80,256]{2,1,0:T(8,128)(2,1)S(1)}, u32[]{:S(2)}, u32[]{:S(2)}) collective-permute-start(bf16[8,80,256]{2,1,0:T(8,128)(2,1)S(1)} %get-tuple-element.42), channel_id=1, source_target_pairs={{0,1},{1,0},{2,3},{3,2},{4,5},{5,4},{6,7},{7,6},{8,9},{9,8},{10,11... | collective-permute-start | bytes 983048 | tf_op jit(solution)/shard_map/ppermute | solution.py:499

commit v13 on v12

--- a/solution.py
+++ b/solution.py
@@ -9,8 +9,9 @@
 
 MASK_DEV = 24
 MOST = 72
-EARLY = 40
-LATE = (MOST - EARLY) // 2
+EARLY = 48
+LATE = MOST - EARLY
+UNUSED = 100.0
 SLOT = 80
 TEACH = 1.0 / 0.07
 STUD = 1.0 / 0.1
@@ -109,11 +110,10 @@
     dims = (((0,), (0,)), ((), ()))
     teacher = lax.dot_general(chosen, teacher_ref[...], dims, preferred_element_type=F32)
     student = lax.dot_general(chosen, student_ref[...], dims, preferred_element_type=F32)
-    count = jnp.full((SLOT - MOST, width), count_ref[0, 0], jnp.int32).astype(F32)
-    sent_ref[...] = jnp.concatenate([teacher[:MOST], count, student[:EARLY]], axis=0).astype(BF16)
-    for half in range(2):
-        late = student[EARLY + half * LATE : EARLY + (half + 1) * LATE]
-        late_ref[half] = jnp.concatenate([late[:, :LANES], late[:, LANES:]], axis=0).astype(BF16)
+    teacher = jnp.where(iota((MOST, width), 0) < count_ref[0, 0], teacher[:MOST], UNUSED)
+    sent_ref[...] = jnp.concatenate([student[:EARLY], teacher], axis=0).astype(BF16)
+    late = student[EARLY:MOST]
+    late_ref[...] = jnp.concatenate([late[:, :LANES], late[:, LANES:]], axis=0).astype(BF16)
     picked_ref[...] = student[:SLOT].astype(BF16)
 
 
@@ -142,7 +142,8 @@
 def column_kernel(gathered_ref, index_ref, far_ref, share_ref, rows_ref, places_ref, near_ref, sems):
     block, blocks = fetch(far_ref, near_ref, sems)
     images = gathered_ref.shape[0]
-    counts = gathered_ref[:, MOST:SLOT, :LANES].astype(F32)[:, 0]
+    teacher = gathered_ref[:, EARLY:]
+    counts = jnp.sum((teacher[:, :, :LANES].astype(F32) < UNUSED / 2).astype(F32), axis=1)
     before = (iota((images, images), 1) < iota((images, images), 0)).astype(BF16)
     starts = jnp.dot(before, counts.astype(BF16), preferred_element_type=F32)
     half, core = images // 2, index_ref[0, 0] % 2
@@ -153,7 +154,7 @@
     places_ref[1] = jnp.dot((other == image).astype(BF16), counts.astype(BF16), preferred_element_type=F32)
     places_ref[2] = starts
     places_ref[3] = counts
-    rows = compact(gathered_ref[:, :SLOT], starts, counts, rows_ref.shape[0], 0, MOST, 0).astype(BF16)
+    rows = compact(teacher, starts, counts, rows_ref.shape[0], 0, MOST, 0).astype(BF16)
     rows_ref[...] = rows
     for b in blocks:
         logits = jnp.dot(rows, block(b), preferred_element_type=F32) * TEACH
@@ -193,11 +194,9 @@
     top = functools.reduce(jnp.maximum, highs)
     total = sum(jnp.exp(high - top) * part for high, part in zip(highs, sums))
     own = jnp.concatenate([part.astype(F32) for part in split(to_lanes(top + jnp.log(total)), 3)], axis=0)
-    blank = jnp.zeros((share_ref.shape[2] - 2 * LATE - own.shape[0], LANES), F32)
-    numbers = jnp.concatenate([own, blank], axis=0).astype(BF16)
-    for half in range(2):
-        chunk = jnp.concatenate([late_ref[half], numbers], axis=0)
-        share_ref[:, half] = jnp.broadcast_to(chunk[None], (share_ref.shape[0],) + chunk.shape)
+    blank = jnp.zeros((share_ref.shape[1] - 2 * LATE - own.shape[0], LANES), F32)
+    chunk = jnp.concatenate([late_ref[...].astype(F32), own, blank], axis=0).astype(BF16)
+    share_ref[...] = jnp.broadcast_to(chunk[None], share_ref.shape)
 
 
 def column_sums(matrix_ref, scale, share_ref):
@@ -208,8 +207,7 @@
         share_ref[:, lines_of(b)] = jnp.broadcast_to(lines[None], shape).astype(share_ref.dtype)
 
 
-def first_column_kernel(shares_ref, high_ref, matrix_ref, share_ref, scale_ref, late_ref):
-    late_ref[...] = shares_ref[:, : 2 * LATE]
+def first_column_kernel(shares_ref, high_ref, matrix_ref, share_ref, scale_ref):
     lines = scale_ref.shape[1] // LANES
     numbers = shares_ref[:, 2 * LATE :].astype(F32)
     row_lse = merged(sum(numbers[:, k * lines : (k + 1) * lines] for k in range(3)))
@@ -315,18 +313,16 @@
 
 
 def student_kernel(
-    gathered_ref, late_ref, came_ref, index_ref, places_ref, protos_ref, own_ref, other_ref, rows_ref, sums, top, total
+    gathered_ref, shares_ref, places_ref, protos_ref, own_ref, other_ref, rows_ref, sums, top, total
 ):
     step = pl.program_id(0)
 
     @pl.when(step == 0)
     def _():
-        starts, counts, core = places_ref[2], places_ref[3], index_ref[0, 0] % 2
-        rows = rows_ref.shape[0]
-        found = compact(gathered_ref[:, SLOT:], starts, counts, rows, 0, EARLY, 0)
-        for ref, half in ((late_ref, core), (came_ref, 1 - core)):
-            late = jnp.concatenate([ref[:, :LATE], ref[:, LATE : 2 * LATE]], axis=2)
-            found += compact(late, starts, counts, rows, 0, LATE, EARLY + half * LATE)
+        starts, counts, rows = places_ref[2], places_ref[3], rows_ref.shape[0]
+        late = jnp.concatenate([shares_ref[:, :LATE], shares_ref[:, LATE : 2 * LATE]], axis=2)
+        found = compact(gathered_ref[...], starts, counts, rows, 0, EARLY, 0)
+        found += compact(late, starts, counts, rows, 0, LATE, EARLY)
         rows_ref[...] = found.astype(BF16)
         top[...] = jnp.full(top.shape, -1e30, F32)
         total[...] = jnp.zeros(total.shape, F32)
@@ -399,7 +395,7 @@
 
     sent, late, picked = call(
         pick_kernel,
-        [((SLOT + EARLY, bot), BF16), ((2, 2 * LATE, LANES), BF16), pltpu.HBM((SLOT, bot), BF16)],
+        [((EARLY + MOST, bot), BF16), ((2 * LATE, LANES), BF16), pltpu.HBM((SLOT, bot), BF16)],
         teacher_patches,
         student_patches,
         mask_order,
@@ -422,7 +418,7 @@
     shares = over(share, "dp")
     matrix, high, share = call(
         row_kernel,
-        [((rows, protos), BF16), ((steps, rows, 1), F32), ((width // 2, 2, 2 * LATE + 16, LANES), BF16)],
+        [((rows, protos), BF16), ((steps, rows, 1), F32), ((width, 2 * LATE + 16, LANES), BF16)],
         shares,
         teacher_rows,
         near_teacher,
@@ -431,13 +427,12 @@
         moved=2 * bot * protos + 2 * rows * protos,
     )
     swap = [(p, p ^ 1) for p in range(width)]
-    shares = over(share.reshape((width,) + share.shape[2:]), "proto")
-    share, scale, late = call(
+    shares = row_shares = over(share, "proto")
+    share, scale = call(
         first_column_kernel,
         [
             ((groups, protos // LANES, LANES), BF16),
             ((steps, rows, 1), F32),
-            pltpu.HBM((width, 2 * LATE, LANES), BF16),
         ],
         shares,
         high,
@@ -447,7 +442,7 @@
     shares = over(share, "dp")
     share = call(
         later_row_kernel,
-        [pltpu.HBM((width, depth, LANES), F32)],
+        [((width, depth, LANES), F32)],
         shares,
         scale,
         matrix,
@@ -462,19 +457,16 @@
         matrix,
         moved=2 * rows * protos,
     )
-    late_came = lax.ppermute(late, "proto", swap)
     packed = ((width // 2, SLOT, bot), BF16)
     student_own, student_other = call(
         student_kernel,
         [pltpu.HBM(*packed), pltpu.HBM(*packed)],
         far(gathered),
-        far(late),
-        late_came,
-        index,
+        far(row_shares),
         far(places),
         student_protos,
         grid=grid,
-        in_specs=[VMEM, VMEM, VMEM, SMEM, VMEM, wide],
+        in_specs=[pl.BlockSpec((width, EARLY, bot), lambda k: (0, 0, 0)), VMEM, VMEM, wide],
         scratch=[pltpu.VMEM((rows, bot), BF16), pltpu.VMEM((rows, bot), F32), column, column],
         flops=2 * dot,
         moved=2 * bot * protos,

time: 162 us -> 160 us (0.988)
  blocking collectives: 106 us -> 119 us
  starting transfers between devices: 16.7 us -> 9.28 us
  waiting for transfers between devices: 8.64 us -> 2.76 us
  Pallas kernels: 27.7 us -> 25.6 us
    all_to_all x1 -> x2, blocking collectives: 16.4 us -> 28.9 us  [the longest x1 17.8 us: body(): shares = row_shares = over(share, 'proto')]
    all_to_all x1 -> x0, waiting for transfers between devices: 5.74 us -> none  [body(): shares = over(share, 'proto')]
    all_to_all x1 -> x0, starting transfers between devices: 5.45 us -> none  [body(): shares = over(share, 'proto')]
    ppermute x1 -> x0, starting transfers between devices: 2.19 us -> none  [body(): late_came = lax.ppermute(late, 'proto', swap)]
    pallas_call x10, Pallas kernels: 27.7 us -> 25.6 us  [call(): pl.pallas_call(kernel, out_shape=out_shape, in_specs=[VMEM] * len(args) i...]
  transfers between devices with their start and end apart: 5 -> 3, of which waited for: 3 -> 2; matrix products, arithmetic and copies ran while one was open for 0% -> 0% of each run, Pallas kernels for 7% -> 5%
where the time goes in v13:
time: 160 us; the launch traced here: 159 us
  blocking collectives  119 us (74%)
  Pallas kernels  25.6 us (16%)
  starting transfers between devices  9.28 us (6%)
  waiting for transfers between devices  2.76 us (2%)
    all_to_all x2, blocking collectives, body(): shares = over(share, 'dp')  43.8 us
    pallas_call x10, Pallas kernels, call(): pl.pallas_call(kernel, out_shape=out_shape, in_specs=[VMEM] * len(args) i...  25.6 us
    all_gather x1, blocking collectives, body(): gathered = lax.all_gather(sent, 'proto', axis=0, tiled=False)  24.3 us
    all_to_all x1, blocking collectives, body(): back = over(sent, 'proto', axis_index_groups=same_core)  22.5 us
    all_to_all x1, blocking collectives, body(): shares = row_shares = over(share, 'proto')  17.8 us
    all_to_all x1, blocking collectives, body(): shares = over(share, 'proto')  11.2 us
    all_to_all x1, starting transfers between devices, body(): shares = over(share, 'dp')  4.05 us
  transfers between devices with their start and end apart: 3, of which 2 were waited for; matrix products, arithmetic and copies ran while one was open for 0% of the time, Pallas kernels for 5%

profile of v13, /device:TPU:1, one launch (start us, length us, event | category | flops | bytes accessed | tf_op | source)
XLA Modules:
  0.0 159.2 jit_solution(16183178576163226069)
XLA Ops:
  1.3 1.8 %shard_map.77 = (bf16[120,256]{1,0:T(8,128)(2,1)S(1)}, bf16[48,128]{1,0:T(8,128)(2,1)S(1)}, bf16[80,256]{1,0:T(8,128)(2,1)}) custom-call(bf16[256,256]{1,0:T(8,128)(2,1)} %bitcast.7, bf16[256,256]{1,0:T(8,128)(2,1)} %bitcast.8, s32[1,256]{1,0:T(1,128)} %order_ref.3, s32[1,1]{1,0:T(1,128)S(6)} %copy.8.count_ref), custom_call_target="tpu_custom_call" | custom-call | bytes 262144 | tf_op jit(solution)/shard_map/pallas_call | solution.py:34
  3.1 24.3 %all-gather = bf16[1920,256]{1,0:T(8,128)(2,1)S(1)} all-gather(bf16[120,256]{1,0:T(8,128)(2,1)S(1)} %get-tuple-element.24), channel_id=2, replica_groups=mesh['dp'=32,'proto'=16] {'proto'}, dimensions={0}, use_global_device_ids=true | all-gather | bytes 1044480 | tf_op jit(solution)/shard_map/all_gather | solution.py:406
  27.4 0.0 copy-start
  27.4 4.0 %shard_map.78 = (f32[32,32,128]{2,1,0:T(8,128)S(1)}, bf16[384,256]{1,0:T(8,128)(2,1)S(1)}, f32[4,16,128]{2,1,0:T(8,128)}, bf16[256,4096]{1,0:T(8,128)(2,1)S(1)}) custom-call(bf16[16,120,256]{2,1,0:T(8,128)(2,1)S(1)} %bitcast.5, s32[1,1]{1,0:T(1,128)} %bitcast.3.index_ref, bf16[256,4096]{1,0:T(8,128)(2,1)} %far_ref.1), custom_call_target="tpu_custom_call" | custom-call | flops 805306368 | bytes 2097152 | tf_op jit(solution)/shard_map/pallas_call | solution.py:34
  31.3 26.8 %all_to_all.30.shares_ref = f32[32,32,128]{2,1,0:T(8,128)S(1)} all-to-all(f32[32,32,128]{2,1,0:T(8,128)S(1)} %get-tuple-element.25), channel_id=1, replica_groups=mesh['dp'=32,'proto'=16] {'dp'}, dimensions={0} | all-to-all | bytes 1048576 | tf_op jit(solution)/shard_map/all_to_all | solution.py:418
  58.1 0.0 copy-done
  58.1 2.2 %shard_map.79 = (bf16[384,4096]{1,0:T(8,128)(2,1)S(1)}, f32[2,384,1]{2,1,0:T(8,128)S(1)}, bf16[16,64,128]{2,1,0:T(8,128)(2,1)S(1)}) custom-call(f32[32,32,128]{2,1,0:T(8,128)S(1)} %all_to_all.30.shares_ref, bf16[384,256]{1,0:T(8,128)(2,1)S(1)} %get-tuple-element.26.rows_ref, bf16[256,4096]{1,0:T(8,128)(2,1)S(1)} %get-tuple-element.27.protos_ref, ...), custom_call_target="tpu_custom_call" | custom-call | flops 805306368 | bytes 5242880 | tf_op jit(solution)/shard_map/pallas_call | solution.py:34
  60.3 17.8 %all_to_all.31.shares_ref = bf16[16,64,128]{2,1,0:T(8,128)(2,1)S(1)} all-to-all(bf16[16,64,128]{2,1,0:T(8,128)(2,1)S(1)} %get-tuple-element.29), channel_id=1, replica_groups=mesh['dp'=32,'proto'=16] {'proto'}, dimensions={0} | all-to-all | bytes 524288 | tf_op jit(solution)/shard_map/all_to_all | solution.py:430
  78.1 0.0 copy-start.1
  78.1 0.9 shard_map.80
  79.0 17.0 %all_to_all.32.shares_ref = bf16[32,32,128]{2,1,0:T(8,128)(2,1)S(1)} all-to-all(bf16[32,32,128]{2,1,0:T(8,128)(2,1)S(1)} %get-tuple-element.32), channel_id=1, replica_groups=mesh['dp'=32,'proto'=16] {'dp'}, dimensions={0} | all-to-all | bytes 524288 | tf_op jit(solution)/shard_map/all_to_all | solution.py:442
  96.0 0.0 copy-done.1
  96.0 0.9 shard_map.81
  96.9 11.2 %all_to_all.33.shares_ref = f32[16,8,128]{2,1,0:T(8,128)S(1)} all-to-all(f32[16,8,128]{2,1,0:T(8,128)S(1)} %shard_map.81), channel_id=1, replica_groups=mesh['dp'=32,'proto'=16] {'proto'}, dimensions={0} | all-to-all | bytes 131072 | tf_op jit(solution)/shard_map/all_to_all | solution.py:451
  108.1 1.5 shard_map.82
  109.6 4.0 %all-to-all-start.4 = ((bf16[32,32,128]{2,1,0:T(8,128)(2,1)}), bf16[32,32,128]{2,1,0:T(8,128)(2,1)S(1)}, u32[]{:S(2)}, u32[]{:S(2)}) async-start(bf16[32,32,128]{2,1,0:T(8,128)(2,1)} %get-tuple-element.34), calls=%async_computation.4 | async-start | bytes 524288 | tf_op jit(solution)/shard_map/all_to_all | solution.py:475
  113.6 8.1 %shard_map.83 = (bf16[8,80,256]{2,1,0:T(8,128)(2,1)}, bf16[8,80,256]{2,1,0:T(8,128)(2,1)}) custom-call(bf16[16,120,256]{2,1,0:T(8,128)(2,1)} %bitcast.6, bf16[16,64,128]{2,1,0:T(8,128)(2,1)} %copy-done.1, f32[4,16,128]{2,1,0:T(8,128)} %get-tuple-element.35.places_ref, bf16[256,4096]{1,0:T(8,128)(2,1)} %protos_ref.3), custom_call_target="tpu_custom_call" | custom-call | flops 1610612736 | bytes 2097152 | tf_op jit(solution)/shard_map/pallas_call | solution.py:34
  121.8 2.2 %collective-permute-start = (bf16[8,80,256]{2,1,0:T(8,128)(2,1)}, bf16[8,80,256]{2,1,0:T(8,128)(2,1)S(1)}, u32[]{:S(2)}, u32[]{:S(2)}) collective-permute-start(bf16[8,80,256]{2,1,0:T(8,128)(2,1)} %get-tuple-element.36), channel_id=1, source_target_pairs={{0,1},{1,0},{2,3},{3,2},{4,5},{5,4},{6,7},{7,6},{8,9},{9,8},{10,11... | collective-permute-start | bytes 983048 | tf_op jit(solution)/shard_map/ppermute | solution.py:474
  124.0 1.5 collective-permute-done.student_came_ref
  125.5 0.0 copy-start.3
  125.5 0.7 copy-done.3
  126.2 0.0 all-to-all-done.4.shares_ref
  126.2 0.0 copy-start.2
  126.2 0.0 copy-start.4
  126.2 4.0 %shard_map.84 = (bf16[8,80,256]{2,1,0:T(8,128)(2,1)S(1)}, bf16[8,80,256]{2,1,0:T(8,128)(2,1)S(1)}) custom-call(bf16[32,32,128]{2,1,0:T(8,128)(2,1)S(1)} %all-to-all-done.4.shares_ref, f32[2,3,128]{2,1,0:T(4,128)} %get-tuple-element.38.scale_ref, bf16[384,4096]{1,0:T(8,128)(2,1)S(1)} %get-tuple-element.31.matrix_ref, bf16[256,4096]{1,0:T(8,128)(2,1)} %protos_ref.3, ...), custom_call_target="tpu_custom_call" | custom-call | flops 805306368 | bytes 3145728 | tf_op jit(solution)/shard_map/pallas_call | solution.py:34
  130.3 0.0 copy-start.5
  130.3 3.0 %collective-permute-start.1 = (bf16[8,80,256]{2,1,0:T(8,128)(2,1)S(1)}, bf16[8,80,256]{2,1,0:T(8,128)(2,1)S(1)}, u32[]{:S(2)}, u32[]{:S(2)}) collective-permute-start(bf16[8,80,256]{2,1,0:T(8,128)(2,1)S(1)} %get-tuple-element.40), channel_id=1, source_target_pairs={{0,1},{1,0},{2,3},{3,2},{4,5},{5,4},{6,7},{7,6},{8,9},{9,8},{10,11... | collective-permute-start | bytes 983048 | tf_op jit(solution)/shard_map/ppermute | solution.py:491
  133.3 1.2 collective-permute-done.1.came_ref
  134.6 0.0 copy-done.2
  134.6 0.0 copy-done.4
  134.6 0.4 shard_map.85
  135.0 22.5 %all_to_all.34.back_ref = bf16[8,152,256]{2,1,0:T(8,128)(2,1)S(1)} all-to-all(bf16[8,152,256]{2,1,0:T(8,128)(2,1)S(1)} %shard_map.85), channel_id=1, replica_groups={{0,2,4,6,8,10,12,14},{1,3,5,7,9,11,13,15},{16,18,20,22,24,26,28,30},{17..., dimensions={0} | all-to-all | bytes 1245184 | tf_op jit(solution)/shard_map/all_to_all | solution.py:496
  157.4 0.0 copy-done.5
  157.4 1.7 %shard_map.86 = (bf16[256,256]{1,0:T(8,128)(2,1)}, f32[1,1]{1,0:T(1,128)}) custom-call(bf16[8,152,256]{2,1,0:T(8,128)(2,1)S(1)} %all_to_all.34.back_ref, bf16[80,256]{1,0:T(8,128)(2,1)S(1)} %copy-done.5, s32[1,256]{1,0:T(1,128)} %order_ref.3, s32[1,1]{1,0:T(1,128)S(6)} %copy.8.count_ref), custom_call_target="tpu_custom_call" | custom-call | bytes 131072 | tf_op jit(solution)/shard_map/pallas_call | solution.py:34
Async XLA Ops:
  27.4 30.7 %copy-start = (bf16[1920,256]{1,0:T(8,128)(2,1)}, bf16[1920,256]{1,0:T(8,128)(2,1)S(1)}, u32[]{:S(2)}) copy-start(bf16[1920,256]{1,0:T(8,128)(2,1)S(1)} %all-gather) | copy-start | bytes 2949124
  78.1 17.9 %copy-start.1 = (bf16[16,64,128]{2,1,0:T(8,128)(2,1)}, bf16[16,64,128]{2,1,0:T(8,128)(2,1)S(1)}, u32[]{:S(2)}) copy-start(bf16[16,64,128]{2,1,0:T(8,128)(2,1)S(1)} %all_to_all.31.shares_ref) | copy-start | bytes 786436
  109.6 16.6 %all-to-all-start.4 = ((bf16[32,32,128]{2,1,0:T(8,128)(2,1)}), bf16[32,32,128]{2,1,0:T(8,128)(2,1)S(1)}, u32[]{:S(2)}, u32[]{:S(2)}) async-start(bf16[32,32,128]{2,1,0:T(8,128)(2,1)} %get-tuple-element.34), calls=%async_computation.4 | async-start | bytes 524288 | tf_op jit(solution)/shard_map/all_to_all | solution.py:475
  121.8 3.7 %collective-permute-start = (bf16[8,80,256]{2,1,0:T(8,128)(2,1)}, bf16[8,80,256]{2,1,0:T(8,128)(2,1)S(1)}, u32[]{:S(2)}, u32[]{:S(2)}) collective-permute-start(bf16[8,80,256]{2,1,0:T(8,128)(2,1)} %get-tuple-element.36), channel_id=1, source_target_pairs={{0,1},{1,0},{2,3},{3,2},{4,5},{5,4},{6,7},{7,6},{8,9},{9,8},{10,11... | collective-permute-start | bytes 983048 | tf_op jit(solution)/shard_map/ppermute | solution.py:474
  125.5 0.7 copy-start.3
  126.2 8.3 %copy-start.2 = (bf16[8,80,256]{2,1,0:T(8,128)(2,1)S(1)}, bf16[8,80,256]{2,1,0:T(8,128)(2,1)}, u32[]{:S(2)}) copy-start(bf16[8,80,256]{2,1,0:T(8,128)(2,1)} %get-tuple-element.41.student_own_ref) | copy-start | bytes 983044
  126.2 8.3 %copy-start.4 = (bf16[8,80,256]{2,1,0:T(8,128)(2,1)S(1)}, bf16[8,80,256]{2,1,0:T(8,128)(2,1)}, u32[]{:S(2)}) copy-start(bf16[8,80,256]{2,1,0:T(8,128)(2,1)} %copy-done.3) | copy-start | bytes 983044
  130.3 27.2 %copy-start.5 = (bf16[80,256]{1,0:T(8,128)(2,1)S(1)}, bf16[80,256]{1,0:T(8,128)(2,1)}, u32[]{:S(2)}) copy-start(bf16[80,256]{1,0:T(8,128)(2,1)} %get-tuple-element.43.picked_ref) | copy-start | bytes 122884
  130.3 4.3 %collective-permute-start.1 = (bf16[8,80,256]{2,1,0:T(8,128)(2,1)S(1)}, bf16[8,80,256]{2,1,0:T(8,128)(2,1)S(1)}, u32[]{:S(2)}, u32[]{:S(2)}) collective-permute-start(bf16[8,80,256]{2,1,0:T(8,128)(2,1)S(1)} %get-tuple-element.40), channel_id=1, source_target_pairs={{0,1},{1,0},{2,3},{3,2},{4,5},{5,4},{6,7},{7,6},{8,9},{9,8},{10,11... | collective-permute-start | bytes 983048 | tf_op jit(solution)/shard_map/ppermute | solution.py:491

commit v14 on v13

--- a/solution.py
+++ b/solution.py
@@ -9,12 +9,13 @@
 
 MASK_DEV = 24
 MOST = 72
-EARLY = 48
+EARLY = 54
 LATE = MOST - EARLY
 UNUSED = 100.0
 SLOT = 80
 TEACH = 1.0 / 0.07
 STUD = 1.0 / 0.1
+LOG2E = 1.4426950408889634
 F32 = jnp.float32
 BF16 = jnp.bfloat16
 LANES = 128
@@ -111,7 +112,7 @@
     teacher = lax.dot_general(chosen, teacher_ref[...], dims, preferred_element_type=F32)
     student = lax.dot_general(chosen, student_ref[...], dims, preferred_element_type=F32)
     teacher = jnp.where(iota((MOST, width), 0) < count_ref[0, 0], teacher[:MOST], UNUSED)
-    sent_ref[...] = jnp.concatenate([student[:EARLY], teacher], axis=0).astype(BF16)
+    sent_ref[...] = jnp.concatenate([teacher, student[:EARLY]], axis=0).astype(BF16)
     late = student[EARLY:MOST]
     late_ref[...] = jnp.concatenate([late[:, :LANES], late[:, LANES:]], axis=0).astype(BF16)
     picked_ref[...] = student[:SLOT].astype(BF16)
@@ -130,6 +131,12 @@
     return jnp.dot(chosen, gathered.reshape(total, width), preferred_element_type=F32)
 
 
+def padded(values):
+    images, slots, width = values.shape
+    blank = jnp.zeros((images, -slots % 8, width), F32)
+    return jnp.concatenate([values, blank], axis=1).astype(BF16)
+
+
 def spread(starts, counts, slots, rows):
     images = starts.shape[0]
     shape = (images, slots, rows)
@@ -142,7 +149,7 @@
 def column_kernel(gathered_ref, index_ref, far_ref, share_ref, rows_ref, places_ref, near_ref, sems):
     block, blocks = fetch(far_ref, near_ref, sems)
     images = gathered_ref.shape[0]
-    teacher = gathered_ref[:, EARLY:]
+    teacher = gathered_ref[:, :MOST]
     counts = jnp.sum((teacher[:, :, :LANES].astype(F32) < UNUSED / 2).astype(F32), axis=1)
     before = (iota((images, images), 1) < iota((images, images), 0)).astype(BF16)
     starts = jnp.dot(before, counts.astype(BF16), preferred_element_type=F32)
@@ -157,10 +164,10 @@
     rows = compact(teacher, starts, counts, rows_ref.shape[0], 0, MOST, 0).astype(BF16)
     rows_ref[...] = rows
     for b in blocks:
-        logits = jnp.dot(rows, block(b), preferred_element_type=F32) * TEACH
-        high = jnp.max(logits, axis=0, keepdims=True)
-        total = jnp.sum(jnp.exp(logits - high), axis=0, keepdims=True)
-        lines = to_lines(high + jnp.log(total))
+        products = jnp.dot(rows, block(b), preferred_element_type=F32)
+        high = jnp.max(products, axis=0, keepdims=True)
+        total = jnp.sum(jnp.exp2((products - high) * (TEACH * LOG2E)), axis=0, keepdims=True)
+        lines = to_lines(high * TEACH + jnp.log(total))
         share_ref[:, lines_of(b)] = jnp.broadcast_to(lines[None], (share_ref.shape[0],) + lines.shape)
 
 
@@ -183,10 +190,11 @@
     rows = rows_ref[...]
     highs, sums = [], []
     for b in range(high_ref.shape[0]):
-        logits = jnp.dot(rows, protos_ref[:, columns(b)], preferred_element_type=F32) * TEACH
-        shifted = logits - to_row(column[lines_of(b)])
+        products = jnp.dot(rows, protos_ref[:, columns(b)], preferred_element_type=F32)
+        shifted = products * (TEACH * LOG2E) - to_row(column[lines_of(b)] * LOG2E)
         high = jnp.max(shifted, axis=1, keepdims=True)
-        exact = jnp.exp(shifted - high)
+        exact = jnp.exp2(shifted - high)
+        high = high * (1.0 / LOG2E)
         matrix_ref[:, columns(b)] = exact.astype(BF16)
         high_ref[b] = high
         highs.append(high)
@@ -209,7 +217,7 @@
 
 def first_column_kernel(shares_ref, high_ref, matrix_ref, share_ref, scale_ref):
     lines = scale_ref.shape[1] // LANES
-    numbers = shares_ref[:, 2 * LATE :].astype(F32)
+    numbers = shares_ref[...].astype(F32)[:, 2 * LATE :]
     row_lse = merged(sum(numbers[:, k * lines : (k + 1) * lines] for k in range(3)))
     scale = jnp.exp(high_ref[...] - to_column(row_lse)[None])
     scale_ref[...] = scale
@@ -320,20 +328,22 @@
     @pl.when(step == 0)
     def _():
         starts, counts, rows = places_ref[2], places_ref[3], rows_ref.shape[0]
-        late = jnp.concatenate([shares_ref[:, :LATE], shares_ref[:, LATE : 2 * LATE]], axis=2)
-        found = compact(gathered_ref[...], starts, counts, rows, 0, EARLY, 0)
-        found += compact(late, starts, counts, rows, 0, LATE, EARLY)
+        late = shares_ref[...].astype(F32)
+        late = jnp.concatenate([late[:, :LATE], late[:, LATE : 2 * LATE]], axis=2)
+        early = gathered_ref[:, MOST:].astype(F32)
+        found = compact(padded(early), starts, counts, rows, 0, EARLY, 0)
+        found += compact(padded(late), starts, counts, rows, 0, LATE, EARLY)
         rows_ref[...] = found.astype(BF16)
         top[...] = jnp.full(top.shape, -1e30, F32)
         total[...] = jnp.zeros(total.shape, F32)
         sums[...] = jnp.zeros(sums.shape, F32)
 
     protos = protos_ref[...]
-    logits = jnp.dot(rows_ref[...], protos, preferred_element_type=F32) * STUD
+    products = jnp.dot(rows_ref[...], protos, preferred_element_type=F32)
     before = top[...]
-    high = jnp.maximum(before, jnp.max(logits, axis=1, keepdims=True))
-    shrink = jnp.exp(before - high)
-    exact = jnp.exp(logits - high)
+    high = jnp.maximum(before, jnp.max(products, axis=1, keepdims=True))
+    shrink = jnp.exp2((before - high) * (STUD * LOG2E))
+    exact = jnp.exp2((products - high) * (STUD * LOG2E))
     total[...] = total[...] * shrink + jnp.sum(exact, axis=1, keepdims=True)
     part = lax.dot_general(exact.astype(BF16), protos, (((1,), (1,)), ((), ())), preferred_element_type=F32)
     sums[...] = sums[...] * shrink + part
@@ -341,7 +351,7 @@
 
     @pl.when(step == pl.num_programs(0) - 1)
     def _():
-        mean, own_lse = sums[...] / total[...], top[...] + jnp.log(total[...])
+        mean, own_lse = sums[...] / total[...], top[...] * STUD + jnp.log(total[...])
         put(own_ref, other_ref, *pack(mean, own_lse, 3, places_ref[0], places_ref[1]))
 
 
@@ -418,7 +428,7 @@
     shares = over(share, "dp")
     matrix, high, share = call(
         row_kernel,
-        [((rows, protos), BF16), ((steps, rows, 1), F32), ((width, 2 * LATE + 16, LANES), BF16)],
+        [((rows, protos), BF16), ((steps, rows, 1), F32), ((width, 48, LANES), BF16)],
         shares,
         teacher_rows,
         near_teacher,
@@ -466,7 +476,7 @@
         far(places),
         student_protos,
         grid=grid,
-        in_specs=[pl.BlockSpec((width, EARLY, bot), lambda k: (0, 0, 0)), VMEM, VMEM, wide],
+        in_specs=[VMEM, VMEM, VMEM, wide],
         scratch=[pltpu.VMEM((rows, bot), BF16), pltpu.VMEM((rows, bot), F32), column, column],
         flops=2 * dot,
         moved=2 * bot * protos,

time: 160 us -> 158 us (0.988)
  no operation moved by 1% of the time
where the time goes in v14:
time: 158 us
  blocking collectives  118 us (75%)
  Pallas kernels  25.3 us (16%)
  starting transfers between devices  9.11 us (6%)
  waiting for transfers between devices  2.88 us (2%)
    all_to_all x2, blocking collectives, body(): shares = over(share, 'dp')  43.1 us
    pallas_call x10, Pallas kernels, call(): pl.pallas_call(kernel, out_shape=out_shape, in_specs=[VMEM] * len(args) i...  25.3 us
    all_gather x1, blocking collectives, body(): gathered = lax.all_gather(sent, 'proto', axis=0, tiled=False)  24.5 us
    all_to_all x1, blocking collectives, body(): back = over(sent, 'proto', axis_index_groups=same_core)  22.5 us
    all_to_all x1, blocking collectives, body(): shares = row_shares = over(share, 'proto')  16.4 us
    all_to_all x1, blocking collectives, body(): shares = over(share, 'proto')  11.8 us
    all_to_all x1, starting transfers between devices, body(): shares = over(share, 'dp')  4.05 us
  transfers between devices with their start and end apart: 3, of which 2 were waited for; matrix products, arithmetic and copies ran while one was open for 0% of the time, Pallas kernels for 5%

profile of v14, /device:TPU:1, one launch (start us, length us, event | category | flops | bytes accessed | tf_op | source)
XLA Modules:
  0.0 157.8 jit_solution(3644368448694437935)
XLA Ops:
  1.3 1.8 %shard_map.77 = (bf16[126,256]{1,0:T(8,128)(2,1)S(1)}, bf16[36,128]{1,0:T(8,128)(2,1)S(1)}, bf16[80,256]{1,0:T(8,128)(2,1)}) custom-call(bf16[256,256]{1,0:T(8,128)(2,1)} %bitcast.6, bf16[256,256]{1,0:T(8,128)(2,1)} %bitcast.7, s32[1,256]{1,0:T(1,128)} %order_ref.3, s32[1,1]{1,0:T(1,128)S(6)} %copy.8.count_ref), custom_call_target="tpu_custom_call" | custom-call | bytes 262144 | tf_op jit(solution)/shard_map/pallas_call | solution.py:35
  3.1 24.5 %all-gather.1.gathered_ref = bf16[16,126,256]{2,1,0:T(8,128)(2,1)S(1)} all-gather(bf16[1,126,256]{2,1,0:T(8,128)(2,1)S(1)} %bitcast.5), channel_id=2, replica_groups=mesh['dp'=32,'proto'=16] {'proto'}, dimensions={0}, use_global_device_ids=true | all-gather | bytes 1096704 | tf_op jit(solution)/shard_map/all_gather | solution.py:416
  27.6 0.0 copy-start
  27.6 3.7 %shard_map.78 = (f32[32,32,128]{2,1,0:T(8,128)S(1)}, bf16[384,256]{1,0:T(8,128)(2,1)S(1)}, f32[4,16,128]{2,1,0:T(8,128)}, bf16[256,4096]{1,0:T(8,128)(2,1)S(1)}) custom-call(bf16[16,126,256]{2,1,0:T(8,128)(2,1)S(1)} %all-gather.1.gathered_ref, s32[1,1]{1,0:T(1,128)} %bitcast.3.index_ref, bf16[256,4096]{1,0:T(8,128)(2,1)} %far_ref.1), custom_call_target="tpu_custom_call" | custom-call | flops 805306368 | bytes 2097152 | tf_op jit(solution)/shard_map/pallas_call | solution.py:35
  31.3 26.7 %all_to_all.30.shares_ref = f32[32,32,128]{2,1,0:T(8,128)S(1)} all-to-all(f32[32,32,128]{2,1,0:T(8,128)S(1)} %get-tuple-element.25), channel_id=1, replica_groups=mesh['dp'=32,'proto'=16] {'dp'}, dimensions={0} | all-to-all | bytes 1048576 | tf_op jit(solution)/shard_map/all_to_all | solution.py:428
  58.0 0.0 copy-done
  58.0 2.1 %shard_map.79 = (bf16[384,4096]{1,0:T(8,128)(2,1)S(1)}, f32[2,384,1]{2,1,0:T(8,128)S(1)}, bf16[16,48,128]{2,1,0:T(8,128)(2,1)S(1)}) custom-call(f32[32,32,128]{2,1,0:T(8,128)S(1)} %all_to_all.30.shares_ref, bf16[384,256]{1,0:T(8,128)(2,1)S(1)} %get-tuple-element.26.rows_ref, bf16[256,4096]{1,0:T(8,128)(2,1)S(1)} %get-tuple-element.27.protos_ref, ...), custom_call_target="tpu_custom_call" | custom-call | flops 805306368 | bytes 5242880 | tf_op jit(solution)/shard_map/pallas_call | solution.py:35
  60.2 16.4 %all_to_all.31.shares_ref = bf16[16,48,128]{2,1,0:T(8,128)(2,1)S(1)} all-to-all(bf16[16,48,128]{2,1,0:T(8,128)(2,1)S(1)} %get-tuple-element.29), channel_id=1, replica_groups=mesh['dp'=32,'proto'=16] {'proto'}, dimensions={0} | all-to-all | bytes 393216 | tf_op jit(solution)/shard_map/all_to_all | solution.py:440
  76.6 0.0 copy-start.1
  76.6 0.9 shard_map.80
  77.5 16.5 %all_to_all.32.shares_ref = bf16[32,32,128]{2,1,0:T(8,128)(2,1)S(1)} all-to-all(bf16[32,32,128]{2,1,0:T(8,128)(2,1)S(1)} %get-tuple-element.32), channel_id=1, replica_groups=mesh['dp'=32,'proto'=16] {'dp'}, dimensions={0} | all-to-all | bytes 524288 | tf_op jit(solution)/shard_map/all_to_all | solution.py:452
  94.0 0.0 copy-done.1
  94.0 0.9 shard_map.81
  94.9 11.8 %all_to_all.33.shares_ref = f32[16,8,128]{2,1,0:T(8,128)S(1)} all-to-all(f32[16,8,128]{2,1,0:T(8,128)S(1)} %shard_map.81), channel_id=1, replica_groups=mesh['dp'=32,'proto'=16] {'proto'}, dimensions={0} | all-to-all | bytes 131072 | tf_op jit(solution)/shard_map/all_to_all | solution.py:461
  106.7 1.5 shard_map.82
  108.2 4.0 %all-to-all-start.4 = ((bf16[32,32,128]{2,1,0:T(8,128)(2,1)}), bf16[32,32,128]{2,1,0:T(8,128)(2,1)S(1)}, u32[]{:S(2)}, u32[]{:S(2)}) async-start(bf16[32,32,128]{2,1,0:T(8,128)(2,1)} %get-tuple-element.34), calls=%async_computation.4 | async-start | bytes 524288 | tf_op jit(solution)/shard_map/all_to_all | solution.py:485
  112.3 8.2 %shard_map.83 = (bf16[8,80,256]{2,1,0:T(8,128)(2,1)}, bf16[8,80,256]{2,1,0:T(8,128)(2,1)}) custom-call(bf16[16,126,256]{2,1,0:T(8,128)(2,1)} %copy-done, bf16[16,48,128]{2,1,0:T(8,128)(2,1)} %copy-done.1, f32[4,16,128]{2,1,0:T(8,128)} %get-tuple-element.35.places_ref, bf16[256,4096]{1,0:T(8,128)(2,1)} %protos_ref.3), custom_call_target="tpu_custom_call" | custom-call | flops 1610612736 | bytes 2097152 | tf_op jit(solution)/shard_map/pallas_call | solution.py:35
  120.5 2.1 %collective-permute-start = (bf16[8,80,256]{2,1,0:T(8,128)(2,1)}, bf16[8,80,256]{2,1,0:T(8,128)(2,1)S(1)}, u32[]{:S(2)}, u32[]{:S(2)}) collective-permute-start(bf16[8,80,256]{2,1,0:T(8,128)(2,1)} %get-tuple-element.36), channel_id=1, source_target_pairs={{0,1},{1,0},{2,3},{3,2},{4,5},{5,4},{6,7},{7,6},{8,9},{9,8},{10,11... | collective-permute-start | bytes 983048 | tf_op jit(solution)/shard_map/ppermute | solution.py:484
  122.5 1.6 %collective-permute-done.student_came_ref = bf16[8,80,256]{2,1,0:T(8,128)(2,1)S(1)} collective-permute-done((bf16[8,80,256]{2,1,0:T(8,128)(2,1)}, bf16[8,80,256]{2,1,0:T(8,128)(2,1)S(1)}, u32[]{:S(2)}, u32[]{:S(2)}) %collective-permute-start) | collective-permute-done | bytes 327712 | tf_op jit(solution)/shard_map/ppermute | solution.py:484
  124.2 0.0 copy-start.3
  124.2 0.7 copy-done.3
  124.9 0.0 all-to-all-done.4.shares_ref
  124.9 0.0 copy-start.2
  124.9 0.0 copy-start.4
  124.9 4.0 %shard_map.84 = (bf16[8,80,256]{2,1,0:T(8,128)(2,1)S(1)}, bf16[8,80,256]{2,1,0:T(8,128)(2,1)S(1)}) custom-call(bf16[32,32,128]{2,1,0:T(8,128)(2,1)S(1)} %all-to-all-done.4.shares_ref, f32[2,3,128]{2,1,0:T(4,128)} %get-tuple-element.38.scale_ref, bf16[384,4096]{1,0:T(8,128)(2,1)S(1)} %get-tuple-element.31.matrix_ref, bf16[256,4096]{1,0:T(8,128)(2,1)} %protos_ref.3, ...), custom_call_target="tpu_custom_call" | custom-call | flops 805306368 | bytes 3145728 | tf_op jit(solution)/shard_map/pallas_call | solution.py:35
  128.9 0.0 copy-start.5
  129.0 3.0 %collective-permute-start.1 = (bf16[8,80,256]{2,1,0:T(8,128)(2,1)S(1)}, bf16[8,80,256]{2,1,0:T(8,128)(2,1)S(1)}, u32[]{:S(2)}, u32[]{:S(2)}) collective-permute-start(bf16[8,80,256]{2,1,0:T(8,128)(2,1)S(1)} %get-tuple-element.40), channel_id=1, source_target_pairs={{0,1},{1,0},{2,3},{3,2},{4,5},{5,4},{6,7},{7,6},{8,9},{9,8},{10,11... | collective-permute-start | bytes 983048 | tf_op jit(solution)/shard_map/ppermute | solution.py:501
  132.0 1.2 collective-permute-done.1.came_ref
  133.2 0.0 copy-done.2
  133.2 0.0 copy-done.4
  133.2 0.4 shard_map.85
  133.6 22.5 %all_to_all.34.back_ref = bf16[8,152,256]{2,1,0:T(8,128)(2,1)S(1)} all-to-all(bf16[8,152,256]{2,1,0:T(8,128)(2,1)S(1)} %shard_map.85), channel_id=1, replica_groups={{0,2,4,6,8,10,12,14},{1,3,5,7,9,11,13,15},{16,18,20,22,24,26,28,30},{17..., dimensions={0} | all-to-all | bytes 1245184 | tf_op jit(solution)/shard_map/all_to_all | solution.py:506
  156.1 0.0 copy-done.5
  156.1 1.7 %shard_map.86 = (bf16[256,256]{1,0:T(8,128)(2,1)}, f32[1,1]{1,0:T(1,128)}) custom-call(bf16[8,152,256]{2,1,0:T(8,128)(2,1)S(1)} %all_to_all.34.back_ref, bf16[80,256]{1,0:T(8,128)(2,1)S(1)} %copy-done.5, s32[1,256]{1,0:T(1,128)} %order_ref.3, s32[1,1]{1,0:T(1,128)S(6)} %copy.8.count_ref), custom_call_target="tpu_custom_call" | custom-call | bytes 131072 | tf_op jit(solution)/shard_map/pallas_call | solution.py:35
Async XLA Ops:
  27.6 30.4 %copy-start = (bf16[16,126,256]{2,1,0:T(8,128)(2,1)}, bf16[16,126,256]{2,1,0:T(8,128)(2,1)S(1)}, u32[]{:S(2)}) copy-start(bf16[16,126,256]{2,1,0:T(8,128)(2,1)S(1)} %all-gather.1.gathered_ref) | copy-start | bytes 3096580
  76.6 17.4 %copy-start.1 = (bf16[16,48,128]{2,1,0:T(8,128)(2,1)}, bf16[16,48,128]{2,1,0:T(8,128)(2,1)S(1)}, u32[]{:S(2)}) copy-start(bf16[16,48,128]{2,1,0:T(8,128)(2,1)S(1)} %all_to_all.31.shares_ref) | copy-start | bytes 589828
  108.2 16.7 %all-to-all-start.4 = ((bf16[32,32,128]{2,1,0:T(8,128)(2,1)}), bf16[32,32,128]{2,1,0:T(8,128)(2,1)S(1)}, u32[]{:S(2)}, u32[]{:S(2)}) async-start(bf16[32,32,128]{2,1,0:T(8,128)(2,1)} %get-tuple-element.34), calls=%async_computation.4 | async-start | bytes 524288 | tf_op jit(solution)/shard_map/all_to_all | solution.py:485
  120.5 3.7 %collective-permute-start = (bf16[8,80,256]{2,1,0:T(8,128)(2,1)}, bf16[8,80,256]{2,1,0:T(8,128)(2,1)S(1)}, u32[]{:S(2)}, u32[]{:S(2)}) collective-permute-start(bf16[8,80,256]{2,1,0:T(8,128)(2,1)} %get-tuple-element.36), channel_id=1, source_target_pairs={{0,1},{1,0},{2,3},{3,2},{4,5},{5,4},{6,7},{7,6},{8,9},{9,8},{10,11... | collective-permute-start | bytes 983048 | tf_op jit(solution)/shard_map/ppermute | solution.py:484
  124.2 0.7 copy-start.3
  124.9 8.3 %copy-start.2 = (bf16[8,80,256]{2,1,0:T(8,128)(2,1)S(1)}, bf16[8,80,256]{2,1,0:T(8,128)(2,1)}, u32[]{:S(2)}) copy-start(bf16[8,80,256]{2,1,0:T(8,128)(2,1)} %get-tuple-element.41.student_own_ref) | copy-start | bytes 983044
  124.9 8.3 %copy-start.4 = (bf16[8,80,256]{2,1,0:T(8,128)(2,1)S(1)}, bf16[8,80,256]{2,1,0:T(8,128)(2,1)}, u32[]{:S(2)}) copy-start(bf16[8,80,256]{2,1,0:T(8,128)(2,1)} %copy-done.3) | copy-start | bytes 983044
  128.9 27.1 %copy-start.5 = (bf16[80,256]{1,0:T(8,128)(2,1)S(1)}, bf16[80,256]{1,0:T(8,128)(2,1)}, u32[]{:S(2)}) copy-start(bf16[80,256]{1,0:T(8,128)(2,1)} %get-tuple-element.43.picked_ref) | copy-start | bytes 122884
  129.0 4.2 %collective-permute-start.1 = (bf16[8,80,256]{2,1,0:T(8,128)(2,1)S(1)}, bf16[8,80,256]{2,1,0:T(8,128)(2,1)S(1)}, u32[]{:S(2)}, u32[]{:S(2)}) collective-permute-start(bf16[8,80,256]{2,1,0:T(8,128)(2,1)S(1)} %get-tuple-element.40), channel_id=1, source_target_pairs={{0,1},{1,0},{2,3},{3,2},{4,5},{5,4},{6,7},{7,6},{8,9},{9,8},{10,11... | collective-permute-start | bytes 983048 | tf_op jit(solution)/shard_map/ppermute | solution.py:501

commit v15 on v14

--- a/solution.py
+++ b/solution.py
@@ -288,9 +288,11 @@
 def target_kernel(shares_ref, scale_ref, matrix_ref, protos_ref, places_ref, own_ref, other_ref, sums, total):
     step = pl.program_id(0)
     scale = to_column(scale_ref[step])
-    weights = (matrix_ref[...].astype(F32) * to_row(inverse_of(shares_ref))).astype(BF16)
-    part = scale * lax.dot_general(weights, protos_ref[...], (((1,), (1,)), ((), ())), preferred_element_type=F32)
-    mass = scale * jnp.sum(weights.astype(F32), axis=1, keepdims=True)
+    here = pl.ds(pl.multiple_of(step * BLOCK, BLOCK), BLOCK)
+    weights = matrix_ref[:, here].astype(F32) * to_row(inverse_of(shares_ref))
+    narrow = weights.astype(BF16)
+    part = scale * lax.dot_general(narrow, protos_ref[...], (((1,), (1,)), ((), ())), preferred_element_type=F32)
+    mass = scale * jnp.sum(weights, axis=1, keepdims=True)
 
     @pl.when(step == 0)
     def _():
@@ -493,7 +495,7 @@
         student_protos,
         far(places),
         grid=grid,
-        in_specs=[peer, VMEM, square, wide, VMEM],
+        in_specs=[peer, VMEM, VMEM, wide, VMEM],
         scratch=[pltpu.VMEM((rows, bot), F32), column],
         flops=dot,
         moved=2 * rows * protos,

time: 158 us -> 158 us (level)
  no operation moved by 1% of the time
where the time goes in v15:
time: 158 us
  blocking collectives  118 us (75%)
  Pallas kernels  25 us (16%)
  starting transfers between devices  9.12 us (6%)
  waiting for transfers between devices  2.88 us (2%)
    all_to_all x2, blocking collectives, body(): shares = over(share, 'dp')  43.1 us
    pallas_call x10, Pallas kernels, call(): pl.pallas_call(kernel, out_shape=out_shape, in_specs=[VMEM] * len(args) i...  25 us
    all_gather x1, blocking collectives, body(): gathered = lax.all_gather(sent, 'proto', axis=0, tiled=False)  24.5 us
    all_to_all x1, blocking collectives, body(): back = over(sent, 'proto', axis_index_groups=same_core)  22.5 us
    all_to_all x1, blocking collectives, body(): shares = row_shares = over(share, 'proto')  16.4 us
    all_to_all x1, blocking collectives, body(): shares = over(share, 'proto')  11.8 us
    all_to_all x1, starting transfers between devices, body(): shares = over(share, 'dp')  4.05 us
  transfers between devices with their start and end apart: 3, of which 2 were waited for; matrix products, arithmetic and copies ran while one was open for 0% of the time, Pallas kernels for 5%

profile of v15, /device:TPU:1, one launch (start us, length us, event | category | flops | bytes accessed | tf_op | source)
XLA Modules:
  0.0 157.5 jit_solution(6678159368027406102)
XLA Ops:
  1.3 1.8 %shard_map.77 = (bf16[126,256]{1,0:T(8,128)(2,1)S(1)}, bf16[36,128]{1,0:T(8,128)(2,1)S(1)}, bf16[80,256]{1,0:T(8,128)(2,1)}) custom-call(bf16[256,256]{1,0:T(8,128)(2,1)} %bitcast.6, bf16[256,256]{1,0:T(8,128)(2,1)} %bitcast.7, s32[1,256]{1,0:T(1,128)} %order_ref.3, s32[1,1]{1,0:T(1,128)S(6)} %copy.8.count_ref), custom_call_target="tpu_custom_call" | custom-call | bytes 262144 | tf_op jit(solution)/shard_map/pallas_call | solution.py:35
  3.1 24.5 %all-gather.1.gathered_ref = bf16[16,126,256]{2,1,0:T(8,128)(2,1)S(1)} all-gather(bf16[1,126,256]{2,1,0:T(8,128)(2,1)S(1)} %bitcast.5), channel_id=2, replica_groups=mesh['dp'=32,'proto'=16] {'proto'}, dimensions={0}, use_global_device_ids=true | all-gather | bytes 1096704 | tf_op jit(solution)/shard_map/all_gather | solution.py:418
  27.6 0.0 copy-start
  27.6 3.7 %shard_map.78 = (f32[32,32,128]{2,1,0:T(8,128)S(1)}, bf16[384,256]{1,0:T(8,128)(2,1)S(1)}, f32[4,16,128]{2,1,0:T(8,128)}, bf16[256,4096]{1,0:T(8,128)(2,1)S(1)}) custom-call(bf16[16,126,256]{2,1,0:T(8,128)(2,1)S(1)} %all-gather.1.gathered_ref, s32[1,1]{1,0:T(1,128)} %bitcast.3.index_ref, bf16[256,4096]{1,0:T(8,128)(2,1)} %far_ref.1), custom_call_target="tpu_custom_call" | custom-call | flops 805306368 | bytes 2097152 | tf_op jit(solution)/shard_map/pallas_call | solution.py:35
  31.3 26.7 %all_to_all.30.shares_ref = f32[32,32,128]{2,1,0:T(8,128)S(1)} all-to-all(f32[32,32,128]{2,1,0:T(8,128)S(1)} %get-tuple-element.25), channel_id=1, replica_groups=mesh['dp'=32,'proto'=16] {'dp'}, dimensions={0} | all-to-all | bytes 1048576 | tf_op jit(solution)/shard_map/all_to_all | solution.py:430
  58.0 0.0 copy-done
  58.0 2.1 %shard_map.79 = (bf16[384,4096]{1,0:T(8,128)(2,1)S(1)}, f32[2,384,1]{2,1,0:T(8,128)S(1)}, bf16[16,48,128]{2,1,0:T(8,128)(2,1)S(1)}) custom-call(f32[32,32,128]{2,1,0:T(8,128)S(1)} %all_to_all.30.shares_ref, bf16[384,256]{1,0:T(8,128)(2,1)S(1)} %get-tuple-element.26.rows_ref, bf16[256,4096]{1,0:T(8,128)(2,1)S(1)} %get-tuple-element.27.protos_ref, ...), custom_call_target="tpu_custom_call" | custom-call | flops 805306368 | bytes 5242880 | tf_op jit(solution)/shard_map/pallas_call | solution.py:35
  60.2 16.4 %all_to_all.31.shares_ref = bf16[16,48,128]{2,1,0:T(8,128)(2,1)S(1)} all-to-all(bf16[16,48,128]{2,1,0:T(8,128)(2,1)S(1)} %get-tuple-element.29), channel_id=1, replica_groups=mesh['dp'=32,'proto'=16] {'proto'}, dimensions={0} | all-to-all | bytes 393216 | tf_op jit(solution)/shard_map/all_to_all | solution.py:442
  76.6 0.0 copy-start.1
  76.6 0.9 shard_map.80
  77.5 16.5 %all_to_all.32.shares_ref = bf16[32,32,128]{2,1,0:T(8,128)(2,1)S(1)} all-to-all(bf16[32,32,128]{2,1,0:T(8,128)(2,1)S(1)} %get-tuple-element.32), channel_id=1, replica_groups=mesh['dp'=32,'proto'=16] {'dp'}, dimensions={0} | all-to-all | bytes 524288 | tf_op jit(solution)/shard_map/all_to_all | solution.py:454
  94.0 0.0 copy-done.1
  94.0 0.9 shard_map.81
  94.9 11.8 %all_to_all.33.shares_ref = f32[16,8,128]{2,1,0:T(8,128)S(1)} all-to-all(f32[16,8,128]{2,1,0:T(8,128)S(1)} %shard_map.81), channel_id=1, replica_groups=mesh['dp'=32,'proto'=16] {'proto'}, dimensions={0} | all-to-all | bytes 131072 | tf_op jit(solution)/shard_map/all_to_all | solution.py:463
  106.7 1.5 shard_map.82
  108.2 4.0 %all-to-all-start.4 = ((bf16[32,32,128]{2,1,0:T(8,128)(2,1)}), bf16[32,32,128]{2,1,0:T(8,128)(2,1)S(1)}, u32[]{:S(2)}, u32[]{:S(2)}) async-start(bf16[32,32,128]{2,1,0:T(8,128)(2,1)} %get-tuple-element.34), calls=%async_computation.4 | async-start | bytes 524288 | tf_op jit(solution)/shard_map/all_to_all | solution.py:487
  112.3 8.2 %shard_map.83 = (bf16[8,80,256]{2,1,0:T(8,128)(2,1)}, bf16[8,80,256]{2,1,0:T(8,128)(2,1)}) custom-call(bf16[16,126,256]{2,1,0:T(8,128)(2,1)} %copy-done, bf16[16,48,128]{2,1,0:T(8,128)(2,1)} %copy-done.1, f32[4,16,128]{2,1,0:T(8,128)} %get-tuple-element.35.places_ref, bf16[256,4096]{1,0:T(8,128)(2,1)} %protos_ref.3), custom_call_target="tpu_custom_call" | custom-call | flops 1610612736 | bytes 2097152 | tf_op jit(solution)/shard_map/pallas_call | solution.py:35
  120.5 2.1 %collective-permute-start = (bf16[8,80,256]{2,1,0:T(8,128)(2,1)}, bf16[8,80,256]{2,1,0:T(8,128)(2,1)S(1)}, u32[]{:S(2)}, u32[]{:S(2)}) collective-permute-start(bf16[8,80,256]{2,1,0:T(8,128)(2,1)} %get-tuple-element.36), channel_id=1, source_target_pairs={{0,1},{1,0},{2,3},{3,2},{4,5},{5,4},{6,7},{7,6},{8,9},{9,8},{10,11... | collective-permute-start | bytes 983048 | tf_op jit(solution)/shard_map/ppermute | solution.py:486
  122.5 1.6 %collective-permute-done.student_came_ref = bf16[8,80,256]{2,1,0:T(8,128)(2,1)S(1)} collective-permute-done((bf16[8,80,256]{2,1,0:T(8,128)(2,1)}, bf16[8,80,256]{2,1,0:T(8,128)(2,1)S(1)}, u32[]{:S(2)}, u32[]{:S(2)}) %collective-permute-start) | collective-permute-done | bytes 327712 | tf_op jit(solution)/shard_map/ppermute | solution.py:486
  124.2 0.0 copy-start.3
  124.2 0.7 copy-done.3
  124.9 0.0 all-to-all-done.4.shares_ref
  124.9 0.0 copy-start.2
  124.9 0.0 copy-start.4
  124.9 3.8 %shard_map.84 = (bf16[8,80,256]{2,1,0:T(8,128)(2,1)S(1)}, bf16[8,80,256]{2,1,0:T(8,128)(2,1)S(1)}) custom-call(bf16[32,32,128]{2,1,0:T(8,128)(2,1)S(1)} %all-to-all-done.4.shares_ref, f32[2,3,128]{2,1,0:T(4,128)} %get-tuple-element.38.scale_ref, bf16[384,4096]{1,0:T(8,128)(2,1)S(1)} %get-tuple-element.31.matrix_ref, bf16[256,4096]{1,0:T(8,128)(2,1)} %protos_ref.3, ...), custom_call_target="tpu_custom_call" | custom-call | flops 805306368 | bytes 3145728 | tf_op jit(solution)/shard_map/pallas_call | solution.py:35
  128.7 0.0 copy-start.5
  128.7 3.0 %collective-permute-start.1 = (bf16[8,80,256]{2,1,0:T(8,128)(2,1)S(1)}, bf16[8,80,256]{2,1,0:T(8,128)(2,1)S(1)}, u32[]{:S(2)}, u32[]{:S(2)}) collective-permute-start(bf16[8,80,256]{2,1,0:T(8,128)(2,1)S(1)} %get-tuple-element.40), channel_id=1, source_target_pairs={{0,1},{1,0},{2,3},{3,2},{4,5},{5,4},{6,7},{7,6},{8,9},{9,8},{10,11... | collective-permute-start | bytes 983048 | tf_op jit(solution)/shard_map/ppermute | solution.py:503
  131.7 1.2 collective-permute-done.1.came_ref
  132.9 0.0 copy-done.2
  132.9 0.0 copy-done.4
  132.9 0.4 shard_map.85
  133.4 22.5 %all_to_all.34.back_ref = bf16[8,152,256]{2,1,0:T(8,128)(2,1)S(1)} all-to-all(bf16[8,152,256]{2,1,0:T(8,128)(2,1)S(1)} %shard_map.85), channel_id=1, replica_groups={{0,2,4,6,8,10,12,14},{1,3,5,7,9,11,13,15},{16,18,20,22,24,26,28,30},{17..., dimensions={0} | all-to-all | bytes 1245184 | tf_op jit(solution)/shard_map/all_to_all | solution.py:508
  155.8 0.0 copy-done.5
  155.8 1.7 %shard_map.86 = (bf16[256,256]{1,0:T(8,128)(2,1)}, f32[1,1]{1,0:T(1,128)}) custom-call(bf16[8,152,256]{2,1,0:T(8,128)(2,1)S(1)} %all_to_all.34.back_ref, bf16[80,256]{1,0:T(8,128)(2,1)S(1)} %copy-done.5, s32[1,256]{1,0:T(1,128)} %order_ref.3, s32[1,1]{1,0:T(1,128)S(6)} %copy.8.count_ref), custom_call_target="tpu_custom_call" | custom-call | bytes 131072 | tf_op jit(solution)/shard_map/pallas_call | solution.py:35
Async XLA Ops:
  27.6 30.4 %copy-start = (bf16[16,126,256]{2,1,0:T(8,128)(2,1)}, bf16[16,126,256]{2,1,0:T(8,128)(2,1)S(1)}, u32[]{:S(2)}) copy-start(bf16[16,126,256]{2,1,0:T(8,128)(2,1)S(1)} %all-gather.1.gathered_ref) | copy-start | bytes 3096580
  76.6 17.4 %copy-start.1 = (bf16[16,48,128]{2,1,0:T(8,128)(2,1)}, bf16[16,48,128]{2,1,0:T(8,128)(2,1)S(1)}, u32[]{:S(2)}) copy-start(bf16[16,48,128]{2,1,0:T(8,128)(2,1)S(1)} %all_to_all.31.shares_ref) | copy-start | bytes 589828
  108.2 16.7 %all-to-all-start.4 = ((bf16[32,32,128]{2,1,0:T(8,128)(2,1)}), bf16[32,32,128]{2,1,0:T(8,128)(2,1)S(1)}, u32[]{:S(2)}, u32[]{:S(2)}) async-start(bf16[32,32,128]{2,1,0:T(8,128)(2,1)} %get-tuple-element.34), calls=%async_computation.4 | async-start | bytes 524288 | tf_op jit(solution)/shard_map/all_to_all | solution.py:487
  120.5 3.7 %collective-permute-start = (bf16[8,80,256]{2,1,0:T(8,128)(2,1)}, bf16[8,80,256]{2,1,0:T(8,128)(2,1)S(1)}, u32[]{:S(2)}, u32[]{:S(2)}) collective-permute-start(bf16[8,80,256]{2,1,0:T(8,128)(2,1)} %get-tuple-element.36), channel_id=1, source_target_pairs={{0,1},{1,0},{2,3},{3,2},{4,5},{5,4},{6,7},{7,6},{8,9},{9,8},{10,11... | collective-permute-start | bytes 983048 | tf_op jit(solution)/shard_map/ppermute | solution.py:486
  124.2 0.7 copy-start.3
  124.9 8.1 %copy-start.2 = (bf16[8,80,256]{2,1,0:T(8,128)(2,1)S(1)}, bf16[8,80,256]{2,1,0:T(8,128)(2,1)}, u32[]{:S(2)}) copy-start(bf16[8,80,256]{2,1,0:T(8,128)(2,1)} %get-tuple-element.41.student_own_ref) | copy-start | bytes 983044
  124.9 8.1 %copy-start.4 = (bf16[8,80,256]{2,1,0:T(8,128)(2,1)S(1)}, bf16[8,80,256]{2,1,0:T(8,128)(2,1)}, u32[]{:S(2)}) copy-start(bf16[8,80,256]{2,1,0:T(8,128)(2,1)} %copy-done.3) | copy-start | bytes 983044
  128.7 27.1 %copy-start.5 = (bf16[80,256]{1,0:T(8,128)(2,1)S(1)}, bf16[80,256]{1,0:T(8,128)(2,1)}, u32[]{:S(2)}) copy-start(bf16[80,256]{1,0:T(8,128)(2,1)} %get-tuple-element.43.picked_ref) | copy-start | bytes 122884
  128.7 4.2 %collective-permute-start.1 = (bf16[8,80,256]{2,1,0:T(8,128)(2,1)S(1)}, bf16[8,80,256]{2,1,0:T(8,128)(2,1)S(1)}, u32[]{:S(2)}, u32[]{:S(2)}) collective-permute-start(bf16[8,80,256]{2,1,0:T(8,128)(2,1)S(1)} %get-tuple-element.40), channel_id=1, source_target_pairs={{0,1},{1,0},{2,3},{3,2},{4,5},{5,4},{6,7},{7,6},{8,9},{9,8},{10,11... | collective-permute-start | bytes 983048 | tf_op jit(solution)/shard_map/ppermute | solution.py:503

commit v16 on v15

--- a/solution.py
+++ b/solution.py
@@ -401,6 +401,7 @@
     column = pltpu.VMEM((rows, 1), F32)
     sems = [pltpu.SemaphoreType.DMA((protos // PIECE,))]
     far = functools.partial(pltpu.with_memory_space_constraint, memory_space=pltpu.HBM)
+    near_order = mask_order
     student_patches, teacher_patches, mask_order = far(student_patches[0]), far(teacher_patches[0]), far(mask_order)
     student_protos, teacher_protos = far(student_protos), far(teacher_protos)
     dot = 2 * rows * protos * bot
@@ -511,7 +512,7 @@
         [((patches, bot), BF16), ((1, 1), F32)],
         back,
         picked,
-        mask_order,
+        near_order,
         counts,
         in_specs=[VMEM, VMEM, VMEM, SMEM],
         moved=2 * patches * bot,

time: 158 us -> 158 us (level)
  no operation moved by 1% of the time
where the time goes in v16:
time: 158 us; the launch traced here: 157 us
  blocking collectives  118 us (75%)
  Pallas kernels  24.4 us (15%)
  starting transfers between devices  9.24 us (6%)
  waiting for transfers between devices  2.88 us (2%)
    all_to_all x2, blocking collectives, body(): shares = over(share, 'dp')  43.1 us
    all_gather x1, blocking collectives, body(): gathered = lax.all_gather(sent, 'proto', axis=0, tiled=False)  24.5 us
    pallas_call x10, Pallas kernels, call(): pl.pallas_call(kernel, out_shape=out_shape, in_specs=[VMEM] * len(args) i...  24.4 us
    all_to_all x1, blocking collectives, body(): back = over(sent, 'proto', axis_index_groups=same_core)  22.5 us
    all_to_all x1, blocking collectives, body(): shares = row_shares = over(share, 'proto')  16.4 us
    all_to_all x1, blocking collectives, body(): shares = over(share, 'proto')  11.8 us
    all_to_all x1, starting transfers between devices, body(): shares = over(share, 'dp')  4.05 us
  transfers between devices with their start and end apart: 3, of which 2 were waited for; matrix products, arithmetic and copies ran while one was open for 0% of the time, Pallas kernels for 5%

profile of v16, /device:TPU:1, one launch (start us, length us, event | category | flops | bytes accessed | tf_op | source)
XLA Modules:
  0.0 157.0 jit_solution(15256329306947944512)
XLA Ops:
  1.3 1.8 %shard_map.77 = (bf16[126,256]{1,0:T(8,128)(2,1)S(1)}, bf16[36,128]{1,0:T(8,128)(2,1)S(1)}, bf16[80,256]{1,0:T(8,128)(2,1)}) custom-call(bf16[256,256]{1,0:T(8,128)(2,1)} %bitcast.6, bf16[256,256]{1,0:T(8,128)(2,1)} %bitcast.7, s32[1,256]{1,0:T(1,128)} %order_ref.3, s32[1,1]{1,0:T(1,128)S(6)} %copy.8.count_ref), custom_call_target="tpu_custom_call" | custom-call | bytes 262144 | tf_op jit(solution)/shard_map/pallas_call | solution.py:35
  3.1 24.5 %all-gather.1.gathered_ref = bf16[16,126,256]{2,1,0:T(8,128)(2,1)S(1)} all-gather(bf16[1,126,256]{2,1,0:T(8,128)(2,1)S(1)} %bitcast.5), channel_id=2, replica_groups=mesh['dp'=32,'proto'=16] {'proto'}, dimensions={0}, use_global_device_ids=true | all-gather | bytes 1096704 | tf_op jit(solution)/shard_map/all_gather | solution.py:419
  27.6 0.0 copy-start
  27.6 3.7 %shard_map.78 = (f32[32,32,128]{2,1,0:T(8,128)S(1)}, bf16[384,256]{1,0:T(8,128)(2,1)S(1)}, f32[4,16,128]{2,1,0:T(8,128)}, bf16[256,4096]{1,0:T(8,128)(2,1)S(1)}) custom-call(bf16[16,126,256]{2,1,0:T(8,128)(2,1)S(1)} %all-gather.1.gathered_ref, s32[1,1]{1,0:T(1,128)} %bitcast.3.index_ref, bf16[256,4096]{1,0:T(8,128)(2,1)} %far_ref.1), custom_call_target="tpu_custom_call" | custom-call | flops 805306368 | bytes 2097152 | tf_op jit(solution)/shard_map/pallas_call | solution.py:35
  31.3 26.7 %all_to_all.30.shares_ref = f32[32,32,128]{2,1,0:T(8,128)S(1)} all-to-all(f32[32,32,128]{2,1,0:T(8,128)S(1)} %get-tuple-element.25), channel_id=1, replica_groups=mesh['dp'=32,'proto'=16] {'dp'}, dimensions={0} | all-to-all | bytes 1048576 | tf_op jit(solution)/shard_map/all_to_all | solution.py:431
  58.0 0.0 copy-done
  58.0 2.1 %shard_map.79 = (bf16[384,4096]{1,0:T(8,128)(2,1)S(1)}, f32[2,384,1]{2,1,0:T(8,128)S(1)}, bf16[16,48,128]{2,1,0:T(8,128)(2,1)S(1)}) custom-call(f32[32,32,128]{2,1,0:T(8,128)S(1)} %all_to_all.30.shares_ref, bf16[384,256]{1,0:T(8,128)(2,1)S(1)} %get-tuple-element.26.rows_ref, bf16[256,4096]{1,0:T(8,128)(2,1)S(1)} %get-tuple-element.27.protos_ref, ...), custom_call_target="tpu_custom_call" | custom-call | flops 805306368 | bytes 5242880 | tf_op jit(solution)/shard_map/pallas_call | solution.py:35
  60.2 16.4 %all_to_all.31.shares_ref = bf16[16,48,128]{2,1,0:T(8,128)(2,1)S(1)} all-to-all(bf16[16,48,128]{2,1,0:T(8,128)(2,1)S(1)} %get-tuple-element.29), channel_id=1, replica_groups=mesh['dp'=32,'proto'=16] {'proto'}, dimensions={0} | all-to-all | bytes 393216 | tf_op jit(solution)/shard_map/all_to_all | solution.py:443
  76.6 0.0 copy-start.1
  76.6 0.9 shard_map.80
  77.5 16.5 %all_to_all.32.shares_ref = bf16[32,32,128]{2,1,0:T(8,128)(2,1)S(1)} all-to-all(bf16[32,32,128]{2,1,0:T(8,128)(2,1)S(1)} %get-tuple-element.32), channel_id=1, replica_groups=mesh['dp'=32,'proto'=16] {'dp'}, dimensions={0} | all-to-all | bytes 524288 | tf_op jit(solution)/shard_map/all_to_all | solution.py:455
  94.0 0.0 copy-done.1
  94.0 0.9 shard_map.81
  94.9 11.8 %all_to_all.33.shares_ref = f32[16,8,128]{2,1,0:T(8,128)S(1)} all-to-all(f32[16,8,128]{2,1,0:T(8,128)S(1)} %shard_map.81), channel_id=1, replica_groups=mesh['dp'=32,'proto'=16] {'proto'}, dimensions={0} | all-to-all | bytes 131072 | tf_op jit(solution)/shard_map/all_to_all | solution.py:464
  106.7 1.6 shard_map.82
  108.2 4.0 %all-to-all-start.4 = ((bf16[32,32,128]{2,1,0:T(8,128)(2,1)}), bf16[32,32,128]{2,1,0:T(8,128)(2,1)S(1)}, u32[]{:S(2)}, u32[]{:S(2)}) async-start(bf16[32,32,128]{2,1,0:T(8,128)(2,1)} %get-tuple-element.34), calls=%async_computation.4 | async-start | bytes 524288 | tf_op jit(solution)/shard_map/all_to_all | solution.py:488
  112.3 8.2 %shard_map.83 = (bf16[8,80,256]{2,1,0:T(8,128)(2,1)}, bf16[8,80,256]{2,1,0:T(8,128)(2,1)}) custom-call(bf16[16,126,256]{2,1,0:T(8,128)(2,1)} %copy-done, bf16[16,48,128]{2,1,0:T(8,128)(2,1)} %copy-done.1, f32[4,16,128]{2,1,0:T(8,128)} %get-tuple-element.35.places_ref, bf16[256,4096]{1,0:T(8,128)(2,1)} %protos_ref.3), custom_call_target="tpu_custom_call" | custom-call | flops 1610612736 | bytes 2097152 | tf_op jit(solution)/shard_map/pallas_call | solution.py:35
  120.5 2.1 %collective-permute-start = (bf16[8,80,256]{2,1,0:T(8,128)(2,1)}, bf16[8,80,256]{2,1,0:T(8,128)(2,1)S(1)}, u32[]{:S(2)}, u32[]{:S(2)}) collective-permute-start(bf16[8,80,256]{2,1,0:T(8,128)(2,1)} %get-tuple-element.36), channel_id=1, source_target_pairs={{0,1},{1,0},{2,3},{3,2},{4,5},{5,4},{6,7},{7,6},{8,9},{9,8},{10,11... | collective-permute-start | bytes 983048 | tf_op jit(solution)/shard_map/ppermute | solution.py:487
  122.6 1.6 %collective-permute-done.student_came_ref = bf16[8,80,256]{2,1,0:T(8,128)(2,1)S(1)} collective-permute-done((bf16[8,80,256]{2,1,0:T(8,128)(2,1)}, bf16[8,80,256]{2,1,0:T(8,128)(2,1)S(1)}, u32[]{:S(2)}, u32[]{:S(2)}) %collective-permute-start) | collective-permute-done | bytes 327712 | tf_op jit(solution)/shard_map/ppermute | solution.py:487
  124.2 0.0 copy-start.3
  124.2 0.7 copy-done.3
  124.9 0.0 all-to-all-done.4.shares_ref
  124.9 0.0 copy-start.2
  124.9 0.0 copy-start.4
  124.9 3.8 %shard_map.84 = (bf16[8,80,256]{2,1,0:T(8,128)(2,1)S(1)}, bf16[8,80,256]{2,1,0:T(8,128)(2,1)S(1)}) custom-call(bf16[32,32,128]{2,1,0:T(8,128)(2,1)S(1)} %all-to-all-done.4.shares_ref, f32[2,3,128]{2,1,0:T(4,128)} %get-tuple-element.38.scale_ref, bf16[384,4096]{1,0:T(8,128)(2,1)S(1)} %get-tuple-element.31.matrix_ref, bf16[256,4096]{1,0:T(8,128)(2,1)} %protos_ref.3, ...), custom_call_target="tpu_custom_call" | custom-call | flops 805306368 | bytes 3145728 | tf_op jit(solution)/shard_map/pallas_call | solution.py:35
  128.7 0.0 copy-start.5
  128.7 0.0 copy-start.6
  128.7 3.1 %collective-permute-start.1 = (bf16[8,80,256]{2,1,0:T(8,128)(2,1)S(1)}, bf16[8,80,256]{2,1,0:T(8,128)(2,1)S(1)}, u32[]{:S(2)}, u32[]{:S(2)}) collective-permute-start(bf16[8,80,256]{2,1,0:T(8,128)(2,1)S(1)} %get-tuple-element.40), channel_id=1, source_target_pairs={{0,1},{1,0},{2,3},{3,2},{4,5},{5,4},{6,7},{7,6},{8,9},{9,8},{10,11... | collective-permute-start | bytes 983048 | tf_op jit(solution)/shard_map/ppermute | solution.py:504
  131.9 1.2 collective-permute-done.1.came_ref
  133.1 0.0 copy-done.2
  133.1 0.0 copy-done.4
  133.1 0.4 shard_map.85
  133.5 22.5 %all_to_all.34.back_ref = bf16[8,152,256]{2,1,0:T(8,128)(2,1)S(1)} all-to-all(bf16[8,152,256]{2,1,0:T(8,128)(2,1)S(1)} %shard_map.85), channel_id=1, replica_groups={{0,2,4,6,8,10,12,14},{1,3,5,7,9,11,13,15},{16,18,20,22,24,26,28,30},{17..., dimensions={0} | all-to-all | bytes 1245184 | tf_op jit(solution)/shard_map/all_to_all | solution.py:509
  156.0 0.0 copy-done.5
  156.0 0.0 copy-done.6
  156.0 1.0 shard_map.86
Async XLA Ops:
  27.6 30.4 %copy-start = (bf16[16,126,256]{2,1,0:T(8,128)(2,1)}, bf16[16,126,256]{2,1,0:T(8,128)(2,1)S(1)}, u32[]{:S(2)}) copy-start(bf16[16,126,256]{2,1,0:T(8,128)(2,1)S(1)} %all-gather.1.gathered_ref) | copy-start | bytes 3096580
  76.6 17.4 %copy-start.1 = (bf16[16,48,128]{2,1,0:T(8,128)(2,1)}, bf16[16,48,128]{2,1,0:T(8,128)(2,1)S(1)}, u32[]{:S(2)}) copy-start(bf16[16,48,128]{2,1,0:T(8,128)(2,1)S(1)} %all_to_all.31.shares_ref) | copy-start | bytes 589828
  108.2 16.7 %all-to-all-start.4 = ((bf16[32,32,128]{2,1,0:T(8,128)(2,1)}), bf16[32,32,128]{2,1,0:T(8,128)(2,1)S(1)}, u32[]{:S(2)}, u32[]{:S(2)}) async-start(bf16[32,32,128]{2,1,0:T(8,128)(2,1)} %get-tuple-element.34), calls=%async_computation.4 | async-start | bytes 524288 | tf_op jit(solution)/shard_map/all_to_all | solution.py:488
  120.5 3.7 %collective-permute-start = (bf16[8,80,256]{2,1,0:T(8,128)(2,1)}, bf16[8,80,256]{2,1,0:T(8,128)(2,1)S(1)}, u32[]{:S(2)}, u32[]{:S(2)}) collective-permute-start(bf16[8,80,256]{2,1,0:T(8,128)(2,1)} %get-tuple-element.36), channel_id=1, source_target_pairs={{0,1},{1,0},{2,3},{3,2},{4,5},{5,4},{6,7},{7,6},{8,9},{9,8},{10,11... | collective-permute-start | bytes 983048 | tf_op jit(solution)/shard_map/ppermute | solution.py:487
  124.2 0.7 copy-start.3
  124.9 8.2 %copy-start.2 = (bf16[8,80,256]{2,1,0:T(8,128)(2,1)S(1)}, bf16[8,80,256]{2,1,0:T(8,128)(2,1)}, u32[]{:S(2)}) copy-start(bf16[8,80,256]{2,1,0:T(8,128)(2,1)} %get-tuple-element.41.student_own_ref) | copy-start | bytes 983044
  124.9 8.2 %copy-start.4 = (bf16[8,80,256]{2,1,0:T(8,128)(2,1)S(1)}, bf16[8,80,256]{2,1,0:T(8,128)(2,1)}, u32[]{:S(2)}) copy-start(bf16[8,80,256]{2,1,0:T(8,128)(2,1)} %copy-done.3) | copy-start | bytes 983044
  128.7 27.3 %copy-start.5 = (bf16[80,256]{1,0:T(8,128)(2,1)S(1)}, bf16[80,256]{1,0:T(8,128)(2,1)}, u32[]{:S(2)}) copy-start(bf16[80,256]{1,0:T(8,128)(2,1)} %get-tuple-element.43.picked_ref) | copy-start | bytes 122884
  128.7 27.3 %copy-start.6 = (s32[1,256]{1,0:T(1,128)S(1)}, s32[1,256]{1,0:T(1,128)}, u32[]{:S(2)}) copy-start(s32[1,256]{1,0:T(1,128)} %order_ref.3) | copy-start | bytes 3076
  128.7 4.4 %collective-permute-start.1 = (bf16[8,80,256]{2,1,0:T(8,128)(2,1)S(1)}, bf16[8,80,256]{2,1,0:T(8,128)(2,1)S(1)}, u32[]{:S(2)}, u32[]{:S(2)}) collective-permute-start(bf16[8,80,256]{2,1,0:T(8,128)(2,1)S(1)} %get-tuple-element.40), channel_id=1, source_target_pairs={{0,1},{1,0},{2,3},{3,2},{4,5},{5,4},{6,7},{7,6},{8,9},{9,8},{10,11... | collective-permute-start | bytes 983048 | tf_op jit(solution)/shard_map/ppermute | solution.py:504
